TPU v7x, 32 devices: a whole 2x2x4 slice. The times are simulated.
32 devices in a mesh: dp: 16 (over z, x, core), mp: 2 (over y).
Axes of the slice: x: 2, y: 2, z: 4, core: 2. Of those that a mesh axis runs over, the one named last changes fastest.
Arguments:
- image_tokens: bfloat16 [65536, 768], P('dp'), may hold values from -6 to 6
- norm1_gain: bfloat16 [768], replicated, may hold values from 0.5 to 1.5
- norm1_shift: bfloat16 [768], replicated, may hold values from -4 to 4
- qkv_weight: bfloat16 [3, 768, 768], P(None, None, 'mp'), may hold values from -0.21875 to 0.21875
- qv_bias: bfloat16 [2, 768], P(None, 'mp'), may hold values from -4 to 4
- rel_rows: bfloat16 [27, 64], replicated, may hold values from -2 to 2
- rel_cols: bfloat16 [27, 64], replicated, may hold values from -2 to 2
- proj_weight: bfloat16 [768, 768], P('mp'), may hold values from -0.875 to 0.875
- proj_bias: bfloat16 [768], replicated, may hold values from -4 to 4
- norm2_gain: bfloat16 [768], replicated, may hold values from 0.5 to 1.5
- norm2_shift: bfloat16 [768], replicated, may hold values from -4 to 4
- fc1_weight: bfloat16 [768, 3072], P(None, 'mp'), may hold values from -0.21875 to 0.21875
- fc1_bias: bfloat16 [3072], P('mp'), may hold values from -4 to 4
- fc2_weight: bfloat16 [3072, 768], P('mp'), may hold values from -0.109375 to 0.109375
- fc2_bias: bfloat16 [768], replicated, may hold values from -4 to 4
- out_cotangent: bfloat16 [65536, 768], P(('dp', 'mp')), may hold values from -6 to 6
Outputs:
- block_out: bfloat16 [65536, 768], P(('dp', 'mp'))
- input_grad: bfloat16 [65536, 768], P(('dp', 'mp'))
- norm1_gain_grad: float32 [768], replicated
- norm1_shift_grad: float32 [768], replicated
- qkv_weight_grad: float32 [3, 768, 768], P(None, None, 'mp')
- qv_bias_grad: float32 [2, 768], P(None, 'mp')
- rel_rows_grad: float32 [27, 64], replicated
- rel_cols_grad: float32 [27, 64], replicated
- proj_weight_grad: float32 [768, 768], P('mp')
- proj_bias_grad: float32 [768], replicated
- norm2_gain_grad: float32 [768], replicated
- norm2_shift_grad: float32 [768], replicated
- fc1_weight_grad: float32 [768, 3072], P(None, 'mp')
- fc1_bias_grad: float32 [3072], P('mp')
- fc2_weight_grad: float32 [3072, 768], P('mp')
- fc2_bias_grad: float32 [768], replicated
All inputs are finite; a program needn't handle non-finite values.
Results may differ from a plain program's by a relative error of at most 0.017.
Values may be sent and summed in bfloat16 or wider, within the bound.
A program may use at most 320 MiB of HBM per device.

v0:
```python
from functools import partial

import jax
import jax.numpy as jnp
from jax import lax
from jax.sharding import PartitionSpec as P

HD = 64
WIN = 14
SIDE = 64
NWIN = 5
PAD = 70
RELS = 27


EPSILON = 1e-06
PRECISE = lax.Precision.HIGHEST


def norm_rows_of(values):
    average = jnp.mean(values, axis=-1, keepdims=True)
    centred = values - average
    inverse = lax.rsqrt(jnp.mean(centred * centred, axis=-1, keepdims=True) + EPSILON)
    return (centred * inverse, inverse)


def norm_back(upstream, scaled, inverse, gain_vec):
    scaled_up = upstream * gain_vec
    first_mean = jnp.mean(scaled_up, axis=-1, keepdims=True)
    second_mean = jnp.mean(scaled_up * scaled, axis=-1, keepdims=True)
    input_term = inverse * (scaled_up - first_mean - scaled * second_mean)
    return (input_term, jnp.sum(upstream * scaled, axis=0), jnp.sum(upstream, axis=0))


def offsets_onehot():
    coords = jnp.arange(WIN, dtype=jnp.int32)
    offset_index = coords[:, None] - coords[None, :] + WIN - 1
    targets = jnp.arange(RELS, dtype=jnp.int32)
    return (offset_index[:, :, None] == targets[None, None, :]).astype(jnp.float32)


def key_spread():
    keys = jnp.arange(WIN * WIN, dtype=jnp.int32)
    coords = jnp.arange(WIN, dtype=jnp.int32)
    high_part = (coords[:, None] == (keys // WIN)[None, :]).astype(jnp.float32)
    wide_part = (coords[:, None] == (keys % WIN)[None, :]).astype(jnp.float32)
    return jnp.concatenate([high_part, wide_part], axis=0)


def to_windows(token_rows, images):
    channels = token_rows.shape[-1]
    layout = token_rows.reshape(images, SIDE, SIDE, channels)
    layout = jnp.pad(layout, ((0, 0), (0, PAD - SIDE), (0, PAD - SIDE), (0, 0)))
    layout = layout.reshape(images, NWIN, WIN, NWIN, WIN, channels).transpose(0, 1, 3, 2, 4, 5)
    return layout.reshape(images * NWIN, NWIN, WIN * WIN, channels)


def from_windows(blocks, images):
    channels = blocks.shape[-1]
    layout = blocks.reshape(images, NWIN, NWIN, WIN, WIN, channels).transpose(0, 1, 3, 2, 4, 5)
    layout = layout.reshape(images, PAD, PAD, channels)[:, :SIDE, :SIDE]
    return layout.reshape(images * SIDE * SIDE, channels)


def window_scores(queries, key_rows, rows_table, cols_table, spread_table):
    length = queries.shape[0]
    head_count = queries.shape[-1] // HD
    query_heads = queries.reshape(length, WIN * WIN, head_count, HD)
    key_heads = key_rows.reshape(length, WIN * WIN, head_count, HD)
    base = jnp.einsum(
        "nthe,nshe->nhts", query_heads, key_heads, preferred_element_type=jnp.float32
    ) * HD ** (-0.5)
    query_grid = queries.reshape(length, WIN, WIN, head_count, HD)
    along_high = jnp.einsum(
        "nyxhe,yke->nhyxk", query_grid, rows_table, preferred_element_type=jnp.float32
    )
    along_wide = jnp.einsum(
        "nyxhe,xke->nhyxk", query_grid, cols_table, preferred_element_type=jnp.float32
    )
    along = jnp.concatenate([along_high, along_wide], axis=-1).reshape(
        length, head_count, WIN * WIN, 2 * WIN
    )
    relative = jnp.einsum("nhtc,cs->nhts", along, spread_table, precision=PRECISE)
    return base + relative


def attend_rows(rows_table, cols_table, spread_table, window_block):
    queries, key_rows, values = window_block
    length = queries.shape[0]
    head_count = queries.shape[-1] // HD
    scores = window_scores(queries, key_rows, rows_table, cols_table, spread_table)
    row_peak = jnp.max(scores, axis=-1, keepdims=True)
    log_total = row_peak + jnp.log(jnp.sum(jnp.exp(scores - row_peak), axis=-1, keepdims=True))
    probabilities = jnp.exp(scores - log_total).astype(jnp.bfloat16)
    value_heads = values.reshape(length, WIN * WIN, head_count, HD)
    context = jnp.einsum(
        "nhts,nshe->nthe", probabilities, value_heads, preferred_element_type=jnp.float32
    )
    context = context.astype(jnp.bfloat16).reshape(length, WIN * WIN, head_count * HD)
    return (context, log_total[..., 0])


def attend_back(rows_table, cols_table, spread_table, window_block):
    queries, key_rows, values, log_total, upstream = window_block
    length = queries.shape[0]
    head_count = queries.shape[-1] // HD
    score_scale = HD ** (-0.5)
    scores = window_scores(queries, key_rows, rows_table, cols_table, spread_table)
    probabilities = jnp.exp(scores - log_total[..., None])
    query_heads = queries.reshape(length, WIN * WIN, head_count, HD)
    key_heads = key_rows.reshape(length, WIN * WIN, head_count, HD)
    value_heads = values.reshape(length, WIN * WIN, head_count, HD)
    upstream_heads = upstream.reshape(length, WIN * WIN, head_count, HD)
    prob_grad = jnp.einsum(
        "nthe,nshe->nhts", upstream_heads, value_heads, preferred_element_type=jnp.float32
    )
    row_total = jnp.sum(prob_grad * probabilities, axis=-1, keepdims=True)
    score_grad = (probabilities * (prob_grad - row_total)).astype(jnp.bfloat16)
    value_grad = jnp.einsum(
        "nhts,nthe->nshe",
        probabilities.astype(jnp.bfloat16),
        upstream_heads,
        preferred_element_type=jnp.float32,
    )
    key_grad = (
        jnp.einsum("nhts,nthe->nshe", score_grad, query_heads, preferred_element_type=jnp.float32)
        * score_scale
    )
    query_grad = (
        jnp.einsum("nhts,nshe->nthe", score_grad, key_heads, preferred_element_type=jnp.float32)
        * score_scale
    )
    both_sums = jnp.einsum(
        "nhts,cs->nhtc",
        score_grad,
        spread_table.astype(jnp.bfloat16),
        preferred_element_type=jnp.float32,
    )
    high_grad = both_sums[..., :WIN].reshape(length, head_count, WIN, WIN, WIN)
    wide_grad = both_sums[..., WIN:].reshape(length, head_count, WIN, WIN, WIN)
    rows_wide = rows_table.astype(jnp.float32)
    cols_wide = cols_table.astype(jnp.float32)
    query_grad = query_grad.reshape(length, WIN, WIN, head_count, HD)
    query_grad = query_grad + jnp.einsum(
        "nhyxk,yke->nyxhe", high_grad, rows_wide, precision=PRECISE
    )
    query_grad = query_grad + jnp.einsum(
        "nhyxk,xke->nyxhe", wide_grad, cols_wide, precision=PRECISE
    )
    query_wide = queries.astype(jnp.float32).reshape(length, WIN, WIN, head_count, HD)
    rows_part = jnp.einsum("nhyxk,nyxhe->yke", high_grad, query_wide, precision=PRECISE)
    cols_part = jnp.einsum("nhyxk,nyxhe->xke", wide_grad, query_wide, precision=PRECISE)
    inner = head_count * HD
    return (
        query_grad.reshape(length, WIN * WIN, inner).astype(jnp.bfloat16),
        key_grad.reshape(length, WIN * WIN, inner).astype(jnp.bfloat16),
        value_grad.reshape(length, WIN * WIN, inner).astype(jnp.bfloat16),
        rows_part,
        cols_part,
    )


def on_device(
    image_tokens,
    norm1_gain,
    norm1_shift,
    qkv_weight,
    qv_bias,
    rel_rows,
    rel_cols,
    proj_weight,
    proj_bias,
    norm2_gain,
    norm2_shift,
    fc1_weight,
    fc1_bias,
    fc2_weight,
    fc2_bias,
    out_cotangent,
):
    total_rows = image_tokens.shape[0]
    images = total_rows // (SIDE * SIDE)
    pieces = lax.axis_size("mp")
    own_rows = total_rows // pieces
    offset = lax.axis_index("mp") * own_rows
    inputs = image_tokens.astype(jnp.float32)
    scaled_one, inverse_one = norm_rows_of(inputs)
    gain_one = norm1_gain.astype(jnp.float32)
    normed_one = (scaled_one * gain_one + norm1_shift.astype(jnp.float32)).astype(jnp.bfloat16)
    windows = to_windows(normed_one, images)
    projected = jnp.einsum(
        "bntd,kde->kbnte", windows, qkv_weight, preferred_element_type=jnp.float32
    )
    bias_wide = qv_bias.astype(jnp.float32)
    bias_rows = jnp.stack([bias_wide[0], jnp.zeros_like(bias_wide[0]), bias_wide[1]])
    qkv_low = (projected + bias_rows[:, None, None, None, :]).astype(jnp.bfloat16)
    queries, key_rows, values = (qkv_low[0], qkv_low[1], qkv_low[2])
    onehot = offsets_onehot()
    spread_table = key_spread()
    rows_table = jnp.einsum(
        "yki,ie->yke", onehot, rel_rows.astype(jnp.float32), precision=PRECISE
    ).astype(jnp.bfloat16)
    cols_table = jnp.einsum(
        "yki,ie->yke", onehot, rel_cols.astype(jnp.float32), precision=PRECISE
    ).astype(jnp.bfloat16)
    context, log_total = lax.map(
        partial(attend_rows, rows_table, cols_table, spread_table), (queries, key_rows, values)
    )
    context_rows = from_windows(context, images)
    piece = context_rows
    attn_half = lax.psum_scatter(
        jnp.dot(piece, proj_weight, preferred_element_type=jnp.float32).astype(jnp.bfloat16),
        "mp",
        scatter_dimension=0,
        tiled=True,
    ).astype(jnp.float32)
    inputs_half = lax.dynamic_slice_in_dim(inputs, offset, own_rows, 0)
    middle = inputs_half + (attn_half + proj_bias.astype(jnp.float32))
    scaled_two, inverse_two = norm_rows_of(middle)
    gain_two = norm2_gain.astype(jnp.float32)
    normed_two = (scaled_two * gain_two + norm2_shift.astype(jnp.float32)).astype(jnp.bfloat16)
    cot_half = out_cotangent.astype(jnp.float32)
    fc2_bias_grad = jnp.sum(cot_half, axis=0)
    normed_full = lax.all_gather(normed_two, "mp", axis=0, tiled=True)
    pre_gelu = jnp.dot(
        normed_full, fc1_weight, preferred_element_type=jnp.float32
    ) + fc1_bias.astype(jnp.float32)
    hidden = jax.nn.gelu(pre_gelu, approximate=False).astype(jnp.bfloat16)
    piece = hidden
    mlp_half = lax.psum_scatter(
        jnp.dot(piece, fc2_weight, preferred_element_type=jnp.float32).astype(jnp.bfloat16),
        "mp",
        scatter_dimension=0,
        tiled=True,
    ).astype(jnp.float32)
    block_out = (middle + (mlp_half + fc2_bias.astype(jnp.float32))).astype(jnp.bfloat16)
    cot_full = lax.all_gather(out_cotangent, "mp", axis=0, tiled=True)
    fc2_grad = jnp.dot(hidden.T, cot_full, preferred_element_type=jnp.float32)
    hidden_grad = jnp.dot(cot_full, fc2_weight.T, preferred_element_type=jnp.float32)
    _, gelu_pull = jax.vjp(partial(jax.nn.gelu, approximate=False), pre_gelu)
    pre_grad = gelu_pull(hidden_grad)[0].astype(jnp.bfloat16)
    fc1_grad = jnp.dot(normed_full.T, pre_grad, preferred_element_type=jnp.float32)
    fc1_bias_grad = jnp.sum(pre_grad, axis=0, dtype=jnp.float32)
    piece = pre_grad
    norm_two_grad = lax.psum_scatter(
        jnp.dot(piece, fc1_weight.T, preferred_element_type=jnp.float32).astype(jnp.bfloat16),
        "mp",
        scatter_dimension=0,
        tiled=True,
    ).astype(jnp.float32)
    middle_back, gain_two_grad, shift_two_grad = norm_back(
        norm_two_grad, scaled_two, inverse_two, gain_two
    )
    middle_grad = cot_half + middle_back
    resid_low = middle_grad.astype(jnp.bfloat16)
    proj_bias_grad = jnp.sum(resid_low, axis=0, dtype=jnp.float32)
    resid_full = lax.all_gather(resid_low, "mp", axis=0, tiled=True)
    proj_grad = jnp.dot(context_rows.T, resid_full, preferred_element_type=jnp.float32)
    context_grad = jnp.dot(resid_full, proj_weight.T, preferred_element_type=jnp.float32).astype(
        jnp.bfloat16
    )
    upstream = to_windows(context_grad, images)
    query_grad, key_grad, value_grad, rows_parts, cols_parts = lax.map(
        partial(attend_back, rows_table, cols_table, spread_table),
        (queries, key_rows, values, log_total, upstream),
    )
    rows_grad = jnp.einsum("yki,yke->ie", onehot, jnp.sum(rows_parts, axis=0), precision=PRECISE)
    cols_grad = jnp.einsum("yki,yke->ie", onehot, jnp.sum(cols_parts, axis=0), precision=PRECISE)
    qv_grad = jnp.stack(
        [
            jnp.sum(query_grad, axis=(0, 1, 2), dtype=jnp.float32),
            jnp.sum(value_grad, axis=(0, 1, 2), dtype=jnp.float32),
        ]
    )
    stacked = jnp.stack([query_grad, key_grad, value_grad])
    qkv_rows = jax.vmap(lambda member: from_windows(member, images))(stacked)
    qkv_grad = jnp.einsum("rd,kre->kde", normed_one, qkv_rows, preferred_element_type=jnp.float32)
    piece = qkv_rows
    norm_one_grad = lax.psum_scatter(
        jnp.einsum("kre,kde->rd", piece, qkv_weight, preferred_element_type=jnp.float32).astype(
            jnp.bfloat16
        ),
        "mp",
        scatter_dimension=0,
        tiled=True,
    ).astype(jnp.float32)
    scaled_half = lax.dynamic_slice_in_dim(scaled_one, offset, own_rows, 0)
    inverse_half = lax.dynamic_slice_in_dim(inverse_one, offset, own_rows, 0)
    input_back, gain_one_grad, shift_one_grad = norm_back(
        norm_one_grad, scaled_half, inverse_half, gain_one
    )
    input_grad = (middle_grad + input_back).astype(jnp.bfloat16)
    shared = lax.psum(
        (
            gain_one_grad,
            shift_one_grad,
            rows_grad,
            cols_grad,
            proj_bias_grad,
            gain_two_grad,
            shift_two_grad,
            fc2_bias_grad,
        ),
        ("dp", "mp"),
    )
    qkv_grad, qv_grad, proj_grad, fc1_grad, fc1_bias_grad, fc2_grad = lax.psum(
        (qkv_grad, qv_grad, proj_grad, fc1_grad, fc1_bias_grad, fc2_grad), "dp"
    )
    return (
        block_out,
        input_grad,
        shared[0],
        shared[1],
        qkv_grad,
        qv_grad,
        shared[2],
        shared[3],
        proj_grad,
        shared[4],
        shared[5],
        shared[6],
        fc1_grad,
        fc1_bias_grad,
        fc2_grad,
        shared[7],
    )


def solution(mesh):
    in_specs = (
        P("dp", None),
        P(),
        P(),
        P(None, None, "mp"),
        P(None, "mp"),
        P(),
        P(),
        P("mp", None),
        P(),
        P(),
        P(),
        P(None, "mp"),
        P("mp"),
        P("mp", None),
        P(),
        P(("dp", "mp"), None),
    )
    out_specs = (
        P(("dp", "mp"), None),
        P(("dp", "mp"), None),
        P(),
        P(),
        P(None, None, "mp"),
        P(None, "mp"),
        P(),
        P(),
        P("mp", None),
        P(),
        P(),
        P(),
        P(None, "mp"),
        P("mp"),
        P("mp", None),
        P(),
    )
    return jax.shard_map(
        on_device, mesh=mesh, in_specs=in_specs, out_specs=out_specs, check_vma=False
    )
```

profile of v0, /device:TPU:0, one launch (start us, length us, event | category | flops | bytes accessed | tf_op | source)
XLA Modules:
  0.0 1952.3 jit_solution(10539157736485201429)
XLA Ops:
  26.7 11.5 reshape.301
  45.9 11.4 reshape.320
  57.5 13.5 fusion.57
  95.7 175.2 %while.31 = (s32[]{:T(128)}, bf16[5,5,196,384]{3,2,1,0:T(8,128)(2,1)}, f32[5,5,6,196]{3,2,1,0:T(8,128)}, bf16[5,5,196,384]{2,3,1,0:T(8,128)(2,1)}, bf16[5,5,196,...) while((s32[]{:T(128)}, ...), condition=%wide.region_5.6_spmd, body=%wide.region_2.5_spmd.sunk | while | flops 711944512 | bytes 52994464 | solution.py:206
  298.3 8.3 convert_element_type.184
  306.6 71.5 %reduce-scatter.5.cloned.1.call-done = bf16[2048,768]{1,0:T(8,128)(2,1)} async-done(((bf16[4096,768]{1,0:T(8,128)(2,1)}), bf16[2048,768]{1,0:T(8,128)(2,1)}) %reduce-scatter.5.cloned.1.call-update) | async-done | bytes 3145744 | tf_op jit(solution)/shard_map/reduce_scatter | solution.py:211
  389.1 79.7 %all-gather.4.cloned.1.call-done = bf16[4096,768]{1,0:T(8,128)(2,1)} async-done(((bf16[2048,768]{1,0:T(8,128)(2,1)}), bf16[4096,768]{1,0:T(8,128)(2,1)}) %all-gather.4.cloned.1.call-update) | async-done | bytes 6291472 | tf_op jit(solution)/shard_map/all_gather | solution.py:224
  468.8 65.7 %multiply_convert_fusion.2 = (bf16[4096,1536]{1,0:T(8,128)(2,1)}, f32[4096,1536]{1,0:T(8,128)}, f32[4096,1536]{1,0:T(8,128)}) fusion(f32[1536]{0:T(1024)S(1)} %convert_element_type.199, bf16[4096,768]{1,0:T(8,128)(2,1)} %all-gather.4.cloned.1.call-done, bf16[768,1536]{1,0:T(8,128)(2,1)S(1)} %copy-done), kind=kOutput, calls=%fused_computation.69 | convolution fusion | flops 10078912512 | bytes 71571456 | tf_op jit(solution)/shard_map/dot_general | solution.py:225
  534.5 16.3 all-gather.6.cloned.1.call-done
  550.8 31.5 %convert_reduce_fusion = (f32[1536]{0:T(1024)}, bf16[4096,1536]{1,0:T(8,128)(2,1)}) fusion(f32[4096,1536]{1,0:T(8,128)} %get-tuple-element.444, bf16[4096,768]{1,0:T(8,128)(2,1)} %all-gather.6.cloned.1.call-done, bf16[1536,768]{1,0:T(8,128)(2,1)} %param.33, f32[4096,1536]{1,0:T(8,128)} %get-tuple-element.468, f32[1536]{0:T(1024)S(1)} %convert_element_type.199), kind=kOutput, calls=%fused_computation.67 | convolution fusion | flops 9770629120 | bytes 71577600 | tf_op jit(solution)/shard_map/dot_general | solution.py:239
  582.3 14.8 convolution_convert_fusion
  598.8 14.6 convolution_convert_fusion.1
  614.1 60.3 %reduce-scatter.9.cloned.1.call-done = bf16[2048,768]{1,0:T(8,128)(2,1)} async-done(((bf16[4096,768]{1,0:T(8,128)(2,1)}), bf16[2048,768]{1,0:T(8,128)(2,1)}) %reduce-scatter.9.cloned.1.call-update) | async-done | bytes 3145744 | tf_op jit(solution)/shard_map/reduce_scatter | solution.py:245
  680.2 73.4 %reduce-scatter.7.cloned.1.call-done = bf16[2048,768]{1,0:T(8,128)(2,1)} async-done(((bf16[4096,768]{1,0:T(8,128)(2,1)}), bf16[2048,768]{1,0:T(8,128)(2,1)}) %reduce-scatter.7.cloned.1.call-update) | async-done | bytes 3145744 | tf_op jit(solution)/shard_map/reduce_scatter | solution.py:230
  753.6 13.1 convert_reduce_fusion.7
  766.9 16.5 fusion.101
  783.4 16.7 fusion.100
  800.1 47.2 %all-gather.8.cloned.1.call-done = bf16[4096,768]{1,0:T(8,128)(2,1)} async-done(((bf16[2048,768]{1,0:T(8,128)(2,1)}), bf16[4096,768]{1,0:T(8,128)(2,1)}) %all-gather.8.cloned.1.call-update) | async-done | bytes 6291472 | tf_op jit(solution)/shard_map/all_gather | solution.py:257
  878.4 580.6 %while.32 = (s32[]{:T(128)}, bf16[5,5,196,384]{3,2,1,0:T(8,128)(2,1)}, bf16[5,5,196,384]{3,2,1,0:T(8,128)(2,1)}, bf16[5,5,196,384]{2,3,1,0:T(8,128)(2,1)}, f32[5...) while((s32[]{:T(128)}, ...), condition=%wide.region_15.16_spmd, body=%wide.region_13.15_spmd.sunk | while | flops 1476485632 | bytes 166287792 | solution.py:263
  920.7 8.4 subtract_exponential_fusion.2
  1030.7 8.4 subtract_exponential_fusion.2
  1140.8 8.4 subtract_exponential_fusion.2
  1250.9 8.4 subtract_exponential_fusion.2
  1361.0 8.4 subtract_exponential_fusion.2
  1499.2 17.9 reshape.309
  1517.2 8.6 slice.44
  1525.8 13.1 fusion.77
  1546.8 14.2 bitcast_convert_fusion
  1567.5 64.9 %all-reduce.3 = (f32[2,384]{1,0:T(2,128)}, f32[1536]{0:T(1024)}) all-reduce(f32[2,384]{1,0:T(2,128)S(1)} %pad_maximum_fusion.3, f32[1536]{0:T(1024)S(1)} %copy-done.44), channel_id=1, replica_groups=mesh['dp'=16,'mp'=2] {'dp'}, use_global_device_ids=true, to_apply=%region_26.27 | all-reduce | flops 2304 | bytes 18432 | tf_op jit(solution)/shard_map/psum | solution.py:306
  1633.1 171.7 %all-reduce.7.cloned.1.call-done = (f32[3,768,384]{1,2,0:T(8,128)}, f32[384,768]{1,0:T(8,128)}, f32[768,1536]{1,0:T(8,128)}, f32[1536,768]{1,0:T(8,128)}) async-done(((f32[3,768,384]{1,2,0:T(8,128)}, f32[384,768]{1,0:T(8,128)}, f32[768,1536]{1,0:T(8,128)}, f32[1536,768]{1,0:T(8,128)}), (f32[3,768,384]{1,2,0:T(8,128)}, f32[384,768]{1,0:T(8,128)}, f32[768,1536]{1,0:T(8,128)}, ...) | async-done | bytes 14155792 | tf_op jit(solution)/shard_map/psum | solution.py:306
  1810.0 74.3 %reduce-scatter.11.cloned.1.call-done = bf16[2048,768]{1,0:T(8,128)(2,1)} async-done(((bf16[4096,768]{1,0:T(8,128)(2,1)}), bf16[2048,768]{1,0:T(8,128)(2,1)}) %reduce-scatter.11.cloned.1.call-update) | async-done | bytes 3145744 | tf_op jit(solution)/shard_map/reduce_scatter | solution.py:279
  1889.3 40.8 %all-reduce.2 = (f32[768]{0:T(1024)}, f32[768]{0:T(1024)}, f32[27,64]{1,0:T(8,128)}, f32[27,64]{1,0:T(8,128)}, f32[768]{0:T(1024)}, /*index=5*/f32[768]{0:T(1024)}, f32[768]{0:T(1024)}, f32[768]{0:T(1024)}) all-reduce(f32[768]{0:T(1024)S(1)} %get-tuple-element.368, ...), channel_id=1, replica_groups=mesh['dp'=16,'mp'=2] {'dp','mp'}, use_global_device_ids=true, to_apply=%region_20.21 | all-reduce | flops 8064 | bytes 64512 | tf_op jit(solution)/shard_map/psum | solution.py:293
  (614 shorter events, 891.9 us)
Async XLA Ops:
  7.2 461.6 %copy-start = (bf16[768,1536]{1,0:T(8,128)(2,1)S(1)}, bf16[768,1536]{1,0:T(8,128)(2,1)}, u32[]{:S(2)}) copy-start(bf16[768,1536]{1,0:T(8,128)(2,1)} %param.31) | copy-start | bytes 7077892
  7.2 370.9 %reduce-scatter.5.cloned.1.call-start = ((), (), s32[]{:S(2)}) async-start(), calls=%async_computation.4 | async-start | bytes 9437184 | tf_op jit(solution)/shard_map/reduce_scatter | solution.py:211
  7.3 85.2 %copy-start.31 = (s32[14,14]{0,1:T(8,128)}, s32[14,14]{0,1:T(8,128)S(1)}, u32[]{:S(2)}) copy-start(s32[14,14]{0,1:T(8,128)S(1)} %subtract_add_fusion) | copy-start | bytes 2356
  45.9 11.4 copy-start.45
  270.9 11.1 copy-start.19
  270.9 11.1 copy-start.21
  271.0 11.1 copy-start.23
  298.2 170.6 %all-gather.4.cloned.1.call-start = ((), (), s32[]{:S(2)}) async-start(), calls=%async_computation.5 | async-start | bytes 9437184 | tf_op jit(solution)/shard_map/all_gather | solution.py:224
  306.6 77.0 %copy-start.38 = (f32[768]{0:T(1024)}, f32[768]{0:T(1024)S(1)}, u32[]{:S(2)}) copy-start(f32[768]{0:T(1024)S(1)} %convert_element_type.196) | copy-start | bytes 9220
  388.3 162.6 %all-gather.6.cloned.1.call-start = ((), (), s32[]{:S(2)}) async-start(), calls=%async_computation.7 | async-start | bytes 9437184 | tf_op jit(solution)/shard_map/all_gather | solution.py:237
  389.0 285.4 %reduce-scatter.9.cloned.1.call-start = ((), (), s32[]{:S(2)}) async-start(), calls=%async_computation.8 | async-start | bytes 9437184 | tf_op jit(solution)/shard_map/reduce_scatter | solution.py:245
  597.2 156.4 %reduce-scatter.7.cloned.1.call-start = ((), (), s32[]{:S(2)}) async-start(), calls=%async_computation.6 | async-start | bytes 9437184 | tf_op jit(solution)/shard_map/reduce_scatter | solution.py:230
  613.4 61.0 %copy-start.30 = (f32[2048]{0:T(1024)S(1)}, f32[2048]{0:T(1024)}, u32[]{:S(2)}) copy-start(f32[2048]{0:T(1024)} %copy-done.29) | copy-start | bytes 24580
  613.4 61.0 %copy-start.34 = (f32[2048]{0:T(1024)S(1)}, f32[2048]{0:T(1024)}, u32[]{:S(2)}) copy-start(f32[2048]{0:T(1024)} %copy-done.33) | copy-start | bytes 24580
  613.4 61.0 %copy-start.39 = (f32[768]{0:T(1024)S(1)}, f32[768]{0:T(1024)}, u32[]{:S(2)}) copy-start(f32[768]{0:T(1024)} %copy-done.38) | copy-start | bytes 9220
  613.5 233.9 %all-gather.8.cloned.1.call-start = ((), (), s32[]{:S(2)}) async-start(), calls=%async_computation.9 | async-start | bytes 9437184 | tf_op jit(solution)/shard_map/all_gather | solution.py:257
  766.8 1038.0 %all-reduce.7.cloned.1.call-start = ((), (), s32[]{:S(2)}) async-start(), calls=%async_computation.11 | async-start | bytes 28311552 | tf_op jit(solution)/shard_map/psum | solution.py:306
  783.4 64.0 %copy-start.56 = (bf16[384,768]{1,0:T(8,128)(2,1)S(1)}, bf16[384,768]{1,0:T(8,128)(2,1)}, u32[]{:S(2)}) copy-start(bf16[384,768]{1,0:T(8,128)(2,1)} %param.27) | copy-start | bytes 1769476
  867.4 11.0 copy-start.20
  867.4 11.0 copy-start.22
  867.4 11.0 copy-start.24
  867.4 11.0 copy-start.26
  1525.8 13.1 copy-start.18
  1545.3 339.0 %reduce-scatter.11.cloned.1.call-start = ((), (), s32[]{:S(2)}) async-start(), calls=%async_computation.10 | async-start | bytes 9437184 | tf_op jit(solution)/shard_map/reduce_scatter | solution.py:279
  1561.1 71.3 %copy-start.32 = (s32[14,14]{0,1:T(8,128)S(1)}, s32[14,14]{0,1:T(8,128)}, u32[]{:S(2)}) copy-start(s32[14,14]{0,1:T(8,128)} %copy-done.31) | copy-start | bytes 2356
  1564.0 320.3 %copy-start.37 = (f32[768]{0:T(1024)S(1)}, f32[768]{0:T(1024)}, u32[]{:S(2)}) copy-start(f32[768]{0:T(1024)} %copy-done.36) | copy-start | bytes 9220
  1810.0 79.3 %copy-start.40 = (f32[768]{0:T(1024)S(1)}, f32[768]{0:T(1024)}, u32[]{:S(2)}) copy-start(f32[768]{0:T(1024)} %get-tuple-element.370) | copy-start | bytes 9220
  1810.0 79.3 %copy-start.41 = (f32[768]{0:T(1024)S(1)}, f32[768]{0:T(1024)}, u32[]{:S(2)}) copy-start(f32[768]{0:T(1024)} %get-tuple-element.374) | copy-start | bytes 9220
  1810.0 79.3 %copy-start.42 = (f32[768]{0:T(1024)S(1)}, f32[768]{0:T(1024)}, u32[]{:S(2)}) copy-start(f32[768]{0:T(1024)} %get-tuple-element.440) | copy-start | bytes 9220
  1810.0 79.4 %copy-start.43 = (f32[768]{0:T(1024)S(1)}, f32[768]{0:T(1024)}, u32[]{:S(2)}) copy-start(f32[768]{0:T(1024)} %get-tuple-element.463) | copy-start | bytes 9220
  1810.0 120.2 %dynamic-slice-start = ((f32[4096]{0:T(1024)}, s32[]{:T(128)}), f32[2048]{0:T(1024)S(1)}, s32[]{:S(2)}) async-start(f32[4096]{0:T(1024)} %copy-done.35, s32[]{:T(128)} %select_n.25), calls=%async_computation.18 | async-start | bytes 16896 | tf_op jit(solution)/shard_map/dynamic-slice
  1884.3 55.1 %slice-start.4 = ((s8[4718592]{0:T(1024)(128)(4,1)}), s8[524288]{0:T(1024)(128)(4,1)S(1)}, s32[]{:S(2)}) async-start(s8[4718592]{0:T(1024)(128)(4,1)} %bitcast.309), calls=%async_computation.16 | async-start | bytes 1048576
  (98 other events, 485.0 us)
Sparse Core Ops, SparseCore 0:
  298.3 79.7 reduce-scatter.4
  388.4 80.3 all-gather.3
  470.4 80.3 all-gather.5
  597.3 77.0 reduce-scatter.8
  676.5 77.0 reduce-scatter.6
  766.9 80.3 all-gather.7
  1545.5 259.3 all-reduce.6
  1807.2 77.0 reduce-scatter.10
where the time goes:
time: 1960 us; the launch traced here: 1950 us
  local copies, waits for them, and re-layouts  603 us (31%)
  waiting for transfers between devices  595 us (30%)
  matrix products  500 us (26%)
  blocking collectives  106 us (5%)
  other arithmetic  101 us (5%)
  loops' own time  31.8 us (2%)
    psum x1, waiting for transfers between devices, on_device(): lax.psum((qkv_grad, qv_grad, proj_grad, fc1_grad, fc1_bias_grad, fc2_grad...  172 us
    reshape x15, local copies, waits for them, and re-layouts, attend_back(): wide_grad = both_sums[..., WIN:].reshape(length, head_count, WIN, WIN, WIN)  86.5 us
    all_gather x1, waiting for transfers between devices, on_device(): normed_full = lax.all_gather(normed_two, 'mp', axis=0, tiled=True)  79.7 us
    reduce_scatter x1, waiting for transfers between devices, on_device(): lax.psum_scatter(jnp.einsum('kre,kde->rd', piece, qkv_weight, preferred_e...  74.3 us
    reduce_scatter x1, waiting for transfers between devices, on_device(): lax.psum_scatter(jnp.dot(piece, fc2_weight, preferred_element_type=jnp.fl...  73.4 us
    dynamic_slice x40, local copies, waits for them, and re-layouts, on_device(): lax.map(partial(attend_rows, rows_table, cols_table, spread_table), (quer...  71.7 us
    reduce_scatter x1, waiting for transfers between devices, on_device(): lax.psum_scatter(jnp.dot(piece, proj_weight, preferred_element_type=jnp.f...  71.5 us
    dot_general x10, matrix products, window_scores(): jnp.einsum('nhtc,cs->nhts', along, spread_table, precision=PRECISE)  69.8 us
  transfers between devices with their start and end apart: 8, of which 8 were waited for; matrix products, arithmetic and copies ran while one was open for 8% of the time, Pallas kernels for 0%

commit v1 on v0

v1 whole, which is shorter than its diff:
```python
import jax
import jax.numpy as jnp
import numpy as np
from jax import lax
from jax.experimental import pallas as pl
from jax.experimental.pallas import tpu as pltpu
from jax.sharding import PartitionSpec as P

D = 768
HEADS = 12
HD = 64
FF = 3072
WIN = 14
SIDE = 64
NWIN = 5
RELS = 27
EPSILON = 1e-06
F32 = jnp.float32
BF = jnp.bfloat16

SLOTS = 256
KEYS = WIN * 16
PAIR = 2 * SIDE
GREL = 80
OWN = SIDE * SIDE // 2

NN = (((1,), (0,)), ((), ()))
NT = (((1,), (1,)), ((), ()))
TN = (((0,), (0,)), ((), ()))


def dot(left, right, dims=NN):
    return lax.dot_general(left, right, dims, preferred_element_type=F32)


def params(limit=60):
    return pltpu.CompilerParams(vmem_limit_bytes=limit * 2**20)


def whole(shape):
    return pl.BlockSpec(shape, lambda *_: (0,) * len(shape), pipeline_mode=pl.Buffered(1))


STARTS = np.array([[0, 14, 28], [42, 28, 56]], np.int32)


def pair_tables(place):
    block = np.zeros((2, 24), np.int32)
    valid = np.zeros((2, 24), np.int32)
    local = np.zeros((2, 24), np.int32)
    owned = np.zeros((2, 24), np.int32)
    band_of = np.zeros((2, 16), np.int32)
    step_of = np.zeros((2, 16), np.int32)
    for m in range(2):
        for s in range(3):
            for t in range(7):
                row = STARTS[m, s] + 2 * t
                at = s * 8 + t
                block[m, at] = min(row // 2, 31)
                valid[m, at] = row < SIDE
                if 32 * m <= row < 32 * m + 32:
                    local[m, at] = (row - 32 * m) // 2
                    owned[m, at] = 1
                    band_of[m, local[m, at]] = s
                    step_of[m, local[m, at]] = t
            block[m, s * 8 + 7] = block[m, s * 8 + 6]
    pick = lambda table: jnp.where(place == 0, jnp.asarray(table[0]), jnp.asarray(table[1]))
    return tuple(pick(t) for t in (block, valid, local, owned, band_of, step_of))


def spread_rows():
    table = np.zeros((NWIN, 2, 16, PAIR), np.float32)
    for w in range(NWIN):
        for r in range(2):
            for j in range(WIN):
                if WIN * w + j < SIDE:
                    table[w, r, j, r * SIDE + WIN * w + j] = 1
    return table.reshape(NWIN * 32, PAIR)


def rel_order():
    rows = np.full(GREL, -1)
    for m in range(21):
        rows[m] = 26 - (m + 6)
        rows[24 + m] = 26 - m
    cols = np.full(GREL, -1)
    for m in range(RELS):
        cols[48 + m] = 26 - m
    return rows, cols


def rel_onehots():
    rows, cols = rel_order()
    high = (rows[:, None] == np.arange(RELS)[None, :]).astype(np.float32)
    wide = (cols[:, None] == np.arange(RELS)[None, :]).astype(np.float32)
    return high, wide


def norm_parts(values):
    average = jnp.mean(values, axis=-1, keepdims=True)
    centred = values - average
    inverse = lax.rsqrt(jnp.mean(centred * centred, axis=-1, keepdims=True) + EPSILON)
    return centred * inverse, inverse


def window_kernel(block, valid, x, gain, shift, spread, out):
    at = pl.program_id(0) * 8 + pl.program_id(1)

    @pl.when(valid[at] == 1)
    def _():
        scaled, _ = norm_parts(x[...].astype(F32))
        normed = (scaled * gain[...] + shift[...]).astype(BF)
        out[...] = dot(spread[...], normed).astype(BF).reshape(1, NWIN, 32, D)

    @pl.when(valid[at] == 0)
    def _():
        out[...] = jnp.zeros_like(out)


def windows_of(x, gain, shift, spread, block, valid):
    return pl.pallas_call(
        window_kernel,
        grid_spec=pltpu.PrefetchScalarGridSpec(
            num_scalar_prefetch=2,
            grid=(3, 8),
            in_specs=[
                pl.BlockSpec((PAIR, D), lambda s, t, block, valid: (block[s * 8 + t], 0)),
                whole((1, D)),
                whole((1, D)),
                whole((NWIN * 32, PAIR)),
            ],
            out_specs=pl.BlockSpec((1, NWIN, 32, D), lambda s, t, block, valid: (s, 0, t, 0)),
        ),
        out_shape=jax.ShapeDtypeStruct((3, NWIN, SLOTS, D), BF),
        compiler_params=params(),
    )(block, valid, x, gain, shift, spread)


def shift_masks(lanes_from):
    lane = lax.broadcasted_iota(jnp.int32, (1, 128), 1) + lanes_from
    high = lane // 16
    row_shift = jnp.where(lane < 128, 7 - high, jnp.maximum(13 - high, 0))
    col_shift = jnp.maximum(13 - lane % 16, 0)
    return row_shift, col_shift


def skew(table, shift, bits):
    size = table.shape[0]
    for bit in bits:
        moved = pltpu.roll(table, size - bit, 0)
        table = jnp.where((shift & bit) != 0, moved, table)
    return table


def unskew(table, shift, bits):
    for bit in bits:
        moved = pltpu.roll(table, bit, 0)
        table = jnp.where((shift & bit) != 0, moved, table)
    return table


def attend_kernel(x, weights, biases, rel_even, rel_odd, q_out, k_out, v_out, p_out, ctx_out, xt_out, vt):
    band = pl.program_id(0)
    block = x[...].reshape(SLOTS, D)
    xt_out[...] = block.T
    q_out[...] = (dot(block, weights[0]) + biases[0:1, :]).astype(BF).reshape(1, 1, SLOTS, D)
    k_out[...] = dot(block, weights[1]).astype(BF).reshape(1, 1, SLOTS, D)
    values = (dot(block, weights[2]) + biases[2:3, :]).astype(BF)
    v_out[...] = values.reshape(1, 1, SLOTS, D)
    vt[...] = values.T

    def pair_step(pair, lanes):
        cols = pl.ds(pl.multiple_of(pair * 128, 128), 128)
        queries = q_out[0, 0, 0:lanes, cols]
        keys = k_out[0, 0, 0:KEYS, cols]
        even = lax.broadcasted_iota(jnp.int32, (1, 128), 1) < HD
        contexts = []
        for odd in range(2):
            rel = rel_odd if odd else rel_even
            kept = jnp.where(even != (odd == 1), keys, jnp.zeros_like(keys))
            raw = dot(jnp.concatenate([kept, rel[...]], axis=0), queries, NT)
            parts = []
            for tile in range(lanes // 128):
                row_shift, col_shift = shift_masks(tile * 128)
                raw_t = raw[:, tile * 128 : tile * 128 + 128]
                base = raw_t[0:KEYS]
                high = skew(raw_t[KEYS + 24 * tile : KEYS + 24 * tile + 24], row_shift, (4, 2, 1))[0:16]
                wide = skew(raw_t[KEYS + 48 : KEYS + 80], col_shift, (8, 4, 2, 1))[0:16]
                place = lax.broadcasted_iota(jnp.int32, (16, 128), 0)
                wide = jnp.where(place < WIN, wide, -1e30)
                scores = base.reshape(WIN, 16, 128) + wide[None] + high[0:WIN][:, None, :]
                scores = scores.reshape(KEYS, 128)
                peak = jnp.max(scores, axis=0, keepdims=True)
                grown = jnp.exp(scores - peak)
                total = jnp.sum(grown, axis=0, keepdims=True)
                parts.append((grown * (1.0 / total)).astype(BF))
            probs = parts[0] if len(parts) == 1 else jnp.concatenate(parts, axis=1)
            p_out[0, 0, pair * 2 + odd, :, 0:lanes] = probs
            rows = pl.ds(pl.multiple_of(pair * 128 + odd * HD, HD), HD)
            contexts.append(dot(vt[rows, 0:KEYS], probs).astype(BF))
        ctx_out[0, 0, 0:lanes, cols] = jnp.concatenate(contexts, axis=0).T

    @pl.when(band < 2)
    def _():
        for pair in range(HEADS // 2):
            pair_step(pair, 256)

    @pl.when(band == 2)
    def _():
        for pair in range(HEADS // 2):
            pair_step(pair, 128)


def attend(x, weights, biases, rel_even, rel_odd):
    one = pl.BlockSpec((1, 1, SLOTS, D), lambda s, w: (s, w, 0, 0))
    full = jax.ShapeDtypeStruct((3, NWIN, SLOTS, D), BF)
    return pl.pallas_call(
        attend_kernel,
        grid=(3, NWIN),
        in_specs=[one, whole((3, D, D)), whole((8, D)), whole((GREL, 128)), whole((GREL, 128))],
        out_specs=[
            one,
            one,
            one,
            pl.BlockSpec((1, 1, HEADS, KEYS, SLOTS), lambda s, w: (s, w, 0, 0, 0)),
            one,
            pl.BlockSpec((D, SLOTS), lambda s, w: (0, s * NWIN + w)),
        ],
        out_shape=[
            full,
            full,
            full,
            jax.ShapeDtypeStruct((3, NWIN, HEADS, KEYS, SLOTS), BF),
            full,
            jax.ShapeDtypeStruct((D, 3 * NWIN * SLOTS), BF),
        ],
        scratch_shapes=[pltpu.VMEM((D, SLOTS), BF)],
        compiler_params=params(),
    )(x, weights, biases, rel_even, rel_odd)


def middle_kernel(
    band_of, step_of, offset, ctx_a, ctx_b, x, cot, proj, bias, gain, shift, gather,
    middle, normed, normed_t, cot_t, ctx_out,
):
    pieces = [dot(gather[...], c[...].reshape(NWIN * 32, D)).astype(BF) for c in (ctx_a, ctx_b)]
    context = jnp.concatenate(pieces, axis=0)
    ctx_out[...] = context
    value = x[...].astype(F32) + (dot(context, proj[...]) + bias[...])
    middle[...] = value
    scaled, _ = norm_parts(value)
    low = (scaled * gain[...] + shift[...]).astype(BF)
    normed[...] = low
    normed_t[...] = low.T
    cot_t[...] = cot[...].T


def middle_of(ctx, x, cot, proj, bias, gain, shift, gather, band_of, step_of, offset):
    rows = 2 * PAIR
    at = lambda k: lambda i, band_of, step_of, offset: (band_of[2 * i + k], 0, step_of[2 * i + k], 0)
    row_block = pl.BlockSpec((rows, D), lambda i, *_: (i, 0))
    col_block = pl.BlockSpec((D, rows), lambda i, *_: (0, i))
    return pl.pallas_call(
        middle_kernel,
        grid_spec=pltpu.PrefetchScalarGridSpec(
            num_scalar_prefetch=3,
            grid=(OWN // rows,),
            in_specs=[
                pl.BlockSpec((1, NWIN, 32, D), at(0)),
                pl.BlockSpec((1, NWIN, 32, D), at(1)),
                pl.BlockSpec((rows, D), lambda i, band_of, step_of, offset: (offset[0] + i, 0)),
                row_block,
                whole((D, D)),
                whole((1, D)),
                whole((1, D)),
                whole((1, D)),
                whole((PAIR, NWIN * 32)),
            ],
            out_specs=[row_block, row_block, col_block, col_block, row_block],
        ),
        out_shape=[
            jax.ShapeDtypeStruct((OWN, D), F32),
            jax.ShapeDtypeStruct((OWN, D), BF),
            jax.ShapeDtypeStruct((D, OWN), BF),
            jax.ShapeDtypeStruct((D, OWN), BF),
            jax.ShapeDtypeStruct((OWN, D), BF),
        ],
        compiler_params=params(),
    )(band_of, step_of, offset, ctx, ctx, x, cot, proj, bias, gain, shift, gather)


CHUNK = 512
CHUNKS = FF // CHUNK


def feed_kernel(
    normed, normed_t, cot, cot_t, one_a, one_b, bias, two_a, two_b,
    forward, back, one_own, one_other, two_own, two_other, sums, one, two, hidden, grads,
):
    step = pl.program_id(0)

    @pl.when(step == 0)
    def _():
        forward[...] = jnp.zeros_like(forward)
        back[...] = jnp.zeros_like(back)

    @pl.when(step < CHUNKS // 2)
    def _():
        one[...] = one_a[...]
        two[...] = two_a[...]

    @pl.when(step >= CHUNKS // 2)
    def _():
        one[...] = one_b[...]
        two[...] = two_b[...]

    total = jnp.zeros((1, CHUNK), F32)
    for t in range(OWN // 512):
        rows = slice(t * 512, t * 512 + 512)
        pre = dot(normed[rows, :], one[...]) + bias[...]
        phi = 0.5 * (1.0 + lax.erf(pre * 0.7071067811865476))
        slope = phi + pre * (jnp.exp(-0.5 * pre * pre) * 0.3989422804014327)
        low = (pre * phi).astype(BF)
        grad = (dot(cot[rows, :], two[...], NT) * slope).astype(BF)
        hidden[rows, :] = low
        grads[rows, :] = grad
        total += jnp.sum(grad.astype(F32), axis=0, keepdims=True)
        forward[rows, :] += dot(low, two[...])
        back[rows, :] += dot(grad, one[...], NT)
    sums[...] = total

    one_grad = dot(normed_t[...], grads[...]).astype(BF)
    two_grad = dot(cot_t[...], hidden[...]).astype(BF)

    @pl.when(step < CHUNKS // 2)
    def _():
        one_own[...] = one_grad
        two_own[...] = two_grad

    @pl.when(step >= CHUNKS // 2)
    def _():
        one_other[...] = one_grad
        two_other[...] = two_grad


def feed(normed, normed_t, cot, cot_t, one_a, one_b, bias, two_a, two_b):
    half = CHUNKS // 2
    own = lambda j: jnp.minimum(j, half - 1)
    other = lambda j: jnp.maximum(j - half, 0)
    grad_shape = jax.ShapeDtypeStruct((D, FF // 2), BF)
    wide_own = pl.BlockSpec((D, CHUNK), lambda j: (0, own(j)))
    wide_other = pl.BlockSpec((D, CHUNK), lambda j: (0, other(j)))
    return pl.pallas_call(
        feed_kernel,
        grid=(CHUNKS,),
        in_specs=[
            whole((OWN, D)),
            whole((D, OWN)),
            whole((OWN, D)),
            whole((D, OWN)),
            wide_own,
            wide_other,
            pl.BlockSpec((1, CHUNK), lambda j: (0, j)),
            pl.BlockSpec((CHUNK, D), lambda j: (own(j), 0)),
            pl.BlockSpec((CHUNK, D), lambda j: (other(j), 0)),
        ],
        out_specs=[
            pl.BlockSpec((OWN, D), lambda j: (0, 0)),
            pl.BlockSpec((OWN, D), lambda j: (0, 0)),
            wide_own,
            wide_other,
            wide_own,
            wide_other,
            pl.BlockSpec((1, CHUNK), lambda j: (0, j)),
        ],
        out_shape=[
            jax.ShapeDtypeStruct((OWN, D), F32),
            jax.ShapeDtypeStruct((OWN, D), F32),
            grad_shape,
            grad_shape,
            grad_shape,
            grad_shape,
            jax.ShapeDtypeStruct((1, FF), F32),
        ],
        scratch_shapes=[
            pltpu.VMEM((D, CHUNK), BF),
            pltpu.VMEM((CHUNK, D), BF),
            pltpu.VMEM((OWN, CHUNK), BF),
            pltpu.VMEM((OWN, CHUNK), BF),
        ],
        compiler_params=params(62),
    )(normed, normed_t, cot, cot_t, one_a, one_b, bias, two_a, two_b)


def add_row(sums, row, values):
    sums[row : row + 1, :] += jnp.sum(values, axis=0, keepdims=True)


def resid_kernel(middle, forward, back, cot, context, proj, bias, gain, block_out, grad_out, ctx_grad, proj_grad, sums):
    step = pl.program_id(0)

    @pl.when(step == 0)
    def _():
        proj_grad[...] = jnp.zeros_like(proj_grad)
        sums[...] = jnp.zeros_like(sums)

    value = middle[...]
    block_out[...] = (value + (forward[...] + bias[...])).astype(BF)
    scaled, inverse = norm_parts(value)
    upstream = back[...]
    scaled_up = upstream * gain[...]
    first = jnp.mean(scaled_up, axis=-1, keepdims=True)
    second = jnp.mean(scaled_up * scaled, axis=-1, keepdims=True)
    cotangent = cot[...].astype(F32)
    grad = cotangent + inverse * (scaled_up - first - scaled * second)
    grad_out[...] = grad
    low = grad.astype(BF)
    ctx_grad[...] = dot(low, proj[...], NT).astype(BF)
    proj_grad[...] += dot(context[...], low, TN)
    add_row(sums, 0, upstream * scaled)
    add_row(sums, 1, upstream)
    add_row(sums, 2, cotangent)
    add_row(sums, 3, low.astype(F32))


def resid_of(middle, forward, back, cot, context, proj, bias, gain):
    rows = 512
    row_block = pl.BlockSpec((rows, D), lambda i: (i, 0))
    return pl.pallas_call(
        resid_kernel,
        grid=(OWN // rows,),
        in_specs=[row_block] * 5 + [whole((D, D)), whole((1, D)), whole((1, D))],
        out_specs=[
            row_block,
            row_block,
            row_block,
            pl.BlockSpec((D, D), lambda i: (0, 0)),
            pl.BlockSpec((8, D), lambda i: (0, 0)),
        ],
        out_shape=[
            jax.ShapeDtypeStruct((OWN, D), BF),
            jax.ShapeDtypeStruct((OWN, D), F32),
            jax.ShapeDtypeStruct((OWN, D), BF),
            jax.ShapeDtypeStruct((D, D), F32),
            jax.ShapeDtypeStruct((8, D), F32),
        ],
        compiler_params=params(),
    )(middle, forward, back, cot, context, proj, bias, gain)


def attend_back_kernel(
    local, owned, q, k, v, p, ctx_grad, spread, rel_even, rel_odd, fold,
    dq, dk, dv, rel_grad, sums, upstream, kt,
):
    band = pl.program_id(0)
    window = pl.program_id(1)

    @pl.when((band == 0) & (window == 0))
    def _():
        rel_grad[...] = jnp.zeros_like(rel_grad)
        sums[...] = jnp.zeros_like(sums)

    @pl.when(window == 0)
    def _():
        for t in range(7):
            at = band * 8 + t
            rows = pl.ds(pl.multiple_of(local[at] * PAIR, PAIR), PAIR)
            moved = dot(spread[...], ctx_grad[rows, :])
            moved = moved * owned[at].astype(F32)
            upstream[:, 32 * t : 32 * t + 32, :] = moved.astype(BF).reshape(NWIN, 32, D)
        upstream[:, 224:256, :] = jnp.zeros((NWIN, 32, D), BF)

    kt[...] = k[...].reshape(SLOTS, D).T
    even = lax.broadcasted_iota(jnp.int32, (1, 128), 1) < HD

    def pair_step(pair, lanes):
        cols = pl.ds(pl.multiple_of(pair * 128, 128), 128)
        queries = q[0, 0, 0:lanes, cols]
        values = v[0, 0, 0:KEYS, cols]
        ups = upstream[window, 0:lanes, cols]
        dvs, dks, dqs, drs = [], [], [], []
        for odd in range(2):
            rel = rel_odd if odd else rel_even
            kept = jnp.where(even != (odd == 1), values, jnp.zeros_like(values))
            prob_grad = dot(kept, ups, NT)
            probs_low = p[0, 0, pair * 2 + odd, :, 0:lanes]
            probs = probs_low.astype(F32)
            total = jnp.sum(prob_grad * probs, axis=0, keepdims=True)
            score_grad = (probs * (prob_grad - total)).astype(BF)
            dvs.append(dot(probs_low, ups))
            rows = pl.ds(pl.multiple_of(pair * 128 + odd * HD, HD), HD)
            left = jnp.concatenate([kt[rows, 0:KEYS], fold[...]], axis=0)
            both = dot(left, score_grad)
            tables = []
            zero8 = jnp.zeros((8, 128), F32)
            zero24 = jnp.zeros((24, 128), F32)
            zero16 = jnp.zeros((16, 128), F32)
            for tile in range(lanes // 128):
                row_shift, col_shift = shift_masks(tile * 128)
                part = both[:, tile * 128 : tile * 128 + 128]
                high = jnp.concatenate([part[HD : HD + 16], zero8], axis=0)
                wide = jnp.concatenate([part[HD + 16 : HD + 32], zero16], axis=0)
                high = unskew(high, row_shift, (1, 2, 4))
                wide = unskew(wide, col_shift, (1, 2, 4, 8))
                stack = [high, zero24, wide] if tile == 0 else [zero24, high, wide]
                tables.append(jnp.concatenate(stack, axis=0))
            table = tables[0] if len(tables) == 1 else jnp.concatenate(tables, axis=1)
            table = table.astype(BF)
            grads = dot(jnp.concatenate([score_grad, table], axis=0), queries)
            dks.append(grads[0:KEYS])
            drs.append(grads[KEYS:])
            from_rel = dot(rel[...], table, TN)
            dqs.append(both[0:HD] + from_rel[odd * HD : odd * HD + HD])
        dv[0, 0, 0:KEYS, cols] = jnp.where(even, dvs[0], dvs[1]).astype(BF)
        dk[0, 0, 0:KEYS, cols] = (jnp.where(even, dks[0], dks[1]) * HD ** (-0.5)).astype(BF)
        rel_grad[...] += jnp.where(even, drs[0], drs[1])
        dq[0, 0, 0:lanes, cols] = jnp.concatenate(dqs, axis=0).astype(BF).T

    dk[0, 0, KEYS:, :] = jnp.zeros((SLOTS - KEYS, D), BF)
    dv[0, 0, KEYS:, :] = jnp.zeros((SLOTS - KEYS, D), BF)

    @pl.when(band < 2)
    def _():
        for pair in range(HEADS // 2):
            pair_step(pair, 256)

    @pl.when(band == 2)
    def _():
        for pair in range(HEADS // 2):
            pair_step(pair, 128)
        dq[0, 0, 128:, :] = jnp.zeros((128, D), BF)

    sums[0:1, :] += jnp.sum(dq[...].reshape(SLOTS, D).astype(F32), axis=0, keepdims=True)
    sums[1:2, :] += jnp.sum(dv[...].reshape(SLOTS, D).astype(F32), axis=0, keepdims=True)


def fold_table():
    table = np.zeros((32, WIN, 16), np.float32)
    for k in range(WIN):
        for l in range(WIN):
            table[k, k, l] = 1
            table[16 + l, k, l] = 1
    return table.reshape(32, KEYS)


def attend_back(q, k, v, p, ctx_grad, spread, rel_even, rel_odd, fold, local, owned):
    one = pl.BlockSpec((1, 1, SLOTS, D), lambda s, w, *_: (s, w, 0, 0))
    full = jax.ShapeDtypeStruct((3, NWIN, SLOTS, D), BF)
    return pl.pallas_call(
        attend_back_kernel,
        grid_spec=pltpu.PrefetchScalarGridSpec(
            num_scalar_prefetch=2,
            grid=(3, NWIN),
            in_specs=[
                one,
                one,
                one,
                pl.BlockSpec((1, 1, HEADS, KEYS, SLOTS), lambda s, w, *_: (s, w, 0, 0, 0)),
                whole((OWN, D)),
                whole((NWIN * 32, PAIR)),
                whole((GREL, 128)),
                whole((GREL, 128)),
                whole((32, KEYS)),
            ],
            out_specs=[
                one,
                one,
                one,
                pl.BlockSpec((GREL, 128), lambda s, w, *_: (0, 0)),
                pl.BlockSpec((8, D), lambda s, w, *_: (0, 0)),
            ],
            scratch_shapes=[pltpu.VMEM((NWIN, SLOTS, D), BF), pltpu.VMEM((D, SLOTS), BF)],
        ),
        out_shape=[
            full,
            full,
            full,
            jax.ShapeDtypeStruct((GREL, 128), F32),
            jax.ShapeDtypeStruct((8, D), F32),
        ],
        compiler_params=params(),
    )(local, owned, q, k, v, p, ctx_grad, spread, rel_even, rel_odd, fold)


def norm_grad_kernel(dq, dk, dv, weights, gather, out):
    flat = lambda ref: ref[...].reshape(NWIN * 32, D)
    total = dot(flat(dq), weights[0], NT) + dot(flat(dk), weights[1], NT) + dot(flat(dv), weights[2], NT)
    out[...] = dot(gather[...], total.astype(BF)).astype(BF).reshape(1, PAIR, D)


def norm_grad(dq, dk, dv, weights, gather):
    one = pl.BlockSpec((1, NWIN, 32, D), lambda s, t: (s, 0, t, 0))
    return pl.pallas_call(
        norm_grad_kernel,
        grid=(3, 7),
        in_specs=[one, one, one, whole((3, D, D)), whole((PAIR, NWIN * 32))],
        out_specs=pl.BlockSpec((1, PAIR, D), lambda s, t: (s, t, 0)),
        out_shape=jax.ShapeDtypeStruct((3, 7 * PAIR, D), BF),
        compiler_params=params(),
    )(dq, dk, dv, weights, gather)


def qkv_grad_kernel(xt, d, own, other):
    total = dot(xt[...], d[...]).astype(BF)
    own[...] = total[:, : D // 2]
    other[...] = total[:, D // 2 :]


def qkv_grad(xt, d):
    rows = 3 * NWIN * SLOTS
    shape = jax.ShapeDtypeStruct((D, D // 2), BF)
    block = pl.BlockSpec((D // 3, D // 2), lambda i: (i, 0))
    return pl.pallas_call(
        qkv_grad_kernel,
        grid=(3,),
        in_specs=[pl.BlockSpec((D // 3, rows), lambda i: (i, 0)), whole((rows, D))],
        out_specs=[block, block],
        out_shape=[shape, shape],
        compiler_params=params(),
    )(xt, d)


def input_kernel(offset, x, middle_grad, up_a, up_b, gain, out, sums):
    step = pl.program_id(0)

    @pl.when(step == 0)
    def _():
        sums[...] = jnp.zeros_like(sums)

    scaled, inverse = norm_parts(x[...].astype(F32))
    upstream = up_a[...].astype(F32) + up_b[...].astype(F32)
    scaled_up = upstream * gain[...]
    first = jnp.mean(scaled_up, axis=-1, keepdims=True)
    second = jnp.mean(scaled_up * scaled, axis=-1, keepdims=True)
    out[...] = (middle_grad[...] + inverse * (scaled_up - first - scaled * second)).astype(BF)
    add_row(sums, 0, upstream * scaled)
    add_row(sums, 1, upstream)


def input_of(x, middle_grad, up_a, up_b, gain, offset):
    rows = 256
    row_block = pl.BlockSpec((rows, D), lambda i, *_: (i, 0))
    return pl.pallas_call(
        input_kernel,
        grid_spec=pltpu.PrefetchScalarGridSpec(
            num_scalar_prefetch=1,
            grid=(OWN // rows,),
            in_specs=[
                pl.BlockSpec((rows, D), lambda i, offset: (offset[0] + i, 0)),
                row_block,
                row_block,
                row_block,
                whole((1, D)),
            ],
            out_specs=[row_block, pl.BlockSpec((8, D), lambda i, *_: (0, 0))],
        ),
        out_shape=[jax.ShapeDtypeStruct((OWN, D), BF), jax.ShapeDtypeStruct((8, D), F32)],
        compiler_params=params(),
    )(offset, x, middle_grad, up_a, up_b, gain)


def on_device(
    image_tokens,
    norm1_gain,
    norm1_shift,
    qkv_weight,
    qv_bias,
    rel_rows,
    rel_cols,
    proj_weight,
    proj_bias,
    norm2_gain,
    norm2_shift,
    fc1_weight,
    fc1_bias,
    fc2_weight,
    fc2_bias,
    out_cotangent,
):
    place = lax.axis_index("mp")
    swap = lambda value: lax.ppermute(value, "mp", [(0, 1), (1, 0)])
    block, valid, local, owned, band_of, step_of = pair_tables(place)
    offset = (place * (OWN // (2 * PAIR))).astype(jnp.int32).reshape(1)
    row = lambda vector: vector.astype(F32).reshape(1, -1)
    spread = jnp.asarray(spread_rows(), BF)
    gather = jnp.asarray(spread_rows().T, BF)
    fold = jnp.asarray(fold_table(), BF)
    high_hot, wide_hot = (jnp.asarray(t, F32) for t in rel_onehots())
    precise = lax.Precision.HIGHEST
    table = jnp.dot(high_hot, rel_rows.astype(F32), precision=precise)
    table += jnp.dot(wide_hot, rel_cols.astype(F32), precision=precise)
    table = table.astype(BF)
    blank = jnp.zeros_like(table)
    rel_even = jnp.concatenate([table, blank], axis=1)
    rel_odd = jnp.concatenate([blank, table], axis=1)

    scale = jnp.asarray([1.0, HD ** (-0.5), 1.0], BF).reshape(3, 1, 1)
    qkv_all = jnp.concatenate([qkv_weight, swap(qkv_weight)], axis=2) * scale
    small = swap((qv_bias, fc1_bias))
    bias_q = jnp.concatenate([qv_bias[0], small[0][0]])
    bias_v = jnp.concatenate([qv_bias[1], small[0][1]])
    biases = jnp.zeros((8, D), F32).at[0].set(bias_q.astype(F32)).at[2].set(bias_v.astype(F32))
    proj_all = jnp.concatenate([proj_weight, swap(proj_weight)], axis=0)
    fc1_other = swap(fc1_weight)
    fc2_other = swap(fc2_weight)
    fc1_bias_all = row(jnp.concatenate([fc1_bias, small[1]]))

    x_windows = windows_of(image_tokens, row(norm1_gain), row(norm1_shift), spread, block, valid)
    q, k, v, p, ctx, xt = attend(x_windows, qkv_all, biases, rel_even, rel_odd)
    middle, normed, normed_t, cot_t, context = middle_of(
        ctx, image_tokens, out_cotangent, proj_all, row(proj_bias), row(norm2_gain), row(norm2_shift),
        gather, band_of, step_of, offset,
    )
    forward, back, one_own, one_other, two_own, two_other, fc1_sums = feed(
        normed, normed_t, out_cotangent, cot_t, fc1_weight, fc1_other, fc1_bias_all, fc2_weight, fc2_other
    )
    block_out, middle_grad, ctx_grad, proj_grad, two_sums = resid_of(
        middle, forward, back, out_cotangent, context, proj_all, row(fc2_bias), row(norm2_gain)
    )
    dq, dk, dv, rel_grad, qv_sums = attend_back(
        q, k, v, p, ctx_grad, spread, rel_even, rel_odd, fold, local, owned
    )
    back_weights = qkv_all * jnp.asarray([1.0, HD**0.5, 1.0], BF).reshape(3, 1, 1)
    up = norm_grad(dq, dk, dv, back_weights, gather)
    flat = lambda value: value.reshape(3 * NWIN * SLOTS, D)
    wgrads = [qkv_grad(xt, flat(value)) for value in (dq, dk, dv)]

    tokens = lambda band, first, count: up[band, first * SIDE : (first + count) * SIDE]
    zeros = lambda count: jnp.zeros((count * SIDE, D), BF)
    sent = jnp.where(place == 0, tokens(2, 4, 10), jnp.concatenate([tokens(1, 0, 4), zeros(6)]))
    taken = swap(sent)
    up_own = jnp.where(
        place == 0,
        jnp.concatenate([tokens(0, 0, 14), tokens(1, 0, 14), tokens(2, 0, 4)]),
        jnp.concatenate([tokens(1, 4, 10), tokens(0, 0, 14), tokens(2, 0, 8)]),
    )
    up_taken = jnp.where(
        place == 0,
        jnp.concatenate([zeros(28), taken[: 4 * SIDE]]),
        jnp.concatenate([taken, zeros(22)]),
    )
    input_grad, one_sums = input_of(
        image_tokens, middle_grad, up_own, up_taken, row(norm1_gain), offset
    )

    rel_grad = rel_grad[:, :HD] + rel_grad[:, HD:]
    rows_grad = jnp.dot(high_hot.T, rel_grad, precision=precise)
    cols_grad = jnp.dot(wide_hot.T, rel_grad, precision=precise)
    shared = lax.psum(
        (one_sums[0], one_sums[1], rows_grad, cols_grad, two_sums[3], two_sums[0], two_sums[1], two_sums[2]),
        ("dp", "mp"),
    )
    half = D // 2
    proj_low = proj_grad.astype(BF)
    others = swap(
        (
            jnp.stack([g[1] for g in wgrads]),
            proj_low[half:],
            one_other,
            two_other,
            qv_sums[0:2, half:],
            fc1_sums[0, FF // 2 :],
        )
    )
    mine = (
        jnp.stack([g[0] for g in wgrads]),
        proj_low[:half],
        one_own,
        two_own,
        qv_sums[0:2, :half],
        fc1_sums[0, : FF // 2],
    )
    sums = lax.psum(tuple(a + b for a, b in zip(mine, others)), "dp")
    qkv_sum, proj_sum, one_sum, two_sum, qv_sum, fc1_bias_sum = sums
    return (
        block_out,
        input_grad,
        shared[0],
        shared[1],
        qkv_sum.astype(F32),
        qv_sum,
        shared[2],
        shared[3],
        proj_sum.astype(F32),
        shared[4],
        shared[5],
        shared[6],
        one_sum.astype(F32),
        fc1_bias_sum,
        two_sum.astype(F32).T,
        shared[7],
    )


def solution(mesh):
    in_specs = (
        P("dp", None),
        P(),
        P(),
        P(None, None, "mp"),
        P(None, "mp"),
        P(),
        P(),
        P("mp", None),
        P(),
        P(),
        P(),
        P(None, "mp"),
        P("mp"),
        P("mp", None),
        P(),
        P(("dp", "mp"), None),
    )
    out_specs = (
        P(("dp", "mp"), None),
        P(("dp", "mp"), None),
        P(),
        P(),
        P(None, None, "mp"),
        P(None, "mp"),
        P(),
        P(),
        P("mp", None),
        P(),
        P(),
        P(),
        P(None, "mp"),
        P("mp"),
        P("mp", None),
        P(),
    )
    return jax.shard_map(
        on_device, mesh=mesh, in_specs=in_specs, out_specs=out_specs, check_vma=False
    )
```

time: 1960 us -> 717 us (0.37)
  local copies, waits for them, and re-layouts: 603 us -> 22.4 us
  matrix products: 500 us -> 2.5 us
  waiting for transfers between devices: 595 us -> 162 us
  Pallas kernels: 0 us -> 360 us
  other arithmetic: 101 us -> 34.8 us
  loops' own time: 31.8 us -> 0 us
    dot_general x106 -> x4, matrix products: 500 us -> 2.5 us  [the longest x1 1 us: on_device(): table += jnp.dot(wide_hot, rel_cols.astype(F32), precision=precise)]
    pallas_call x0 -> x11, Pallas kernels: none -> 360 us  [the longest x1 80.8 us: attend_back(): pl.pallas_call(attend_back_kernel, grid_spec=pltpu.PrefetchScalarGridSpec...]
    reduce_scatter x4 -> x0, waiting for transfers between devices: 279 us -> none  [the longest x1 74.3 us: on_device(): lax.psum_scatter(jnp.einsum('kre,kde->rd', piece, qkv_weight, preferred_e...]
    reshape x52 -> x6, local copies, waits for them, and re-layouts: 257 us -> 7.57 us  [on_device(): row = lambda vector: vector.astype(F32).reshape(1, -1)]
    psum x1, waiting for transfers between devices: 172 us -> 0.01 us  [on_device(): sums = lax.psum(tuple((a + b for a, b in zip(mine, others))), 'dp')]
    ppermute x0 -> x13, waiting for transfers between devices: none -> 162 us  [on_device(): swap = lambda value: lax.ppermute(value, 'mp', [(0, 1), (1, 0)])]
    all_gather x3 -> x0, waiting for transfers between devices: 143 us -> none  [the longest x1 79.7 us: on_device(): normed_full = lax.all_gather(normed_two, 'mp', axis=0, tiled=True)]
    dynamic_slice x40 -> x0, local copies, waits for them, and re-layouts: 71.7 us -> none  [on_device(): lax.map(partial(attend_rows, rows_table, cols_table, spread_table), (quer...]
  transfers between devices with their start and end apart: 8 -> 14, of which waited for: 8 -> 2; matrix products, arithmetic and copies ran while one was open for 8% -> 6% of each run, Pallas kernels for 0% -> 40%
where the time goes in v1:
time: 717 us; the launch traced here: 708 us
  Pallas kernels  360 us (50%)
  waiting for transfers between devices  162 us (23%)
  blocking collectives  97.3 us (14%)
  other arithmetic  34.8 us (5%)
  local copies, waits for them, and re-layouts  22.4 us (3%)
  between operations  14.8 us (2%)
  starting transfers between devices  14.2 us (2%)
    ppermute x13, waiting for transfers between devices, on_device(): swap = lambda value: lax.ppermute(value, 'mp', [(0, 1), (1, 0)])  162 us
    pallas_call x1, Pallas kernels, attend_back(): pl.pallas_call(attend_back_kernel, grid_spec=pltpu.PrefetchScalarGridSpec...  80.8 us
    pallas_call x1, Pallas kernels, feed(): pl.pallas_call(feed_kernel, grid=(CHUNKS,), in_specs=[whole((OWN, D)), wh...  80.4 us
    pallas_call x1, Pallas kernels, attend(): pl.pallas_call(attend_kernel, grid=(3, NWIN), in_specs=[one, whole((3, D,...  71.4 us
    psum x1, blocking collectives, on_device(): sums = lax.psum(tuple((a + b for a, b in zip(mine, others))), 'dp')  58.2 us
    psum x1, blocking collectives, on_device(): lax.psum((one_sums[0], one_sums[1], rows_grad, cols_grad, two_sums[3], tw...  39.1 us
    pallas_call x1, Pallas kernels, norm_grad(): pl.pallas_call(norm_grad_kernel, grid=(3, 7), in_specs=[one, one, one, wh...  36.1 us
    pallas_call x3, Pallas kernels, qkv_grad(): pl.pallas_call(qkv_grad_kernel, grid=(3,), in_specs=[pl.BlockSpec((D // 3...  27.8 us
  transfers between devices with their start and end apart: 14, of which 2 were waited for; matrix products, arithmetic and copies ran while one was open for 6% of the time, Pallas kernels for 40%

profile of v1, /device:TPU:0, one launch (start us, length us, event | category | flops | bytes accessed | tf_op | source)
XLA Modules:
  0.0 708.1 jit_solution(9451770644230236924)
XLA Ops:
  7.2 3.0 collective-permute-start.1
  10.4 1.9 collective-permute-start.2
  12.4 1.9 collective-permute-start.5
  30.2 19.4 %shard_map.450.x = bf16[3,5,256,768]{3,2,1,0:T(8,128)(2,1)} custom-call(s32[24]{0:T(128)} %get-tuple-element.181.block, s32[24]{0:T(128)} %get-tuple-element.180.valid, bf16[4096,768]{1,0:T(8,128)(2,1)} %x.17, f32[1,768]{1,0:T(1,128)} %reshape.211.gain, f32[1,768]{1,0:T(1,128)} %reshape.213.shift, bf16[160,128]{1,0:T(8,128)(2,1)} %constant.119.clone.spread), custom_call_target="tpu_custom_call" | custom-call | tf_op jit(solution)/shard_map/pallas_call | solution.py:121
  50.3 1.4 scatter.14.biases
  51.6 112.9 %collective-permute-done.4 = bf16[1536]{0:T(1024)(128)(2,1)} collective-permute-done((bf16[1536]{0:T(1024)(128)(2,1)}, bf16[1536]{0:T(1024)(128)(2,1)}, u32[]{:S(2)}, u32[]{:S(2)}) %collective-permute-start.4) | collective-permute-done | bytes 3104 | tf_op jit(solution)/shard_map/ppermute | solution.py:681
  165.9 5.2 broadcast_multiply_fusion
  171.1 71.4 %shard_map.451 = (bf16[3,5,256,768]{3,2,1,0:T(8,128)(2,1)}, bf16[3,5,256,768]{3,2,1,0:T(8,128)(2,1)}, bf16[3,5,256,768]{3,2,1,0:T(8,128)(2,1)}, bf16[3,5,12,224,...) custom-call(bf16[3,5,256,768]{3,2,1,0:T(8,128)(2,1)} %shard_map.450.x, ...), custom_call_target="tpu_custom_call" | custom-call | tf_op jit(solution)/shard_map/pallas_call | solution.py:217
  242.5 16.5 %shard_map.452 = (f32[2048,768]{1,0:T(8,128)}, bf16[2048,768]{1,0:T(8,128)(2,1)}, bf16[768,2048]{1,0:T(8,128)(2,1)}, bf16[768,2048]{1,0:T(8,128)(2,1)}, bf16[2048,768]{1,0:T(8,128)(2,1)}) custom-call(s32[16]{0:T(128)} %get-tuple-element.183.band_of, s32[16]{0:T(128)} %get-tuple-element.182.step_of, s32[1]{0:T(128)} %bitcast.offset, ...), custom_call_target="tpu_custom_call" | custom-call | tf_op jit(solution)/shard_map/pallas_call | solution.py:263
  259.1 80.4 %shard_map.453 = (f32[2048,768]{1,0:T(8,128)}, f32[2048,768]{1,0:T(8,128)}, bf16[768,1536]{1,0:T(8,128)(2,1)}, bf16[768,1536]{1,0:T(8,128)(2,1)}, bf16[768,1536]...) custom-call(bf16[2048,768]{1,0:T(8,128)(2,1)} %get-tuple-element.78.normed, ...), custom_call_target="tpu_custom_call" | custom-call | tf_op jit(solution)/shard_map/pallas_call | solution.py:353
  339.9 1.6 collective-permute-start.12
  342.1 16.9 %shard_map.454 = (bf16[2048,768]{1,0:T(8,128)(2,1)}, f32[2048,768]{1,0:T(8,128)}, bf16[2048,768]{1,0:T(8,128)(2,1)}, f32[768,768]{1,0:T(8,128)}, f32[8,768]{1,0:T(8,128)}) custom-call(f32[2048,768]{1,0:T(8,128)} %get-tuple-element.77.middle, f32[2048,768]{1,0:T(8,128)} %get-tuple-element.81.forward, f32[2048,768]{1,0:T(8,128)} %get-tuple-element.82.back, ...), custom_call_target="tpu_custom_call" | custom-call | tf_op jit(solution)/shard_map/pallas_call | solution.py:429
  359.0 80.8 %shard_map.455 = (bf16[3,5,256,768]{3,2,1,0:T(8,128)(2,1)}, bf16[3,5,256,768]{3,2,1,0:T(8,128)(2,1)}, bf16[3,5,256,768]{3,2,1,0:T(8,128)(2,1)}, f32[80,128]{1,0:T(8,128)}, f32[8,768]{1,0:T(8,128)}) custom-call(s32[24]{0:T(128)} %get-tuple-element.179.local, s32[24]{0:T(128)} %get-tuple-element.178.owned, bf16[3,5,256,768]{3,2,1,0:T(8,128)(2,1)} %get-tuple-element.86.q, ...), custom_call_target="tpu_custom_call" | custom-call | tf_op jit(solution)/shard_map/pallas_call | solution.py:549
  439.9 9.1 %shard_map.458 = (bf16[768,384]{1,0:T(8,128)(2,1)}, bf16[768,384]{1,0:T(8,128)(2,1)}) custom-call(bf16[768,3840]{1,0:T(8,128)(2,1)} %get-tuple-element.96.xt, bf16[3840,768]{1,0:T(8,128)(2,1)} %bitcast.34), custom_call_target="tpu_custom_call" | custom-call | tf_op jit(solution)/shard_map/pallas_call | solution.py:613
  449.0 9.1 %shard_map.459 = (bf16[768,384]{1,0:T(8,128)(2,1)}, bf16[768,384]{1,0:T(8,128)(2,1)}) custom-call(bf16[768,3840]{1,0:T(8,128)(2,1)} %get-tuple-element.96.xt, bf16[3840,768]{1,0:T(8,128)(2,1)} %bitcast.35), custom_call_target="tpu_custom_call" | custom-call | tf_op jit(solution)/shard_map/pallas_call | solution.py:613
  458.1 9.5 %shard_map.460 = (bf16[768,384]{1,0:T(8,128)(2,1)}, bf16[768,384]{1,0:T(8,128)(2,1)}) custom-call(bf16[768,3840]{1,0:T(8,128)(2,1)} %get-tuple-element.96.xt, bf16[3840,768]{1,0:T(8,128)(2,1)} %bitcast.36), custom_call_target="tpu_custom_call" | custom-call | tf_op jit(solution)/shard_map/pallas_call | solution.py:613
  467.6 1.5 pad_maximum_fusion
  469.7 1.7 collective-permute-start.9
  471.4 49.0 %collective-permute-done.9 = bf16[384,768]{1,0:T(8,128)(2,1)S(1)} collective-permute-done((bf16[384,768]{1,0:T(8,128)(2,1)S(1)}, bf16[384,768]{1,0:T(8,128)(2,1)S(1)}, u32[]{:S(2)}, u32[]{:S(2)}) %collective-permute-start.9) | collective-permute-done | bytes 589856 | tf_op jit(solution)/shard_map/ppermute | solution.py:681
  521.4 1.6 maximum_add_fusion
  523.0 3.9 add.73
  526.9 1.6 add_bitcast_fusion
  532.1 36.1 %shard_map.456 = bf16[3,896,768]{2,1,0:T(8,128)(2,1)} custom-call(bf16[3,5,256,768]{3,2,1,0:T(8,128)(2,1)} %get-tuple-element.91.dq, bf16[3,5,256,768]{3,2,1,0:T(8,128)(2,1)} %get-tuple-element.92.dk, bf16[3,5,256,768]{3,2,1,0:T(8,128)(2,1)} %get-tuple-element.93.dv, bf16[3,768,768]{2,1,0:T(8,128)(2,1)} %get-tuple-element.170.weights, ...), custom_call_target="tpu_custom_call" | custom-call | tf_op jit(solution)/shard_map/pallas_call | solution.py:593
  569.5 1.6 fusion
  574.5 2.1 maximum_select_fusion.up_a
  577.3 58.2 %all-reduce.7 = (f32[2,384]{1,0:T(2,128)}, f32[1536]{0:T(1024)}) all-reduce(f32[2,384]{1,0:T(2,128)S(1)} %slice_add_fusion.4, f32[1536]{0:T(1024)S(1)} %add.74), channel_id=1, replica_groups=mesh['dp'=16,'mp'=2] {'dp'}, use_global_device_ids=true, to_apply=%region_3.4 | all-reduce | flops 2304 | bytes 18432 | tf_op jit(solution)/shard_map/psum | solution.py:773
  635.6 2.0 pad_select_fusion.up_b
  637.6 11.0 %shard_map.457 = (bf16[2048,768]{1,0:T(8,128)(2,1)}, f32[8,768]{1,0:T(8,128)}) custom-call(s32[1]{0:T(128)} %bitcast.offset, bf16[4096,768]{1,0:T(8,128)(2,1)} %x.17, f32[2048,768]{1,0:T(8,128)} %get-tuple-element.85.middle_grad, bf16[2048,768]{1,0:T(8,128)(2,1)} %maximum_select_fusion.up_a, bf16[2048,768]{1,0:T(8,128)(2,1)} %pad_select_fusion.up_b, ...), custom_call_target="tpu_custom_call" | custom-call | tf_op jit(solution)/shard_map/pallas_call | solution.py:643
  649.5 39.1 %all-reduce.6 = (f32[768]{0:T(1024)}, f32[768]{0:T(1024)}, f32[27,64]{1,0:T(8,128)}, f32[27,64]{1,0:T(8,128)}, f32[768]{0:T(1024)}, /*index=5*/f32[768]{0:T(1024)}, f32[768]{0:T(1024)}, f32[768]{0:T(1024)}) all-reduce(f32[768]{0:T(1024)S(1)} %get-tuple-element.149, ...), channel_id=1, replica_groups=mesh['dp'=16,'mp'=2] {'dp','mp'}, use_global_device_ids=true, to_apply=%region_0.1 | all-reduce | flops 8064 | bytes 64512 | tf_op jit(solution)/shard_map/psum | solution.py:749
  688.5 4.6 convert_element_type.56
  693.2 3.0 copy.55
  696.1 3.6 convert_element_type.53
  (111 shorter events, 31.5 us)
Async XLA Ops:
  7.2 7.2 %copy-start = (bf16[27,64]{1,0:T(8,128)(2,1)S(1)}, bf16[27,64]{1,0:T(8,128)(2,1)}, u32[]{:S(2)}) copy-start(bf16[27,64]{1,0:T(8,128)(2,1)} %param.44) | copy-start | bytes 10372
  7.2 681.3 %all-reduce.11.cloned.1.call-start = ((), (), s32[]{:S(2)}) async-start(), calls=%async_computation | async-start | bytes 14155776 | tf_op jit(solution)/shard_map/psum | solution.py:773
  7.2 42.4 %collective-permute-start.1 = (bf16[2,384]{1,0:T(2,128)(2,1)}, bf16[2,384]{1,0:T(2,128)(2,1)S(1)}, u32[]{:S(2)}, u32[]{:S(2)}) collective-permute-start(bf16[2,384]{1,0:T(2,128)(2,1)} %param.43), channel_id=1, source_target_pairs={{0,1},{1,0},{2,3},{3,2},{4,5},{5,4},{6,7},{7,6},{8,9},{9,8},{10,11... | collective-permute-start | bytes 4616 | tf_op jit(solution)/shard_map/ppermute | solution.py:681
  10.3 155.6 %collective-permute-start = (bf16[3,768,384]{2,1,0:T(8,128)(2,1)}, bf16[3,768,384]{2,1,0:T(8,128)(2,1)}, u32[]{:S(2)}, u32[]{:S(2)}) collective-permute-start(bf16[3,768,384]{2,1,0:T(8,128)(2,1)} %param.42), channel_id=1, source_target_pairs={{0,1},{1,0},{2,3},{3,2},{4,5},{5,4},{6,7},{7,6},{8,9},{9,8},{10,11... | collective-permute-start | bytes 5308424 | tf_op jit(solution)/shard_map/ppermute | solution.py:681
  10.4 155.5 %collective-permute-start.2 = (bf16[384,768]{1,0:T(8,128)(2,1)}, bf16[384,768]{1,0:T(8,128)(2,1)S(1)}, u32[]{:S(2)}, u32[]{:S(2)}) collective-permute-start(bf16[384,768]{1,0:T(8,128)(2,1)} %param.46), channel_id=1, source_target_pairs={{0,1},{1,0},{2,3},{3,2},{4,5},{5,4},{6,7},{7,6},{8,9},{9,8},{10,11... | collective-permute-start | bytes 1769480 | tf_op jit(solution)/shard_map/ppermute | solution.py:681
  12.3 246.7 %collective-permute-start.3 = (bf16[768,1536]{1,0:T(8,128)(2,1)}, bf16[768,1536]{1,0:T(8,128)(2,1)}, u32[]{:S(2)}, u32[]{:S(2)}) collective-permute-start(bf16[768,1536]{1,0:T(8,128)(2,1)} %one_a.1), channel_id=1, source_target_pairs={{0,1},{1,0},{2,3},{3,2},{4,5},{5,4},{6,7},{7,6},{8,9},{9,8},{10,11... | collective-permute-start | bytes 7077896 | tf_op jit(solution)/shard_map/ppermute | solution.py:681
  12.4 246.6 %collective-permute-start.5 = (bf16[1536,768]{1,0:T(8,128)(2,1)}, bf16[1536,768]{1,0:T(8,128)(2,1)}, u32[]{:S(2)}, u32[]{:S(2)}) collective-permute-start(bf16[1536,768]{1,0:T(8,128)(2,1)} %two_a.1), channel_id=1, source_target_pairs={{0,1},{1,0},{2,3},{3,2},{4,5},{5,4},{6,7},{7,6},{8,9},{9,8},{10,11... | collective-permute-start | bytes 7077896 | tf_op jit(solution)/shard_map/ppermute | solution.py:681
  30.2 20.1 %copy-start.20 = (bf16[1,384]{1,0:T(2,128)(2,1)S(1)}, bf16[1,384]{1,0:T(2,128)(2,1)}, u32[]{:S(2)}) copy-start(bf16[1,384]{1,0:T(2,128)(2,1)} %get-tuple-element.174) | copy-start | bytes 2308
  30.2 135.7 %copy-start.8 = (bf16[3,768,384]{2,1,0:T(8,128)(2,1)S(1)}, bf16[3,768,384]{2,1,0:T(8,128)(2,1)}, u32[]{:S(2)}) copy-start(bf16[3,768,384]{2,1,0:T(8,128)(2,1)} %param.42) | copy-start | bytes 5308420
  49.6 114.9 %collective-permute-start.4 = (bf16[1536]{0:T(1024)(128)(2,1)}, bf16[1536]{0:T(1024)(128)(2,1)}, u32[]{:S(2)}, u32[]{:S(2)}) collective-permute-start(bf16[1536]{0:T(1024)(128)(2,1)} %param.51), channel_id=1, source_target_pairs={{0,1},{1,0},{2,3},{3,2},{4,5},{5,4},{6,7},{7,6},{8,9},{9,8},{10,11... | collective-permute-start | bytes 9224 | tf_op jit(solution)/shard_map/ppermute | solution.py:681
  165.9 5.2 copy-start.3
  259.0 82.5 %copy-start.21 = (s32[24]{0:T(128)S(1)}, s32[24]{0:T(128)}, u32[]{:S(2)}) copy-start(s32[24]{0:T(128)} %constant.111.clone) | copy-start | bytes 292
  259.0 82.5 %copy-start.22 = (s32[24]{0:T(128)S(1)}, s32[24]{0:T(128)}, u32[]{:S(2)}) copy-start(s32[24]{0:T(128)} %constant.112.clone) | copy-start | bytes 292
  259.1 82.5 %copy-start.23 = (s32[24]{0:T(128)S(1)}, s32[24]{0:T(128)}, u32[]{:S(2)}) copy-start(s32[24]{0:T(128)} %constant.113.clone) | copy-start | bytes 292
  259.1 82.5 %copy-start.24 = (s32[24]{0:T(128)S(1)}, s32[24]{0:T(128)}, u32[]{:S(2)}) copy-start(s32[24]{0:T(128)} %constant.114.clone) | copy-start | bytes 292
  339.5 183.5 %collective-permute-start.10 = (bf16[768,1536]{1,0:T(8,128)(2,1)}, bf16[768,1536]{1,0:T(8,128)(2,1)}, u32[]{:S(2)}, u32[]{:S(2)}) collective-permute-start(bf16[768,1536]{1,0:T(8,128)(2,1)} %get-tuple-element.108), channel_id=1, source_target_pairs={{0,1},{1,0},{2,3},{3,2},{4,5},{5,4},{6,7},{7,6},{8,9},{9,8},{10,11... | collective-permute-start | bytes 7077896 | tf_op jit(solution)/shard_map/ppermute | solution.py:681
  339.9 186.9 %collective-permute-start.12 = (bf16[768,1536]{1,0:T(8,128)(2,1)}, bf16[768,1536]{1,0:T(8,128)(2,1)S(1)}, u32[]{:S(2)}, u32[]{:S(2)}) collective-permute-start(bf16[768,1536]{1,0:T(8,128)(2,1)} %get-tuple-element.111), channel_id=1, source_target_pairs={{0,1},{1,0},{2,3},{3,2},{4,5},{5,4},{6,7},{7,6},{8,9},{9,8},{10,11... | collective-permute-start | bytes 7077896 | tf_op jit(solution)/shard_map/ppermute | solution.py:681
  458.1 9.5 %copy-start.10 = (bf16[768,384]{1,0:T(8,128)(2,1)S(1)}, bf16[768,384]{1,0:T(8,128)(2,1)}, u32[]{:S(2)}) copy-start(bf16[768,384]{1,0:T(8,128)(2,1)} %get-tuple-element.100) | copy-start | bytes 1769476
  458.1 9.5 %copy-start.11 = (bf16[768,384]{1,0:T(8,128)(2,1)S(1)}, bf16[768,384]{1,0:T(8,128)(2,1)}, u32[]{:S(2)}) copy-start(bf16[768,384]{1,0:T(8,128)(2,1)} %get-tuple-element.101) | copy-start | bytes 1769476
  469.1 52.3 %collective-permute-start.7 = (bf16[3,768,384]{2,1,0:T(8,128)(2,1)S(1)}, bf16[3,768,384]{2,1,0:T(8,128)(2,1)S(1)}, u32[]{:S(2)}, u32[]{:S(2)}) collective-permute-start(bf16[3,768,384]{2,1,0:T(8,128)(2,1)S(1)} %pad_maximum_fusion), channel_id=1, source_target_pairs={{0,1},{1,0},{2,3},{3,2},{4,5},{5,4},{6,7},{7,6},{8,9},{9,8},{10,11... | collective-permute-start | bytes 5308424 | tf_op jit(solution)/shard_map/ppermute | solution.py:681
  469.5 51.8 %copy-start.12 = (bf16[768,384]{1,0:T(8,128)(2,1)S(1)}, bf16[768,384]{1,0:T(8,128)(2,1)}, u32[]{:S(2)}) copy-start(bf16[768,384]{1,0:T(8,128)(2,1)} %get-tuple-element.97) | copy-start | bytes 1769476
  469.5 51.8 %copy-start.13 = (bf16[768,384]{1,0:T(8,128)(2,1)S(1)}, bf16[768,384]{1,0:T(8,128)(2,1)}, u32[]{:S(2)}) copy-start(bf16[768,384]{1,0:T(8,128)(2,1)} %get-tuple-element.98) | copy-start | bytes 1769476
  469.5 51.8 %copy-start.14 = (bf16[768,384]{1,0:T(8,128)(2,1)S(1)}, bf16[768,384]{1,0:T(8,128)(2,1)}, u32[]{:S(2)}) copy-start(bf16[768,384]{1,0:T(8,128)(2,1)} %get-tuple-element.99) | copy-start | bytes 1769476
  469.7 53.3 %copy-start.6 = (bf16[768,1536]{1,0:T(8,128)(2,1)S(1)}, bf16[768,1536]{1,0:T(8,128)(2,1)}, u32[]{:S(2)}) copy-start(bf16[768,1536]{1,0:T(8,128)(2,1)} %get-tuple-element.107) | copy-start | bytes 7077892
  469.7 50.7 %collective-permute-start.9 = (bf16[384,768]{1,0:T(8,128)(2,1)S(1)}, bf16[384,768]{1,0:T(8,128)(2,1)S(1)}, u32[]{:S(2)}, u32[]{:S(2)}) collective-permute-start(bf16[384,768]{1,0:T(8,128)(2,1)S(1)} %slice.145), channel_id=1, source_target_pairs={{0,1},{1,0},{2,3},{3,2},{4,5},{5,4},{6,7},{7,6},{8,9},{9,8},{10,11... | collective-permute-start | bytes 1769480 | tf_op jit(solution)/shard_map/ppermute | solution.py:681
  529.3 48.1 %collective-permute-start.11 = (f32[1536]{0:T(1024)S(1)}, f32[1536]{0:T(1024)S(1)}, u32[]{:S(2)}, u32[]{:S(2)}) collective-permute-start(f32[1536]{0:T(1024)S(1)} %get-tuple-element.150), channel_id=1, source_target_pairs={{0,1},{1,0},{2,3},{3,2},{4,5},{5,4},{6,7},{7,6},{8,9},{9,8},{10,11... | collective-permute-start | bytes 18440 | tf_op jit(solution)/shard_map/ppermute | solution.py:681
  530.7 45.9 %collective-permute-start.8 = (f32[2,384]{1,0:T(2,128)S(1)}, f32[2,384]{1,0:T(2,128)S(1)}, u32[]{:S(2)}, u32[]{:S(2)}) collective-permute-start(f32[2,384]{1,0:T(2,128)S(1)} %slice.123), channel_id=1, source_target_pairs={{0,1},{1,0},{2,3},{3,2},{4,5},{5,4},{6,7},{7,6},{8,9},{9,8},{10,11... | collective-permute-start | bytes 9224 | tf_op jit(solution)/shard_map/ppermute | solution.py:681
  532.1 39.8 %copy-start.16 = (f32[80,27]{1,0:T(8,128)S(1)}, f32[80,27]{1,0:T(8,128)}, u32[]{:S(2)}) copy-start(f32[80,27]{1,0:T(8,128)} %constant.123.clone) | copy-start | bytes 25924
  532.1 39.8 %copy-start.17 = (f32[80,128]{1,0:T(8,128)S(1)}, f32[80,128]{1,0:T(8,128)}, u32[]{:S(2)}) copy-start(f32[80,128]{1,0:T(8,128)} %get-tuple-element.104) | copy-start | bytes 122884
  568.1 5.2 copy-start.2
  571.1 64.5 %collective-permute-start.6 = (bf16[640,768]{1,0:T(8,128)(2,1)S(1)}, bf16[640,768]{1,0:T(8,128)(2,1)S(1)}, u32[]{:S(2)}, u32[]{:S(2)}) collective-permute-start(bf16[640,768]{1,0:T(8,128)(2,1)S(1)} %fusion), channel_id=1, source_target_pairs={{0,1},{1,0},{2,3},{3,2},{4,5},{5,4},{6,7},{7,6},{8,9},{9,8},{10,11... | collective-permute-start | bytes 2949128 | tf_op jit(solution)/shard_map/ppermute | solution.py:681
  696.1 4.7 copy-start.1
  (7 other events, 17.6 us)
Sparse Core Ops, SparseCore 0:
  528.7 153.1 all-reduce.10

commit v2 on v1

v2 whole, which is shorter than its diff:
```python
import jax
import jax.numpy as jnp
import numpy as np
from jax import lax
from jax.experimental import pallas as pl
from jax.experimental.pallas import tpu as pltpu
from jax.sharding import PartitionSpec as P

D = 768
HEADS = 12
HD = 64
FF = 3072
WIN = 14
SIDE = 64
NWIN = 5
RELS = 27
EPSILON = 1e-06
F32 = jnp.float32
BF = jnp.bfloat16

SLOTS = 256
KEYS = WIN * 16
PAIR = 2 * SIDE
GREL = 80
OWN = SIDE * SIDE // 2

HALF = D // 2
TRIO = 3 * HALF
PAIRS = HEADS // 4

NN = (((1,), (0,)), ((), ()))
NT = (((1,), (1,)), ((), ()))
TN = (((0,), (0,)), ((), ()))


def dot(left, right, dims=NN):
    return lax.dot_general(left, right, dims, preferred_element_type=F32)


def params(limit=60):
    return pltpu.CompilerParams(vmem_limit_bytes=limit * 2**20)


def cost(flops, moved, exps=0):
    return pl.CostEstimate(flops=int(flops), bytes_accessed=int(moved), transcendentals=int(exps))


def whole(shape):
    return pl.BlockSpec(shape, lambda *_: (0,) * len(shape), pipeline_mode=pl.Buffered(1))


STARTS = np.array([[0, 14, 28], [42, 28, 56]], np.int32)


def pair_tables(place):
    block = np.zeros((2, 24), np.int32)
    valid = np.zeros((2, 24), np.int32)
    local = np.zeros((2, 24), np.int32)
    owned = np.zeros((2, 24), np.int32)
    band_of = np.zeros((2, 16), np.int32)
    step_of = np.zeros((2, 16), np.int32)
    taken_of = np.zeros((2, 16), np.int32)
    has_taken = np.zeros((2, 16), np.int32)
    taken_of[0, 14:16], has_taken[0, 14:16] = np.arange(2), 1
    taken_of[1, 0:5], has_taken[1, 0:5] = np.arange(5), 1
    for m in range(2):
        for s in range(3):
            for t in range(7):
                row = STARTS[m, s] + 2 * t
                at = s * 8 + t
                block[m, at] = min(row // 2, 31)
                valid[m, at] = row < SIDE
                if 32 * m <= row < 32 * m + 32:
                    local[m, at] = (row - 32 * m) // 2
                    owned[m, at] = 1
                    band_of[m, local[m, at]] = s
                    step_of[m, local[m, at]] = t
            block[m, s * 8 + 7] = block[m, s * 8 + 6]
    pick = lambda table: jnp.where(place == 0, jnp.asarray(table[0]), jnp.asarray(table[1]))
    return tuple(pick(t) for t in (block, valid, local, owned, band_of, step_of, taken_of, has_taken))


def spread_rows():
    table = np.zeros((NWIN, 2, 16, PAIR), np.float32)
    for w in range(NWIN):
        for r in range(2):
            for j in range(WIN):
                if WIN * w + j < SIDE:
                    table[w, r, j, r * SIDE + WIN * w + j] = 1
    return table.reshape(NWIN * 32, PAIR)


def rel_order():
    rows = np.full(GREL, -1)
    for m in range(21):
        rows[m] = 26 - (m + 6)
        rows[24 + m] = 26 - m
    cols = np.full(GREL, -1)
    for m in range(RELS):
        cols[48 + m] = 26 - m
    return rows, cols


def rel_onehots():
    rows, cols = rel_order()
    high = (rows[:, None] == np.arange(RELS)[None, :]).astype(np.float32)
    wide = (cols[:, None] == np.arange(RELS)[None, :]).astype(np.float32)
    return high, wide


GAIN_ONE, SHIFT_ONE, PROJ_BIAS, GAIN_TWO, SHIFT_TWO, FC2_BIAS = range(6)


def norm_parts(values):
    average = jnp.mean(values, axis=-1, keepdims=True)
    centred = values - average
    inverse = lax.rsqrt(jnp.mean(centred * centred, axis=-1, keepdims=True) + EPSILON)
    return centred * inverse, inverse


def vec(table, row):
    return table[row : row + 1, :]


def window_kernel(block, valid, *refs):
    xs, (vectors, spread, out) = refs[:7], refs[7:]
    band = pl.program_id(0)
    for t in range(7):
        scaled, _ = norm_parts(xs[t][...].astype(F32))
        normed = scaled * vec(vectors, GAIN_ONE) + vec(vectors, SHIFT_ONE)
        normed = (normed * valid[band * 8 + t].astype(F32)).astype(BF)
        moved = dot(spread[...], normed).astype(BF)
        out[:, :, 32 * t : 32 * t + 32, :] = moved.reshape(1, NWIN, 32, D)
    out[:, :, 224:, :] = jnp.zeros((1, NWIN, 32, D), BF)


def windows_of(x, vectors, spread, block, valid):
    at = lambda t: lambda s, block, valid: (block[s * 8 + t], 0)
    return pl.pallas_call(
        window_kernel,
        grid_spec=pltpu.PrefetchScalarGridSpec(
            num_scalar_prefetch=2,
            grid=(3,),
            in_specs=[pl.BlockSpec((PAIR, D), at(t)) for t in range(7)]
            + [whole((8, D)), whole((NWIN * 32, PAIR))],
            out_specs=pl.BlockSpec((1, NWIN, SLOTS, D), lambda s, *_: (s, 0, 0, 0)),
        ),
        out_shape=jax.ShapeDtypeStruct((3, NWIN, SLOTS, D), BF),
        compiler_params=params(),
        cost_estimate=cost(3 * 7 * 160 * 128 * 768 * 2, 10e6),
    )(block, valid, *([x] * 7), vectors, spread)


def shift_masks(lanes_from):
    lane = lax.broadcasted_iota(jnp.int32, (1, 128), 1) + lanes_from
    high = lane // 16
    row_shift = jnp.where(lane < 128, 7 - high, jnp.maximum(13 - high, 0))
    col_shift = jnp.maximum(13 - lane % 16, 0)
    return row_shift, col_shift


def skew(table, shift, bits):
    size = table.shape[0]
    for bit in bits:
        moved = pltpu.roll(table, size - bit, 0)
        table = jnp.where((shift & bit) != 0, moved, table)
    return table


def unskew(table, shift, bits):
    for bit in bits:
        moved = pltpu.roll(table, bit, 0)
        table = jnp.where((shift & bit) != 0, moved, table)
    return table


def attend_kernel(x, weights, biases, rel_even, rel_odd, qkv_out, p_out, ctx_out, xt_out, joined, vt):
    band = pl.program_id(0)

    @pl.when((band == 0) & (pl.program_id(1) == 0))
    def _():
        for s in range(3):
            joined[:, s * HALF : s * HALF + HALF] = weights[s]

    block = x[...].reshape(SLOTS, D)
    if xt_out is not None:
        xt_out[...] = block.T
    scales = jnp.where(lax.broadcasted_iota(jnp.int32, (1, TRIO), 1) // HALF == 1, HD ** (-0.5), 1.0)
    low = ((dot(block, joined[...]) + biases[...]) * scales).astype(BF)
    qkv_out[0, 0] = low
    vt[...] = low[:, 2 * HALF :].T

    def pair_step(pair, lanes):
        cols = slice(pair * 128, pair * 128 + 128)
        queries = qkv_out[0, 0, 0:lanes, cols]
        keys = qkv_out[0, 0, 0:KEYS, HALF + pair * 128 : HALF + pair * 128 + 128]
        even = lax.broadcasted_iota(jnp.int32, (1, 128), 1) < HD
        contexts = []
        for odd in range(2):
            rel = rel_odd if odd else rel_even
            kept = jnp.where(even != (odd == 1), keys, jnp.zeros_like(keys))
            raw = dot(jnp.concatenate([kept, rel[...]], axis=0), queries, NT)
            parts = []
            for tile in range(lanes // 128):
                row_shift, col_shift = shift_masks(tile * 128)
                raw_t = raw[:, tile * 128 : tile * 128 + 128]
                base = raw_t[0:KEYS]
                high = skew(raw_t[KEYS + 24 * tile : KEYS + 24 * tile + 24], row_shift, (4, 2, 1))[0:16]
                wide = skew(raw_t[KEYS + 48 : KEYS + 80], col_shift, (8, 4, 2, 1))[0:16]
                place = lax.broadcasted_iota(jnp.int32, (16, 128), 0)
                wide = jnp.where(place < WIN, wide, -1e30)
                scores = base.reshape(WIN, 16, 128) + wide[None] + high[0:WIN][:, None, :]
                scores = scores.reshape(KEYS, 128)
                peak = jnp.max(scores, axis=0, keepdims=True)
                grown = jnp.exp(scores - peak)
                total = jnp.sum(grown, axis=0, keepdims=True)
                parts.append((grown * (1.0 / total)).astype(BF))
            probs = parts[0] if len(parts) == 1 else jnp.concatenate(parts, axis=1)
            p_out[0, 0, pair * 2 + odd, :, 0:lanes] = probs
            rows = slice(pair * 128 + odd * HD, pair * 128 + odd * HD + HD)
            contexts.append(dot(vt[rows, 0:KEYS], probs).astype(BF))
        ctx_out[0, 0, 0:lanes, cols] = jnp.concatenate(contexts, axis=0).T

    @pl.when(band < 2)
    def _():
        for pair in range(PAIRS):
            pair_step(pair, 256)

    @pl.when(band == 2)
    def _():
        for pair in range(PAIRS):
            pair_step(pair, 128)


def attend_plain(x, weights, biases, rel_even, rel_odd, qkv_out, p_out, ctx_out, joined, vt):
    attend_kernel(x, weights, biases, rel_even, rel_odd, qkv_out, p_out, ctx_out, None, joined, vt)


def attend(x, weights, biases, rel_even, rel_odd, first):
    block = lambda width: pl.BlockSpec((1, 1, SLOTS, width), lambda s, w: (s, w, 0, 0))
    shape = lambda width: jax.ShapeDtypeStruct((3, NWIN, SLOTS, width), BF)
    out_specs = [
        block(TRIO),
        pl.BlockSpec((1, 1, HEADS // 2, KEYS, SLOTS), lambda s, w: (s, w, 0, 0, 0)),
        block(HALF),
    ]
    out_shape = [
        shape(TRIO),
        jax.ShapeDtypeStruct((3, NWIN, HEADS // 2, KEYS, SLOTS), BF),
        shape(HALF),
    ]
    if first:
        out_specs.append(pl.BlockSpec((D, SLOTS), lambda s, w: (0, s * NWIN + w)))
        out_shape.append(jax.ShapeDtypeStruct((D, 3 * NWIN * SLOTS), BF))
    return pl.pallas_call(
        attend_kernel if first else attend_plain,
        grid=(3, NWIN),
        in_specs=[block(D), whole((3, D, HALF)), whole((1, TRIO)), whole((GREL, 128)), whole((GREL, 128))],
        out_specs=out_specs,
        out_shape=out_shape,
        scratch_shapes=[pltpu.VMEM((D, TRIO), BF), pltpu.VMEM((HALF, SLOTS), BF)],
        compiler_params=params(),
        cost_estimate=cost(15e9, 45e6, 4e6),
    )(x, weights, biases, rel_even, rel_odd)


def middle_kernel(
    band_of, step_of, offset, own_a, own_b, other_a, other_b, x, cot, proj_own, proj_other, vectors, gather,
    middle, normed, normed_t, cot_t, ctx_out, proj,
):
    @pl.when(pl.program_id(0) == 0)
    def _():
        proj[0:HALF, :] = proj_own[...]
        proj[HALF:, :] = proj_other[...]

    for row, parts in ((0, (own_a, other_a)), (PAIR, (own_b, other_b))):
        for side in range(2):
            moved = dot(gather[...], parts[side][...].reshape(NWIN * 32, HALF)).astype(BF)
            ctx_out[row : row + PAIR, side * HALF : side * HALF + HALF] = moved
    value = x[...].astype(F32) + (dot(ctx_out[...], proj[...]) + vec(vectors, PROJ_BIAS))
    middle[...] = value
    scaled, _ = norm_parts(value)
    low = (scaled * vec(vectors, GAIN_TWO) + vec(vectors, SHIFT_TWO)).astype(BF)
    normed[...] = low
    normed_t[...] = low.T
    cot_t[...] = cot[...].T


def middle_of(ctx_own, ctx_other, x, cot, proj_own, proj_other, vectors, gather, band_of, step_of, offset):
    rows = 2 * PAIR
    at = lambda k: lambda i, band_of, step_of, offset: (band_of[2 * i + k], 0, step_of[2 * i + k], 0)
    row_block = pl.BlockSpec((rows, D), lambda i, *_: (i, 0))
    col_block = pl.BlockSpec((D, rows), lambda i, *_: (0, i))
    return pl.pallas_call(
        middle_kernel,
        grid_spec=pltpu.PrefetchScalarGridSpec(
            num_scalar_prefetch=3,
            grid=(OWN // rows,),
            in_specs=[
                pl.BlockSpec((1, NWIN, 32, HALF), at(0)),
                pl.BlockSpec((1, NWIN, 32, HALF), at(1)),
                pl.BlockSpec((1, NWIN, 32, HALF), at(0)),
                pl.BlockSpec((1, NWIN, 32, HALF), at(1)),
                pl.BlockSpec((rows, D), lambda i, band_of, step_of, offset: (offset[0] + i, 0)),
                row_block,
                whole((HALF, D)),
                whole((HALF, D)),
                whole((8, D)),
                whole((PAIR, NWIN * 32)),
            ],
            out_specs=[row_block, row_block, col_block, col_block, row_block],
            scratch_shapes=[pltpu.VMEM((D, D), BF)],
        ),
        out_shape=[
            jax.ShapeDtypeStruct((OWN, D), F32),
            jax.ShapeDtypeStruct((OWN, D), BF),
            jax.ShapeDtypeStruct((D, OWN), BF),
            jax.ShapeDtypeStruct((D, OWN), BF),
            jax.ShapeDtypeStruct((OWN, D), BF),
        ],
        compiler_params=params(),
        cost_estimate=cost(3e9, 30e6),
    )(band_of, step_of, offset, ctx_own, ctx_own, ctx_other, ctx_other, x, cot, proj_own, proj_other, vectors, gather)


CHUNK = 512
CHUNKS = FF // CHUNK


def feed_kernel(
    normed, normed_t, cot, cot_t, one_a, one_b, bias, two_a, two_b,
    forward, back, one_grad, two_grad, sums, one, two, hidden, grads,
):
    step = pl.program_id(0)

    @pl.when(step == 0)
    def _():
        forward[...] = jnp.zeros_like(forward)
        back[...] = jnp.zeros_like(back)

    @pl.when(step < CHUNKS // 2)
    def _():
        one[...] = one_a[...]
        two[...] = two_a[...]

    @pl.when(step >= CHUNKS // 2)
    def _():
        one[...] = one_b[...]
        two[...] = two_b[...]

    total = jnp.zeros((1, CHUNK), F32)
    for t in range(OWN // 512):
        rows = slice(t * 512, t * 512 + 512)
        pre = dot(normed[rows, :], one[...]) + bias[...]
        phi = 0.5 * (1.0 + lax.erf(pre * 0.7071067811865476))
        slope = phi + pre * (jnp.exp(-0.5 * pre * pre) * 0.3989422804014327)
        low = (pre * phi).astype(BF)
        grad = (dot(cot[rows, :], two[...], NT) * slope).astype(BF)
        hidden[rows, :] = low
        grads[rows, :] = grad
        total += jnp.sum(grad.astype(F32), axis=0, keepdims=True)
        forward[rows, :] += dot(low, two[...])
        back[rows, :] += dot(grad, one[...], NT)
    sums[...] = total

    one_grad[0] = dot(normed_t[...], grads[...]).astype(BF)
    two_grad[0] = dot(cot_t[...], hidden[...]).astype(BF).T


def feed(normed, normed_t, cot, cot_t, one_a, one_b, bias, two_a, two_b):
    half = CHUNKS // 2
    own = lambda j: jnp.minimum(j, half - 1)
    other = lambda j: jnp.maximum(j - half, 0)
    grad_shape = jax.ShapeDtypeStruct((2, D, FF // 2), BF)
    grad_block = pl.BlockSpec((1, D, CHUNK), lambda j: (j // half, 0, j % half))
    return pl.pallas_call(
        feed_kernel,
        grid=(CHUNKS,),
        in_specs=[
            whole((OWN, D)),
            whole((D, OWN)),
            whole((OWN, D)),
            whole((D, OWN)),
            pl.BlockSpec((D, CHUNK), lambda j: (0, own(j))),
            pl.BlockSpec((D, CHUNK), lambda j: (0, other(j))),
            pl.BlockSpec((1, CHUNK), lambda j: (0, j)),
            pl.BlockSpec((CHUNK, D), lambda j: (own(j), 0)),
            pl.BlockSpec((CHUNK, D), lambda j: (other(j), 0)),
        ],
        out_specs=[
            pl.BlockSpec((OWN, D), lambda j: (0, 0)),
            pl.BlockSpec((OWN, D), lambda j: (0, 0)),
            grad_block,
            pl.BlockSpec((1, CHUNK, D), lambda j: (j // half, j % half, 0)),
            pl.BlockSpec((1, CHUNK), lambda j: (0, j)),
        ],
        out_shape=[
            jax.ShapeDtypeStruct((OWN, D), F32),
            jax.ShapeDtypeStruct((OWN, D), F32),
            grad_shape,
            jax.ShapeDtypeStruct((2, FF // 2, D), BF),
            jax.ShapeDtypeStruct((1, FF), F32),
        ],
        scratch_shapes=[
            pltpu.VMEM((D, CHUNK), BF),
            pltpu.VMEM((CHUNK, D), BF),
            pltpu.VMEM((OWN, CHUNK), BF),
            pltpu.VMEM((OWN, CHUNK), BF),
        ],
        compiler_params=params(62),
        cost_estimate=cost(58e9, 60e6, 12e6),
    )(normed, normed_t, cot, cot_t, one_a, one_b, bias, two_a, two_b)


def add_row(sums, row, values):
    sums[row : row + 1, :] += jnp.sum(values, axis=0, keepdims=True)


def resid_kernel(
    middle, forward, back, cot, context, proj_own, proj_other, vectors,
    block_out, grad_out, ctx_grad, grad_own, grad_other, sums, proj, proj_grad,
):
    step = pl.program_id(0)

    @pl.when(step == 0)
    def _():
        proj[0:HALF, :] = proj_own[...]
        proj[HALF:, :] = proj_other[...]
        proj_grad[...] = jnp.zeros_like(proj_grad)
        sums[...] = jnp.zeros_like(sums)

    value = middle[...]
    block_out[...] = (value + (forward[...] + vec(vectors, FC2_BIAS))).astype(BF)
    scaled, inverse = norm_parts(value)
    upstream = back[...]
    scaled_up = upstream * vec(vectors, GAIN_TWO)
    first = jnp.mean(scaled_up, axis=-1, keepdims=True)
    second = jnp.mean(scaled_up * scaled, axis=-1, keepdims=True)
    cotangent = cot[...].astype(F32)
    grad = cotangent + inverse * (scaled_up - first - scaled * second)
    grad_out[...] = grad
    low = grad.astype(BF)
    ctx_grad[...] = dot(low, proj[...], NT).astype(BF)
    proj_grad[...] += dot(context[...], low, TN)
    add_row(sums, 0, upstream * scaled)
    add_row(sums, 1, upstream)
    add_row(sums, 2, cotangent)
    add_row(sums, 3, low.astype(F32))

    @pl.when(step == pl.num_programs(0) - 1)
    def _():
        for out, row in ((grad_own, 0), (grad_other, HALF)):
            for col in (0, HALF):
                out[col : col + HALF, :] = proj_grad[row : row + HALF, col : col + HALF].astype(BF)


def resid_of(middle, forward, back, cot, context, proj_own, proj_other, vectors):
    rows = 512
    row_block = pl.BlockSpec((rows, D), lambda i: (i, 0))
    half_block = pl.BlockSpec((D, HALF), lambda i: (0, 0))
    return pl.pallas_call(
        resid_kernel,
        grid=(OWN // rows,),
        in_specs=[row_block] * 5 + [whole((HALF, D)), whole((HALF, D)), whole((8, D))],
        out_specs=[
            row_block,
            row_block,
            row_block,
            half_block,
            half_block,
            pl.BlockSpec((8, D), lambda i: (0, 0)),
        ],
        out_shape=[
            jax.ShapeDtypeStruct((OWN, D), BF),
            jax.ShapeDtypeStruct((OWN, D), F32),
            jax.ShapeDtypeStruct((OWN, D), BF),
            jax.ShapeDtypeStruct((D, HALF), BF),
            jax.ShapeDtypeStruct((D, HALF), BF),
            jax.ShapeDtypeStruct((8, D), F32),
        ],
        scratch_shapes=[pltpu.VMEM((D, D), BF), pltpu.VMEM((D, D), F32)],
        compiler_params=params(),
        cost_estimate=cost(5e9, 40e6),
    )(middle, forward, back, cot, context, proj_own, proj_other, vectors)


def attend_back_kernel(first, local, owned, qkv, p, ctx_grad, spread, rel_even, rel_odd, fold, *refs):
    d_out, rel_grad, sums, upstream, kt = refs[-5:]
    band = pl.program_id(0) + first
    window = pl.program_id(1)

    @pl.when((band == first) & (window == 0))
    def _():
        rel_grad[...] = jnp.zeros_like(rel_grad)
        sums[...] = jnp.zeros_like(sums)

    @pl.when(window == 0)
    def _():
        for t in range(7):
            at = band * 8 + t
            rows = pl.ds(pl.multiple_of(local[at] * PAIR, PAIR), PAIR)
            moved = dot(spread[...], ctx_grad[rows, :])
            moved = moved * owned[at].astype(F32)
            upstream[:, 32 * t : 32 * t + 32, :] = moved.astype(BF).reshape(NWIN, 32, HALF)
        upstream[:, 224:256, :] = jnp.zeros((NWIN, 32, HALF), BF)

    kt[...] = qkv[0, 0, :, HALF : 2 * HALF].T
    even = lax.broadcasted_iota(jnp.int32, (1, 128), 1) < HD

    def pair_step(pair, lanes):
        cols = slice(pair * 128, pair * 128 + 128)
        shifted = lambda by: slice(by * HALF + pair * 128, by * HALF + pair * 128 + 128)
        queries = qkv[0, 0, 0:lanes, shifted(0)]
        values = qkv[0, 0, 0:KEYS, shifted(2)]
        ups = upstream[window, 0:lanes, cols]
        dvs, dks, dqs, drs = [], [], [], []
        for odd in range(2):
            rel = rel_odd if odd else rel_even
            kept = jnp.where(even != (odd == 1), values, jnp.zeros_like(values))
            prob_grad = dot(kept, ups, NT)
            probs_low = p[0, 0, pair * 2 + odd, :, 0:lanes]
            probs = probs_low.astype(F32)
            total = jnp.sum(prob_grad * probs, axis=0, keepdims=True)
            score_grad = (probs * (prob_grad - total)).astype(BF)
            dvs.append(dot(probs_low, ups))
            rows = slice(pair * 128 + odd * HD, pair * 128 + odd * HD + HD)
            left = jnp.concatenate([kt[rows, 0:KEYS], fold[...]], axis=0)
            both = dot(left, score_grad)
            tables = []
            zero8 = jnp.zeros((8, 128), F32)
            zero24 = jnp.zeros((24, 128), F32)
            zero16 = jnp.zeros((16, 128), F32)
            for tile in range(lanes // 128):
                row_shift, col_shift = shift_masks(tile * 128)
                part = both[:, tile * 128 : tile * 128 + 128]
                high = jnp.concatenate([part[HD : HD + 16], zero8], axis=0)
                wide = jnp.concatenate([part[HD + 16 : HD + 32], zero16], axis=0)
                high = unskew(high, row_shift, (1, 2, 4))
                wide = unskew(wide, col_shift, (1, 2, 4, 8))
                stack = [high, zero24, wide] if tile == 0 else [zero24, high, wide]
                tables.append(jnp.concatenate(stack, axis=0))
            table = tables[0] if len(tables) == 1 else jnp.concatenate(tables, axis=1)
            table = table.astype(BF)
            grads = dot(jnp.concatenate([score_grad, table], axis=0), queries)
            dks.append(grads[0:KEYS])
            drs.append(grads[KEYS:])
            from_rel = dot(rel[...], table, TN)
            dqs.append(both[0:HD] + from_rel[odd * HD : odd * HD + HD])
        d_out[0, 0, 0:lanes, shifted(0)] = jnp.concatenate(dqs, axis=0).astype(BF).T
        d_out[0, 0, 0:KEYS, shifted(1)] = (jnp.where(even, dks[0], dks[1]) * HD ** (-0.5)).astype(BF)
        d_out[0, 0, 0:KEYS, shifted(2)] = jnp.where(even, dvs[0], dvs[1]).astype(BF)
        rel_grad[...] += jnp.where(even, drs[0], drs[1])

    d_out[0, 0, KEYS:, HALF:] = jnp.zeros((SLOTS - KEYS, 2 * HALF), BF)

    @pl.when(band < 2)
    def _():
        for pair in range(PAIRS):
            pair_step(pair, 256)

    @pl.when(band == 2)
    def _():
        for pair in range(PAIRS):
            pair_step(pair, 128)
        d_out[0, 0, 128:, 0:HALF] = jnp.zeros((128, HALF), BF)

    sums[0:1, :] += jnp.sum(d_out[...].reshape(SLOTS, TRIO).astype(F32), axis=0, keepdims=True)


def fold_table():
    table = np.zeros((32, WIN, 16), np.float32)
    for k in range(WIN):
        for l in range(WIN):
            table[k, k, l] = 1
            table[16 + l, k, l] = 1
    return table.reshape(32, KEYS)


def attend_back(qkv, p, ctx_grad, side, spread, rel_even, rel_odd, fold, local, owned, bands, *d_in):
    first, last = bands
    block = pl.BlockSpec((1, 1, SLOTS, TRIO), lambda s, w, *_: (s + first, w, 0, 0))
    share = (last - first) / 3
    return pl.pallas_call(
        lambda *refs: attend_back_kernel(first, *refs),
        grid_spec=pltpu.PrefetchScalarGridSpec(
            num_scalar_prefetch=2,
            grid=(last - first, NWIN),
            in_specs=[
                block,
                pl.BlockSpec((1, 1, HEADS // 2, KEYS, SLOTS), lambda s, w, *_: (s + first, w, 0, 0, 0)),
                pl.BlockSpec((OWN, HALF), lambda *_: (0, side), pipeline_mode=pl.Buffered(1)),
                whole((NWIN * 32, PAIR)),
                whole((GREL, 128)),
                whole((GREL, 128)),
                whole((32, KEYS)),
            ]
            + [pl.BlockSpec(memory_space=pl.ANY)] * len(d_in),
            out_specs=[
                block,
                pl.BlockSpec((GREL, 128), lambda s, w, *_: (0, 0)),
                pl.BlockSpec((8, TRIO), lambda s, w, *_: (0, 0)),
            ],
            scratch_shapes=[pltpu.VMEM((NWIN, SLOTS, HALF), BF), pltpu.VMEM((HALF, SLOTS), BF)],
        ),
        out_shape=[
            jax.ShapeDtypeStruct((3, NWIN, SLOTS, TRIO), BF),
            jax.ShapeDtypeStruct((GREL, 128), F32),
            jax.ShapeDtypeStruct((8, TRIO), F32),
        ],
        input_output_aliases={9: 0} if d_in else {},
        compiler_params=params(),
        cost_estimate=cost(20e9 * share, 45e6 * share),
    )(local, owned, qkv, p, ctx_grad, spread, rel_even, rel_odd, fold, *d_in)


def norm_grad_kernel(own, other, weights_own, weights_other, gather, *refs):
    out, joined = refs[-2:]

    @pl.when((pl.program_id(0) == 0) & (pl.program_id(1) == 0))
    def _():
        for s in range(3):
            joined[:, s * HALF : s * HALF + HALF] = weights_own[s]
            joined[:, TRIO + s * HALF : TRIO + s * HALF + HALF] = weights_other[s]

    rows = NWIN * 128
    left = jnp.concatenate([own[...].reshape(rows, TRIO), other[...].reshape(rows, TRIO)], axis=1)
    total = dot(left, joined[...], NT).astype(BF).reshape(NWIN, 4, 32, D)
    for t in range(4):
        moved = dot(gather[...], total[:, t].reshape(NWIN * 32, D)).astype(BF)
        out[:, t * PAIR : t * PAIR + PAIR, :] = moved.reshape(1, PAIR, D)


def norm_grad(own, other, weights_own, weights_other, gather, bands, *before):
    first, last = bands
    share = (last - first) / 3
    block = pl.BlockSpec((1, NWIN, 128, TRIO), lambda s, t: (s + first, 0, t, 0))
    return pl.pallas_call(
        norm_grad_kernel,
        grid=(last - first, 2),
        in_specs=[block, block, whole((3, D, HALF)), whole((3, D, HALF)), whole((PAIR, NWIN * 32))]
        + [pl.BlockSpec(memory_space=pl.ANY)] * len(before),
        out_specs=pl.BlockSpec((1, 4 * PAIR, D), lambda s, t: (s + first, t, 0)),
        out_shape=jax.ShapeDtypeStruct((3, 8 * PAIR, D), BF),
        input_output_aliases={5: 0} if before else {},
        scratch_shapes=[pltpu.VMEM((D, 2 * TRIO), BF)],
        compiler_params=params(),
        cost_estimate=cost(14e9 * share, 30e6 * share),
    )(own, other, weights_own, weights_other, gather, *before)


def qkv_grad_kernel(xt, d, out, total):
    step = pl.program_id(0)
    part = dot(xt[...], d[...])

    @pl.when(step == 0)
    def _():
        total[...] = part

    @pl.when(step > 0)
    def _():
        total[...] += part

    @pl.when(step == pl.num_programs(0) - 1)
    def _():
        for s in range(3):
            out[s] = total[:, s * HALF : s * HALF + HALF].astype(BF)


def qkv_grad(xt, d):
    rows = NWIN * SLOTS
    return pl.pallas_call(
        qkv_grad_kernel,
        grid=(3,),
        in_specs=[pl.BlockSpec((D, rows), lambda i: (0, i)), pl.BlockSpec((rows, TRIO), lambda i: (i, 0))],
        out_specs=pl.BlockSpec((3, D, HALF), lambda i: (0, 0, 0)),
        out_shape=jax.ShapeDtypeStruct((3, D, HALF), BF),
        scratch_shapes=[pltpu.VMEM((D, TRIO), F32)],
        compiler_params=params(),
        cost_estimate=cost(7e9, 16e6),
    )(xt, d.reshape(3 * rows, TRIO))


def input_kernel(
    band_of, step_of, taken_of, has_taken, offset, x, middle_grad, up_a, up_b, taken_a, taken_b, vectors, out, sums
):
    step = pl.program_id(0)

    @pl.when(step == 0)
    def _():
        sums[...] = jnp.zeros_like(sums)

    for k, (up, taken) in enumerate(((up_a, taken_a), (up_b, taken_b))):
        rows = slice(k * PAIR, k * PAIR + PAIR)
        scaled, inverse = norm_parts(x[rows, :].astype(F32))
        shared = taken[...].astype(F32) * has_taken[2 * step + k].astype(F32)
        upstream = up[0].astype(F32) + shared
        scaled_up = upstream * vec(vectors, GAIN_ONE)
        first = jnp.mean(scaled_up, axis=-1, keepdims=True)
        second = jnp.mean(scaled_up * scaled, axis=-1, keepdims=True)
        out[rows, :] = (middle_grad[rows, :] + inverse * (scaled_up - first - scaled * second)).astype(BF)
        add_row(sums, 0, upstream * scaled)
        add_row(sums, 1, upstream)


def input_of(x, middle_grad, up, taken, vectors, band_of, step_of, taken_of, has_taken, offset):
    rows = 2 * PAIR
    row_block = pl.BlockSpec((rows, D), lambda i, *_: (i, 0))
    up_at = lambda k: lambda i, band_of, step_of, *_: (band_of[2 * i + k], step_of[2 * i + k], 0)
    taken_at = lambda k: lambda i, band_of, step_of, taken_of, *_: (taken_of[2 * i + k], 0)
    return pl.pallas_call(
        input_kernel,
        grid_spec=pltpu.PrefetchScalarGridSpec(
            num_scalar_prefetch=5,
            grid=(OWN // rows,),
            in_specs=[
                pl.BlockSpec((rows, D), lambda i, b, s, t, h, offset: (offset[0] + i, 0)),
                row_block,
                pl.BlockSpec((1, PAIR, D), up_at(0)),
                pl.BlockSpec((1, PAIR, D), up_at(1)),
                pl.BlockSpec((PAIR, D), taken_at(0)),
                pl.BlockSpec((PAIR, D), taken_at(1)),
                whole((8, D)),
            ],
            out_specs=[row_block, pl.BlockSpec((8, D), lambda i, *_: (0, 0))],
        ),
        out_shape=[jax.ShapeDtypeStruct((OWN, D), BF), jax.ShapeDtypeStruct((8, D), F32)],
        compiler_params=params(),
        cost_estimate=cost(1e8, 20e6),
    )(band_of, step_of, taken_of, has_taken, offset, x, middle_grad, up, up, taken, taken, vectors)


MESH = pl.DeviceIdType.MESH
SMALL = 24


def bits_of(size):
    return size.bit_length() - 1


def line_plan(order, rows):
    plan, doubles = [], [("double", order[0], 2 * rows)]
    for bit in order[1:]:
        if rows % 32 == 0:
            doubles.append(("double", bit, rows))
            rows //= 2
            plan.append(("halve", bit, rows))
        else:
            plan.append(("both", bit, rows))
    return plan + doubles[::-1]


def last_kernel(bits, plans, orders, *refs):
    (line_a, line_b, one_sums, two_sums, fc1_sums, sums_a, sums_c, sums_b, sums_d) = refs[:9]
    rel_a, rel_b, rel_c, rel_d, hots, out, small, rel = refs[9:17]
    result, core_landed, small_landed, rel_landed, sends, recvs = refs[17:23]
    rooms = refs[23:]
    dp, mp = lax.axis_index("dp"), lax.axis_index("mp")
    bit_at = lambda bit: mp if bit == 0 else (dp // bit) % 2

    def partner(bit):
        if bit == 0:
            return (dp, 1 - mp)
        return (jnp.where(bit_at(bit) == 0, dp + bit, dp - bit), mp)

    barrier = pltpu.get_barrier_semaphore()
    every = [1] + bits + [0]
    for bit in every:
        pl.semaphore_signal(barrier, inc=1, device_id=partner(bit), device_id_type=MESH)

    small[...] = jnp.zeros_like(small)
    small[0:2, :] = one_sums[0:2, :]
    small[2:6, :] = two_sums[0:4, :]
    first = mp == 0
    own = [sums_a[0:1, :] + sums_c[0:1, :], fc1_sums[0:1, 0 : FF // 2]]
    other = [sums_b[0:1, :] + sums_d[0:1, :], fc1_sums[0:1, FF // 2 :]]
    for row, flip in ((6, False), (9, True)):
        picked = [jnp.where(first != flip, a, b) for a, b in zip(own, other)]
        small[row : row + 1, 0:HALF] = picked[0][:, 0:HALF]
        small[row : row + 1, HALF:] = picked[0][:, 2 * HALF :]
        small[row + 1 : row + 2, :] = picked[1][:, 0:D]
        small[row + 2 : row + 3, :] = picked[1][:, D:]
    table = rel_a[...] + rel_b[...] + rel_c[...] + rel_d[...]
    table = lax.dot_general(hots[...], table, TN, precision=lax.Precision.HIGHEST, preferred_element_type=F32)
    rel[...] = table + pltpu.roll(table, HD, 1)
    pl.semaphore_wait(barrier, len(every))

    count = [0]

    def send(src, dst, bit):
        at = count[0]
        count[0] += 1
        copy = pltpu.make_async_remote_copy(
            src_ref=src,
            dst_ref=dst,
            send_sem=sends.at[at],
            recv_sem=recvs.at[at],
            device_id=partner(bit),
            device_id_type=MESH,
        )
        copy.start()
        return copy

    values = [line_a, line_b]
    starts = [bit_at(order[0]) * (D // 2) for order in orders]
    sizes = [D // 2 for _ in orders]
    placed = [False, False]
    small_bits = bits + [0, 1]
    used = 0
    for at in range(max([len(small_bits)] + [len(plan) for plan in plans])):
        copies, adds = [], []
        if at < len(small_bits):
            copies.append(send(small, small_landed.at[at], small_bits[at]))
            copies.append(send(rel, rel_landed.at[at], small_bits[at]))
        for k, plan in enumerate(plans):
            if at >= len(plan):
                continue
            kind, bit, after = plan[at]
            if kind == "double":
                here = pl.ds(pl.multiple_of(starts[k], 16), sizes[k])
                if not placed[k]:
                    result[k, here, :] = values[k][...]
                    placed[k] = True
                copies.append(send(result.at[k, here], result.at[k, here], bit))
                starts[k] = starts[k] - bit_at(bit) * sizes[k]
            else:
                mine = bit_at(bit) if kind == "halve" else 0
                gone = 1 - mine if kind == "halve" else 0
                room, total = rooms[used], rooms[used + 1]
                used += 2
                gone = pl.ds(pl.multiple_of(gone * after, 16), after)
                copies.append(send(values[k].at[gone], room, bit))
                adds.append((k, pl.ds(pl.multiple_of(mine * after, 16), after), room, total))
                starts[k] = starts[k] + mine * after
            sizes[k] = after
        for copy in copies:
            copy.wait()
        for k, rows, room, total in adds:
            total[...] = (values[k][rows, :].astype(F32) + room[...].astype(F32)).astype(BF)
            values[k] = total
        if at < len(small_bits):
            small[...] += small_landed[at]
            rel[...] += rel_landed[at]
    copy = send(result, core_landed, 1)
    mine = pl.ds(pl.multiple_of(dp % 2 * 2, 2), 2)
    theirs = pl.ds(pl.multiple_of((1 - dp % 2) * 2, 2), 2)
    out[mine] = result[...]
    copy.wait()
    out[theirs] = core_landed[...]


def last_sums(bits, orders, lines, sums, rels, hots):
    vmem = pl.BlockSpec(memory_space=pltpu.VMEM)
    rounds = len(bits) + 2
    copies = 2 * rounds + 4 * len(bits) + 1
    plans = [line_plan(order, D // 2) for order in orders]
    rooms = []
    for at in range(len(plans[0])):
        for plan in plans:
            if plan[at][0] != "double":
                rooms += [pltpu.VMEM((plan[at][2], HALF), BF)] * 2
    return pl.pallas_call(
        lambda *refs: last_kernel(bits, plans, orders, *refs),
        in_specs=[vmem] * (2 + len(sums) + len(rels) + 1),
        out_specs=[vmem] * 3,
        out_shape=[
            jax.ShapeDtypeStruct((4, D, HALF), BF),
            jax.ShapeDtypeStruct((SMALL, D), F32),
            jax.ShapeDtypeStruct((56, 128), F32),
        ],
        scratch_shapes=[
            pltpu.VMEM((2, D, HALF), BF),
            pltpu.VMEM((2, D, HALF), BF),
            pltpu.VMEM((rounds, SMALL, D), F32),
            pltpu.VMEM((rounds, 56, 128), F32),
            pltpu.SemaphoreType.DMA((copies,)),
            pltpu.SemaphoreType.DMA((copies,)),
        ]
        + rooms,
        compiler_params=pltpu.CompilerParams(
            collective_id=0, has_side_effects=True, vmem_limit_bytes=40 * 2**20
        ),
    )(*lines, *sums, *rels, hots)


CORE, PAIRED = 1, 0


def bit_of(bit):
    return lax.axis_index("mp") if bit == PAIRED else (lax.axis_index("dp") // bit) % 2


def exchange(value, bit):
    if bit == PAIRED:
        return lax.ppermute(value, "mp", [(0, 1), (1, 0)])
    return lax.ppermute(value, "dp", [(i, i ^ bit) for i in range(lax.axis_size("dp"))])


class Line:
    def __init__(self, value, places, order, back):
        self.value = value
        self.places = list(places)
        self.steps = [("halve", bit) for bit in order] + [("double", bit) for bit in back]
        self.rank = {bit: at for at, bit in enumerate(places)}
        self.sent = self.kept = self.taken = None

    def prepare(self):
        kind, bit = self.steps[0]
        if kind != "halve":
            self.sent = self.value
            return
        axis = self.places.index(bit)
        if bit == PAIRED:
            part = lambda at: lax.index_in_dim(self.value, at, axis, keepdims=False)
            self.kept, self.sent = part(0), part(1)
        else:
            mine = bit_of(bit)
            part = lambda at: lax.dynamic_index_in_dim(self.value, at, axis, keepdims=False)
            self.kept, self.sent = part(mine), part(1 - mine)

    def launch(self):
        self.taken = exchange(self.sent, self.steps[0][1])

    def land(self):
        kind, bit = self.steps.pop(0)
        if kind == "halve":
            self.places.remove(bit)
            self.value = self.kept + self.taken
        elif kind == "pass":
            self.value = self.taken
        else:
            self.places = sorted(self.places + [bit], key=self.rank.get)
            first = bit_of(bit) == 0
            ends = (lambda v: v.astype(F32)) if not self.steps else (lambda v: v)
            low = ends(jnp.where(first, self.value, self.taken))
            high = ends(jnp.where(first, self.taken, self.value))
            self.value = jnp.stack([low, high], axis=self.places.index(bit))
        self.taken = None


def advance(anchor, lines):
    flying = [line for line in lines if line.taken is not None]
    anchor, taken = lax.optimization_barrier((anchor, [line.taken for line in flying]))
    for line, value in zip(flying, taken):
        line.taken = value
        line.land()
    going = [line for line in lines if line.steps]
    for line in going:
        line.prepare()
    anchor, sent = lax.optimization_barrier((anchor, [line.sent for line in going]))
    for line, value in zip(going, sent):
        line.sent = value
        line.launch()
    return anchor


def finish(lines):
    while any(line.steps for line in lines):
        for line in lines:
            if not line.steps:
                continue
            if line.taken is None:
                line.prepare()
                line.launch()
        for line in lines:
            if line.taken is not None:
                line.land()


def on_device(
    image_tokens,
    norm1_gain,
    norm1_shift,
    qkv_weight,
    qv_bias,
    rel_rows,
    rel_cols,
    proj_weight,
    proj_bias,
    norm2_gain,
    norm2_shift,
    fc1_weight,
    fc1_bias,
    fc2_weight,
    fc2_bias,
    out_cotangent,
):
    place = lax.axis_index("mp")
    core = lax.axis_index("dp") % 2
    swap = lambda value: lax.ppermute(value, "mp", [(0, 1), (1, 0)])
    size = lax.axis_size("dp")
    core_swap = lambda value: lax.ppermute(value, "dp", [(i, i ^ 1) for i in range(size)])

    def from_partner(weight):
        rows = weight.shape[-2] // 2
        half = lax.dynamic_slice_in_dim(weight, core * rows, rows, weight.ndim - 2)
        mine = swap(half)
        theirs = core_swap(mine)
        low = jnp.where(core == 0, mine, theirs)
        high = jnp.where(core == 0, theirs, mine)
        return jnp.concatenate([low, high], axis=weight.ndim - 2)

    block, valid, local, owned, band_of, step_of, taken_of, has_taken = pair_tables(place)
    offset = (place * (OWN // (2 * PAIR))).astype(jnp.int32).reshape(1)
    zero_row = jnp.zeros((D,), BF)
    vectors = jnp.stack(
        [norm1_gain, norm1_shift, proj_bias, norm2_gain, norm2_shift, fc2_bias, zero_row, zero_row]
    ).astype(F32)
    spread = jnp.asarray(spread_rows(), BF)
    gather = jnp.asarray(spread_rows().T, BF)
    fold = jnp.asarray(fold_table(), BF)
    high_hot, wide_hot = (jnp.asarray(t, F32) for t in rel_onehots())
    precise = lax.Precision.HIGHEST
    hots = jnp.concatenate([high_hot, wide_hot], axis=1)
    rels = jnp.concatenate([rel_rows, rel_cols], axis=0)
    table = jnp.dot(hots.astype(BF), rels, preferred_element_type=F32).astype(BF)
    blank = jnp.zeros_like(table)
    rel_even = jnp.concatenate([table, blank], axis=1)
    rel_odd = jnp.concatenate([blank, table], axis=1)

    trio = lambda q, v: jnp.concatenate([q, jnp.zeros((HALF,), BF), v]).astype(F32).reshape(1, TRIO)
    bias_own = trio(qv_bias[0], qv_bias[1])
    qkv_other = from_partner(qkv_weight)

    x_windows = windows_of(image_tokens, vectors, spread, block, valid)
    biases, x_windows = lax.optimization_barrier((jnp.concatenate([qv_bias.reshape(-1), fc1_bias]), x_windows))
    small = swap(biases)
    qkv_a, p_a, ctx_a, xt = attend(x_windows, qkv_weight, bias_own, rel_even, rel_odd, True)
    bias_other = trio(small[:HALF], small[HALF:D])
    fc1_bias_all = jnp.concatenate([fc1_bias, small[D:]]).astype(F32).reshape(1, FF)
    late = lax.optimization_barrier((qkv_other, proj_weight, fc1_weight, fc2_weight))
    qkv_other = late[0]
    proj_other, fc1_other, fc2_other = (from_partner(w) for w in late[1:])
    qkv_b, p_b, ctx_b = attend(x_windows, qkv_other, bias_other, rel_even, rel_odd, False)
    middle, normed, normed_t, cot_t, context = middle_of(
        ctx_a, ctx_b, image_tokens, out_cotangent, proj_weight, proj_other, vectors,
        gather, band_of, step_of, offset,
    )
    forward, back, one_grad, two_grad, fc1_sums = feed(
        normed, normed_t, out_cotangent, cot_t, fc1_weight, fc1_other, fc1_bias_all, fc2_weight, fc2_other
    )
    bits = [2**k for k in range(1, bits_of(size))]
    turned = bits[1:2] + bits[0:1] + bits[2:]
    count = 2 ** (len(bits) + 1)
    places = [CORE] + bits

    def feed_line(value, order, back):
        value = value.reshape((2,) * (len(bits) + 2) + (value.shape[1] // count, value.shape[2]))
        return Line(value, [PAIRED] + places, [CORE] + order, back + [CORE])

    one_line = feed_line(one_grad, [PAIRED] + bits, bits[::-1])
    two_line = feed_line(two_grad, bits[:2] + [PAIRED] + bits[2:], turned[::-1])
    feed_lines = [one_line, two_line]

    middle = advance(middle, feed_lines)
    block_out, middle_grad, ctx_grad, proj_own, proj_oth, two_sums = resid_of(
        middle, forward, back, out_cotangent, context, proj_weight, proj_other, vectors
    )
    back_of = lambda qkv, p, side, grad, bands, *d: attend_back(
        qkv, p, grad, side, spread, rel_even, rel_odd, fold, local, owned, bands, *d
    )
    joined = lambda qkv, proj: jnp.concatenate([qkv.reshape(3 * D, HALF), proj], axis=0).reshape(
        (2,) * (len(bits) + 1) + (4 * D // count, HALF)
    )
    ctx_grad = advance(ctx_grad, feed_lines)
    d_b, rel_b, sums_b = back_of(qkv_b, p_b, 1, ctx_grad, (1, 3))
    d_b = advance(d_b, feed_lines)
    d_b, rel_b0, sums_b0 = back_of(qkv_b, p_b, 1, ctx_grad, (0, 1), d_b)
    d_b = advance(d_b, feed_lines)
    grad_b = qkv_grad(xt, d_b)
    line_b = Line(joined(grad_b, proj_oth), places, [CORE], [])
    line_b.steps.append(("pass", PAIRED))
    lines = feed_lines + [line_b]
    ctx_grad, grad_b = lax.optimization_barrier((ctx_grad, grad_b))
    ctx_grad = advance(ctx_grad, lines)
    d_a, rel_a, sums_a = back_of(qkv_a, p_a, 0, ctx_grad, (1, 3))
    d_a = advance(d_a, lines)
    up = norm_grad(d_a, d_b, qkv_weight, qkv_other, gather, (1, 3))
    tokens = lambda band, first, count: up[band, first * SIDE : (first + count) * SIDE]
    fill = jnp.zeros((6 * SIDE, D), BF)
    sent = jnp.where(place == 0, tokens(2, 4, 10), jnp.concatenate([tokens(1, 0, 4), fill]))
    shared_line = Line(sent, [], [], [])
    shared_line.steps.append(("pass", PAIRED))
    d_a = advance(d_a, [shared_line])
    d_a, rel_a0, sums_a0 = back_of(qkv_a, p_a, 0, ctx_grad, (0, 1), d_a)
    d_a = advance(d_a, lines + [shared_line])
    taken = shared_line.value
    grad_a = qkv_grad(xt, d_a)
    line_a = Line(joined(grad_a, proj_own), places, [CORE], [])
    lines = feed_lines + [line_a]
    grad_a, d_a = lax.optimization_barrier((grad_a, d_a))
    d_a = advance(d_a, lines)
    up = norm_grad(d_a, d_b, qkv_weight, qkv_other, gather, (0, 1), up)
    up = advance(up, lines)
    both = (line_a.value + line_b.value).reshape(2, 2, D // 2, HALF)
    q_lines = [Line(both[0], bits[:1], bits[:1], []), Line(both[1], turned[:1], turned[:1], [])]
    up = advance(up, q_lines)
    input_grad, one_sums = input_of(
        image_tokens, middle_grad, up, taken, vectors, band_of, step_of, taken_of, has_taken, offset
    )
    one_sums = advance(one_sums, feed_lines + q_lines)
    finish(feed_lines)
    four, small, rel = last_sums(
        bits,
        [bits, turned],
        [line.value for line in q_lines],
        [one_sums, two_sums, fc1_sums, sums_a, sums_a0, sums_b, sums_b0],
        [rel_a, rel_a0, rel_b, rel_b0],
        jnp.pad(hots, ((0, 0), (0, 2))),
    )
    one_sum = one_line.value.reshape(D, FF // 2)
    two_sum = two_line.value.reshape(FF // 2, D)
    mine = jnp.where(place == 0, small[6:9], small[9:12])
    return (
        block_out,
        input_grad,
        small[0],
        small[1],
        four[0:3].astype(F32),
        mine[0].reshape(2, HALF),
        rel[:RELS, :HD],
        rel[RELS : 2 * RELS, :HD],
        jnp.concatenate([four[3, :HALF], four[3, HALF:]], axis=1).astype(F32),
        small[5],
        small[2],
        small[3],
        one_sum,
        mine[1:3].reshape(-1),
        two_sum,
        small[4],
    )


def solution(mesh):
    in_specs = (
        P("dp", None),
        P(),
        P(),
        P(None, None, "mp"),
        P(None, "mp"),
        P(),
        P(),
        P("mp", None),
        P(),
        P(),
        P(),
        P(None, "mp"),
        P("mp"),
        P("mp", None),
        P(),
        P(("dp", "mp"), None),
    )
    out_specs = (
        P(("dp", "mp"), None),
        P(("dp", "mp"), None),
        P(),
        P(),
        P(None, None, "mp"),
        P(None, "mp"),
        P(),
        P(),
        P("mp", None),
        P(),
        P(),
        P(),
        P(None, "mp"),
        P("mp"),
        P("mp", None),
        P(),
    )
    return jax.shard_map(
        on_device, mesh=mesh, in_specs=in_specs, out_specs=out_specs, check_vma=False
    )
```

time: 717 us -> 585 us (0.82)
  waiting for transfers between devices: 162 us -> 42.4 us
  blocking collectives: 97.3 us -> 0 us
  Pallas kernels: 360 us -> 410 us
  other arithmetic: 34.8 us -> 59.1 us
  starting transfers between devices: 14.2 us -> 28.7 us
  between operations: 14.8 us -> 2.16 us
  local copies, waits for them, and re-layouts: 22.4 us -> 32.9 us
    ppermute x13 -> x5, waiting for transfers between devices: 162 us -> 8.62 us  [on_device(): swap = lambda value: lax.ppermute(value, 'mp', [(0, 1), (1, 0)])]
    psum x2 -> x0, blocking collectives: 97.3 us -> none  [the longest x1 58.2 us: on_device(): sums = lax.psum(tuple((a + b for a, b in zip(mine, others))), 'dp')]
    pallas_call x6 -> x11, Pallas kernels: 216 us -> 279 us  [the longest x4 95.4 us: attend_back(): pl.pallas_call(lambda *refs: attend_back_kernel(first, *refs), grid_spec=...]
    ppermute x0 -> x28, waiting for transfers between devices: none -> 33.7 us  [the longest x4 25.2 us: exchange(): return lax.ppermute(value, 'mp', [(0, 1), (1, 0)])]
    ppermute x0 -> x28, starting transfers between devices: none -> 21.8 us  [the longest x20 17.1 us: exchange(): lax.ppermute(value, 'dp', [(i, i ^ bit) for i in range(lax.axis_size('dp'...]
    add x5 -> x14, other arithmetic: 7.17 us -> 18.9 us  [the longest x13 17.4 us: land(): self.value = self.kept + self.taken]
    pallas_call x1, Pallas kernels: 19.4 us -> 8.71 us  [windows_of(): pl.pallas_call(window_kernel, grid_spec=pltpu.PrefetchScalarGridSpec(num_...]
    another operation x1 -> x16, other arithmetic: 1.45 us -> 12.1 us  [land(): self.value = jnp.stack([low, high], axis=self.places.index(bit))]
  transfers between devices with their start and end apart: 14 -> 33, of which waited for: 2 -> 8; matrix products, arithmetic and copies ran while one was open for 6% -> 5% of each run, Pallas kernels for 40% -> 45%
where the time goes in v2:
time: 585 us; the launch traced here: 575 us
  Pallas kernels  410 us (70%)
  other arithmetic  59.1 us (10%)
  waiting for transfers between devices  42.4 us (7%)
  local copies, waits for them, and re-layouts  32.9 us (6%)
  starting transfers between devices  28.7 us (5%)
    pallas_call x4, Pallas kernels, attend_back(): pl.pallas_call(lambda *refs: attend_back_kernel(first, *refs), grid_spec=...  95.4 us
    pallas_call x2, Pallas kernels, attend(): pl.pallas_call(attend_kernel if first else attend_plain, grid=(3, NWIN),...  86.1 us
    pallas_call x1, Pallas kernels, feed(): pl.pallas_call(feed_kernel, grid=(CHUNKS,), in_specs=[whole((OWN, D)), wh...  75.6 us
    pallas_call x1, Pallas kernels, last_sums(): pl.pallas_call(lambda *refs: last_kernel(bits, plans, orders, *refs), in_...  44.2 us
    pallas_call x2, Pallas kernels, norm_grad(): pl.pallas_call(norm_grad_kernel, grid=(last - first, 2), in_specs=[block,...  27.2 us
    pallas_call x2, Pallas kernels, qkv_grad(): pl.pallas_call(qkv_grad_kernel, grid=(3,), in_specs=[pl.BlockSpec((D, row...  25.7 us
    ppermute x4, waiting for transfers between devices, exchange(): return lax.ppermute(value, 'mp', [(0, 1), (1, 0)])  25.2 us
    pallas_call x1, Pallas kernels, resid_of(): pl.pallas_call(resid_kernel, grid=(OWN // rows,), in_specs=[row_block] *...  18.5 us
  transfers between devices with their start and end apart: 33, of which 8 were waited for; matrix products, arithmetic and copies ran while one was open for 5% of the time, Pallas kernels for 45%

profile of v2, /device:TPU:0, one launch (start us, length us, event | category | flops | bytes accessed | tf_op | source)
XLA Modules:
  0.0 575.3 jit_solution(4806048228409429827)
XLA Ops:
  2.0 3.0 collective-permute-start
  11.7 8.7 %shard_map.468.x = bf16[3,5,256,768]{3,2,1,0:T(8,128)(2,1)} custom-call(s32[24]{0:T(128)} %get-tuple-element.297.block, s32[24]{0:T(128)} %get-tuple-element.296.valid, bf16[4096,768]{1,0:T(8,128)(2,1)} %x.11, bf16[4096,768]{1,0:T(8,128)(2,1)} %x.11, bf16[4096,768]{1,0:T(8,128)(2,1)} %x.11, bf16[4096,768]{1,0:T(8,128)(2,1)} %x.11, bf16[4096,768]{1,0:T(8,128)(2,1)} %x.11, ...), custom_call_target="tpu_custom_call" | custom-call | flops 660602880 | bytes 10000000 | tf_op jit(solution)/shard_map/pallas_call | solution.py:139
  21.0 3.7 collective-permute-done
  32.4 43.4 %shard_map.469 = (bf16[3,5,256,1152]{3,2,1,0:T(8,128)(2,1)}, bf16[3,5,6,224,256]{4,3,2,1,0:T(8,128)(2,1)}, bf16[3,5,256,384]{3,2,1,0:T(8,128)(2,1)}, bf16[768,3840]{1,0:T(8,128)(2,1)}) custom-call(bf16[3,5,256,768]{3,2,1,0:T(8,128)(2,1)} %shard_map.468.x, bf16[3,768,384]{2,1,0:T(8,128)(2,1)} %weights_own.3, f32[1,1152]{1,0:T(1,128)} %get-tuple-element.291.biases, ...), custom_call_target="tpu_custom_call" | custom-call | flops 15000000512 | bytes 45000000 | tf_op jit(solution)/shard_map/pallas_call | solution.py:255
  76.8 2.4 constant_dynamic-slice_fusion.2
  81.0 4.9 collective-permute-done.3
  86.4 42.7 %shard_map.470 = (bf16[3,5,256,1152]{3,2,1,0:T(8,128)(2,1)}, bf16[3,5,6,224,256]{4,3,2,1,0:T(8,128)(2,1)}, bf16[3,5,256,384]{3,2,1,0:T(8,128)(2,1)}) custom-call(bf16[3,5,256,768]{3,2,1,0:T(8,128)(2,1)} %shard_map.468.x, bf16[3,768,384]{2,1,0:T(8,128)(2,1)} %pad_maximum_fusion.6.weights.weights_other, f32[1,1152]{1,0:T(1,128)} %get-tuple-element.290.biases, ...), custom_call_target="tpu_custom_call" | custom-call | flops 15000000512 | bytes 45000000 | tf_op jit(solution)/shard_map/pallas_call | solution.py:255
  130.0 16.4 %shard_map.471 = (f32[2048,768]{1,0:T(8,128)}, bf16[2048,768]{1,0:T(8,128)(2,1)}, bf16[768,2048]{1,0:T(8,128)(2,1)}, bf16[768,2048]{1,0:T(8,128)(2,1)}, bf16[2048,768]{1,0:T(8,128)(2,1)}) custom-call(s32[16]{0:T(128)} %get-tuple-element.301.band_of, s32[16]{0:T(128)} %get-tuple-element.300.step_of, s32[1]{0:T(128)} %bitcast.offset, ...), custom_call_target="tpu_custom_call" | custom-call | flops 3000000000 | bytes 30000000 | tf_op jit(solution)/shard_map/pallas_call | solution.py:294
  152.4 75.6 %shard_map.472 = (f32[2048,768]{1,0:T(8,128)}, f32[2048,768]{1,0:T(8,128)}, bf16[2,768,1536]{2,1,0:T(8,128)(2,1)}, bf16[2,1536,768]{2,1,0:T(8,128)(2,1)}, f32[1,3072]{1,0:T(1,128)}) custom-call(bf16[2048,768]{1,0:T(8,128)(2,1)} %get-tuple-element.139.normed, bf16[768,2048]{1,0:T(8,128)(2,1)} %get-tuple-element.140.normed_t, bf16[2048,768]{1,0:T(8,128)(2,1)} %cot.5, ...), custom_call_target="tpu_custom_call" | custom-call | flops 57999998976 | bytes 60000000 | tf_op jit(solution)/shard_map/pallas_call | solution.py:376
  228.0 2.8 constant_dynamic-slice_fusion
  236.6 18.5 %shard_map.473 = (bf16[2048,768]{1,0:T(8,128)(2,1)}, f32[2048,768]{1,0:T(8,128)}, bf16[2048,768]{1,0:T(8,128)(2,1)}, bf16[768,384]{1,0:T(8,128)(2,1)}, bf16[768,384]{1,0:T(8,128)(2,1)}, /*index=5*/f32[8,768]{1,0:T(8,128)}) custom-call(f32[2048,768]{1,0:T(8,128)} %get-tuple-element.146.middle, f32[2048,768]{1,0:T(8,128)} %get-tuple-element.147.forward, ...), custom_call_target="tpu_custom_call" | custom-call | flops 5000000000 | bytes 40000000 | tf_op jit(solution)/shard_map/pallas_call | solution.py:461
  255.1 2.6 bitcast_add_fusion.1
  259.0 2.1 bitcast_add_fusion
  264.4 31.6 %shard_map.474 = (bf16[3,5,256,1152]{3,2,1,0:T(8,128)(2,1)}, f32[80,128]{1,0:T(8,128)}, f32[8,1152]{1,0:T(8,128)}) custom-call(s32[24]{0:T(128)} %get-tuple-element.295.refs_0_, s32[24]{0:T(128)} %get-tuple-element.294.refs_1_, bf16[3,5,256,1152]{3,2,1,0:T(8,128)(2,1)} %get-tuple-element.162.refs_2_, ...), custom_call_target="tpu_custom_call" | custom-call | flops 13333332992 | bytes 30000000 | tf_op jit(solution)/shard_map/pallas_call | solution.py:583
  302.7 16.1 %shard_map.475 = (bf16[3,5,256,1152]{3,2,1,0:T(8,128)(2,1)}, f32[80,128]{1,0:T(8,128)}, f32[8,1152]{1,0:T(8,128)}) custom-call(s32[24]{0:T(128)} %get-tuple-element.295.refs_0_, s32[24]{0:T(128)} %get-tuple-element.294.refs_1_, bf16[3,5,256,1152]{3,2,1,0:T(8,128)(2,1)} %get-tuple-element.162.refs_2_, ...), custom_call_target="tpu_custom_call", output_to_operand_aliasing={{0}: (9, {})} | custom-call | flops 6666666496 | bytes 15000000 | tf_op jit(solution)/shard_map/pallas_call | solution.py:583
  324.7 13.0 %shard_map.476 = bf16[3,768,384]{2,1,0:T(8,128)(2,1)} custom-call(bf16[768,3840]{1,0:T(8,128)(2,1)} %get-tuple-element.152.xt, bf16[3840,1152]{1,0:T(8,128)(2,1)} %bitcast.129), custom_call_target="tpu_custom_call" | custom-call | flops 7000000000 | bytes 16000000 | tf_op jit(solution)/shard_map/pallas_call | solution.py:671
  343.3 2.6 collective-permute-start.17
  346.2 31.5 %shard_map.477 = (bf16[3,5,256,1152]{3,2,1,0:T(8,128)(2,1)}, f32[80,128]{1,0:T(8,128)}, f32[8,1152]{1,0:T(8,128)}) custom-call(s32[24]{0:T(128)} %get-tuple-element.295.refs_0_, s32[24]{0:T(128)} %get-tuple-element.294.refs_1_, bf16[3,5,256,1152]{3,2,1,0:T(8,128)(2,1)} %get-tuple-element.153.refs_2_, ...), custom_call_target="tpu_custom_call" | custom-call | flops 13333332992 | bytes 30000000 | tf_op jit(solution)/shard_map/pallas_call | solution.py:583
  377.7 2.5 bitcast_add_fusion.3
  382.8 16.8 %shard_map.478.refs_0_ = bf16[3,1024,768]{2,1,0:T(8,128)(2,1)} custom-call(bf16[3,5,256,1152]{3,2,1,0:T(8,128)(2,1)} %get-tuple-element.195.own.refs_9_, bf16[3,5,256,1152]{3,2,1,0:T(8,128)(2,1)} %get-tuple-element.177.other, bf16[3,768,384]{2,1,0:T(8,128)(2,1)} %weights_own.3, bf16[3,768,384]{2,1,0:T(8,128)(2,1)} %pad_maximum_fusion.6.weights.weights_other, ...), custom_call_target="tpu_custom_call" | custom-call | flops 9333332992 | bytes 20000000 | tf_op jit(solution)/shard_map/pallas_call | solution.py:637
  401.1 2.4 fusion.2
  405.1 2.6 collective-permute-start.20
  408.1 16.3 %shard_map.479 = (bf16[3,5,256,1152]{3,2,1,0:T(8,128)(2,1)}, f32[80,128]{1,0:T(8,128)}, f32[8,1152]{1,0:T(8,128)}) custom-call(s32[24]{0:T(128)} %get-tuple-element.295.refs_0_, s32[24]{0:T(128)} %get-tuple-element.294.refs_1_, bf16[3,5,256,1152]{3,2,1,0:T(8,128)(2,1)} %get-tuple-element.153.refs_2_, ...), custom_call_target="tpu_custom_call", output_to_operand_aliasing={{0}: (9, {})} | custom-call | flops 6666666496 | bytes 15000000 | tf_op jit(solution)/shard_map/pallas_call | solution.py:583
  424.4 25.2 %collective-permute-done.23.taken_a.taken_b = bf16[640,768]{1,0:T(8,128)(2,1)S(1)} collective-permute-done((bf16[640,768]{1,0:T(8,128)(2,1)}, bf16[640,768]{1,0:T(8,128)(2,1)S(1)}, u32[]{:S(2)}, u32[]{:S(2)}) %collective-permute-start.23) | collective-permute-done | bytes 983072 | tf_op jit(solution)/shard_map/ppermute | solution.py:894
  452.5 12.8 %shard_map.480 = bf16[3,768,384]{2,1,0:T(8,128)(2,1)} custom-call(bf16[768,3840]{1,0:T(8,128)(2,1)} %get-tuple-element.152.xt, bf16[3840,1152]{1,0:T(8,128)(2,1)} %bitcast.128), custom_call_target="tpu_custom_call" | custom-call | flops 7000000000 | bytes 16000000 | tf_op jit(solution)/shard_map/pallas_call | solution.py:671
  471.4 2.1 collective-permute-done.24
  478.4 10.4 %shard_map.481.up_a.up_b = bf16[3,1024,768]{2,1,0:T(8,128)(2,1)} custom-call(bf16[3,5,256,1152]{3,2,1,0:T(8,128)(2,1)} %get-tuple-element.212.own, bf16[3,5,256,1152]{3,2,1,0:T(8,128)(2,1)} %get-tuple-element.177.other, bf16[3,768,384]{2,1,0:T(8,128)(2,1)} %weights_own.3, ...), custom_call_target="tpu_custom_call", output_to_operand_aliasing={{}: (5, {})} | custom-call | flops 4666666496 | bytes 10000000 | tf_op jit(solution)/shard_map/pallas_call | solution.py:637
  488.8 3.7 collective-permute-done.26
  502.9 11.9 %shard_map.482 = (bf16[2048,768]{1,0:T(8,128)(2,1)}, f32[8,768]{1,0:T(8,128)}) custom-call(s32[16]{0:T(128)} %get-tuple-element.301.band_of, s32[16]{0:T(128)} %get-tuple-element.300.step_of, s32[16]{0:T(128)} %get-tuple-element.299.taken_of, s32[16]{0:T(128)} %get-tuple-element.298.has_taken, s32[1]{0:T(128)} %bitcast.offset, bf16[4096,768]{1,0:T(8,128)(2,1)} %x.11, ...), custom_call_target="tpu_custom_call" | custom-call | flops 100000000 | bytes 20000000 | tf_op jit(solution)/shard_map/pallas_call | solution.py:710
  515.8 44.2 %shard_map.483 = (bf16[4,768,384]{2,1,0:T(8,128)(2,1)S(1)}, f32[24,768]{1,0:T(8,128)S(1)}, f32[56,128]{1,0:T(8,128)S(1)}) custom-call(bf16[384,384]{1,0:T(8,128)(2,1)S(1)} %bitcast_add_fusion.8.refs_0_, bf16[384,384]{1,0:T(8,128)(2,1)S(1)} %bitcast_add_fusion.7.refs_1_, f32[8,768]{1,0:T(8,128)S(1)} %copy-done.12, f32[8,768]{1,0:T(8,128)S(1)} %copy-done.11, ...), custom_call_target="tpu_custom_call" | custom-call | tf_op jit(solution)/shard_map/pallas_call | solution.py:861
  564.4 2.7 bitcast_convert_fusion
  568.9 3.0 bitcast_convert_fusion.1
  (278 shorter events, 95.2 us)
Async XLA Ops:
  2.0 22.7 %collective-permute-start = (bf16[3,384,384]{2,1,0:T(8,128)(2,1)S(1)}, bf16[3,384,384]{2,1,0:T(8,128)(2,1)S(1)}, u32[]{:S(2)}, u32[]{:S(2)}) collective-permute-start(bf16[3,384,384]{2,1,0:T(8,128)(2,1)S(1)} %constant_dynamic-slice_fusion.5), channel_id=1, source_target_pairs={{0,1},{1,0},{2,3},{3,2},{4,5},{5,4},{6,7},{7,6},{8,9},{9,8},{10,11... | collective-permute-start | bytes 2654216 | tf_op jit(solution)/shard_map/ppermute | solution.py:989
  20.5 5.6 collective-permute-start.2
  30.7 55.2 %collective-permute-start.5 = (bf16[384,1536]{1,0:T(8,128)(2,1)}, bf16[384,1536]{1,0:T(8,128)(2,1)S(1)}, u32[]{:S(2)}, u32[]{:S(2)}) collective-permute-start(bf16[384,1536]{1,0:T(8,128)(2,1)} %constant_dynamic-slice_fusion.3), channel_id=1, source_target_pairs={{0,1},{1,0},{2,3},{3,2},{4,5},{5,4},{6,7},{7,6},{8,9},{9,8},{10,11... | collective-permute-start | bytes 3538952 | tf_op jit(solution)/shard_map/ppermute | solution.py:989
  75.9 10.0 %collective-permute-start.3 = (bf16[192,768]{1,0:T(8,128)(2,1)S(1)}, bf16[192,768]{1,0:T(8,128)(2,1)S(1)}, u32[]{:S(2)}, u32[]{:S(2)}) collective-permute-start(bf16[192,768]{1,0:T(8,128)(2,1)S(1)} %constant_dynamic-slice_fusion.4), channel_id=1, source_target_pairs={{0,1},{1,0},{2,3},{3,2},{4,5},{5,4},{6,7},{7,6},{8,9},{9,8},{10,11... | collective-permute-start | bytes 884744 | tf_op jit(solution)/shard_map/ppermute | solution.py:989
  79.2 50.7 %collective-permute-start.7 = (bf16[768,768]{1,0:T(8,128)(2,1)}, bf16[768,768]{1,0:T(8,128)(2,1)S(1)}, u32[]{:S(2)}, u32[]{:S(2)}) collective-permute-start(bf16[768,768]{1,0:T(8,128)(2,1)} %constant_dynamic-slice_fusion.2), channel_id=1, source_target_pairs={{0,1},{1,0},{2,3},{3,2},{4,5},{5,4},{6,7},{7,6},{8,9},{9,8},{10,11... | collective-permute-start | bytes 3538952 | tf_op jit(solution)/shard_map/ppermute | solution.py:989
  85.8 43.2 %collective-permute-start.4 = (bf16[192,768]{1,0:T(8,128)(2,1)S(1)}, bf16[192,768]{1,0:T(8,128)(2,1)S(1)}, u32[]{:S(2)}, u32[]{:S(2)}) collective-permute-start(bf16[192,768]{1,0:T(8,128)(2,1)S(1)} %collective-permute-done.3), channel_id=1, source_target_pairs={{0,2},{2,0},{4,6},{6,4},{8,10},{10,8},{12,14},{14,12},{16,18},{18,... | collective-permute-start | bytes 884744 | tf_op jit(solution)/shard_map/ppermute | solution.py:991
  85.9 60.5 %collective-permute-start.6 = (bf16[384,1536]{1,0:T(8,128)(2,1)S(1)}, bf16[384,1536]{1,0:T(8,128)(2,1)}, u32[]{:S(2)}, u32[]{:S(2)}) collective-permute-start(bf16[384,1536]{1,0:T(8,128)(2,1)S(1)} %collective-permute-done.5), channel_id=1, source_target_pairs={{0,2},{2,0},{4,6},{6,4},{8,10},{10,8},{12,14},{14,12},{16,18},{18,... | collective-permute-start | bytes 3538952 | tf_op jit(solution)/shard_map/ppermute | solution.py:991
  129.9 19.5 %collective-permute-start.8 = (bf16[768,768]{1,0:T(8,128)(2,1)S(1)}, bf16[768,768]{1,0:T(8,128)(2,1)}, u32[]{:S(2)}, u32[]{:S(2)}) collective-permute-start(bf16[768,768]{1,0:T(8,128)(2,1)S(1)} %collective-permute-done.7), channel_id=1, source_target_pairs={{0,2},{2,0},{4,6},{6,4},{8,10},{10,8},{12,14},{14,12},{16,18},{18,... | collective-permute-start | bytes 3538952 | tf_op jit(solution)/shard_map/ppermute | solution.py:991
  235.6 19.5 %collective-permute-start.10 = (bf16[2,2,2,2,96,768]{5,4,3,2,0,1:T(8,128)(2,1)}, bf16[2,2,2,2,96,768]{5,4,3,2,0,1:T(8,128)(2,1)}, u32[]{:S(2)}, u32[]{:S(2)}) collective-permute-start(bf16[2,2,2,2,96,768]{5,4,3,2,0,1:T(8,128)(2,1)} %bitcast.127), channel_id=1, source_target_pairs={{0,2},{2,0},{4,6},{6,4},{8,10},{10,8},{12,14},{14,12},{16,18},{18,... | collective-permute-start | bytes 7077896 | tf_op jit(solution)/shard_map/ppermute | solution.py:895
  236.1 19.0 %collective-permute-start.9 = (bf16[2,2,2,2,48,1536]{5,4,3,2,1,0:T(8,128)(2,1)}, bf16[2,2,2,2,48,1536]{5,4,3,2,1,0:T(8,128)(2,1)}, u32[]{:S(2)}, u32[]{:S(2)}) collective-permute-start(bf16[2,2,2,2,48,1536]{5,4,3,2,1,0:T(8,128)(2,1)} %dynamic-slice_bitcast_fusion), channel_id=1, source_target_pairs={{0,2},{2,0},{4,6},{6,4},{8,10},{10,8},{12,14},{14,12},{16,18},{18,... | collective-permute-start | bytes 7077896 | tf_op jit(solution)/shard_map/ppermute | solution.py:895
  262.4 33.6 %collective-permute-start.11 = (bf16[2,2,2,48,1536]{4,3,2,1,0:T(8,128)(2,1)}, bf16[2,2,2,48,1536]{4,3,2,1,0:T(8,128)(2,1)S(1)}, u32[]{:S(2)}, u32[]{:S(2)}) collective-permute-start(bf16[2,2,2,48,1536]{4,3,2,1,0:T(8,128)(2,1)} %slice_bitcast_fusion.1), channel_id=1, source_target_pairs={{0,1},{1,0},{2,3},{3,2},{4,5},{5,4},{6,7},{7,6},{8,9},{9,8},{10,11... | collective-permute-start | bytes 3538952 | tf_op jit(solution)/shard_map/ppermute | solution.py:894
  262.6 33.3 %collective-permute-start.12 = (bf16[2,2,2,96,768]{4,3,2,1,0:T(8,128)(2,1)}, bf16[2,2,2,96,768]{4,3,2,1,0:T(8,128)(2,1)}, u32[]{:S(2)}, u32[]{:S(2)}) collective-permute-start(bf16[2,2,2,96,768]{4,3,2,1,0:T(8,128)(2,1)} %dynamic-slice_bitcast_fusion.3), channel_id=1, source_target_pairs={{0,4},{2,6},{4,0},{6,2},{8,12},{10,14},{12,8},{14,10},{16,20},{18,... | collective-permute-start | bytes 3538952 | tf_op jit(solution)/shard_map/ppermute | solution.py:895
  300.5 18.2 %collective-permute-start.13 = (bf16[2,2,48,1536]{3,2,1,0:T(8,128)(2,1)S(1)}, bf16[2,2,48,1536]{3,2,1,0:T(8,128)(2,1)}, u32[]{:S(2)}, u32[]{:S(2)}) collective-permute-start(bf16[2,2,48,1536]{3,2,1,0:T(8,128)(2,1)S(1)} %dynamic-slice_bitcast_fusion.5), channel_id=1, source_target_pairs={{0,4},{2,6},{4,0},{6,2},{8,12},{10,14},{12,8},{14,10},{16,20},{18,... | collective-permute-start | bytes 1769480 | tf_op jit(solution)/shard_map/ppermute | solution.py:895
  300.9 17.9 %collective-permute-start.14 = (bf16[2,2,96,768]{3,2,1,0:T(8,128)(2,1)S(1)}, bf16[2,2,96,768]{3,2,1,0:T(8,128)(2,1)}, u32[]{:S(2)}, u32[]{:S(2)}) collective-permute-start(bf16[2,2,96,768]{3,2,1,0:T(8,128)(2,1)S(1)} %dynamic-slice_bitcast_fusion.4), channel_id=1, source_target_pairs={{0,8},{2,10},{4,12},{6,14},{8,0},{10,2},{12,4},{14,6},{16,24},{18,... | collective-permute-start | bytes 1769480 | tf_op jit(solution)/shard_map/ppermute | solution.py:895
  322.7 16.8 %collective-permute-start.15 = (bf16[2,48,1536]{2,1,0:T(8,128)(2,1)}, bf16[2,48,1536]{2,1,0:T(8,128)(2,1)S(1)}, u32[]{:S(2)}, u32[]{:S(2)}) collective-permute-start(bf16[2,48,1536]{2,1,0:T(8,128)(2,1)} %dynamic-slice_bitcast_fusion.8), channel_id=1, source_target_pairs={{0,8},{2,10},{4,12},{6,14},{8,0},{10,2},{12,4},{14,6},{16,24},{18,... | collective-permute-start | bytes 884744 | tf_op jit(solution)/shard_map/ppermute | solution.py:895
  322.9 16.6 %collective-permute-start.16 = (bf16[2,96,768]{2,1,0:T(8,128)(2,1)}, bf16[2,96,768]{2,1,0:T(8,128)(2,1)}, u32[]{:S(2)}, u32[]{:S(2)}) collective-permute-start(bf16[2,96,768]{2,1,0:T(8,128)(2,1)} %slice_bitcast_fusion.5), channel_id=1, source_target_pairs={{0,1},{1,0},{2,3},{3,2},{4,5},{5,4},{6,7},{7,6},{8,9},{9,8},{10,11... | collective-permute-start | bytes 884744 | tf_op jit(solution)/shard_map/ppermute | solution.py:894
  343.3 34.4 %collective-permute-start.19 = (bf16[2,2,2,192,384]{4,3,2,1,0:T(8,128)(2,1)S(1)}, bf16[2,2,2,192,384]{4,3,2,1,0:T(8,128)(2,1)}, u32[]{:S(2)}, u32[]{:S(2)}) collective-permute-start(bf16[2,2,2,192,384]{4,3,2,1,0:T(8,128)(2,1)S(1)} %dynamic-slice_bitcast_fusion.2), channel_id=1, source_target_pairs={{0,2},{2,0},{4,6},{6,4},{8,10},{10,8},{12,14},{14,12},{16,18},{18,... | collective-permute-start | bytes 3538952 | tf_op jit(solution)/shard_map/ppermute | solution.py:895
  343.3 34.4 %collective-permute-start.17 = (bf16[48,1536]{1,0:T(8,128)(2,1)}, bf16[48,1536]{1,0:T(8,128)(2,1)}, u32[]{:S(2)}, u32[]{:S(2)}) collective-permute-start(bf16[48,1536]{1,0:T(8,128)(2,1)} %dynamic-slice_bitcast_fusion.10), channel_id=1, source_target_pairs={{0,16},{2,18},{4,20},{6,22},{8,24},{10,26},{12,28},{14,30},{16,0},... | collective-permute-start | bytes 442376 | tf_op jit(solution)/shard_map/ppermute | solution.py:895
  345.9 31.8 %collective-permute-start.18 = (bf16[96,768]{1,0:T(8,128)(2,1)S(1)}, bf16[96,768]{1,0:T(8,128)(2,1)}, u32[]{:S(2)}, u32[]{:S(2)}) collective-permute-start(bf16[96,768]{1,0:T(8,128)(2,1)S(1)} %dynamic-slice_bitcast_fusion.9), channel_id=1, source_target_pairs={{0,16},{2,18},{4,20},{6,22},{8,24},{10,26},{12,28},{14,30},{16,0},... | collective-permute-start | bytes 442376 | tf_op jit(solution)/shard_map/ppermute | solution.py:895
  400.7 49.0 %collective-permute-start.22 = (bf16[2,2,2,192,384]{4,3,2,1,0:T(8,128)(2,1)S(1)}, bf16[2,2,2,192,384]{4,3,2,1,0:T(8,128)(2,1)S(1)}, u32[]{:S(2)}, u32[]{:S(2)}) collective-permute-start(bf16[2,2,2,192,384]{4,3,2,1,0:T(8,128)(2,1)S(1)} %copy-done.38), channel_id=1, source_target_pairs={{0,1},{1,0},{2,3},{3,2},{4,5},{5,4},{6,7},{7,6},{8,9},{9,8},{10,11... | collective-permute-start | bytes 3538952 | tf_op jit(solution)/shard_map/ppermute | solution.py:894
  403.4 46.2 %collective-permute-start.23 = (bf16[640,768]{1,0:T(8,128)(2,1)}, bf16[640,768]{1,0:T(8,128)(2,1)S(1)}, u32[]{:S(2)}, u32[]{:S(2)}) collective-permute-start(bf16[640,768]{1,0:T(8,128)(2,1)} %fusion.2), channel_id=1, source_target_pairs={{0,1},{1,0},{2,3},{3,2},{4,5},{5,4},{6,7},{7,6},{8,9},{9,8},{10,11... | collective-permute-start | bytes 2949128 | tf_op jit(solution)/shard_map/ppermute | solution.py:894
  405.1 19.3 %collective-permute-start.20 = (bf16[48,1536]{1,0:T(8,128)(2,1)S(1)}, bf16[48,1536]{1,0:T(8,128)(2,1)S(1)}, u32[]{:S(2)}, u32[]{:S(2)}) collective-permute-start(bf16[48,1536]{1,0:T(8,128)(2,1)S(1)} %bitcast_add_fusion.11), channel_id=1, source_target_pairs={{0,16},{2,18},{4,20},{6,22},{8,24},{10,26},{12,28},{14,30},{16,0},... | collective-permute-start | bytes 442376 | tf_op jit(solution)/shard_map/ppermute | solution.py:895
  407.7 16.7 %collective-permute-start.21 = (bf16[96,768]{1,0:T(8,128)(2,1)}, bf16[96,768]{1,0:T(8,128)(2,1)}, u32[]{:S(2)}, u32[]{:S(2)}) collective-permute-start(bf16[96,768]{1,0:T(8,128)(2,1)} %bitcast_add_fusion.10), channel_id=1, source_target_pairs={{0,16},{2,18},{4,20},{6,22},{8,24},{10,26},{12,28},{14,30},{16,0},... | collective-permute-start | bytes 442376 | tf_op jit(solution)/shard_map/ppermute | solution.py:895
  465.3 8.2 %collective-permute-start.24 = (bf16[2,48,1536]{2,1,0:T(8,128)(2,1)}, bf16[2,48,1536]{2,1,0:T(8,128)(2,1)S(1)}, u32[]{:S(2)}, u32[]{:S(2)}) collective-permute-start(bf16[2,48,1536]{2,1,0:T(8,128)(2,1)} %pad_maximum_fusion.12), channel_id=1, source_target_pairs={{0,8},{2,10},{4,12},{6,14},{8,0},{10,2},{12,4},{14,6},{16,24},{18,... | collective-permute-start | bytes 884744 | tf_op jit(solution)/shard_map/ppermute | solution.py:895
  466.8 7.7 %collective-permute-start.25 = (bf16[2,96,768]{2,1,0:T(8,128)(2,1)S(1)}, bf16[2,96,768]{2,1,0:T(8,128)(2,1)S(1)}, u32[]{:S(2)}, u32[]{:S(2)}) collective-permute-start(bf16[2,96,768]{2,1,0:T(8,128)(2,1)S(1)} %pad_maximum_fusion.13), channel_id=1, source_target_pairs={{0,4},{2,6},{4,0},{6,2},{8,12},{10,14},{12,8},{14,10},{16,20},{18,... | collective-permute-start | bytes 884744 | tf_op jit(solution)/shard_map/ppermute | solution.py:895
  476.4 17.3 %collective-permute-start.28 = (bf16[2,2,2,192,384]{4,3,2,1,0:T(8,128)(2,1)}, bf16[2,2,2,192,384]{4,3,2,1,0:T(8,128)(2,1)}, u32[]{:S(2)}, u32[]{:S(2)}) collective-permute-start(bf16[2,2,2,192,384]{4,3,2,1,0:T(8,128)(2,1)} %dynamic-slice_bitcast_fusion.1), channel_id=1, source_target_pairs={{0,2},{2,0},{4,6},{6,4},{8,10},{10,8},{12,14},{14,12},{16,18},{18,... | collective-permute-start | bytes 3538952 | tf_op jit(solution)/shard_map/ppermute | solution.py:895
  476.4 16.1 %collective-permute-start.26 = (bf16[2,2,48,1536]{3,2,1,0:T(8,128)(2,1)}, bf16[2,2,48,1536]{3,2,1,0:T(8,128)(2,1)}, u32[]{:S(2)}, u32[]{:S(2)}) collective-permute-start(bf16[2,2,48,1536]{3,2,1,0:T(8,128)(2,1)} %pad_maximum_fusion.10), channel_id=1, source_target_pairs={{0,4},{2,6},{4,0},{6,2},{8,12},{10,14},{12,8},{14,10},{16,20},{18,... | collective-permute-start | bytes 1769480 | tf_op jit(solution)/shard_map/ppermute | solution.py:895
  477.9 15.8 %collective-permute-start.27 = (bf16[2,2,96,768]{3,2,1,0:T(8,128)(2,1)}, bf16[2,2,96,768]{3,2,1,0:T(8,128)(2,1)}, u32[]{:S(2)}, u32[]{:S(2)}) collective-permute-start(bf16[2,2,96,768]{3,2,1,0:T(8,128)(2,1)} %pad_maximum_fusion.11), channel_id=1, source_target_pairs={{0,8},{2,10},{4,12},{6,14},{8,0},{10,2},{12,4},{14,6},{16,24},{18,... | collective-permute-start | bytes 1769480 | tf_op jit(solution)/shard_map/ppermute | solution.py:895
  498.8 16.0 %collective-permute-start.29 = (bf16[2,2,2,48,1536]{4,3,2,1,0:T(8,128)(2,1)}, bf16[2,2,2,48,1536]{4,3,2,1,0:T(8,128)(2,1)}, u32[]{:S(2)}, u32[]{:S(2)}) collective-permute-start(bf16[2,2,2,48,1536]{4,3,2,1,0:T(8,128)(2,1)} %pad_maximum_fusion.7), channel_id=1, source_target_pairs={{0,2},{2,0},{4,6},{6,4},{8,10},{10,8},{12,14},{14,12},{16,18},{18,... | collective-permute-start | bytes 3538952 | tf_op jit(solution)/shard_map/ppermute | solution.py:895
  498.8 16.0 %collective-permute-start.30 = (bf16[2,2,2,96,768]{4,3,2,1,0:T(8,128)(2,1)}, bf16[2,2,2,96,768]{4,3,2,1,0:T(8,128)(2,1)}, u32[]{:S(2)}, u32[]{:S(2)}) collective-permute-start(bf16[2,2,2,96,768]{4,3,2,1,0:T(8,128)(2,1)} %pad_maximum_fusion.8), channel_id=1, source_target_pairs={{0,2},{2,0},{4,6},{6,4},{8,10},{10,8},{12,14},{14,12},{16,18},{18,... | collective-permute-start | bytes 3538952 | tf_op jit(solution)/shard_map/ppermute | solution.py:895
  501.2 13.6 %collective-permute-start.31 = (bf16[384,384]{1,0:T(8,128)(2,1)S(1)}, bf16[384,384]{1,0:T(8,128)(2,1)S(1)}, u32[]{:S(2)}, u32[]{:S(2)}) collective-permute-start(bf16[384,384]{1,0:T(8,128)(2,1)S(1)} %dynamic-slice_bitcast_fusion.7), channel_id=1, source_target_pairs={{0,4},{2,6},{4,0},{6,2},{8,12},{10,14},{12,8},{14,10},{16,20},{18,... | collective-permute-start | bytes 884744 | tf_op jit(solution)/shard_map/ppermute | solution.py:895
  501.8 13.0 %collective-permute-start.32 = (bf16[384,384]{1,0:T(8,128)(2,1)S(1)}, bf16[384,384]{1,0:T(8,128)(2,1)S(1)}, u32[]{:S(2)}, u32[]{:S(2)}) collective-permute-start(bf16[384,384]{1,0:T(8,128)(2,1)S(1)} %dynamic-slice_bitcast_fusion.6), channel_id=1, source_target_pairs={{0,8},{2,10},{4,12},{6,14},{8,0},{10,2},{12,4},{14,6},{16,24},{18,... | collective-permute-start | bytes 884744 | tf_op jit(solution)/shard_map/ppermute | solution.py:895
  (63 other events, 618.7 us)

commit v3 on v2

v3 whole, which is shorter than its diff:
```python
import jax
import jax.numpy as jnp
import numpy as np
from jax import lax
from jax.experimental import pallas as pl
from jax.experimental.pallas import tpu as pltpu
from jax.sharding import PartitionSpec as P

D = 768
HEADS = 12
HD = 64
FF = 3072
WIN = 14
SIDE = 64
NWIN = 5
RELS = 27
EPSILON = 1e-06
F32 = jnp.float32
BF = jnp.bfloat16

SLOTS = 256
KEYS = WIN * 16
PAIR = 2 * SIDE
GREL = 80
OWN = SIDE * SIDE // 2

HALF = D // 2
TRIO = 3 * HALF
PAIRS = HEADS // 4

NN = (((1,), (0,)), ((), ()))
NT = (((1,), (1,)), ((), ()))
TN = (((0,), (0,)), ((), ()))


def dot(left, right, dims=NN):
    return lax.dot_general(left, right, dims, preferred_element_type=F32)


def params(limit=60):
    return pltpu.CompilerParams(vmem_limit_bytes=limit * 2**20)


def cost(flops, moved, exps=0):
    return pl.CostEstimate(flops=int(flops), bytes_accessed=int(moved), transcendentals=int(exps))


def whole(shape):
    return pl.BlockSpec(shape, lambda *_: (0,) * len(shape), pipeline_mode=pl.Buffered(1))


STARTS = np.array([[0, 14, 28], [42, 28, 56]], np.int32)


def pair_tables(place):
    block = np.zeros((2, 24), np.int32)
    valid = np.zeros((2, 24), np.int32)
    local = np.zeros((2, 24), np.int32)
    owned = np.zeros((2, 24), np.int32)
    band_of = np.zeros((2, 16), np.int32)
    step_of = np.zeros((2, 16), np.int32)
    taken_of = np.zeros((2, 16), np.int32)
    has_taken = np.zeros((2, 16), np.int32)
    taken_of[0, 14:16], has_taken[0, 14:16] = np.arange(2), 1
    taken_of[1, 0:5], has_taken[1, 0:5] = np.arange(5), 1
    for m in range(2):
        for s in range(3):
            for t in range(7):
                row = STARTS[m, s] + 2 * t
                at = s * 8 + t
                block[m, at] = min(row // 2, 31)
                valid[m, at] = row < SIDE
                if 32 * m <= row < 32 * m + 32:
                    local[m, at] = (row - 32 * m) // 2
                    owned[m, at] = 1
                    band_of[m, local[m, at]] = s
                    step_of[m, local[m, at]] = t
            block[m, s * 8 + 7] = block[m, s * 8 + 6]
    pick = lambda table: jnp.where(place == 0, jnp.asarray(table[0]), jnp.asarray(table[1]))
    return tuple(pick(t) for t in (block, valid, local, owned, band_of, step_of, taken_of, has_taken))


def spread_rows():
    table = np.zeros((NWIN, 2, 16, PAIR), np.float32)
    for w in range(NWIN):
        for r in range(2):
            for j in range(WIN):
                if WIN * w + j < SIDE:
                    table[w, r, j, r * SIDE + WIN * w + j] = 1
    return table.reshape(NWIN * 32, PAIR)


def rel_order():
    rows = np.full(GREL, -1)
    for m in range(21):
        rows[m] = 26 - (m + 6)
        rows[24 + m] = 26 - m
    cols = np.full(GREL, -1)
    for m in range(RELS):
        cols[48 + m] = 26 - m
    return rows, cols


def rel_onehots():
    rows, cols = rel_order()
    high = (rows[:, None] == np.arange(RELS)[None, :]).astype(np.float32)
    wide = (cols[:, None] == np.arange(RELS)[None, :]).astype(np.float32)
    return high, wide


def norm_parts(values):
    average = jnp.mean(values, axis=-1, keepdims=True)
    centred = values - average
    inverse = lax.rsqrt(jnp.mean(centred * centred, axis=-1, keepdims=True) + EPSILON)
    return centred * inverse, inverse


def vec(ref):
    return ref[...].astype(F32).reshape(1, D)


def window_kernel(block, valid, *refs):
    xs, (gain, shift, spread, out) = refs[:7], refs[7:]
    band = pl.program_id(0)
    for t in range(7):
        scaled, _ = norm_parts(xs[t][...].astype(F32))
        normed = scaled * vec(gain) + vec(shift)
        normed = (normed * valid[band * 8 + t].astype(F32)).astype(BF)
        moved = dot(spread[...], normed).astype(BF)
        out[:, :, 32 * t : 32 * t + 32, :] = moved.reshape(1, NWIN, 32, D)
    out[:, :, 224:, :] = jnp.zeros((1, NWIN, 32, D), BF)


def windows_of(x, gain, shift, spread, block, valid):
    at = lambda t: lambda s, block, valid: (block[s * 8 + t], 0)
    return pl.pallas_call(
        window_kernel,
        grid_spec=pltpu.PrefetchScalarGridSpec(
            num_scalar_prefetch=2,
            grid=(3,),
            in_specs=[pl.BlockSpec((PAIR, D), at(t)) for t in range(7)]
            + [whole((D,)), whole((D,)), whole((NWIN * 32, PAIR))],
            out_specs=pl.BlockSpec((1, NWIN, SLOTS, D), lambda s, *_: (s, 0, 0, 0)),
        ),
        out_shape=jax.ShapeDtypeStruct((3, NWIN, SLOTS, D), BF),
        compiler_params=params(),
        cost_estimate=cost(3 * 7 * 160 * 128 * 768 * 2, 10e6),
    )(block, valid, *([x] * 7), gain, shift, spread)


def shift_masks(lanes_from):
    lane = lax.broadcasted_iota(jnp.int32, (1, 128), 1) + lanes_from
    high = lane // 16
    row_shift = jnp.where(lane < 128, 7 - high, jnp.maximum(13 - high, 0))
    col_shift = jnp.maximum(13 - lane % 16, 0)
    return row_shift, col_shift


def skew(table, shift, bits):
    size = table.shape[0]
    for bit in bits:
        moved = pltpu.roll(table, size - bit, 0)
        table = jnp.where((shift & bit) != 0, moved, table)
    return table


def unskew(table, shift, bits):
    for bit in bits:
        moved = pltpu.roll(table, bit, 0)
        table = jnp.where((shift & bit) != 0, moved, table)
    return table


def start_own(weights, bias, high_hot, wide_hot, rel_rows, rel_cols, rel_even, rel_odd, joined):
    for s in range(3):
        joined[:, s * HALF : s * HALF + HALF] = weights[s]
    table = (dot(high_hot[...], rel_rows[...]) + dot(wide_hot[...], rel_cols[...])).astype(BF)
    blank = jnp.zeros_like(table)
    rel_even[...] = jnp.concatenate([table, blank], axis=1)
    rel_odd[...] = jnp.concatenate([blank, table], axis=1)


def join_pieces(core, mine, theirs, joined, col):
    for piece, at in ((mine, core), (theirs, 1 - core)):
        rows = pl.ds(pl.multiple_of(at * HALF, HALF), HALF)
        for s in range(3):
            joined[rows, col + s * HALF : col + s * HALF + HALF] = piece[s]


def attend_own(
    x, bias, weights, high_hot, wide_hot, rel_rows, rel_cols,
    qkv_out, p_out, ctx_out, xt_out, rel_even, rel_odd, joined, vt,
):
    @pl.when((pl.program_id(0) == 0) & (pl.program_id(1) == 0))
    def _():
        start_own(weights, bias, high_hot, wide_hot, rel_rows, rel_cols, rel_even, rel_odd, joined)

    attend_window(x, bias, rel_even, rel_odd, qkv_out, p_out, ctx_out, xt_out, joined, vt)


def attend_other(x, bias, core, mine, theirs, rel_even, rel_odd, qkv_out, p_out, ctx_out, joined, vt):
    @pl.when((pl.program_id(0) == 0) & (pl.program_id(1) == 0))
    def _():
        join_pieces(core[0], mine, theirs, joined, 0)

    attend_window(x, bias, rel_even, rel_odd, qkv_out, p_out, ctx_out, None, joined, vt)


def attend_window(x, bias, rel_even, rel_odd, qkv_out, p_out, ctx_out, xt_out, joined, vt):
    band = pl.program_id(0)
    biases = bias[...].astype(F32)
    biases = jnp.concatenate([biases[0:1], jnp.zeros((1, HALF), F32), biases[1:2]], axis=1)
    block = x[...].reshape(SLOTS, D)
    if xt_out is not None:
        xt_out[...] = block.T
    scales = jnp.where(lax.broadcasted_iota(jnp.int32, (1, TRIO), 1) // HALF == 1, HD ** (-0.5), 1.0)
    low = ((dot(block, joined[...]) + biases) * scales).astype(BF)
    qkv_out[0, 0] = low
    vt[...] = low[:, 2 * HALF :].T

    even = lax.broadcasted_iota(jnp.int32, (1, 128), 1) < HD

    def raw_scores(head, lanes):
        col = head // 2 * 128
        keys = qkv_out[0, 0, 0:KEYS, HALF + col : HALF + col + 128]
        kept = jnp.where(even != (head % 2 == 1), keys, jnp.zeros_like(keys))
        rel = rel_odd if head % 2 else rel_even
        left = jnp.concatenate([kept, rel[...]], axis=0)
        return dot(left, qkv_out[0, 0, 0:lanes, col : col + 128], NT)

    def soft(head, raw, lanes):
        parts = []
        for tile in range(lanes // 128):
            row_shift, col_shift = shift_masks(tile * 128)
            raw_t = raw[:, tile * 128 : tile * 128 + 128]
            base = raw_t[0:KEYS]
            high = skew(raw_t[KEYS + 24 * tile : KEYS + 24 * tile + 24], row_shift, (4, 2, 1))[0:16]
            wide = skew(raw_t[KEYS + 48 : KEYS + 80], col_shift, (8, 4, 2, 1))[0:16]
            place = lax.broadcasted_iota(jnp.int32, (16, 128), 0)
            wide = jnp.where(place < WIN, wide, -1e30)
            scores = base.reshape(WIN, 16, 128) + wide[None] + high[0:WIN][:, None, :]
            scores = scores.reshape(KEYS, 128)
            peak = jnp.max(scores, axis=0, keepdims=True)
            grown = jnp.exp(scores - peak)
            total = jnp.sum(grown, axis=0, keepdims=True)
            parts.append((grown * (1.0 / total)).astype(BF))
        probs = parts[0] if len(parts) == 1 else jnp.concatenate(parts, axis=1)
        p_out[0, 0, head, :, 0:lanes] = probs
        return probs

    def all_heads(lanes):
        count = HEADS // 2
        raw = raw_scores(0, lanes)
        contexts = []
        for head in range(count):
            ahead = raw_scores(head + 1, lanes) if head + 1 < count else None
            probs = soft(head, raw, lanes)
            if head:
                contexts.append(dot(vt[(head - 1) * HD : head * HD, 0:KEYS], before).astype(BF))
            if head and head % 2 == 0:
                col = (head - 2) * HD
                ctx_out[0, 0, 0:lanes, col : col + 128] = jnp.concatenate(contexts[-2:], axis=0).T
            before, raw = probs, ahead
        contexts.append(dot(vt[(count - 1) * HD :, 0:KEYS], before).astype(BF))
        ctx_out[0, 0, 0:lanes, HALF - 128 :] = jnp.concatenate(contexts[-2:], axis=0).T

    @pl.when(band < 2)
    def _():
        all_heads(256)

    @pl.when(band == 2)
    def _():
        all_heads(128)


SCALAR = pl.BlockSpec(memory_space=pltpu.SMEM)


def attend(x, bias, first, *operands):
    block = lambda width: pl.BlockSpec((1, 1, SLOTS, width), lambda s, w: (s, w, 0, 0))
    shape = lambda width: jax.ShapeDtypeStruct((3, NWIN, SLOTS, width), BF)
    out_specs = [
        block(TRIO),
        pl.BlockSpec((1, 1, HEADS // 2, KEYS, SLOTS), lambda s, w: (s, w, 0, 0, 0)),
        block(HALF),
    ]
    out_shape = [
        shape(TRIO),
        jax.ShapeDtypeStruct((3, NWIN, HEADS // 2, KEYS, SLOTS), BF),
        shape(HALF),
    ]
    rel = pl.BlockSpec((GREL, 128), lambda s, w: (0, 0))
    if first:
        in_specs = [whole((3, D, HALF)), whole((GREL, RELS)), whole((GREL, RELS)), whole((RELS, HD)), whole((RELS, HD))]
        out_specs += [pl.BlockSpec((D, SLOTS), lambda s, w: (0, s * NWIN + w)), rel, rel]
        out_shape += [jax.ShapeDtypeStruct((D, 3 * NWIN * SLOTS), BF)] + [jax.ShapeDtypeStruct((GREL, 128), BF)] * 2
    else:
        in_specs = [SCALAR, whole((3, HALF, HALF)), whole((3, HALF, HALF)), whole((GREL, 128)), whole((GREL, 128))]
    return pl.pallas_call(
        attend_own if first else attend_other,
        grid=(3, NWIN),
        in_specs=[block(D), whole((2, HALF))] + in_specs,
        out_specs=out_specs,
        out_shape=out_shape,
        scratch_shapes=[pltpu.VMEM((D, TRIO), BF), pltpu.VMEM((HALF, SLOTS), BF)],
        compiler_params=params(),
        cost_estimate=cost(15e9, 45e6, 4e6),
    )(x, bias, *operands)


def middle_kernel(
    band_of, step_of, offset, own_a, own_b, other_a, other_b, x, cot, proj_own, proj_other, bias, gain, shift, gather,
    middle, normed, normed_t, cot_t, ctx_out, proj,
):
    @pl.when(pl.program_id(0) == 0)
    def _():
        proj[0:HALF, :] = proj_own[...]
        proj[HALF:, :] = proj_other[...]

    for row, parts in ((0, (own_a, other_a)), (PAIR, (own_b, other_b))):
        for side in range(2):
            moved = dot(gather[...], parts[side][...].reshape(NWIN * 32, HALF)).astype(BF)
            ctx_out[row : row + PAIR, side * HALF : side * HALF + HALF] = moved
    value = x[...].astype(F32) + (dot(ctx_out[...], proj[...]) + vec(bias))
    middle[...] = value
    scaled, _ = norm_parts(value)
    low = (scaled * vec(gain) + vec(shift)).astype(BF)
    normed[...] = low
    normed_t[...] = low.T
    cot_t[...] = cot[...].T


def middle_of(ctx_own, ctx_other, x, cot, proj_own, proj_other, bias, gain, shift, gather, band_of, step_of, offset):
    rows = 2 * PAIR
    at = lambda k: lambda i, band_of, step_of, offset: (band_of[2 * i + k], 0, step_of[2 * i + k], 0)
    row_block = pl.BlockSpec((rows, D), lambda i, *_: (i, 0))
    col_block = pl.BlockSpec((D, rows), lambda i, *_: (0, i))
    return pl.pallas_call(
        middle_kernel,
        grid_spec=pltpu.PrefetchScalarGridSpec(
            num_scalar_prefetch=3,
            grid=(OWN // rows,),
            in_specs=[
                pl.BlockSpec((1, NWIN, 32, HALF), at(0)),
                pl.BlockSpec((1, NWIN, 32, HALF), at(1)),
                pl.BlockSpec((1, NWIN, 32, HALF), at(0)),
                pl.BlockSpec((1, NWIN, 32, HALF), at(1)),
                pl.BlockSpec((rows, D), lambda i, band_of, step_of, offset: (offset[0] + i, 0)),
                row_block,
                whole((HALF, D)),
                whole((HALF, D)),
                whole((D,)),
                whole((D,)),
                whole((D,)),
                whole((PAIR, NWIN * 32)),
            ],
            out_specs=[row_block, row_block, col_block, col_block, row_block],
            scratch_shapes=[pltpu.VMEM((D, D), BF)],
        ),
        out_shape=[
            jax.ShapeDtypeStruct((OWN, D), F32),
            jax.ShapeDtypeStruct((OWN, D), BF),
            jax.ShapeDtypeStruct((D, OWN), BF),
            jax.ShapeDtypeStruct((D, OWN), BF),
            jax.ShapeDtypeStruct((OWN, D), BF),
        ],
        compiler_params=params(),
        cost_estimate=cost(3e9, 30e6),
    )(band_of, step_of, offset, ctx_own, ctx_own, ctx_other, ctx_other, x, cot, proj_own, proj_other, bias, gain, shift, gather)


CHUNK = 512
CHUNKS = FF // CHUNK


def feed_kernel(
    core, normed, normed_t, cot, cot_t, one_a, one_b, one_c, bias_a, bias_b, two_a, two_b, two_c,
    forward, back, one_kept, one_sent, two_kept, two_sent, sums, one, two, bias, hidden, grads,
):
    step = pl.program_id(0)

    @pl.when(step == 0)
    def _():
        forward[...] = jnp.zeros_like(forward)
        back[...] = jnp.zeros_like(back)

    @pl.when(step < CHUNKS // 2)
    def _():
        bias[...] = bias_a[...].astype(F32).reshape(1, CHUNK)
        one[...] = one_a[...]
        two[...] = two_a[...]

    @pl.when(step >= CHUNKS // 2)
    def _():
        bias[...] = bias_b[...].astype(F32).reshape(1, CHUNK)
        mine = pl.multiple_of(core[0] * HALF, HALF)
        theirs = pl.multiple_of((1 - core[0]) * HALF, HALF)
        one[pl.ds(mine, HALF), :] = one_b[...]
        one[pl.ds(theirs, HALF), :] = one_c[...]
        two[:, pl.ds(mine, HALF)] = two_b[...]
        two[:, pl.ds(theirs, HALF)] = two_c[...]

    total = jnp.zeros((1, CHUNK), F32)
    for t in range(OWN // 256):
        rows = slice(t * 256, t * 256 + 256)
        pre = dot(normed[rows, :], one[...]) + bias[...]
        phi = 0.5 * (1.0 + lax.erf(pre * 0.7071067811865476))
        slope = phi + pre * (jnp.exp(-0.5 * pre * pre) * 0.3989422804014327)
        low = (pre * phi).astype(BF)
        grad = (dot(cot[rows, :], two[...], NT) * slope).astype(BF)
        hidden[rows, :] = low
        grads[rows, :] = grad
        total += jnp.sum(grad.astype(F32), axis=0, keepdims=True)
        forward[rows, :] += dot(low, two[...])
        back[rows, :] += dot(grad, one[...], NT)
    sums[...] = total

    first = core[0] == 0
    one_grad = dot(normed_t[...], grads[...]).astype(BF)
    low, high = one_grad[:HALF], one_grad[HALF:]
    one_kept[0] = jnp.where(first, low, high)
    one_sent[0] = jnp.where(first, high, low)
    two_grad = dot(cot_t[...], hidden[...]).astype(BF)
    low, high = two_grad[:HALF], two_grad[HALF:]
    two_kept[0] = jnp.where(first, low, high).T
    two_sent[0] = jnp.where(first, high, low).T


def feed(core, normed, normed_t, cot, cot_t, one_a, ones, bias_a, bias_b, two_a, twos):
    half = CHUNKS // 2
    own = lambda j: jnp.minimum(j, half - 1)
    other = lambda j: jnp.maximum(j - half, 0)
    one_block = pl.BlockSpec((1, HALF, CHUNK), lambda j, *_: (j // half, 0, j % half))
    two_block = pl.BlockSpec((1, CHUNK, HALF), lambda j, *_: (j // half, j % half, 0))
    one_piece = pl.BlockSpec((HALF, CHUNK), lambda j, *_: (0, other(j)))
    two_piece = pl.BlockSpec((CHUNK, HALF), lambda j, *_: (other(j), 0))
    one_shape = jax.ShapeDtypeStruct((2, HALF, FF // 2), BF)
    two_shape = jax.ShapeDtypeStruct((2, FF // 2, HALF), BF)
    sum_block = pl.BlockSpec((OWN, D), lambda j, *_: (0, 0))
    bias_block = pl.BlockSpec((1, CHUNK), lambda j, *_: (0, j))
    return pl.pallas_call(
        feed_kernel,
        grid_spec=pltpu.PrefetchScalarGridSpec(
            num_scalar_prefetch=1,
            grid=(CHUNKS,),
            in_specs=[
                whole((OWN, D)),
                whole((D, OWN)),
                whole((OWN, D)),
                whole((D, OWN)),
                pl.BlockSpec((D, CHUNK), lambda j, *_: (0, own(j))),
                one_piece,
                one_piece,
                pl.BlockSpec((CHUNK,), lambda j, *_: (own(j),)),
                pl.BlockSpec((CHUNK,), lambda j, *_: (other(j),)),
                pl.BlockSpec((CHUNK, D), lambda j, *_: (own(j), 0)),
                two_piece,
                two_piece,
            ],
            out_specs=[sum_block, sum_block, one_block, one_block, two_block, two_block, bias_block],
            scratch_shapes=[
                pltpu.VMEM((D, CHUNK), BF),
                pltpu.VMEM((CHUNK, D), BF),
                pltpu.VMEM((1, CHUNK), F32),
                pltpu.VMEM((OWN, CHUNK), BF),
                pltpu.VMEM((OWN, CHUNK), BF),
            ],
        ),
        out_shape=[
            jax.ShapeDtypeStruct((OWN, D), F32),
            jax.ShapeDtypeStruct((OWN, D), F32),
            one_shape,
            one_shape,
            two_shape,
            two_shape,
            jax.ShapeDtypeStruct((1, FF), F32),
        ],
        compiler_params=params(62),
        cost_estimate=cost(58e9, 60e6, 12e6),
    )(core, normed, normed_t, cot, cot_t, one_a, *ones, bias_a, bias_b, two_a, *twos)


def add_row(sums, row, values):
    sums[row : row + 1, :] += jnp.sum(values, axis=0, keepdims=True)


def resid_kernel(
    middle, forward, back, cot, context, proj_own, proj_other, bias, gain,
    block_out, grad_out, ctx_grad, grad_own, grad_other, sums, proj, proj_grad,
):
    step = pl.program_id(0)

    @pl.when(step == 0)
    def _():
        proj[0:HALF, :] = proj_own[...]
        proj[HALF:, :] = proj_other[...]
        proj_grad[...] = jnp.zeros_like(proj_grad)
        sums[...] = jnp.zeros_like(sums)

    value = middle[...]
    block_out[...] = (value + (forward[...] + vec(bias))).astype(BF)
    scaled, inverse = norm_parts(value)
    upstream = back[...]
    scaled_up = upstream * vec(gain)
    first = jnp.mean(scaled_up, axis=-1, keepdims=True)
    second = jnp.mean(scaled_up * scaled, axis=-1, keepdims=True)
    cotangent = cot[...].astype(F32)
    grad = cotangent + inverse * (scaled_up - first - scaled * second)
    grad_out[...] = grad
    low = grad.astype(BF)
    ctx_grad[...] = dot(low, proj[...], NT).astype(BF)
    proj_grad[...] += dot(context[...], low, TN)
    add_row(sums, 0, upstream * scaled)
    add_row(sums, 1, upstream)
    add_row(sums, 2, cotangent)
    add_row(sums, 3, low.astype(F32))

    @pl.when(step == pl.num_programs(0) - 1)
    def _():
        for out, row in ((grad_own, 0), (grad_other, HALF)):
            for col in (0, HALF):
                out[col : col + HALF, :] = proj_grad[row : row + HALF, col : col + HALF].astype(BF)


def resid_of(middle, forward, back, cot, context, proj_own, proj_other, bias, gain):
    rows = 512
    row_block = pl.BlockSpec((rows, D), lambda i: (i, 0))
    half_block = pl.BlockSpec((D, HALF), lambda i: (0, 0))
    return pl.pallas_call(
        resid_kernel,
        grid=(OWN // rows,),
        in_specs=[row_block] * 5 + [whole((HALF, D)), whole((HALF, D)), whole((D,)), whole((D,))],
        out_specs=[
            row_block,
            row_block,
            row_block,
            half_block,
            half_block,
            pl.BlockSpec((8, D), lambda i: (0, 0)),
        ],
        out_shape=[
            jax.ShapeDtypeStruct((OWN, D), BF),
            jax.ShapeDtypeStruct((OWN, D), F32),
            jax.ShapeDtypeStruct((OWN, D), BF),
            jax.ShapeDtypeStruct((D, HALF), BF),
            jax.ShapeDtypeStruct((D, HALF), BF),
            jax.ShapeDtypeStruct((8, D), F32),
        ],
        scratch_shapes=[pltpu.VMEM((D, D), BF), pltpu.VMEM((D, D), F32)],
        compiler_params=params(),
        cost_estimate=cost(5e9, 40e6),
    )(middle, forward, back, cot, context, proj_own, proj_other, bias, gain)


def attend_back_kernel(first, local, owned, qkv, p, ctx_grad, spread, rel_even, rel_odd, fold, *refs):
    d_out, rel_grad, sums, upstream, kt = refs[-5:]
    band = pl.program_id(0) + first
    window = pl.program_id(1)

    @pl.when((band == first) & (window == 0))
    def _():
        rel_grad[...] = jnp.zeros_like(rel_grad)
        sums[...] = jnp.zeros_like(sums)

    @pl.when(window == 0)
    def _():
        for t in range(7):
            at = band * 8 + t
            rows = pl.ds(pl.multiple_of(local[at] * PAIR, PAIR), PAIR)
            moved = dot(spread[...], ctx_grad[rows, :])
            moved = moved * owned[at].astype(F32)
            upstream[:, 32 * t : 32 * t + 32, :] = moved.astype(BF).reshape(NWIN, 32, HALF)
        upstream[:, 224:256, :] = jnp.zeros((NWIN, 32, HALF), BF)

    kt[...] = qkv[0, 0, :, HALF : 2 * HALF].T
    even = lax.broadcasted_iota(jnp.int32, (1, 128), 1) < HD

    def shifted(head, by):
        return slice(by * HALF + head // 2 * 128, by * HALF + head // 2 * 128 + 128)

    def prob_grads(head, lanes):
        values = qkv[0, 0, 0:KEYS, shifted(head, 2)]
        kept = jnp.where(even != (head % 2 == 1), values, jnp.zeros_like(values))
        return dot(kept, upstream[window, 0:lanes, shifted(head, 0)], NT)

    def rel_table(both, lanes):
        tables = []
        zero8 = jnp.zeros((8, 128), F32)
        zero24 = jnp.zeros((24, 128), F32)
        zero16 = jnp.zeros((16, 128), F32)
        for tile in range(lanes // 128):
            row_shift, col_shift = shift_masks(tile * 128)
            part = both[:, tile * 128 : tile * 128 + 128]
            high = jnp.concatenate([part[HD : HD + 16], zero8], axis=0)
            wide = jnp.concatenate([part[HD + 16 : HD + 32], zero16], axis=0)
            high = unskew(high, row_shift, (1, 2, 4))
            wide = unskew(wide, col_shift, (1, 2, 4, 8))
            stack = [high, zero24, wide] if tile == 0 else [zero24, high, wide]
            tables.append(jnp.concatenate(stack, axis=0))
        table = tables[0] if len(tables) == 1 else jnp.concatenate(tables, axis=1)
        return table.astype(BF)

    def all_heads(lanes):
        count = HEADS // 2
        dvs, dks, dqs, drs = [], [], [], []

        def last_part(head, score_grad, both):
            rel = rel_odd if head % 2 else rel_even
            table = rel_table(both, lanes)
            queries = qkv[0, 0, 0:lanes, shifted(head, 0)]
            grads = dot(jnp.concatenate([score_grad, table], axis=0), queries)
            dks.append(grads[0:KEYS])
            drs.append(grads[KEYS:])
            from_rel = dot(rel[...], table, TN)
            side = head % 2 * HD
            dqs.append(both[0:HD] + from_rel[side : side + HD])
            if head % 2:
                d_out[0, 0, 0:lanes, shifted(head, 0)] = jnp.concatenate(dqs[-2:], axis=0).astype(BF).T
                d_out[0, 0, 0:KEYS, shifted(head, 1)] = (jnp.where(even, dks[-2], dks[-1]) * HD ** (-0.5)).astype(BF)

        prob_grad = prob_grads(0, lanes)
        before = None
        for head in range(count):
            ahead = prob_grads(head + 1, lanes) if head + 1 < count else None
            probs_low = p[0, 0, head, :, 0:lanes]
            probs = probs_low.astype(F32)
            total = jnp.sum(prob_grad * probs, axis=0, keepdims=True)
            score_grad = (probs * (prob_grad - total)).astype(BF)
            dvs.append(dot(probs_low, upstream[window, 0:lanes, shifted(head, 0)]))
            left = jnp.concatenate([kt[head * HD : head * HD + HD, 0:KEYS], fold[...]], axis=0)
            both = dot(left, score_grad)
            if head % 2:
                d_out[0, 0, 0:KEYS, shifted(head, 2)] = jnp.where(even, dvs[-2], dvs[-1]).astype(BF)
            if before is not None:
                last_part(head - 1, *before)
            before, prob_grad = (score_grad, both), ahead
        last_part(count - 1, *before)
        evens = drs[0] + drs[2] + drs[4]
        odds = drs[1] + drs[3] + drs[5]
        rel_grad[...] += jnp.where(even, evens, odds)

    d_out[0, 0, KEYS:, HALF:] = jnp.zeros((SLOTS - KEYS, 2 * HALF), BF)

    @pl.when(band < 2)
    def _():
        all_heads(256)

    @pl.when(band == 2)
    def _():
        all_heads(128)
        d_out[0, 0, 128:, 0:HALF] = jnp.zeros((128, HALF), BF)

    sums[0:1, :] += jnp.sum(d_out[...].reshape(SLOTS, TRIO).astype(F32), axis=0, keepdims=True)


def fold_table():
    table = np.zeros((32, WIN, 16), np.float32)
    for k in range(WIN):
        for l in range(WIN):
            table[k, k, l] = 1
            table[16 + l, k, l] = 1
    return table.reshape(32, KEYS)


def attend_back(qkv, p, ctx_grad, side, spread, rel_even, rel_odd, fold, local, owned, bands, *d_in):
    first, last = bands
    block = pl.BlockSpec((1, 1, SLOTS, TRIO), lambda s, w, *_: (s + first, w, 0, 0))
    share = (last - first) / 3
    return pl.pallas_call(
        lambda *refs: attend_back_kernel(first, *refs),
        grid_spec=pltpu.PrefetchScalarGridSpec(
            num_scalar_prefetch=2,
            grid=(last - first, NWIN),
            in_specs=[
                block,
                pl.BlockSpec((1, 1, HEADS // 2, KEYS, SLOTS), lambda s, w, *_: (s + first, w, 0, 0, 0)),
                pl.BlockSpec((OWN, HALF), lambda *_: (0, side), pipeline_mode=pl.Buffered(1)),
                whole((NWIN * 32, PAIR)),
                whole((GREL, 128)),
                whole((GREL, 128)),
                whole((32, KEYS)),
            ]
            + [pl.BlockSpec(memory_space=pl.ANY)] * len(d_in),
            out_specs=[
                block,
                pl.BlockSpec((GREL, 128), lambda s, w, *_: (0, 0)),
                pl.BlockSpec((8, TRIO), lambda s, w, *_: (0, 0)),
            ],
            scratch_shapes=[pltpu.VMEM((NWIN, SLOTS, HALF), BF), pltpu.VMEM((HALF, SLOTS), BF)],
        ),
        out_shape=[
            jax.ShapeDtypeStruct((3, NWIN, SLOTS, TRIO), BF),
            jax.ShapeDtypeStruct((GREL, 128), F32),
            jax.ShapeDtypeStruct((8, TRIO), F32),
        ],
        input_output_aliases={9: 0} if d_in else {},
        compiler_params=params(),
        cost_estimate=cost(20e9 * share, 45e6 * share),
    )(local, owned, qkv, p, ctx_grad, spread, rel_even, rel_odd, fold, *d_in)


def norm_grad_kernel(own, other, weights_own, core, mine, theirs, gather, *refs):
    out, joined = refs[-2:]

    @pl.when((pl.program_id(0) == 0) & (pl.program_id(1) == 0))
    def _():
        for s in range(3):
            joined[:, s * HALF : s * HALF + HALF] = weights_own[s]
        join_pieces(core[0], mine, theirs, joined, TRIO)

    rows = NWIN * 128
    left = jnp.concatenate([own[...].reshape(rows, TRIO), other[...].reshape(rows, TRIO)], axis=1)
    total = dot(left, joined[...], NT).astype(BF).reshape(NWIN, 4, 32, D)
    for t in range(4):
        moved = dot(gather[...], total[:, t].reshape(NWIN * 32, D)).astype(BF)
        out[:, t * PAIR : t * PAIR + PAIR, :] = moved.reshape(1, PAIR, D)


def norm_grad(own, other, weights_own, core, mine, theirs, gather, bands, *before):
    first, last = bands
    share = (last - first) / 3
    block = pl.BlockSpec((1, NWIN, 128, TRIO), lambda s, t: (s + first, 0, t, 0))
    return pl.pallas_call(
        norm_grad_kernel,
        grid=(last - first, 2),
        in_specs=[block, block, whole((3, D, HALF)), SCALAR]
        + [whole((3, HALF, HALF)), whole((3, HALF, HALF)), whole((PAIR, NWIN * 32))]
        + [pl.BlockSpec(memory_space=pl.ANY)] * len(before),
        out_specs=pl.BlockSpec((1, 4 * PAIR, D), lambda s, t: (s + first, t, 0)),
        out_shape=jax.ShapeDtypeStruct((3, 8 * PAIR, D), BF),
        input_output_aliases={7: 0} if before else {},
        scratch_shapes=[pltpu.VMEM((D, 2 * TRIO), BF)],
        compiler_params=params(),
        cost_estimate=cost(14e9 * share, 30e6 * share),
    )(own, other, weights_own, core, mine, theirs, gather, *before)


def qkv_grad_kernel(core, xt, d, proj, kept, sent, total):
    step = pl.program_id(0)
    part = dot(xt[...], d[...])

    @pl.when(step == 0)
    def _():
        total[...] = part

    @pl.when(step > 0)
    def _():
        total[...] += part

    @pl.when(step == pl.num_programs(0) - 1)
    def _():
        first = core[0] == 0
        values = [total[:, s * HALF : s * HALF + HALF].astype(BF) for s in range(3)] + [proj[...]]
        for k in range(2):
            kept[k] = jnp.where(first, values[k], values[2 + k])
            sent[k] = jnp.where(first, values[2 + k], values[k])


def qkv_grad(core, xt, d, proj):
    rows = NWIN * SLOTS
    block = pl.BlockSpec((2, D, HALF), lambda i: (0, 0, 0))
    shape = jax.ShapeDtypeStruct((2, D, HALF), BF)
    return pl.pallas_call(
        qkv_grad_kernel,
        grid=(3,),
        in_specs=[
            SCALAR,
            pl.BlockSpec((D, rows), lambda i: (0, i)),
            pl.BlockSpec((rows, TRIO), lambda i: (i, 0)),
            whole((D, HALF)),
        ],
        out_specs=[block, block],
        out_shape=[shape, shape],
        scratch_shapes=[pltpu.VMEM((D, TRIO), F32)],
        compiler_params=params(),
        cost_estimate=cost(7e9, 16e6),
    )(core, xt, d.reshape(3 * rows, TRIO), proj)


def input_kernel(
    band_of, step_of, taken_of, has_taken, offset, core, x, middle_grad, up_a, up_b, taken_a, taken_b, gain,
    one_mine, one_theirs, two_mine, two_theirs, out, sums, one_out, two_out,
):
    step = pl.program_id(0)
    first = core[0] == 0
    mine, theirs = one_mine[...].astype(F32), one_theirs[...].astype(F32)
    one_out[0] = jnp.where(first, mine, theirs)
    one_out[1] = jnp.where(first, theirs, mine)
    mine, theirs = two_mine[...].astype(F32), two_theirs[...].astype(F32)
    two_out[:, 0:HALF] = jnp.where(first, mine, theirs)
    two_out[:, HALF:] = jnp.where(first, theirs, mine)

    @pl.when(step == 0)
    def _():
        sums[...] = jnp.zeros_like(sums)

    for k, (up, taken) in enumerate(((up_a, taken_a), (up_b, taken_b))):
        rows = slice(k * PAIR, k * PAIR + PAIR)
        scaled, inverse = norm_parts(x[rows, :].astype(F32))
        shared = taken[...].astype(F32) * has_taken[2 * step + k].astype(F32)
        upstream = up[0].astype(F32) + shared
        scaled_up = upstream * vec(gain)
        mean = jnp.mean(scaled_up, axis=-1, keepdims=True)
        second = jnp.mean(scaled_up * scaled, axis=-1, keepdims=True)
        out[rows, :] = (middle_grad[rows, :] + inverse * (scaled_up - mean - scaled * second)).astype(BF)
        add_row(sums, 0, upstream * scaled)
        add_row(sums, 1, upstream)


def input_of(x, middle_grad, up, taken, gain, ones, twos, band_of, step_of, taken_of, has_taken, offset, core):
    rows = 2 * PAIR
    row_block = pl.BlockSpec((rows, D), lambda i, *_: (i, 0))
    steps = OWN // rows
    one_rows, two_rows = HALF // steps, FF // 2 // steps
    up_at = lambda k: lambda i, band_of, step_of, *_: (band_of[2 * i + k], step_of[2 * i + k], 0)
    taken_at = lambda k: lambda i, band_of, step_of, taken_of, *_: (taken_of[2 * i + k], 0)
    return pl.pallas_call(
        input_kernel,
        grid_spec=pltpu.PrefetchScalarGridSpec(
            num_scalar_prefetch=6,
            grid=(steps,),
            in_specs=[
                pl.BlockSpec((rows, D), lambda i, b, s, t, h, offset, core: (offset[0] + i, 0)),
                row_block,
                pl.BlockSpec((1, PAIR, D), up_at(0)),
                pl.BlockSpec((1, PAIR, D), up_at(1)),
                pl.BlockSpec((PAIR, D), taken_at(0)),
                pl.BlockSpec((PAIR, D), taken_at(1)),
                whole((D,)),
            ]
            + [pl.BlockSpec((one_rows, FF // 2), lambda i, *_: (i, 0))] * 2
            + [pl.BlockSpec((two_rows, HALF), lambda i, *_: (i, 0))] * 2,
            out_specs=[
                row_block,
                pl.BlockSpec((8, D), lambda i, *_: (0, 0)),
                pl.BlockSpec((2, one_rows, FF // 2), lambda i, *_: (0, i, 0)),
                pl.BlockSpec((two_rows, D), lambda i, *_: (i, 0)),
            ],
        ),
        out_shape=[
            jax.ShapeDtypeStruct((OWN, D), BF),
            jax.ShapeDtypeStruct((8, D), F32),
            jax.ShapeDtypeStruct((2, HALF, FF // 2), F32),
            jax.ShapeDtypeStruct((FF // 2, D), F32),
        ],
        compiler_params=params(),
        cost_estimate=cost(1e8, 35e6),
    )(band_of, step_of, taken_of, has_taken, offset, core, x, middle_grad, up, up, taken, taken, gain, *ones, *twos)


MESH = pl.DeviceIdType.MESH
SMALL = 24


def bits_of(size):
    return size.bit_length() - 1


def line_plan(order, rows):
    plan, doubles = [], [("double", order[0], rows)]
    for bit in order[1:]:
        if rows % 32 == 0:
            doubles.append(("double", bit, rows))
            rows //= 2
            plan.append(("halve", bit, rows))
        else:
            plan.append(("both", bit, rows))
    return plan + doubles[::-1]


PARTS = 2
PART_ROWS = D // 2 // PARTS


def last_kernel(bits, plans, orders, *refs):
    (line_a, line_b, one_sums, two_sums, fc1_sums, sums_a, sums_c, sums_b, sums_d) = refs[:9]
    rel_a, rel_b, rel_c, rel_d, hots, out, small, rel = refs[9:17]
    small_landed, rel_landed, sends, recvs = refs[17:21]
    rooms = list(refs[21:])
    dp, mp = lax.axis_index("dp"), lax.axis_index("mp")
    bit_at = lambda bit: mp if bit == 0 else (dp // bit) % 2

    def partner(bit):
        if bit == 0:
            return (dp, 1 - mp)
        return (jnp.where(bit_at(bit) == 0, dp + bit, dp - bit), mp)

    barrier = pltpu.get_barrier_semaphore()
    every = [1] + bits + [0]
    for bit in every:
        pl.semaphore_signal(barrier, inc=1, device_id=partner(bit), device_id_type=MESH)

    count = [0]

    def send(src, dst, bit):
        at = count[0]
        count[0] += 1
        copy = pltpu.make_async_remote_copy(
            src_ref=src,
            dst_ref=dst,
            send_sem=sends.at[at],
            recv_sem=recvs.at[at],
            device_id=partner(bit),
            device_id_type=MESH,
        )
        copy.start()
        return copy

    def line(k, part):
        order, value = orders[k], (line_a, line_b)[k].at[pl.ds(part * PART_ROWS, PART_ROWS)]
        slot = dp % 2 * 2 + k
        first = bit_at(order[0]) * (D // 2) + part * PART_ROWS
        start, size, placed = first, PART_ROWS, False
        for kind, bit, after in plans[k]:
            if kind == "double":
                here = pl.ds(pl.multiple_of(start, 16), size)
                if not placed:
                    out[slot, here, :] = value[...]
                    placed = True
                copy = send(out.at[slot, here], out.at[slot, here], bit)
                yield
                copy.wait()
                if after != size or bit != order[0]:
                    start, size = start - bit_at(bit) * size, 2 * size
                continue
            mine = bit_at(bit) if kind == "halve" else 0
            gone = 1 - mine if kind == "halve" else 0
            room, total = rooms.pop(0), rooms.pop(0)
            copy = send(value.at[pl.ds(pl.multiple_of(gone * after, 16), after)], room, bit)
            yield
            copy.wait()
            rows = pl.ds(pl.multiple_of(mine * after, 16), after)
            total[...] = (value[rows, :].astype(F32) + room[...].astype(F32)).astype(BF)
            value = total
            start, size = start + mine * after, after
        copies = []
        for half in range(2):
            rows = pl.ds(half * (D // 2) + part * PART_ROWS, PART_ROWS)
            copies.append(send(out.at[slot, rows], out.at[slot, rows], 1))
        yield
        for copy in copies:
            copy.wait()

    def vectors():
        for at, bit in enumerate(bits + [0, 1]):
            copies = [send(small, small_landed.at[at], bit), send(rel, rel_landed.at[at], bit)]
            yield
            for copy in copies:
                copy.wait()
            small[...] += small_landed[at]
            rel[...] += rel_landed[at]

    lines = [line(k, part) for part in range(PARTS) for k in range(2)]
    pl.semaphore_wait(barrier, len(every))
    for one in lines:
        next(one)

    small[...] = jnp.zeros_like(small)
    small[0:2, :] = one_sums[0:2, :]
    small[2:6, :] = two_sums[0:4, :]
    first = mp == 0
    own = [sums_a[0:1, :] + sums_c[0:1, :], fc1_sums[0:1, 0 : FF // 2]]
    other = [sums_b[0:1, :] + sums_d[0:1, :], fc1_sums[0:1, FF // 2 :]]
    for row, flip in ((6, False), (9, True)):
        picked = [jnp.where(first != flip, a, b) for a, b in zip(own, other)]
        small[row : row + 1, 0:HALF] = picked[0][:, 0:HALF]
        small[row : row + 1, HALF:] = picked[0][:, 2 * HALF :]
        small[row + 1 : row + 2, :] = picked[1][:, 0:D]
        small[row + 2 : row + 3, :] = picked[1][:, D:]
    table = rel_a[...] + rel_b[...] + rel_c[...] + rel_d[...]
    table = lax.dot_general(hots[...], table, TN, precision=lax.Precision.HIGHEST, preferred_element_type=F32)
    rel[...] = table + pltpu.roll(table, HD, 1)

    active = lines + [vectors()]
    while active:
        for one in list(active):
            if next(one, "end") == "end":
                active.remove(one)


def last_sums(bits, orders, lines, sums, rels, hots):
    vmem = pl.BlockSpec(memory_space=pltpu.VMEM)
    rounds = len(bits) + 2
    copies = 2 * rounds + 2 * PARTS * (2 * len(bits) + 2)
    plans = [line_plan(order, PART_ROWS) for order in orders]
    rooms = []
    for at in range(len(plans[0])):
        for part in range(PARTS):
            for plan in plans:
                if plan[at][0] != "double":
                    rooms += [pltpu.VMEM((plan[at][2], HALF), BF)] * 2
    return pl.pallas_call(
        lambda *refs: last_kernel(bits, plans, orders, *refs),
        in_specs=[vmem] * (2 + len(sums) + len(rels) + 1),
        out_specs=[vmem] * 3,
        out_shape=[
            jax.ShapeDtypeStruct((4, D, HALF), BF),
            jax.ShapeDtypeStruct((SMALL, D), F32),
            jax.ShapeDtypeStruct((56, 128), F32),
        ],
        scratch_shapes=[
            pltpu.VMEM((rounds, SMALL, D), F32),
            pltpu.VMEM((rounds, 56, 128), F32),
            pltpu.SemaphoreType.DMA((copies,)),
            pltpu.SemaphoreType.DMA((copies,)),
        ]
        + rooms,
        compiler_params=pltpu.CompilerParams(
            collective_id=0, has_side_effects=True, vmem_limit_bytes=40 * 2**20
        ),
    )(*lines, *sums, *rels, hots)


CORE, PAIRED = 1, 0


def bit_of(bit):
    return lax.axis_index("mp") if bit == PAIRED else (lax.axis_index("dp") // bit) % 2


def exchange(value, bit):
    if bit == PAIRED:
        return lax.ppermute(value, "mp", [(0, 1), (1, 0)])
    return lax.ppermute(value, "dp", [(i, i ^ bit) for i in range(lax.axis_size("dp"))])


class Line:
    def __init__(self, value, places, rank, steps, sent=None):
        self.terms = [(value, tuple(places))]
        self.fixed = {}
        self.rank = list(rank)
        self.steps = list(steps)
        self.sent, self.taken = sent, None
        self.value = None

    def part(self, changes):
        fixed = {**self.fixed, **changes}
        total = None
        for term, places in self.terms:
            starts, sizes, shape = [], [], []
            for bit in places:
                starts.append(fixed.get(bit, 0))
                sizes.append(1 if bit in fixed else 2)
                if bit not in fixed:
                    shape.append(2)
            rest = term.shape[len(places) :]
            if places:
                starts = [jnp.asarray(at, jnp.int32) for at in starts + [0] * len(rest)]
                term = lax.dynamic_slice(term, starts, tuple(sizes) + rest).reshape(tuple(shape) + rest)
            total = term.astype(F32) if total is None else total + term.astype(F32)
        return total.astype(BF)

    def prepare(self):
        kind, bit = self.steps[0]
        if kind == "halve":
            mine = 0 if bit == PAIRED else bit_of(bit)
            self.sent = self.part({bit: 1 - mine})
            self.fixed[bit] = mine
        elif kind == "double":
            if self.value is None:
                self.value, self.done = self.part({}), []
            self.sent = self.value
        elif kind == "pass":
            self.sent = self.part({})

    def launch(self):
        self.taken = exchange(self.sent, self.steps[0][1])

    def land(self):
        kind, bit = self.steps.pop(0)
        if kind in ("halve", "give"):
            places = [p for p in self.terms[0][1] if p not in self.fixed]
            self.terms.append((self.taken, tuple(places)))
        elif kind == "pass":
            self.terms = [(self.taken, tuple(p for p in self.terms[0][1] if p not in self.fixed))]
        else:
            if not self.steps:
                self.taken_last, self.taken = self.taken, None
                return
            self.done = sorted(self.done + [bit], key=self.rank.index)
            axis = self.done.index(bit)
            shape = [1] * (self.value.ndim + 1)
            shape[axis] = 2
            mine = jnp.arange(2).reshape(shape) == bit_of(bit)
            wide = lambda v: jnp.expand_dims(v, axis)
            self.value = jnp.where(mine, wide(self.value), wide(self.taken))
        self.taken = None


def advance(anchor, lines):
    flying = [line for line in lines if line.taken is not None]
    anchor, taken = lax.optimization_barrier((anchor, [line.taken for line in flying]))
    for line, value in zip(flying, taken):
        line.taken = value
        line.land()
    going = [line for line in lines if line.steps]
    for line in going:
        line.prepare()
    anchor, sent = lax.optimization_barrier((anchor, [line.sent for line in going]))
    for line, value in zip(going, sent):
        line.sent = value
        line.launch()
    return anchor


def finish(lines):
    while any(line.steps for line in lines):
        for line in lines:
            if not line.steps:
                continue
            if line.taken is None:
                line.prepare()
                line.launch()
        for line in lines:
            if line.taken is not None:
                line.land()


def on_device(
    image_tokens,
    norm1_gain,
    norm1_shift,
    qkv_weight,
    qv_bias,
    rel_rows,
    rel_cols,
    proj_weight,
    proj_bias,
    norm2_gain,
    norm2_shift,
    fc1_weight,
    fc1_bias,
    fc2_weight,
    fc2_bias,
    out_cotangent,
):
    place = lax.axis_index("mp")
    core = lax.axis_index("dp") % 2
    swap = lambda value: lax.ppermute(value, "mp", [(0, 1), (1, 0)])
    size = lax.axis_size("dp")
    core_swap = lambda value: lax.ppermute(value, "dp", [(i, i ^ 1) for i in range(size)])

    def by_core(weight, axis, mine):
        return lax.dynamic_slice_in_dim(weight, (core if mine else 1 - core) * HALF, HALF, axis)

    block, valid, local, owned, band_of, step_of, taken_of, has_taken = pair_tables(place)
    offset = (place * (OWN // (2 * PAIR))).astype(jnp.int32).reshape(1)
    spread = jnp.asarray(spread_rows(), BF)
    gather = jnp.asarray(spread_rows().T, BF)
    fold = jnp.asarray(fold_table(), BF)
    high_hot, wide_hot = rel_onehots()
    hots = jnp.asarray(np.pad(np.concatenate([high_hot, wide_hot], axis=1), ((0, 0), (0, 2))), F32)
    high_hot, wide_hot = jnp.asarray(high_hot, BF), jnp.asarray(wide_hot, BF)
    core_at = core.astype(jnp.int32).reshape(1)
    qkv_mine = swap(by_core(qkv_weight, 1, True))
    bias_other = swap(qv_bias)
    fc1_bias_other = swap(fc1_bias)
    x_windows = windows_of(image_tokens, norm1_gain, norm1_shift, spread, block, valid)
    x_windows, qkv_mine = lax.optimization_barrier((x_windows, qkv_mine))
    late = (by_core(fc1_weight, 0, True), by_core(fc2_weight, 1, True), proj_weight)
    x_windows, qkv_mine, late = lax.optimization_barrier((x_windows, qkv_mine, late))
    qkv_theirs = exchange(qkv_mine, CORE)
    one_mine, two_mine, proj_other = (swap(w) for w in late)
    qkv_a, p_a, ctx_a, xt, rel_even, rel_odd = attend(
        x_windows, qv_bias, True, qkv_weight, high_hot, wide_hot, rel_rows, rel_cols
    )
    qkv_b, p_b, ctx_b = attend(
        x_windows, bias_other, False, core_at, qkv_mine, qkv_theirs, rel_even, rel_odd
    )
    ctx_b, one_mine, two_mine, proj_other = lax.optimization_barrier((ctx_b, one_mine, two_mine, proj_other))
    one_theirs, two_theirs = exchange(one_mine, CORE), exchange(two_mine, CORE)
    middle, normed, normed_t, cot_t, context = middle_of(
        ctx_a, ctx_b, image_tokens, out_cotangent, proj_weight, proj_other, proj_bias, norm2_gain,
        norm2_shift, gather, band_of, step_of, offset,
    )
    forward, back, one_kept, one_sent, two_kept, two_sent, fc1_sums = feed(
        core_at, normed, normed_t, out_cotangent, cot_t, fc1_weight, (one_mine, one_theirs), fc1_bias,
        fc1_bias_other, fc2_weight, (two_mine, two_theirs),
    )
    bits = [2**k for k in range(1, bits_of(size))]
    turned = bits[1:2] + bits[0:1] + bits[2:]
    halves = lambda order: [("halve", bit) for bit in order]
    doubles = lambda order: [("double", bit) for bit in order]

    def cut(value, axis, places):
        shape = value.shape[:axis] + (2,) * len(places) + (value.shape[axis] // 2 ** len(places),)
        return value.reshape(shape + value.shape[axis + 1 :])

    def feed_line(kept, sent, order, back):
        steps = [("give", CORE)] + halves(order) + doubles(back) + [("double", CORE)]
        rank = [CORE] + bits
        return Line(cut(kept, 1, bits), [PAIRED] + bits, rank, steps, cut(sent, 1, bits))

    one_line = feed_line(one_kept, one_sent, [PAIRED] + bits, bits[::-1])
    two_line = feed_line(two_kept, two_sent, bits[:2] + [PAIRED] + bits[2:], turned[::-1])
    feed_lines = [one_line, two_line]

    middle = advance(middle, feed_lines)
    block_out, middle_grad, ctx_grad, proj_own, proj_oth, two_sums = resid_of(
        middle, forward, back, out_cotangent, context, proj_weight, proj_other, fc2_bias, norm2_gain
    )
    back_of = lambda qkv, p, side, grad, bands, *d: attend_back(
        qkv, p, grad, side, spread, rel_even, rel_odd, fold, local, owned, bands, *d
    )
    ctx_grad = advance(ctx_grad, feed_lines)
    d_b, rel_b, sums_b = back_of(qkv_b, p_b, 1, ctx_grad, (1, 3))
    d_b = advance(d_b, feed_lines)
    d_b, rel_b0, sums_b0 = back_of(qkv_b, p_b, 1, ctx_grad, (0, 1), d_b)
    d_b = advance(d_b, feed_lines)
    kept_b, sent_b = qkv_grad(core_at, xt, d_b, proj_oth)
    line_b = Line(kept_b, [], [], [("give", CORE), ("pass", PAIRED)], sent_b)
    lines = feed_lines + [line_b]
    ctx_grad, kept_b = lax.optimization_barrier((ctx_grad, kept_b))
    ctx_grad = advance(ctx_grad, lines)
    d_a, rel_a, sums_a = back_of(qkv_a, p_a, 0, ctx_grad, (1, 3))
    d_a = advance(d_a, lines)
    up = norm_grad(d_a, d_b, qkv_weight, core_at, qkv_mine, qkv_theirs, gather, (1, 3))
    at = [2 - place, (1 - place) * 4 * SIDE, jnp.zeros_like(place)]
    sent = lax.dynamic_slice(up, at, (1, 10 * SIDE, D)).reshape(10 * SIDE, D)
    shared_line = Line(sent, [], [], [("pass", PAIRED)])
    d_a = advance(d_a, [shared_line])
    d_a, rel_a0, sums_a0 = back_of(qkv_a, p_a, 0, ctx_grad, (0, 1), d_a)
    d_a = advance(d_a, feed_lines + [line_b])
    kept_a, sent_a = qkv_grad(core_at, xt, d_a, proj_own)
    line_a = Line(kept_a, [], [], [("give", CORE)], sent_a)
    kept_a, d_a = lax.optimization_barrier((kept_a, d_a))
    d_a = advance(d_a, feed_lines + [line_a, shared_line])
    up = norm_grad(d_a, d_b, qkv_weight, core_at, qkv_mine, qkv_theirs, gather, (0, 1), up)
    up = advance(up, feed_lines + [line_a])
    taken = shared_line.terms[0][0]
    q_lines = []
    for k, order in enumerate((bits, turned)):
        line = Line(None, [], [], halves(order[:1]))
        parts = [term for term, _ in line_a.terms] + [term for term, _ in line_b.terms]
        line.terms = [(part.reshape(2, 2, D // 2, HALF), ("line", order[0])) for part in parts]
        line.fixed = {"line": k}
        q_lines.append(line)
    up = advance(up, q_lines)
    finish(feed_lines)
    flat = lambda line, rows: (line.value.reshape(rows, -1), line.taken_last.reshape(rows, -1))
    input_grad, one_sums, one_sum, two_sum = input_of(
        image_tokens, middle_grad, up, taken, norm1_gain, flat(one_line, HALF), flat(two_line, FF // 2),
        band_of, step_of, taken_of, has_taken, offset, core_at,
    )
    one_sums = advance(one_sums, q_lines)
    four, small, rel = last_sums(
        bits,
        [bits, turned],
        [line.part({}) for line in q_lines],
        [one_sums, two_sums, fc1_sums, sums_a, sums_a0, sums_b, sums_b0],
        [rel_a, rel_a0, rel_b, rel_b0],
        hots,
    )
    one_sum = one_sum.reshape(D, FF // 2)
    mine = jnp.where(place == 0, small[6:9], small[9:12])
    return (
        block_out,
        input_grad,
        small[0],
        small[1],
        four[0:3].astype(F32),
        mine[0].reshape(2, HALF),
        rel[:RELS, :HD],
        rel[RELS : 2 * RELS, :HD],
        jnp.concatenate([four[3, :HALF], four[3, HALF:]], axis=1).astype(F32),
        small[5],
        small[2],
        small[3],
        one_sum,
        mine[1:3].reshape(-1),
        two_sum,
        small[4],
    )


def solution(mesh):
    in_specs = (
        P("dp", None),
        P(),
        P(),
        P(None, None, "mp"),
        P(None, "mp"),
        P(),
        P(),
        P("mp", None),
        P(),
        P(),
        P(),
        P(None, "mp"),
        P("mp"),
        P("mp", None),
        P(),
        P(("dp", "mp"), None),
    )
    out_specs = (
        P(("dp", "mp"), None),
        P(("dp", "mp"), None),
        P(),
        P(),
        P(None, None, "mp"),
        P(None, "mp"),
        P(),
        P(),
        P("mp", None),
        P(),
        P(),
        P(),
        P(None, "mp"),
        P("mp"),
        P("mp", None),
        P(),
    )
    return jax.shard_map(
        on_device, mesh=mesh, in_specs=in_specs, out_specs=out_specs, check_vma=False
    )
```

time: 585 us -> 473 us (0.81)
  Pallas kernels: 410 us -> 353 us
  other arithmetic: 59.1 us -> 35.9 us
  local copies, waits for them, and re-layouts: 32.9 us -> 17.7 us
  waiting for transfers between devices: 42.4 us -> 27.5 us
    pallas_call x4, Pallas kernels: 95.4 us -> 63.1 us  [attend_back(): pl.pallas_call(lambda *refs: attend_back_kernel(first, *refs), grid_spec=...]
    convert_element_type x3 -> x13, other arithmetic: 1.84 us -> 24.4 us  [part(): return total.astype(BF)]
    add x14 -> x0, other arithmetic: 18.9 us -> none  [the longest x13 17.4 us: land(): self.value = self.kept + self.taken]
    pallas_call x5, Pallas kernels: 187 us -> 169 us  [the longest x1 75.3 us: feed(): pl.pallas_call(feed_kernel, grid_spec=pltpu.PrefetchScalarGridSpec(num_sc...]
    ppermute x4, waiting for transfers between devices: 25.2 us -> 10.9 us  [exchange(): return lax.ppermute(value, 'mp', [(0, 1), (1, 0)])]
    another operation x16 -> x0, other arithmetic: 12.1 us -> none  [land(): self.value = jnp.stack([low, high], axis=self.places.index(bit))]
    pallas_call x1, Pallas kernels: 44.2 us -> 33.2 us  [last_sums(): pl.pallas_call(lambda *refs: last_kernel(bits, plans, orders, *refs), in_...]
    concatenate x7 -> x0, other arithmetic: 9.17 us -> none  [the longest x4 5.54 us: from_partner(): return jnp.concatenate([low, high], axis=weight.ndim - 2)]
  transfers between devices with their start and end apart: 33 -> 33, of which waited for: 8 -> 9; matrix products, arithmetic and copies ran while one was open for 5% -> 3% of each run, Pallas kernels for 45% -> 53%
where the time goes in v3:
time: 473 us; the launch traced here: 465 us
  Pallas kernels  353 us (75%)
  other arithmetic  35.9 us (8%)
  starting transfers between devices  29.1 us (6%)
  waiting for transfers between devices  27.5 us (6%)
  local copies, waits for them, and re-layouts  17.7 us (4%)
    pallas_call x1, Pallas kernels, feed(): pl.pallas_call(feed_kernel, grid_spec=pltpu.PrefetchScalarGridSpec(num_sc...  75.3 us
    pallas_call x2, Pallas kernels, attend(): pl.pallas_call(attend_own if first else attend_other, grid=(3, NWIN), in_...  67 us
    pallas_call x4, Pallas kernels, attend_back(): pl.pallas_call(lambda *refs: attend_back_kernel(first, *refs), grid_spec=...  63.1 us
    pallas_call x1, Pallas kernels, last_sums(): pl.pallas_call(lambda *refs: last_kernel(bits, plans, orders, *refs), in_...  33.2 us
    pallas_call x2, Pallas kernels, norm_grad(): pl.pallas_call(norm_grad_kernel, grid=(last - first, 2), in_specs=[block,...  27.2 us
    pallas_call x2, Pallas kernels, qkv_grad(): pl.pallas_call(qkv_grad_kernel, grid=(3,), in_specs=[SCALAR, pl.BlockSpec...  26.8 us
    convert_element_type x13, other arithmetic, part(): return total.astype(BF)  24.4 us
    pallas_call x1, Pallas kernels, resid_of(): pl.pallas_call(resid_kernel, grid=(OWN // rows,), in_specs=[row_block] *...  18.9 us
  transfers between devices with their start and end apart: 33, of which 9 were waited for; matrix products, arithmetic and copies ran while one was open for 3% of the time, Pallas kernels for 53%

profile of v3, /device:TPU:0, one launch (start us, length us, event | category | flops | bytes accessed | tf_op | source)
XLA Modules:
  0.0 465.0 jit_solution(4582909223562321247)
XLA Ops:
  0.7 2.2 constant_dynamic-slice_fusion.2
  2.9 3.0 collective-permute-start
  6.4 8.5 %shard_map.477.x = bf16[3,5,256,768]{3,2,1,0:T(8,128)(2,1)} custom-call(s32[24]{0:T(128)} %get-tuple-element.291.block, s32[24]{0:T(128)} %get-tuple-element.290.valid, bf16[4096,768]{1,0:T(8,128)(2,1)} %x.3, bf16[4096,768]{1,0:T(8,128)(2,1)} %x.3, bf16[4096,768]{1,0:T(8,128)(2,1)} %x.3, bf16[4096,768]{1,0:T(8,128)(2,1)} %x.3, bf16[4096,768]{1,0:T(8,128)(2,1)} %x.3, ...), custom_call_target="tpu_custom_call" | custom-call | flops 660602880 | bytes 10000000 | tf_op jit(solution)/shard_map/pallas_call | solution.py:136
  17.1 8.8 %collective-permute-done.mine = bf16[3,384,384]{2,1,0:T(8,128)(2,1)} collective-permute-done((bf16[3,384,384]{2,1,0:T(8,128)(2,1)}, bf16[3,384,384]{2,1,0:T(8,128)(2,1)}, u32[]{:S(2)}, u32[]{:S(2)}) %collective-permute-start) | collective-permute-done | bytes 884768 | tf_op jit(solution)/shard_map/ppermute | solution.py:1139
  29.6 33.9 %shard_map.478 = (bf16[3,5,256,1152]{3,2,1,0:T(8,128)(2,1)}, bf16[3,5,6,224,256]{4,3,2,1,0:T(8,128)(2,1)}, bf16[3,5,256,384]{3,2,1,0:T(8,128)(2,1)}, bf16[768,38...) custom-call(bf16[3,5,256,768]{3,2,1,0:T(8,128)(2,1)} %shard_map.477.x, bf16[2,384]{1,0:T(2,128)(2,1)} %bias.3, ...), custom_call_target="tpu_custom_call" | custom-call | flops 15000000512 | bytes 45000000 | tf_op jit(solution)/shard_map/pallas_call | solution.py:299
  64.1 33.1 %shard_map.479 = (bf16[3,5,256,1152]{3,2,1,0:T(8,128)(2,1)}, bf16[3,5,6,224,256]{4,3,2,1,0:T(8,128)(2,1)}, bf16[3,5,256,384]{3,2,1,0:T(8,128)(2,1)}) custom-call(bf16[3,5,256,768]{3,2,1,0:T(8,128)(2,1)} %shard_map.477.x, bf16[2,384]{1,0:T(2,128)(2,1)} %copy-done.45, s32[1]{0:T(128)} %bitcast.1.core, bf16[3,384,384]{2,1,0:T(8,128)(2,1)} %collective-permute-done.mine, ...), custom_call_target="tpu_custom_call" | custom-call | flops 15000000512 | bytes 45000000 | tf_op jit(solution)/shard_map/pallas_call | solution.py:299
  98.6 16.5 %shard_map.480 = (f32[2048,768]{1,0:T(8,128)}, bf16[2048,768]{1,0:T(8,128)(2,1)}, bf16[768,2048]{1,0:T(8,128)(2,1)}, bf16[768,2048]{1,0:T(8,128)(2,1)}, bf16[2048,768]{1,0:T(8,128)(2,1)}) custom-call(s32[16]{0:T(128)} %get-tuple-element.295.band_of, s32[16]{0:T(128)} %get-tuple-element.294.step_of, s32[1]{0:T(128)} %bitcast.offset, ...), custom_call_target="tpu_custom_call" | custom-call | flops 3000000000 | bytes 30000000 | tf_op jit(solution)/shard_map/pallas_call | solution.py:338
  116.6 75.3 %shard_map.481 = (f32[2048,768]{1,0:T(8,128)}, f32[2048,768]{1,0:T(8,128)}, bf16[2,384,1536]{2,1,0:T(8,128)(2,1)}, bf16[2,384,1536]{2,1,0:T(8,128)(2,1)}, bf16[2...) custom-call(s32[1]{0:T(128)} %bitcast.1.core, ...), custom_call_target="tpu_custom_call" | custom-call | flops 57999998976 | bytes 60000000 | tf_op jit(solution)/shard_map/pallas_call | solution.py:441
  194.4 18.9 %shard_map.482 = (bf16[2048,768]{1,0:T(8,128)(2,1)}, f32[2048,768]{1,0:T(8,128)}, bf16[2048,768]{1,0:T(8,128)(2,1)}, bf16[768,384]{1,0:T(8,128)(2,1)}, bf16[768,384]{1,0:T(8,128)(2,1)}, /*index=5*/f32[8,768]{1,0:T(8,128)}) custom-call(f32[2048,768]{1,0:T(8,128)} %get-tuple-element.166.middle, f32[2048,768]{1,0:T(8,128)} %get-tuple-element.167.forward, ...), custom_call_target="tpu_custom_call" | custom-call | flops 5000000000 | bytes 40000000 | tf_op jit(solution)/shard_map/pallas_call | solution.py:529
  215.4 2.6 fusion.1
  221.2 20.3 %shard_map.483 = (bf16[3,5,256,1152]{3,2,1,0:T(8,128)(2,1)}, f32[80,128]{1,0:T(8,128)}, f32[8,1152]{1,0:T(8,128)}) custom-call(s32[24]{0:T(128)} %get-tuple-element.289.refs_0_, s32[24]{0:T(128)} %get-tuple-element.288.refs_1_, bf16[3,5,256,1152]{3,2,1,0:T(8,128)(2,1)} %get-tuple-element.184.refs_2_, ...), custom_call_target="tpu_custom_call" | custom-call | flops 13333332992 | bytes 30000000 | tf_op jit(solution)/shard_map/pallas_call | solution.py:669
  241.5 4.7 %collective-permute-done.11 = bf16[2,2,2,48,1536]{4,3,2,1,0:T(8,128)(2,1)S(1)} collective-permute-done((bf16[2,2,2,48,1536]{4,3,2,1,0:T(8,128)(2,1)}, bf16[2,2,2,48,1536]{4,3,2,1,0:T(8,128)(2,1)S(1)}, u32[]{:S(2)}, u32[]{:S(2)}) %collective-permute-start.11) | collective-permute-done | bytes 1179680 | tf_op jit(solution)/shard_map/ppermute | solution.py:1023
  247.7 2.1 fusion.3
  249.8 2.5 fusion.2
  255.3 11.3 %shard_map.484 = (bf16[3,5,256,1152]{3,2,1,0:T(8,128)(2,1)}, f32[80,128]{1,0:T(8,128)}, f32[8,1152]{1,0:T(8,128)}) custom-call(s32[24]{0:T(128)} %get-tuple-element.289.refs_0_, s32[24]{0:T(128)} %get-tuple-element.288.refs_1_, bf16[3,5,256,1152]{3,2,1,0:T(8,128)(2,1)} %get-tuple-element.184.refs_2_, ...), custom_call_target="tpu_custom_call", output_to_operand_aliasing={{0}: (9, {})} | custom-call | flops 6666666496 | bytes 15000000 | tf_op jit(solution)/shard_map/pallas_call | solution.py:669
  267.9 1.9 fusion.5
  273.9 13.5 %shard_map.485 = (bf16[2,768,384]{2,1,0:T(8,128)(2,1)}, bf16[2,768,384]{2,1,0:T(8,128)(2,1)}) custom-call(s32[1]{0:T(128)} %bitcast.1.core, bf16[768,3840]{1,0:T(8,128)(2,1)} %get-tuple-element.172.xt, bf16[3840,1152]{1,0:T(8,128)(2,1)} %bitcast.118, bf16[768,384]{1,0:T(8,128)(2,1)} %get-tuple-element.200.proj), custom_call_target="tpu_custom_call" | custom-call | flops 7000000000 | bytes 16000000 | tf_op jit(solution)/shard_map/pallas_call | solution.py:763
  290.5 2.6 collective-permute-start.17
  293.5 20.3 %shard_map.486 = (bf16[3,5,256,1152]{3,2,1,0:T(8,128)(2,1)}, f32[80,128]{1,0:T(8,128)}, f32[8,1152]{1,0:T(8,128)}) custom-call(s32[24]{0:T(128)} %get-tuple-element.289.refs_0_, s32[24]{0:T(128)} %get-tuple-element.288.refs_1_, bf16[3,5,256,1152]{3,2,1,0:T(8,128)(2,1)} %get-tuple-element.173.refs_2_, ...), custom_call_target="tpu_custom_call" | custom-call | flops 13333332992 | bytes 30000000 | tf_op jit(solution)/shard_map/pallas_call | solution.py:669
  316.7 2.0 fusion.11
  321.6 16.7 %shard_map.487.refs_0_ = bf16[3,1024,768]{2,1,0:T(8,128)(2,1)} custom-call(bf16[3,5,256,1152]{3,2,1,0:T(8,128)(2,1)} %get-tuple-element.219.own.refs_9_, bf16[3,5,256,1152]{3,2,1,0:T(8,128)(2,1)} %get-tuple-element.199.other, bf16[3,768,384]{2,1,0:T(8,128)(2,1)} %weights_own.3, s32[1]{0:T(128)} %bitcast.1.core, ...), custom_call_target="tpu_custom_call" | custom-call | flops 9333332992 | bytes 20000000 | tf_op jit(solution)/shard_map/pallas_call | solution.py:723
  338.2 2.3 dynamic-slice_bitcast_fusion
  340.5 2.6 collective-permute-start.20
  343.4 11.3 %shard_map.488 = (bf16[3,5,256,1152]{3,2,1,0:T(8,128)(2,1)}, f32[80,128]{1,0:T(8,128)}, f32[8,1152]{1,0:T(8,128)}) custom-call(s32[24]{0:T(128)} %get-tuple-element.289.refs_0_, s32[24]{0:T(128)} %get-tuple-element.288.refs_1_, bf16[3,5,256,1152]{3,2,1,0:T(8,128)(2,1)} %get-tuple-element.173.refs_2_, ...), custom_call_target="tpu_custom_call", output_to_operand_aliasing={{0}: (9, {})} | custom-call | flops 6666666496 | bytes 15000000 | tf_op jit(solution)/shard_map/pallas_call | solution.py:669
  358.1 13.4 %shard_map.489 = (bf16[2,768,384]{2,1,0:T(8,128)(2,1)}, bf16[2,768,384]{2,1,0:T(8,128)(2,1)}) custom-call(s32[1]{0:T(128)} %bitcast.1.core, bf16[768,3840]{1,0:T(8,128)(2,1)} %get-tuple-element.172.xt, bf16[3840,1152]{1,0:T(8,128)(2,1)} %bitcast.117, bf16[768,384]{1,0:T(8,128)(2,1)} %get-tuple-element.228.proj), custom_call_target="tpu_custom_call" | custom-call | flops 7000000000 | bytes 16000000 | tf_op jit(solution)/shard_map/pallas_call | solution.py:763
  371.5 6.2 %collective-permute-done.25.taken_a.taken_b = bf16[640,768]{1,0:T(8,128)(2,1)S(1)} collective-permute-done((bf16[640,768]{1,0:T(8,128)(2,1)}, bf16[640,768]{1,0:T(8,128)(2,1)S(1)}, u32[]{:S(2)}, u32[]{:S(2)}) %collective-permute-start.25) | collective-permute-done | bytes 983072 | tf_op jit(solution)/shard_map/ppermute | solution.py:1023
  379.7 10.6 %shard_map.490.up_a.up_b = bf16[3,1024,768]{2,1,0:T(8,128)(2,1)} custom-call(bf16[3,5,256,1152]{3,2,1,0:T(8,128)(2,1)} %get-tuple-element.238.own, bf16[3,5,256,1152]{3,2,1,0:T(8,128)(2,1)} %get-tuple-element.199.other, bf16[3,768,384]{2,1,0:T(8,128)(2,1)} %weights_own.3, s32[1]{0:T(128)} %bitcast.1.core, ...), custom_call_target="tpu_custom_call", output_to_operand_aliasing={{}: (7, {})} | custom-call | flops 4666666496 | bytes 10000000 | tf_op jit(solution)/shard_map/pallas_call | solution.py:723
  390.2 4.2 collective-permute-done.26
  398.2 2.1 fusion.9
  407.3 16.4 %shard_map.491 = (bf16[2048,768]{1,0:T(8,128)(2,1)}, f32[8,768]{1,0:T(8,128)}, f32[2,384,1536]{2,1,0:T(8,128)}, f32[1536,768]{1,0:T(8,128)}) custom-call(s32[16]{0:T(128)} %get-tuple-element.295.band_of, s32[16]{0:T(128)} %get-tuple-element.294.step_of, s32[16]{0:T(128)} %get-tuple-element.293.taken_of, s32[16]{0:T(128)} %get-tuple-element.292.has_taken, ...), custom_call_target="tpu_custom_call" | custom-call | flops 100000000 | bytes 35000000 | tf_op jit(solution)/shard_map/pallas_call | solution.py:817
  425.6 33.2 %shard_map.492 = (bf16[4,768,384]{2,1,0:T(8,128)(2,1)S(1)}, f32[24,768]{1,0:T(8,128)S(1)}, f32[56,128]{1,0:T(8,128)S(1)}) custom-call(bf16[384,384]{1,0:T(8,128)(2,1)S(1)} %get-tuple-element.281.refs_0_, bf16[384,384]{1,0:T(8,128)(2,1)S(1)} %get-tuple-element.280.refs_1_, f32[8,768]{1,0:T(8,128)S(1)} %copy-done.10, f32[8,768]{1,0:T(8,128)S(1)} %copy-done.9, ...), custom_call_target="tpu_custom_call" | custom-call | tf_op jit(solution)/shard_map/pallas_call | solution.py:992
  458.9 2.0 slice_convert_fusion
  (189 shorter events, 58.6 us)
Async XLA Ops:
  2.9 22.9 %collective-permute-start = (bf16[3,384,384]{2,1,0:T(8,128)(2,1)}, bf16[3,384,384]{2,1,0:T(8,128)(2,1)}, u32[]{:S(2)}, u32[]{:S(2)}) collective-permute-start(bf16[3,384,384]{2,1,0:T(8,128)(2,1)} %constant_dynamic-slice_fusion.2), channel_id=1, source_target_pairs={{0,1},{1,0},{2,3},{3,2},{4,5},{5,4},{6,7},{7,6},{8,9},{9,8},{10,11... | collective-permute-start | bytes 2654216 | tf_op jit(solution)/shard_map/ppermute | solution.py:1139
  5.9 57.6 %collective-permute-start.1 = (bf16[2,384]{1,0:T(2,128)(2,1)S(1)}, bf16[2,384]{1,0:T(2,128)(2,1)S(1)}, u32[]{:S(2)}, u32[]{:S(2)}) collective-permute-start(bf16[2,384]{1,0:T(2,128)(2,1)S(1)} %copy-done.44), channel_id=1, source_target_pairs={{0,1},{1,0},{2,3},{3,2},{4,5},{5,4},{6,7},{7,6},{8,9},{9,8},{10,11... | collective-permute-start | bytes 4616 | tf_op jit(solution)/shard_map/ppermute | solution.py:1139
  25.8 37.7 %collective-permute-start.2 = (bf16[3,384,384]{2,1,0:T(8,128)(2,1)}, bf16[3,384,384]{2,1,0:T(8,128)(2,1)}, u32[]{:S(2)}, u32[]{:S(2)}) collective-permute-start(bf16[3,384,384]{2,1,0:T(8,128)(2,1)} %collective-permute-done.mine), channel_id=1, source_target_pairs={{0,2},{2,0},{4,6},{6,4},{8,10},{10,8},{12,14},{14,12},{16,18},{18,... | collective-permute-start | bytes 2654216 | tf_op jit(solution)/shard_map/ppermute | solution.py:1024
  25.9 71.4 %collective-permute-start.3 = (bf16[384,1536]{1,0:T(8,128)(2,1)S(1)}, bf16[384,1536]{1,0:T(8,128)(2,1)}, u32[]{:S(2)}, u32[]{:S(2)}) collective-permute-start(bf16[384,1536]{1,0:T(8,128)(2,1)S(1)} %constant_dynamic-slice_fusion.1), channel_id=1, source_target_pairs={{0,1},{1,0},{2,3},{3,2},{4,5},{5,4},{6,7},{7,6},{8,9},{9,8},{10,11... | collective-permute-start | bytes 3538952 | tf_op jit(solution)/shard_map/ppermute | solution.py:1139
  27.6 69.6 %collective-permute-start.4 = (bf16[1536,384]{1,0:T(8,128)(2,1)S(1)}, bf16[1536,384]{1,0:T(8,128)(2,1)}, u32[]{:S(2)}, u32[]{:S(2)}) collective-permute-start(bf16[1536,384]{1,0:T(8,128)(2,1)S(1)} %constant_dynamic-slice_fusion), channel_id=1, source_target_pairs={{0,1},{1,0},{2,3},{3,2},{4,5},{5,4},{6,7},{7,6},{8,9},{9,8},{10,11... | collective-permute-start | bytes 3538952 | tf_op jit(solution)/shard_map/ppermute | solution.py:1139
  27.9 69.3 %collective-permute-start.5 = (bf16[384,768]{1,0:T(8,128)(2,1)S(1)}, bf16[384,768]{1,0:T(8,128)(2,1)S(1)}, u32[]{:S(2)}, u32[]{:S(2)}) collective-permute-start(bf16[384,768]{1,0:T(8,128)(2,1)S(1)} %copy-done.13), channel_id=1, source_target_pairs={{0,1},{1,0},{2,3},{3,2},{4,5},{5,4},{6,7},{7,6},{8,9},{9,8},{10,11... | collective-permute-start | bytes 1769480 | tf_op jit(solution)/shard_map/ppermute | solution.py:1139
  97.2 17.9 %collective-permute-start.6 = (bf16[384,1536]{1,0:T(8,128)(2,1)}, bf16[384,1536]{1,0:T(8,128)(2,1)S(1)}, u32[]{:S(2)}, u32[]{:S(2)}) collective-permute-start(bf16[384,1536]{1,0:T(8,128)(2,1)} %collective-permute-done.3.one_b), channel_id=1, source_target_pairs={{0,2},{2,0},{4,6},{6,4},{8,10},{10,8},{12,14},{14,12},{16,18},{18,... | collective-permute-start | bytes 3538952 | tf_op jit(solution)/shard_map/ppermute | solution.py:1024
  97.3 17.8 %collective-permute-start.8 = (bf16[1536,384]{1,0:T(8,128)(2,1)}, bf16[1536,384]{1,0:T(8,128)(2,1)S(1)}, u32[]{:S(2)}, u32[]{:S(2)}) collective-permute-start(bf16[1536,384]{1,0:T(8,128)(2,1)} %collective-permute-done.4.two_b), channel_id=1, source_target_pairs={{0,2},{2,0},{4,6},{6,4},{8,10},{10,8},{12,14},{14,12},{16,18},{18,... | collective-permute-start | bytes 3538952 | tf_op jit(solution)/shard_map/ppermute | solution.py:1024
  97.8 17.3 %collective-permute-start.7 = (bf16[1536]{0:T(1024)(128)(2,1)}, bf16[1536]{0:T(1024)(128)(2,1)S(1)}, u32[]{:S(2)}, u32[]{:S(2)}) collective-permute-start(bf16[1536]{0:T(1024)(128)(2,1)} %bias_a.1), channel_id=1, source_target_pairs={{0,1},{1,0},{2,3},{3,2},{4,5},{5,4},{6,7},{7,6},{8,9},{9,8},{10,11... | collective-permute-start | bytes 9224 | tf_op jit(solution)/shard_map/ppermute | solution.py:1139
  191.9 21.4 %collective-permute-start.10 = (bf16[2,2,2,2,192,384]{5,4,3,2,1,0:T(8,128)(2,1)}, bf16[2,2,2,2,192,384]{5,4,3,2,1,0:T(8,128)(2,1)}, u32[]{:S(2)}, u32[]{:S(2)}) collective-permute-start(bf16[2,2,2,2,192,384]{5,4,3,2,1,0:T(8,128)(2,1)} %bitcast.138), channel_id=1, source_target_pairs={{0,2},{2,0},{4,6},{6,4},{8,10},{10,8},{12,14},{14,12},{16,18},{18,... | collective-permute-start | bytes 7077896 | tf_op jit(solution)/shard_map/ppermute | solution.py:1024
  192.0 21.3 %collective-permute-start.9 = (bf16[2,2,2,2,48,1536]{5,4,3,2,1,0:T(8,128)(2,1)}, bf16[2,2,2,2,48,1536]{5,4,3,2,1,0:T(8,128)(2,1)S(1)}, u32[]{:S(2)}, u32[]{:S(2)}) collective-permute-start(bf16[2,2,2,2,48,1536]{5,4,3,2,1,0:T(8,128)(2,1)} %bitcast.137), channel_id=1, source_target_pairs={{0,2},{2,0},{4,6},{6,4},{8,10},{10,8},{12,14},{14,12},{16,18},{18,... | collective-permute-start | bytes 7077896 | tf_op jit(solution)/shard_map/ppermute | solution.py:1024
  218.0 28.2 %collective-permute-start.11 = (bf16[2,2,2,48,1536]{4,3,2,1,0:T(8,128)(2,1)}, bf16[2,2,2,48,1536]{4,3,2,1,0:T(8,128)(2,1)S(1)}, u32[]{:S(2)}, u32[]{:S(2)}) collective-permute-start(bf16[2,2,2,48,1536]{4,3,2,1,0:T(8,128)(2,1)} %fusion), channel_id=1, source_target_pairs={{0,1},{1,0},{2,3},{3,2},{4,5},{5,4},{6,7},{7,6},{8,9},{9,8},{10,11... | collective-permute-start | bytes 3538952 | tf_op jit(solution)/shard_map/ppermute | solution.py:1023
  219.7 28.0 %collective-permute-start.12 = (bf16[2,2,2,192,384]{4,3,2,1,0:T(8,128)(2,1)}, bf16[2,2,2,192,384]{4,3,2,1,0:T(8,128)(2,1)}, u32[]{:S(2)}, u32[]{:S(2)}) collective-permute-start(bf16[2,2,2,192,384]{4,3,2,1,0:T(8,128)(2,1)} %fusion.1), channel_id=1, source_target_pairs={{0,4},{2,6},{4,0},{6,2},{8,12},{10,14},{12,8},{14,10},{16,20},{18,... | collective-permute-start | bytes 3538952 | tf_op jit(solution)/shard_map/ppermute | solution.py:1024
  252.2 14.5 %collective-permute-start.13 = (bf16[2,2,48,1536]{3,2,1,0:T(8,128)(2,1)}, bf16[2,2,48,1536]{3,2,1,0:T(8,128)(2,1)}, u32[]{:S(2)}, u32[]{:S(2)}) collective-permute-start(bf16[2,2,48,1536]{3,2,1,0:T(8,128)(2,1)} %fusion.3), channel_id=1, source_target_pairs={{0,4},{2,6},{4,0},{6,2},{8,12},{10,14},{12,8},{14,10},{16,20},{18,... | collective-permute-start | bytes 1769480 | tf_op jit(solution)/shard_map/ppermute | solution.py:1024
  253.7 14.2 %collective-permute-start.14 = (bf16[2,2,192,384]{3,2,1,0:T(8,128)(2,1)}, bf16[2,2,192,384]{3,2,1,0:T(8,128)(2,1)}, u32[]{:S(2)}, u32[]{:S(2)}) collective-permute-start(bf16[2,2,192,384]{3,2,1,0:T(8,128)(2,1)} %fusion.2), channel_id=1, source_target_pairs={{0,8},{2,10},{4,12},{6,14},{8,0},{10,2},{12,4},{14,6},{16,24},{18,... | collective-permute-start | bytes 1769480 | tf_op jit(solution)/shard_map/ppermute | solution.py:1024
  271.2 16.1 %collective-permute-start.15 = (bf16[2,48,1536]{2,1,0:T(8,128)(2,1)}, bf16[2,48,1536]{2,1,0:T(8,128)(2,1)}, u32[]{:S(2)}, u32[]{:S(2)}) collective-permute-start(bf16[2,48,1536]{2,1,0:T(8,128)(2,1)} %fusion.5), channel_id=1, source_target_pairs={{0,8},{2,10},{4,12},{6,14},{8,0},{10,2},{12,4},{14,6},{16,24},{18,... | collective-permute-start | bytes 884744 | tf_op jit(solution)/shard_map/ppermute | solution.py:1024
  272.9 14.5 %collective-permute-start.16 = (bf16[2,192,384]{2,1,0:T(8,128)(2,1)S(1)}, bf16[2,192,384]{2,1,0:T(8,128)(2,1)}, u32[]{:S(2)}, u32[]{:S(2)}) collective-permute-start(bf16[2,192,384]{2,1,0:T(8,128)(2,1)S(1)} %fusion.4), channel_id=1, source_target_pairs={{0,1},{1,0},{2,3},{3,2},{4,5},{5,4},{6,7},{7,6},{8,9},{9,8},{10,11... | collective-permute-start | bytes 884744 | tf_op jit(solution)/shard_map/ppermute | solution.py:1023
  290.5 23.2 %collective-permute-start.19 = (bf16[2,768,384]{2,1,0:T(8,128)(2,1)}, bf16[2,768,384]{2,1,0:T(8,128)(2,1)S(1)}, u32[]{:S(2)}, u32[]{:S(2)}) collective-permute-start(bf16[2,768,384]{2,1,0:T(8,128)(2,1)} %get-tuple-element.213), channel_id=1, source_target_pairs={{0,2},{2,0},{4,6},{6,4},{8,10},{10,8},{12,14},{14,12},{16,18},{18,... | collective-permute-start | bytes 3538952 | tf_op jit(solution)/shard_map/ppermute | solution.py:1024
  290.5 23.2 %collective-permute-start.17 = (bf16[48,1536]{1,0:T(8,128)(2,1)}, bf16[48,1536]{1,0:T(8,128)(2,1)S(1)}, u32[]{:S(2)}, u32[]{:S(2)}) collective-permute-start(bf16[48,1536]{1,0:T(8,128)(2,1)} %fusion.15), channel_id=1, source_target_pairs={{0,16},{2,18},{4,20},{6,22},{8,24},{10,26},{12,28},{14,30},{16,0},... | collective-permute-start | bytes 442376 | tf_op jit(solution)/shard_map/ppermute | solution.py:1024
  293.1 20.6 %collective-permute-start.18 = (bf16[192,384]{1,0:T(8,128)(2,1)S(1)}, bf16[192,384]{1,0:T(8,128)(2,1)S(1)}, u32[]{:S(2)}, u32[]{:S(2)}) collective-permute-start(bf16[192,384]{1,0:T(8,128)(2,1)S(1)} %fusion.14), channel_id=1, source_target_pairs={{0,16},{2,18},{4,20},{6,22},{8,24},{10,26},{12,28},{14,30},{16,0},... | collective-permute-start | bytes 442376 | tf_op jit(solution)/shard_map/ppermute | solution.py:1024
  320.6 35.6 %collective-permute-start.22 = (bf16[2,768,384]{2,1,0:T(8,128)(2,1)S(1)}, bf16[2,768,384]{2,1,0:T(8,128)(2,1)S(1)}, u32[]{:S(2)}, u32[]{:S(2)}) collective-permute-start(bf16[2,768,384]{2,1,0:T(8,128)(2,1)S(1)} %add_convert_fusion), channel_id=1, source_target_pairs={{0,1},{1,0},{2,3},{3,2},{4,5},{5,4},{6,7},{7,6},{8,9},{9,8},{10,11... | collective-permute-start | bytes 3538952 | tf_op jit(solution)/shard_map/ppermute | solution.py:1023
  340.5 15.3 %collective-permute-start.20 = (bf16[48,1536]{1,0:T(8,128)(2,1)S(1)}, bf16[48,1536]{1,0:T(8,128)(2,1)S(1)}, u32[]{:S(2)}, u32[]{:S(2)}) collective-permute-start(bf16[48,1536]{1,0:T(8,128)(2,1)S(1)} %copy-done.26), channel_id=1, source_target_pairs={{0,16},{2,18},{4,20},{6,22},{8,24},{10,26},{12,28},{14,30},{16,0},... | collective-permute-start | bytes 442376 | tf_op jit(solution)/shard_map/ppermute | solution.py:1024
  343.1 13.1 %collective-permute-start.21 = (bf16[192,384]{1,0:T(8,128)(2,1)S(1)}, bf16[192,384]{1,0:T(8,128)(2,1)S(1)}, u32[]{:S(2)}, u32[]{:S(2)}) collective-permute-start(bf16[192,384]{1,0:T(8,128)(2,1)S(1)} %copy-done.25), channel_id=1, source_target_pairs={{0,16},{2,18},{4,20},{6,22},{8,24},{10,26},{12,28},{14,30},{16,0},... | collective-permute-start | bytes 442376 | tf_op jit(solution)/shard_map/ppermute | solution.py:1024
  354.7 23.0 %collective-permute-start.25 = (bf16[640,768]{1,0:T(8,128)(2,1)}, bf16[640,768]{1,0:T(8,128)(2,1)S(1)}, u32[]{:S(2)}, u32[]{:S(2)}) collective-permute-start(bf16[640,768]{1,0:T(8,128)(2,1)} %dynamic-slice_bitcast_fusion), channel_id=1, source_target_pairs={{0,1},{1,0},{2,3},{3,2},{4,5},{5,4},{6,7},{7,6},{8,9},{9,8},{10,11... | collective-permute-start | bytes 2949128 | tf_op jit(solution)/shard_map/ppermute | solution.py:1023
  357.4 20.3 %collective-permute-start.23 = (bf16[2,48,1536]{2,1,0:T(8,128)(2,1)S(1)}, bf16[2,48,1536]{2,1,0:T(8,128)(2,1)S(1)}, u32[]{:S(2)}, u32[]{:S(2)}) collective-permute-start(bf16[2,48,1536]{2,1,0:T(8,128)(2,1)S(1)} %broadcast_select_fusion.5), channel_id=1, source_target_pairs={{0,8},{2,10},{4,12},{6,14},{8,0},{10,2},{12,4},{14,6},{16,24},{18,... | collective-permute-start | bytes 884744 | tf_op jit(solution)/shard_map/ppermute | solution.py:1024
  357.5 20.2 %collective-permute-start.24 = (bf16[2,192,384]{2,1,0:T(8,128)(2,1)S(1)}, bf16[2,192,384]{2,1,0:T(8,128)(2,1)S(1)}, u32[]{:S(2)}, u32[]{:S(2)}) collective-permute-start(bf16[2,192,384]{2,1,0:T(8,128)(2,1)S(1)} %broadcast_select_fusion.4), channel_id=1, source_target_pairs={{0,4},{2,6},{4,0},{6,2},{8,12},{10,14},{12,8},{14,10},{16,20},{18,... | collective-permute-start | bytes 884744 | tf_op jit(solution)/shard_map/ppermute | solution.py:1024
  378.7 16.0 %collective-permute-start.28 = (bf16[2,768,384]{2,1,0:T(8,128)(2,1)}, bf16[2,768,384]{2,1,0:T(8,128)(2,1)S(1)}, u32[]{:S(2)}, u32[]{:S(2)}) collective-permute-start(bf16[2,768,384]{2,1,0:T(8,128)(2,1)} %get-tuple-element.241), channel_id=1, source_target_pairs={{0,2},{2,0},{4,6},{6,4},{8,10},{10,8},{12,14},{14,12},{16,18},{18,... | collective-permute-start | bytes 3538952 | tf_op jit(solution)/shard_map/ppermute | solution.py:1024
  378.7 15.7 %collective-permute-start.26 = (bf16[2,2,48,1536]{3,2,1,0:T(8,128)(2,1)S(1)}, bf16[2,2,48,1536]{3,2,1,0:T(8,128)(2,1)S(1)}, u32[]{:S(2)}, u32[]{:S(2)}) collective-permute-start(bf16[2,2,48,1536]{3,2,1,0:T(8,128)(2,1)S(1)} %broadcast_select_fusion.3), channel_id=1, source_target_pairs={{0,4},{2,6},{4,0},{6,2},{8,12},{10,14},{12,8},{14,10},{16,20},{18,... | collective-permute-start | bytes 1769480 | tf_op jit(solution)/shard_map/ppermute | solution.py:1024
  379.2 15.5 %collective-permute-start.27 = (bf16[2,2,192,384]{3,2,1,0:T(8,128)(2,1)S(1)}, bf16[2,2,192,384]{3,2,1,0:T(8,128)(2,1)S(1)}, u32[]{:S(2)}, u32[]{:S(2)}) collective-permute-start(bf16[2,2,192,384]{3,2,1,0:T(8,128)(2,1)S(1)} %broadcast_select_fusion.2), channel_id=1, source_target_pairs={{0,8},{2,10},{4,12},{6,14},{8,0},{10,2},{12,4},{14,6},{16,24},{18,... | collective-permute-start | bytes 1769480 | tf_op jit(solution)/shard_map/ppermute | solution.py:1024
  397.4 8.9 %collective-permute-start.30 = (bf16[2,2,2,192,384]{4,3,2,1,0:T(8,128)(2,1)}, bf16[2,2,2,192,384]{4,3,2,1,0:T(8,128)(2,1)}, u32[]{:S(2)}, u32[]{:S(2)}) collective-permute-start(bf16[2,2,2,192,384]{4,3,2,1,0:T(8,128)(2,1)} %broadcast_select_fusion), channel_id=1, source_target_pairs={{0,2},{2,0},{4,6},{6,4},{8,10},{10,8},{12,14},{14,12},{16,18},{18,... | collective-permute-start | bytes 3538952 | tf_op jit(solution)/shard_map/ppermute | solution.py:1024
  400.4 23.4 %collective-permute-start.31 = (bf16[384,384]{1,0:T(8,128)(2,1)}, bf16[384,384]{1,0:T(8,128)(2,1)}, u32[]{:S(2)}, u32[]{:S(2)}) collective-permute-start(bf16[384,384]{1,0:T(8,128)(2,1)} %get-tuple-element.254), channel_id=1, source_target_pairs={{0,4},{2,6},{4,0},{6,2},{8,12},{10,14},{12,8},{14,10},{16,20},{18,... | collective-permute-start | bytes 884744 | tf_op jit(solution)/shard_map/ppermute | solution.py:1024
  401.9 21.9 %collective-permute-start.32 = (bf16[384,384]{1,0:T(8,128)(2,1)}, bf16[384,384]{1,0:T(8,128)(2,1)}, u32[]{:S(2)}, u32[]{:S(2)}) collective-permute-start(bf16[384,384]{1,0:T(8,128)(2,1)} %get-tuple-element.255), channel_id=1, source_target_pairs={{0,8},{2,10},{4,12},{6,14},{8,0},{10,2},{12,4},{14,6},{16,24},{18,... | collective-permute-start | bytes 884744 | tf_op jit(solution)/shard_map/ppermute | solution.py:1024
  (47 other events, 613.1 us)

commit v4 on v3

--- a/solution.py
+++ b/solution.py
@@ -49,35 +49,32 @@
     return pl.BlockSpec(shape, lambda *_: (0,) * len(shape), pipeline_mode=pl.Buffered(1))
 
 
-STARTS = np.array([[0, 14, 28], [42, 28, 56]], np.int32)
-
-
-def pair_tables(place):
-    block = np.zeros((2, 24), np.int32)
-    valid = np.zeros((2, 24), np.int32)
-    local = np.zeros((2, 24), np.int32)
-    owned = np.zeros((2, 24), np.int32)
-    band_of = np.zeros((2, 16), np.int32)
-    step_of = np.zeros((2, 16), np.int32)
-    taken_of = np.zeros((2, 16), np.int32)
-    has_taken = np.zeros((2, 16), np.int32)
-    taken_of[0, 14:16], has_taken[0, 14:16] = np.arange(2), 1
-    taken_of[1, 0:5], has_taken[1, 0:5] = np.arange(5), 1
-    for m in range(2):
-        for s in range(3):
-            for t in range(7):
-                row = STARTS[m, s] + 2 * t
-                at = s * 8 + t
-                block[m, at] = min(row // 2, 31)
-                valid[m, at] = row < SIDE
-                if 32 * m <= row < 32 * m + 32:
-                    local[m, at] = (row - 32 * m) // 2
-                    owned[m, at] = 1
-                    band_of[m, local[m, at]] = s
-                    step_of[m, local[m, at]] = t
-            block[m, s * 8 + 7] = block[m, s * 8 + 6]
-    pick = lambda table: jnp.where(place == 0, jnp.asarray(table[0]), jnp.asarray(table[1]))
-    return tuple(pick(t) for t in (block, valid, local, owned, band_of, step_of, taken_of, has_taken))
+def band_start(place, band):
+    return (1 - place) * (14 * band) + place * (42 - 14 * band + 21 * band * (band - 1))
+
+
+def image_pair(place, band, step):
+    pair = band_start(place, band) // 2 + step
+    return jnp.minimum(pair, SIDE // 2 - 1), pair < SIDE // 2
+
+
+def owned_pair(place, band, step):
+    pair = band_start(place, band) // 2 + step - 16 * place
+    return jnp.clip(pair, 0, 15), (pair >= 0) & (pair < 16)
+
+
+def band_step(place, pair):
+    first = pair // 7, pair % 7
+    band = jnp.where(pair < 5, 1, jnp.where(pair < 12, 0, 2))
+    second = band, jnp.where(pair < 5, pair + 2, jnp.where(pair < 12, pair - 5, pair - 12))
+    return tuple(jnp.where(place == 0, a, b) for a, b in zip(first, second))
+
+
+def taken_pair(place, pair):
+    return (
+        jnp.where(place == 0, jnp.maximum(pair - 14, 0), jnp.minimum(pair, 4)),
+        jnp.where(place == 0, pair >= 14, pair < 5),
+    )
 
 
 def spread_rows():
@@ -119,24 +116,25 @@
     return ref[...].astype(F32).reshape(1, D)
 
 
-def window_kernel(block, valid, *refs):
+def window_kernel(spot, *refs):
     xs, (gain, shift, spread, out) = refs[:7], refs[7:]
     band = pl.program_id(0)
     for t in range(7):
         scaled, _ = norm_parts(xs[t][...].astype(F32))
         normed = scaled * vec(gain) + vec(shift)
-        normed = (normed * valid[band * 8 + t].astype(F32)).astype(BF)
+        valid = image_pair(spot[0], band, t)[1]
+        normed = (normed * valid.astype(F32)).astype(BF)
         moved = dot(spread[...], normed).astype(BF)
         out[:, :, 32 * t : 32 * t + 32, :] = moved.reshape(1, NWIN, 32, D)
     out[:, :, 224:, :] = jnp.zeros((1, NWIN, 32, D), BF)
 
 
-def windows_of(x, gain, shift, spread, block, valid):
-    at = lambda t: lambda s, block, valid: (block[s * 8 + t], 0)
+def windows_of(spot, x, gain, shift, spread):
+    at = lambda t: lambda s, spot: (image_pair(spot[0], s, t)[0], 0)
     return pl.pallas_call(
         window_kernel,
         grid_spec=pltpu.PrefetchScalarGridSpec(
-            num_scalar_prefetch=2,
+            num_scalar_prefetch=1,
             grid=(3,),
             in_specs=[pl.BlockSpec((PAIR, D), at(t)) for t in range(7)]
             + [whole((D,)), whole((D,)), whole((NWIN * 32, PAIR))],
@@ -145,7 +143,7 @@
         out_shape=jax.ShapeDtypeStruct((3, NWIN, SLOTS, D), BF),
         compiler_params=params(),
         cost_estimate=cost(3 * 7 * 160 * 128 * 768 * 2, 10e6),
-    )(block, valid, *([x] * 7), gain, shift, spread)
+    )(spot, *([x] * 7), gain, shift, spread)
 
 
 def shift_masks(lanes_from):
@@ -198,10 +196,10 @@
     attend_window(x, bias, rel_even, rel_odd, qkv_out, p_out, ctx_out, xt_out, joined, vt)
 
 
-def attend_other(x, bias, core, mine, theirs, rel_even, rel_odd, qkv_out, p_out, ctx_out, joined, vt):
+def attend_other(x, bias, spot, mine, theirs, rel_even, rel_odd, qkv_out, p_out, ctx_out, joined, vt):
     @pl.when((pl.program_id(0) == 0) & (pl.program_id(1) == 0))
     def _():
-        join_pieces(core[0], mine, theirs, joined, 0)
+        join_pieces(spot[1], mine, theirs, joined, 0)
 
     attend_window(x, bias, rel_even, rel_odd, qkv_out, p_out, ctx_out, None, joined, vt)
 
@@ -309,8 +307,8 @@
 
 
 def middle_kernel(
-    band_of, step_of, offset, own_a, own_b, other_a, other_b, x, cot, proj_own, proj_other, bias, gain, shift, gather,
-    middle, normed, normed_t, cot_t, ctx_out, proj,
+    spot, own_a, own_b, other_a, other_b, x, proj_own, proj_other, bias, gain, shift, gather,
+    middle, normed, normed_t, ctx_out, proj,
 ):
     @pl.when(pl.program_id(0) == 0)
     def _():
@@ -322,31 +320,37 @@
             moved = dot(gather[...], parts[side][...].reshape(NWIN * 32, HALF)).astype(BF)
             ctx_out[row : row + PAIR, side * HALF : side * HALF + HALF] = moved
     value = x[...].astype(F32) + (dot(ctx_out[...], proj[...]) + vec(bias))
-    middle[...] = value
+    middle[...] = value.astype(BF)
     scaled, _ = norm_parts(value)
     low = (scaled * vec(gain) + vec(shift)).astype(BF)
     normed[...] = low
     normed_t[...] = low.T
-    cot_t[...] = cot[...].T
-
-
-def middle_of(ctx_own, ctx_other, x, cot, proj_own, proj_other, bias, gain, shift, gather, band_of, step_of, offset):
+
+
+def middle_of(spot, ctx_own, ctx_other, x, proj_own, proj_other, bias, gain, shift, gather):
     rows = 2 * PAIR
-    at = lambda k: lambda i, band_of, step_of, offset: (band_of[2 * i + k], 0, step_of[2 * i + k], 0)
+
+    def at(k):
+        def place(i, spot):
+            band, step = band_step(spot[0], 2 * i + k)
+            return band, 0, step, 0
+
+        return pl.BlockSpec((1, NWIN, 32, HALF), place)
+
     row_block = pl.BlockSpec((rows, D), lambda i, *_: (i, 0))
     col_block = pl.BlockSpec((D, rows), lambda i, *_: (0, i))
+    low = jax.ShapeDtypeStruct((OWN, D), BF)
     return pl.pallas_call(
         middle_kernel,
         grid_spec=pltpu.PrefetchScalarGridSpec(
-            num_scalar_prefetch=3,
+            num_scalar_prefetch=1,
             grid=(OWN // rows,),
             in_specs=[
-                pl.BlockSpec((1, NWIN, 32, HALF), at(0)),
-                pl.BlockSpec((1, NWIN, 32, HALF), at(1)),
-                pl.BlockSpec((1, NWIN, 32, HALF), at(0)),
-                pl.BlockSpec((1, NWIN, 32, HALF), at(1)),
-                pl.BlockSpec((rows, D), lambda i, band_of, step_of, offset: (offset[0] + i, 0)),
-                row_block,
+                at(0),
+                at(1),
+                at(0),
+                at(1),
+                pl.BlockSpec((rows, D), lambda i, spot: (spot[0] * (OWN // rows) + i, 0)),
                 whole((HALF, D)),
                 whole((HALF, D)),
                 whole((D,)),
@@ -354,19 +358,30 @@
                 whole((D,)),
                 whole((PAIR, NWIN * 32)),
             ],
-            out_specs=[row_block, row_block, col_block, col_block, row_block],
+            out_specs=[row_block, row_block, col_block, row_block],
             scratch_shapes=[pltpu.VMEM((D, D), BF)],
         ),
-        out_shape=[
-            jax.ShapeDtypeStruct((OWN, D), F32),
-            jax.ShapeDtypeStruct((OWN, D), BF),
-            jax.ShapeDtypeStruct((D, OWN), BF),
-            jax.ShapeDtypeStruct((D, OWN), BF),
-            jax.ShapeDtypeStruct((OWN, D), BF),
-        ],
+        out_shape=[low, low, jax.ShapeDtypeStruct((D, OWN), BF), low],
         compiler_params=params(),
-        cost_estimate=cost(3e9, 30e6),
-    )(band_of, step_of, offset, ctx_own, ctx_own, ctx_other, ctx_other, x, cot, proj_own, proj_other, bias, gain, shift, gather)
+        cost_estimate=cost(3e9, 25e6),
+    )(spot, ctx_own, ctx_own, ctx_other, ctx_other, x, proj_own, proj_other, bias, gain, shift, gather)
+
+
+def turn_kernel(value, out):
+    out[...] = value[...].T
+
+
+def turned_of(value):
+    rows = 512
+    return pl.pallas_call(
+        turn_kernel,
+        grid=(OWN // rows,),
+        in_specs=[pl.BlockSpec((rows, D), lambda i: (i, 0))],
+        out_specs=pl.BlockSpec((D, rows), lambda i: (0, i)),
+        out_shape=jax.ShapeDtypeStruct((D, OWN), BF),
+        compiler_params=params(),
+        cost_estimate=cost(1e6, 6e6),
+    )(value)
 
 
 CHUNK = 512
@@ -374,8 +389,9 @@
 
 
 def feed_kernel(
-    core, normed, normed_t, cot, cot_t, one_a, one_b, one_c, bias_a, bias_b, two_a, two_b, two_c,
-    forward, back, one_kept, one_sent, two_kept, two_sent, sums, one, two, bias, hidden, grads,
+    spot, normed, normed_t, cot, cot_t, one_a, one_b, one_c, bias_a, bias_b, two_a, two_b, two_c,
+    forward_out, back_out, one_kept, one_sent, two_kept, two_sent, sums,
+    forward, back, one, two, bias, hidden, grads,
 ):
     step = pl.program_id(0)
 
@@ -393,8 +409,8 @@
     @pl.when(step >= CHUNKS // 2)
     def _():
         bias[...] = bias_b[...].astype(F32).reshape(1, CHUNK)
-        mine = pl.multiple_of(core[0] * HALF, HALF)
-        theirs = pl.multiple_of((1 - core[0]) * HALF, HALF)
+        mine = pl.multiple_of(spot[1] * HALF, HALF)
+        theirs = pl.multiple_of((1 - spot[1]) * HALF, HALF)
         one[pl.ds(mine, HALF), :] = one_b[...]
         one[pl.ds(theirs, HALF), :] = one_c[...]
         two[:, pl.ds(mine, HALF)] = two_b[...]
@@ -415,7 +431,7 @@
         back[rows, :] += dot(grad, one[...], NT)
     sums[...] = total
 
-    first = core[0] == 0
+    first = spot[1] == 0
     one_grad = dot(normed_t[...], grads[...]).astype(BF)
     low, high = one_grad[:HALF], one_grad[HALF:]
     one_kept[0] = jnp.where(first, low, high)
@@ -425,8 +441,13 @@
     two_kept[0] = jnp.where(first, low, high).T
     two_sent[0] = jnp.where(first, high, low).T
 
-
-def feed(core, normed, normed_t, cot, cot_t, one_a, ones, bias_a, bias_b, two_a, twos):
+    @pl.when(step == pl.num_programs(0) - 1)
+    def _():
+        forward_out[...] = forward[...].astype(BF)
+        back_out[...] = back[...].astype(BF)
+
+
+def feed(spot, normed, normed_t, cot, cot_t, one_a, ones, bias_a, bias_b, two_a, twos):
     half = CHUNKS // 2
     own = lambda j: jnp.minimum(j, half - 1)
     other = lambda j: jnp.maximum(j - half, 0)
@@ -459,6 +480,8 @@
             ],
             out_specs=[sum_block, sum_block, one_block, one_block, two_block, two_block, bias_block],
             scratch_shapes=[
+                pltpu.VMEM((OWN, D), F32),
+                pltpu.VMEM((OWN, D), F32),
                 pltpu.VMEM((D, CHUNK), BF),
                 pltpu.VMEM((CHUNK, D), BF),
                 pltpu.VMEM((1, CHUNK), F32),
@@ -467,8 +490,8 @@
             ],
         ),
         out_shape=[
-            jax.ShapeDtypeStruct((OWN, D), F32),
-            jax.ShapeDtypeStruct((OWN, D), F32),
+            jax.ShapeDtypeStruct((OWN, D), BF),
+            jax.ShapeDtypeStruct((OWN, D), BF),
             one_shape,
             one_shape,
             two_shape,
@@ -477,7 +500,7 @@
         ],
         compiler_params=params(62),
         cost_estimate=cost(58e9, 60e6, 12e6),
-    )(core, normed, normed_t, cot, cot_t, one_a, *ones, bias_a, bias_b, two_a, *twos)
+    )(spot, normed, normed_t, cot, cot_t, one_a, *ones, bias_a, bias_b, two_a, *twos)
 
 
 def add_row(sums, row, values):
@@ -497,17 +520,17 @@
         proj_grad[...] = jnp.zeros_like(proj_grad)
         sums[...] = jnp.zeros_like(sums)
 
-    value = middle[...]
-    block_out[...] = (value + (forward[...] + vec(bias))).astype(BF)
+    value = middle[...].astype(F32)
+    block_out[...] = (value + (forward[...].astype(F32) + vec(bias))).astype(BF)
     scaled, inverse = norm_parts(value)
-    upstream = back[...]
+    upstream = back[...].astype(F32)
     scaled_up = upstream * vec(gain)
     first = jnp.mean(scaled_up, axis=-1, keepdims=True)
     second = jnp.mean(scaled_up * scaled, axis=-1, keepdims=True)
     cotangent = cot[...].astype(F32)
     grad = cotangent + inverse * (scaled_up - first - scaled * second)
-    grad_out[...] = grad
     low = grad.astype(BF)
+    grad_out[...] = low
     ctx_grad[...] = dot(low, proj[...], NT).astype(BF)
     proj_grad[...] += dot(context[...], low, TN)
     add_row(sums, 0, upstream * scaled)
@@ -540,7 +563,7 @@
         ],
         out_shape=[
             jax.ShapeDtypeStruct((OWN, D), BF),
-            jax.ShapeDtypeStruct((OWN, D), F32),
+            jax.ShapeDtypeStruct((OWN, D), BF),
             jax.ShapeDtypeStruct((OWN, D), BF),
             jax.ShapeDtypeStruct((D, HALF), BF),
             jax.ShapeDtypeStruct((D, HALF), BF),
@@ -552,7 +575,7 @@
     )(middle, forward, back, cot, context, proj_own, proj_other, bias, gain)
 
 
-def attend_back_kernel(first, local, owned, qkv, p, ctx_grad, spread, rel_even, rel_odd, fold, *refs):
+def attend_back_kernel(first, spot, qkv, p, ctx_grad, spread, rel_even, rel_odd, fold, *refs):
     d_out, rel_grad, sums, upstream, kt = refs[-5:]
     band = pl.program_id(0) + first
     window = pl.program_id(1)
@@ -565,10 +588,10 @@
     @pl.when(window == 0)
     def _():
         for t in range(7):
-            at = band * 8 + t
-            rows = pl.ds(pl.multiple_of(local[at] * PAIR, PAIR), PAIR)
+            at, owned = owned_pair(spot[0], band, t)
+            rows = pl.ds(pl.multiple_of(at * PAIR, PAIR), PAIR)
             moved = dot(spread[...], ctx_grad[rows, :])
-            moved = moved * owned[at].astype(F32)
+            moved = moved * owned.astype(F32)
             upstream[:, 32 * t : 32 * t + 32, :] = moved.astype(BF).reshape(NWIN, 32, HALF)
         upstream[:, 224:256, :] = jnp.zeros((NWIN, 32, HALF), BF)
 
@@ -662,14 +685,14 @@
     return table.reshape(32, KEYS)
 
 
-def attend_back(qkv, p, ctx_grad, side, spread, rel_even, rel_odd, fold, local, owned, bands, *d_in):
+def attend_back(spot, qkv, p, ctx_grad, side, spread, rel_even, rel_odd, fold, bands, *d_in):
     first, last = bands
     block = pl.BlockSpec((1, 1, SLOTS, TRIO), lambda s, w, *_: (s + first, w, 0, 0))
     share = (last - first) / 3
     return pl.pallas_call(
         lambda *refs: attend_back_kernel(first, *refs),
         grid_spec=pltpu.PrefetchScalarGridSpec(
-            num_scalar_prefetch=2,
+            num_scalar_prefetch=1,
             grid=(last - first, NWIN),
             in_specs=[
                 block,
@@ -693,20 +716,20 @@
             jax.ShapeDtypeStruct((GREL, 128), F32),
             jax.ShapeDtypeStruct((8, TRIO), F32),
         ],
-        input_output_aliases={9: 0} if d_in else {},
+        input_output_aliases={8: 0} if d_in else {},
         compiler_params=params(),
         cost_estimate=cost(20e9 * share, 45e6 * share),
-    )(local, owned, qkv, p, ctx_grad, spread, rel_even, rel_odd, fold, *d_in)
-
-
-def norm_grad_kernel(own, other, weights_own, core, mine, theirs, gather, *refs):
+    )(spot, qkv, p, ctx_grad, spread, rel_even, rel_odd, fold, *d_in)
+
+
+def norm_grad_kernel(own, other, weights_own, spot, mine, theirs, gather, *refs):
     out, joined = refs[-2:]
 
     @pl.when((pl.program_id(0) == 0) & (pl.program_id(1) == 0))
     def _():
         for s in range(3):
             joined[:, s * HALF : s * HALF + HALF] = weights_own[s]
-        join_pieces(core[0], mine, theirs, joined, TRIO)
+        join_pieces(spot[1], mine, theirs, joined, TRIO)
 
     rows = NWIN * 128
     left = jnp.concatenate([own[...].reshape(rows, TRIO), other[...].reshape(rows, TRIO)], axis=1)
@@ -735,21 +758,16 @@
     )(own, other, weights_own, core, mine, theirs, gather, *before)
 
 
-def qkv_grad_kernel(core, xt, d, proj, kept, sent, total):
+def qkv_grad_kernel(spot, xt, d, proj, kept, sent, total):
     step = pl.program_id(0)
-    part = dot(xt[...], d[...])
-
-    @pl.when(step == 0)
-    def _():
-        total[...] = part
-
-    @pl.when(step > 0)
-    def _():
-        total[...] += part
+    for col in range(0, TRIO, 256):
+        cols = slice(col, min(col + 256, TRIO))
+        part = dot(xt[...], d[:, cols])
+        total[:, cols] = jnp.where(step == 0, part, total[:, cols] + part)
 
     @pl.when(step == pl.num_programs(0) - 1)
     def _():
-        first = core[0] == 0
+        first = spot[1] == 0
         values = [total[:, s * HALF : s * HALF + HALF].astype(BF) for s in range(3)] + [proj[...]]
         for k in range(2):
             kept[k] = jnp.where(first, values[k], values[2 + k])
@@ -778,11 +796,11 @@
 
 
 def input_kernel(
-    band_of, step_of, taken_of, has_taken, offset, core, x, middle_grad, up_a, up_b, taken_a, taken_b, gain,
+    spot, x, middle_grad, up_a, up_b, taken_a, taken_b, gain,
     one_mine, one_theirs, two_mine, two_theirs, out, sums, one_out, two_out,
 ):
     step = pl.program_id(0)
-    first = core[0] == 0
+    first = spot[1] == 0
     mine, theirs = one_mine[...].astype(F32), one_theirs[...].astype(F32)
     one_out[0] = jnp.where(first, mine, theirs)
     one_out[1] = jnp.where(first, theirs, mine)
@@ -797,30 +815,30 @@
     for k, (up, taken) in enumerate(((up_a, taken_a), (up_b, taken_b))):
         rows = slice(k * PAIR, k * PAIR + PAIR)
         scaled, inverse = norm_parts(x[rows, :].astype(F32))
-        shared = taken[...].astype(F32) * has_taken[2 * step + k].astype(F32)
+        shared = taken[...].astype(F32) * taken_pair(spot[0], 2 * step + k)[1].astype(F32)
         upstream = up[0].astype(F32) + shared
         scaled_up = upstream * vec(gain)
         mean = jnp.mean(scaled_up, axis=-1, keepdims=True)
         second = jnp.mean(scaled_up * scaled, axis=-1, keepdims=True)
-        out[rows, :] = (middle_grad[rows, :] + inverse * (scaled_up - mean - scaled * second)).astype(BF)
+        out[rows, :] = (middle_grad[rows, :].astype(F32) + inverse * (scaled_up - mean - scaled * second)).astype(BF)
         add_row(sums, 0, upstream * scaled)
         add_row(sums, 1, upstream)
 
 
-def input_of(x, middle_grad, up, taken, gain, ones, twos, band_of, step_of, taken_of, has_taken, offset, core):
+def input_of(spot, x, middle_grad, up, taken, gain, ones, twos):
     rows = 2 * PAIR
     row_block = pl.BlockSpec((rows, D), lambda i, *_: (i, 0))
+    up_at = lambda k: lambda i, spot: band_step(spot[0], 2 * i + k) + (0,)
+    taken_at = lambda k: lambda i, spot: (taken_pair(spot[0], 2 * i + k)[0], 0)
     steps = OWN // rows
     one_rows, two_rows = HALF // steps, FF // 2 // steps
-    up_at = lambda k: lambda i, band_of, step_of, *_: (band_of[2 * i + k], step_of[2 * i + k], 0)
-    taken_at = lambda k: lambda i, band_of, step_of, taken_of, *_: (taken_of[2 * i + k], 0)
     return pl.pallas_call(
         input_kernel,
         grid_spec=pltpu.PrefetchScalarGridSpec(
-            num_scalar_prefetch=6,
+            num_scalar_prefetch=1,
             grid=(steps,),
             in_specs=[
-                pl.BlockSpec((rows, D), lambda i, b, s, t, h, offset, core: (offset[0] + i, 0)),
+                pl.BlockSpec((rows, D), lambda i, spot: (spot[0] * steps + i, 0)),
                 row_block,
                 pl.BlockSpec((1, PAIR, D), up_at(0)),
                 pl.BlockSpec((1, PAIR, D), up_at(1)),
@@ -845,7 +863,7 @@
         ],
         compiler_params=params(),
         cost_estimate=cost(1e8, 35e6),
-    )(band_of, step_of, taken_of, has_taken, offset, core, x, middle_grad, up, up, taken, taken, gain, *ones, *twos)
+    )(spot, x, middle_grad, up, up, taken, taken, gain, *ones, *twos)
 
 
 MESH = pl.DeviceIdType.MESH
@@ -1075,7 +1093,7 @@
             self.terms = [(self.taken, tuple(p for p in self.terms[0][1] if p not in self.fixed))]
         else:
             if not self.steps:
-                self.taken_last, self.taken = self.taken, None
+                self.value, self.taken_last, self.taken = self.sent, self.taken, None
                 return
             self.done = sorted(self.done + [bit], key=self.rank.index)
             axis = self.done.index(bit)
@@ -1083,7 +1101,7 @@
             shape[axis] = 2
             mine = jnp.arange(2).reshape(shape) == bit_of(bit)
             wide = lambda v: jnp.expand_dims(v, axis)
-            self.value = jnp.where(mine, wide(self.value), wide(self.taken))
+            self.value = jnp.where(mine, wide(self.sent), wide(self.taken))
         self.taken = None
 
 
@@ -1143,20 +1161,19 @@
     def by_core(weight, axis, mine):
         return lax.dynamic_slice_in_dim(weight, (core if mine else 1 - core) * HALF, HALF, axis)
 
-    block, valid, local, owned, band_of, step_of, taken_of, has_taken = pair_tables(place)
-    offset = (place * (OWN // (2 * PAIR))).astype(jnp.int32).reshape(1)
+    spot = jnp.stack([place, core]).astype(jnp.int32)
     spread = jnp.asarray(spread_rows(), BF)
     gather = jnp.asarray(spread_rows().T, BF)
     fold = jnp.asarray(fold_table(), BF)
     high_hot, wide_hot = rel_onehots()
     hots = jnp.asarray(np.pad(np.concatenate([high_hot, wide_hot], axis=1), ((0, 0), (0, 2))), F32)
     high_hot, wide_hot = jnp.asarray(high_hot, BF), jnp.asarray(wide_hot, BF)
-    core_at = core.astype(jnp.int32).reshape(1)
     qkv_mine = swap(by_core(qkv_weight, 1, True))
     bias_other = swap(qv_bias)
     fc1_bias_other = swap(fc1_bias)
-    x_windows = windows_of(image_tokens, norm1_gain, norm1_shift, spread, block, valid)
-    x_windows, qkv_mine = lax.optimization_barrier((x_windows, qkv_mine))
+    x_windows = windows_of(spot, image_tokens, norm1_gain, norm1_shift, spread)
+    cot_t = turned_of(out_cotangent)
+    x_windows, cot_t, qkv_mine = lax.optimization_barrier((x_windows, cot_t, qkv_mine))
     late = (by_core(fc1_weight, 0, True), by_core(fc2_weight, 1, True), proj_weight)
     x_windows, qkv_mine, late = lax.optimization_barrier((x_windows, qkv_mine, late))
     qkv_theirs = exchange(qkv_mine, CORE)
@@ -1165,16 +1182,15 @@
         x_windows, qv_bias, True, qkv_weight, high_hot, wide_hot, rel_rows, rel_cols
     )
     qkv_b, p_b, ctx_b = attend(
-        x_windows, bias_other, False, core_at, qkv_mine, qkv_theirs, rel_even, rel_odd
+        x_windows, bias_other, False, spot, qkv_mine, qkv_theirs, rel_even, rel_odd
     )
     ctx_b, one_mine, two_mine, proj_other = lax.optimization_barrier((ctx_b, one_mine, two_mine, proj_other))
     one_theirs, two_theirs = exchange(one_mine, CORE), exchange(two_mine, CORE)
-    middle, normed, normed_t, cot_t, context = middle_of(
-        ctx_a, ctx_b, image_tokens, out_cotangent, proj_weight, proj_other, proj_bias, norm2_gain,
-        norm2_shift, gather, band_of, step_of, offset,
+    middle, normed, normed_t, context = middle_of(
+        spot, ctx_a, ctx_b, image_tokens, proj_weight, proj_other, proj_bias, norm2_gain, norm2_shift, gather
     )
     forward, back, one_kept, one_sent, two_kept, two_sent, fc1_sums = feed(
-        core_at, normed, normed_t, out_cotangent, cot_t, fc1_weight, (one_mine, one_theirs), fc1_bias,
+        spot, normed, normed_t, out_cotangent, cot_t, fc1_weight, (one_mine, one_theirs), fc1_bias,
         fc1_bias_other, fc2_weight, (two_mine, two_theirs),
     )
     bits = [2**k for k in range(1, bits_of(size))]
@@ -1200,32 +1216,32 @@
         middle, forward, back, out_cotangent, context, proj_weight, proj_other, fc2_bias, norm2_gain
     )
     back_of = lambda qkv, p, side, grad, bands, *d: attend_back(
-        qkv, p, grad, side, spread, rel_even, rel_odd, fold, local, owned, bands, *d
+        spot, qkv, p, grad, side, spread, rel_even, rel_odd, fold, bands, *d
     )
     ctx_grad = advance(ctx_grad, feed_lines)
     d_b, rel_b, sums_b = back_of(qkv_b, p_b, 1, ctx_grad, (1, 3))
     d_b = advance(d_b, feed_lines)
     d_b, rel_b0, sums_b0 = back_of(qkv_b, p_b, 1, ctx_grad, (0, 1), d_b)
     d_b = advance(d_b, feed_lines)
-    kept_b, sent_b = qkv_grad(core_at, xt, d_b, proj_oth)
+    kept_b, sent_b = qkv_grad(spot, xt, d_b, proj_oth)
     line_b = Line(kept_b, [], [], [("give", CORE), ("pass", PAIRED)], sent_b)
     lines = feed_lines + [line_b]
     ctx_grad, kept_b = lax.optimization_barrier((ctx_grad, kept_b))
     ctx_grad = advance(ctx_grad, lines)
     d_a, rel_a, sums_a = back_of(qkv_a, p_a, 0, ctx_grad, (1, 3))
     d_a = advance(d_a, lines)
-    up = norm_grad(d_a, d_b, qkv_weight, core_at, qkv_mine, qkv_theirs, gather, (1, 3))
+    up = norm_grad(d_a, d_b, qkv_weight, spot, qkv_mine, qkv_theirs, gather, (1, 3))
     at = [2 - place, (1 - place) * 4 * SIDE, jnp.zeros_like(place)]
     sent = lax.dynamic_slice(up, at, (1, 10 * SIDE, D)).reshape(10 * SIDE, D)
     shared_line = Line(sent, [], [], [("pass", PAIRED)])
     d_a = advance(d_a, [shared_line])
     d_a, rel_a0, sums_a0 = back_of(qkv_a, p_a, 0, ctx_grad, (0, 1), d_a)
     d_a = advance(d_a, feed_lines + [line_b])
-    kept_a, sent_a = qkv_grad(core_at, xt, d_a, proj_own)
+    kept_a, sent_a = qkv_grad(spot, xt, d_a, proj_own)
     line_a = Line(kept_a, [], [], [("give", CORE)], sent_a)
     kept_a, d_a = lax.optimization_barrier((kept_a, d_a))
     d_a = advance(d_a, feed_lines + [line_a, shared_line])
-    up = norm_grad(d_a, d_b, qkv_weight, core_at, qkv_mine, qkv_theirs, gather, (0, 1), up)
+    up = norm_grad(d_a, d_b, qkv_weight, spot, qkv_mine, qkv_theirs, gather, (0, 1), up)
     up = advance(up, feed_lines + [line_a])
     taken = shared_line.terms[0][0]
     q_lines = []
@@ -1239,8 +1255,7 @@
     finish(feed_lines)
     flat = lambda line, rows: (line.value.reshape(rows, -1), line.taken_last.reshape(rows, -1))
     input_grad, one_sums, one_sum, two_sum = input_of(
-        image_tokens, middle_grad, up, taken, norm1_gain, flat(one_line, HALF), flat(two_line, FF // 2),
-        band_of, step_of, taken_of, has_taken, offset, core_at,
+        spot, image_tokens, middle_grad, up, taken, norm1_gain, flat(one_line, HALF), flat(two_line, FF // 2)
     )
     one_sums = advance(one_sums, q_lines)
     four, small, rel = last_sums(

time: 473 us -> 460 us (0.973)
  other arithmetic: 35.9 us -> 29.6 us
  waiting for transfers between devices: 27.5 us -> 22.7 us
    select_n x12 -> x6, other arithmetic: 8.34 us -> 2.83 us  [land(): self.value = jnp.where(mine, wide(self.sent), wide(self.taken))]
    ppermute x6, waiting for transfers between devices: 8.81 us -> 3.69 us  [on_device(): swap = lambda value: lax.ppermute(value, 'mp', [(0, 1), (1, 0)])]
  transfers between devices with their start and end apart: 33 -> 33, of which waited for: 9 -> 9; matrix products, arithmetic and copies ran while one was open for 3% -> 2% of each run, Pallas kernels for 53% -> 53%
where the time goes in v4:
time: 460 us; the launch traced here: 451 us
  Pallas kernels  351 us (76%)
  starting transfers between devices  29.6 us (6%)
  other arithmetic  29.6 us (6%)
  waiting for transfers between devices  22.7 us (5%)
  local copies, waits for them, and re-layouts  16.6 us (4%)
    pallas_call x1, Pallas kernels, feed(): pl.pallas_call(feed_kernel, grid_spec=pltpu.PrefetchScalarGridSpec(num_sc...  78.4 us
    pallas_call x2, Pallas kernels, attend(): pl.pallas_call(attend_own if first else attend_other, grid=(3, NWIN), in_...  67.1 us
    pallas_call x4, Pallas kernels, attend_back(): pl.pallas_call(lambda *refs: attend_back_kernel(first, *refs), grid_spec=...  63.3 us
    pallas_call x1, Pallas kernels, last_sums(): pl.pallas_call(lambda *refs: last_kernel(bits, plans, orders, *refs), in_...  32.7 us
    pallas_call x2, Pallas kernels, norm_grad(): pl.pallas_call(norm_grad_kernel, grid=(last - first, 2), in_specs=[block,...  27.4 us
    pallas_call x2, Pallas kernels, qkv_grad(): pl.pallas_call(qkv_grad_kernel, grid=(3,), in_specs=[SCALAR, pl.BlockSpec...  25 us
    convert_element_type x13, other arithmetic, part(): return total.astype(BF)  23 us
    ppermute x23, starting transfers between devices, exchange(): lax.ppermute(value, 'dp', [(i, i ^ bit) for i in range(lax.axis_size('dp'...  17.5 us
  transfers between devices with their start and end apart: 33, of which 9 were waited for; matrix products, arithmetic and copies ran while one was open for 2% of the time, Pallas kernels for 53%

profile of v4, /device:TPU:0, one launch (start us, length us, event | category | flops | bytes accessed | tf_op | source)
XLA Modules:
  0.0 451.0 jit_solution(16926783915387151672)
XLA Ops:
  1.9 3.0 collective-permute-start
  5.0 4.6 %shard_map.334.cot_t = bf16[768,2048]{1,0:T(8,128)(2,1)} custom-call(bf16[2048,768]{1,0:T(8,128)(2,1)} %cot.3), custom_call_target="tpu_custom_call" | custom-call | flops 1000000 | bytes 6000000 | tf_op jit(solution)/shard_map/pallas_call | solution.py:376
  10.2 8.6 %shard_map.333.x = bf16[3,5,256,768]{3,2,1,0:T(8,128)(2,1)} custom-call(s32[2]{0:T(128)} %pad_add_fusion.spot.refs_0_, bf16[4096,768]{1,0:T(8,128)(2,1)} %x.3, bf16[4096,768]{1,0:T(8,128)(2,1)} %x.3, bf16[4096,768]{1,0:T(8,128)(2,1)} %x.3, bf16[4096,768]{1,0:T(8,128)(2,1)} %x.3, bf16[4096,768]{1,0:T(8,128)(2,1)} %x.3, bf16[4096,768]{1,0:T(8,128)(2,1)} %x.3, ...), custom_call_target="tpu_custom_call" | custom-call | flops 660602880 | bytes 10000000 | tf_op jit(solution)/shard_map/pallas_call | solution.py:134
  21.0 3.7 collective-permute-done.mine
  28.4 33.9 %shard_map.335 = (bf16[3,5,256,1152]{3,2,1,0:T(8,128)(2,1)}, bf16[3,5,6,224,256]{4,3,2,1,0:T(8,128)(2,1)}, bf16[3,5,256,384]{3,2,1,0:T(8,128)(2,1)}, bf16[768,38...) custom-call(bf16[3,5,256,768]{3,2,1,0:T(8,128)(2,1)} %shard_map.333.x, bf16[2,384]{1,0:T(2,128)(2,1)} %bias.3, ...), custom_call_target="tpu_custom_call" | custom-call | flops 15000000512 | bytes 45000000 | tf_op jit(solution)/shard_map/pallas_call | solution.py:297
  63.2 33.2 %shard_map.336 = (bf16[3,5,256,1152]{3,2,1,0:T(8,128)(2,1)}, bf16[3,5,6,224,256]{4,3,2,1,0:T(8,128)(2,1)}, bf16[3,5,256,384]{3,2,1,0:T(8,128)(2,1)}) custom-call(bf16[3,5,256,768]{3,2,1,0:T(8,128)(2,1)} %shard_map.333.x, bf16[2,384]{1,0:T(2,128)(2,1)} %collective-permute-done.1.bias, s32[2]{0:T(128)} %pad_add_fusion.spot.refs_0_, ...), custom_call_target="tpu_custom_call" | custom-call | flops 15000000512 | bytes 45000000 | tf_op jit(solution)/shard_map/pallas_call | solution.py:297
  97.3 12.9 %shard_map.337 = (bf16[2048,768]{1,0:T(8,128)(2,1)}, bf16[2048,768]{1,0:T(8,128)(2,1)}, bf16[768,2048]{1,0:T(8,128)(2,1)}, bf16[2048,768]{1,0:T(8,128)(2,1)}) custom-call(s32[2]{0:T(128)} %pad_add_fusion.spot.refs_0_, bf16[3,5,256,384]{3,2,1,0:T(8,128)(2,1)} %get-tuple-element.148.own_a.own_b, bf16[3,5,256,384]{3,2,1,0:T(8,128)(2,1)} %get-tuple-element.148.own_a.own_b, ...), custom_call_target="tpu_custom_call" | custom-call | flops 3000000000 | bytes 25000000 | tf_op jit(solution)/shard_map/pallas_call | solution.py:343
  111.3 78.4 %shard_map.338 = (bf16[2048,768]{1,0:T(8,128)(2,1)}, bf16[2048,768]{1,0:T(8,128)(2,1)}, bf16[2,384,1536]{2,1,0:T(8,128)(2,1)}, bf16[2,384,1536]{2,1,0:T(8,128)(2...) custom-call(s32[2]{0:T(128)} %pad_add_fusion.spot.refs_0_, ...), custom_call_target="tpu_custom_call" | custom-call | flops 57999998976 | bytes 60000000 | tf_op jit(solution)/shard_map/pallas_call | solution.py:462
  191.7 16.0 %shard_map.339 = (bf16[2048,768]{1,0:T(8,128)(2,1)}, bf16[2048,768]{1,0:T(8,128)(2,1)}, bf16[2048,768]{1,0:T(8,128)(2,1)}, bf16[768,384]{1,0:T(8,128)(2,1)}, bf16[768,384]{1,0:T(8,128)(2,1)}, /*index=5*/f32[8,768]{1,0:T(8,128)}) custom-call(bf16[2048,768]{1,0:T(8,128)(2,1)} %get-tuple-element.166.middle, bf16[2048,768]{1,0:T(8,128)(2,1)} %get-tuple-element.167.forward, ...), custom_call_target="tpu_custom_call" | custom-call | flops 5000000000 | bytes 40000000 | tf_op jit(solution)/shard_map/pallas_call | solution.py:552
  209.9 2.6 fusion.1
  215.7 20.3 %shard_map.340 = (bf16[3,5,256,1152]{3,2,1,0:T(8,128)(2,1)}, f32[80,128]{1,0:T(8,128)}, f32[8,1152]{1,0:T(8,128)}) custom-call(s32[2]{0:T(128)} %pad_add_fusion.spot.refs_0_, bf16[3,5,256,1152]{3,2,1,0:T(8,128)(2,1)} %get-tuple-element.184.refs_1_, bf16[3,5,6,224,256]{4,3,2,1,0:T(8,128)(2,1)} %get-tuple-element.185.refs_2_, ...), custom_call_target="tpu_custom_call" | custom-call | flops 13333332992 | bytes 30000000 | tf_op jit(solution)/shard_map/pallas_call | solution.py:692
  236.0 4.7 %collective-permute-done.11 = bf16[2,2,2,48,1536]{4,3,2,1,0:T(8,128)(2,1)S(1)} collective-permute-done((bf16[2,2,2,48,1536]{4,3,2,1,0:T(8,128)(2,1)}, bf16[2,2,2,48,1536]{4,3,2,1,0:T(8,128)(2,1)S(1)}, u32[]{:S(2)}, u32[]{:S(2)}) %collective-permute-start.11) | collective-permute-done | bytes 1179680 | tf_op jit(solution)/shard_map/ppermute | solution.py:1041
  242.2 2.1 fusion.3
  244.3 2.5 fusion.2
  249.8 11.3 %shard_map.341 = (bf16[3,5,256,1152]{3,2,1,0:T(8,128)(2,1)}, f32[80,128]{1,0:T(8,128)}, f32[8,1152]{1,0:T(8,128)}) custom-call(s32[2]{0:T(128)} %pad_add_fusion.spot.refs_0_, bf16[3,5,256,1152]{3,2,1,0:T(8,128)(2,1)} %get-tuple-element.184.refs_1_, bf16[3,5,6,224,256]{4,3,2,1,0:T(8,128)(2,1)} %get-tuple-element.185.refs_2_, ...), custom_call_target="tpu_custom_call", output_to_operand_aliasing={{0}: (8, {})} | custom-call | flops 6666666496 | bytes 15000000 | tf_op jit(solution)/shard_map/pallas_call | solution.py:692
  268.4 12.5 %shard_map.342 = (bf16[2,768,384]{2,1,0:T(8,128)(2,1)}, bf16[2,768,384]{2,1,0:T(8,128)(2,1)}) custom-call(s32[2]{0:T(128)} %pad_add_fusion.spot.refs_0_, bf16[768,3840]{1,0:T(8,128)(2,1)} %get-tuple-element.172.xt, bf16[3840,1152]{1,0:T(8,128)(2,1)} %bitcast.112, bf16[768,384]{1,0:T(8,128)(2,1)} %get-tuple-element.200.proj), custom_call_target="tpu_custom_call" | custom-call | flops 7000000000 | bytes 16000000 | tf_op jit(solution)/shard_map/pallas_call | solution.py:781
  284.1 2.7 collective-permute-start.17
  287.0 20.5 %shard_map.343 = (bf16[3,5,256,1152]{3,2,1,0:T(8,128)(2,1)}, f32[80,128]{1,0:T(8,128)}, f32[8,1152]{1,0:T(8,128)}) custom-call(s32[2]{0:T(128)} %pad_add_fusion.spot.refs_0_, bf16[3,5,256,1152]{3,2,1,0:T(8,128)(2,1)} %get-tuple-element.173.refs_1_, bf16[3,5,6,224,256]{4,3,2,1,0:T(8,128)(2,1)} %get-tuple-element.174.refs_2_, ...), custom_call_target="tpu_custom_call" | custom-call | flops 13333332992 | bytes 30000000 | tf_op jit(solution)/shard_map/pallas_call | solution.py:692
  307.6 2.0 fusion.13
  309.6 2.0 fusion.11
  312.9 16.7 %shard_map.344.refs_0_ = bf16[3,1024,768]{2,1,0:T(8,128)(2,1)} custom-call(bf16[3,5,256,1152]{3,2,1,0:T(8,128)(2,1)} %get-tuple-element.219.own.refs_8_, bf16[3,5,256,1152]{3,2,1,0:T(8,128)(2,1)} %get-tuple-element.199.other, bf16[3,768,384]{2,1,0:T(8,128)(2,1)} %weights_own.3, s32[2]{0:T(128)} %pad_add_fusion.spot.refs_0_, bf16[3,384,384]{2,1,0:T(8,128)(2,1)} %copy-done.23, ...), custom_call_target="tpu_custom_call" | custom-call | flops 9333332992 | bytes 20000000 | tf_op jit(solution)/shard_map/pallas_call | solution.py:746
  329.7 2.2 dynamic-slice_bitcast_fusion
  331.9 2.6 collective-permute-start.20
  334.8 11.3 %shard_map.345 = (bf16[3,5,256,1152]{3,2,1,0:T(8,128)(2,1)}, f32[80,128]{1,0:T(8,128)}, f32[8,1152]{1,0:T(8,128)}) custom-call(s32[2]{0:T(128)} %pad_add_fusion.spot.refs_0_, bf16[3,5,256,1152]{3,2,1,0:T(8,128)(2,1)} %get-tuple-element.173.refs_1_, bf16[3,5,6,224,256]{4,3,2,1,0:T(8,128)(2,1)} %get-tuple-element.174.refs_2_, ...), custom_call_target="tpu_custom_call", output_to_operand_aliasing={{0}: (8, {})} | custom-call | flops 6666666496 | bytes 15000000 | tf_op jit(solution)/shard_map/pallas_call | solution.py:692
  351.2 12.5 %shard_map.346 = (bf16[2,768,384]{2,1,0:T(8,128)(2,1)}, bf16[2,768,384]{2,1,0:T(8,128)(2,1)}) custom-call(s32[2]{0:T(128)} %pad_add_fusion.spot.refs_0_, bf16[768,3840]{1,0:T(8,128)(2,1)} %get-tuple-element.172.xt, bf16[3840,1152]{1,0:T(8,128)(2,1)} %bitcast.111, bf16[768,384]{1,0:T(8,128)(2,1)} %get-tuple-element.228.proj), custom_call_target="tpu_custom_call" | custom-call | flops 7000000000 | bytes 16000000 | tf_op jit(solution)/shard_map/pallas_call | solution.py:781
  363.7 5.9 %collective-permute-done.25.taken_a.taken_b = bf16[640,768]{1,0:T(8,128)(2,1)S(1)} collective-permute-done((bf16[640,768]{1,0:T(8,128)(2,1)}, bf16[640,768]{1,0:T(8,128)(2,1)S(1)}, u32[]{:S(2)}, u32[]{:S(2)}) %collective-permute-start.25) | collective-permute-done | bytes 983072 | tf_op jit(solution)/shard_map/ppermute | solution.py:1041
  371.0 10.6 %shard_map.347.up_a.up_b = bf16[3,1024,768]{2,1,0:T(8,128)(2,1)} custom-call(bf16[3,5,256,1152]{3,2,1,0:T(8,128)(2,1)} %get-tuple-element.238.own, bf16[3,5,256,1152]{3,2,1,0:T(8,128)(2,1)} %get-tuple-element.199.other, bf16[3,768,384]{2,1,0:T(8,128)(2,1)} %weights_own.3, s32[2]{0:T(128)} %pad_add_fusion.spot.refs_0_, ...), custom_call_target="tpu_custom_call", output_to_operand_aliasing={{}: (7, {})} | custom-call | flops 4666666496 | bytes 10000000 | tf_op jit(solution)/shard_map/pallas_call | solution.py:746
  381.7 4.0 collective-permute-done.26
  390.4 2.1 fusion.9
  395.4 14.6 %shard_map.348 = (bf16[2048,768]{1,0:T(8,128)(2,1)}, f32[8,768]{1,0:T(8,128)}, f32[2,384,1536]{2,1,0:T(8,128)}, f32[1536,768]{1,0:T(8,128)}) custom-call(s32[2]{0:T(128)} %pad_add_fusion.spot.refs_0_, bf16[4096,768]{1,0:T(8,128)(2,1)} %x.3, bf16[2048,768]{1,0:T(8,128)(2,1)} %get-tuple-element.171.middle_grad, bf16[3,1024,768]{2,1,0:T(8,128)(2,1)} %shard_map.347.up_a.up_b, ...), custom_call_target="tpu_custom_call" | custom-call | flops 100000000 | bytes 35000000 | tf_op jit(solution)/shard_map/pallas_call | solution.py:835
  412.1 32.7 %shard_map.349 = (bf16[4,768,384]{2,1,0:T(8,128)(2,1)S(1)}, f32[24,768]{1,0:T(8,128)S(1)}, f32[56,128]{1,0:T(8,128)S(1)}) custom-call(bf16[384,384]{1,0:T(8,128)(2,1)S(1)} %get-tuple-element.281.refs_0_, bf16[384,384]{1,0:T(8,128)(2,1)S(1)} %get-tuple-element.280.refs_1_, f32[8,768]{1,0:T(8,128)S(1)} %copy-done.10, f32[8,768]{1,0:T(8,128)S(1)} %copy-done.9, ...), custom_call_target="tpu_custom_call" | custom-call | tf_op jit(solution)/shard_map/pallas_call | solution.py:1010
  444.9 2.0 slice_convert_fusion
  (151 shorter events, 54.5 us)
Async XLA Ops:
  1.9 22.7 %collective-permute-start = (bf16[3,384,384]{2,1,0:T(8,128)(2,1)S(1)}, bf16[3,384,384]{2,1,0:T(8,128)(2,1)S(1)}, u32[]{:S(2)}, u32[]{:S(2)}) collective-permute-start(bf16[3,384,384]{2,1,0:T(8,128)(2,1)S(1)} %constant_dynamic-slice_fusion.2), channel_id=1, source_target_pairs={{0,1},{1,0},{2,3},{3,2},{4,5},{5,4},{6,7},{7,6},{8,9},{9,8},{10,11... | collective-permute-start | bytes 2654216 | tf_op jit(solution)/shard_map/ppermute | solution.py:1157
  5.0 57.3 %collective-permute-start.1 = (bf16[2,384]{1,0:T(2,128)(2,1)}, bf16[2,384]{1,0:T(2,128)(2,1)}, u32[]{:S(2)}, u32[]{:S(2)}) collective-permute-start(bf16[2,384]{1,0:T(2,128)(2,1)} %bias.3), channel_id=1, source_target_pairs={{0,1},{1,0},{2,3},{3,2},{4,5},{5,4},{6,7},{7,6},{8,9},{9,8},{10,11... | collective-permute-start | bytes 4616 | tf_op jit(solution)/shard_map/ppermute | solution.py:1157
  24.6 37.7 %collective-permute-start.2 = (bf16[3,384,384]{2,1,0:T(8,128)(2,1)S(1)}, bf16[3,384,384]{2,1,0:T(8,128)(2,1)S(1)}, u32[]{:S(2)}, u32[]{:S(2)}) collective-permute-start(bf16[3,384,384]{2,1,0:T(8,128)(2,1)S(1)} %collective-permute-done.mine), channel_id=1, source_target_pairs={{0,2},{2,0},{4,6},{6,4},{8,10},{10,8},{12,14},{14,12},{16,18},{18,... | collective-permute-start | bytes 2654216 | tf_op jit(solution)/shard_map/ppermute | solution.py:1042
  24.6 71.8 %collective-permute-start.3 = (bf16[384,1536]{1,0:T(8,128)(2,1)S(1)}, bf16[384,1536]{1,0:T(8,128)(2,1)}, u32[]{:S(2)}, u32[]{:S(2)}) collective-permute-start(bf16[384,1536]{1,0:T(8,128)(2,1)S(1)} %constant_dynamic-slice_fusion.1), channel_id=1, source_target_pairs={{0,1},{1,0},{2,3},{3,2},{4,5},{5,4},{6,7},{7,6},{8,9},{9,8},{10,11... | collective-permute-start | bytes 3538952 | tf_op jit(solution)/shard_map/ppermute | solution.py:1157
  26.4 70.1 %collective-permute-start.4 = (bf16[1536,384]{1,0:T(8,128)(2,1)S(1)}, bf16[1536,384]{1,0:T(8,128)(2,1)}, u32[]{:S(2)}, u32[]{:S(2)}) collective-permute-start(bf16[1536,384]{1,0:T(8,128)(2,1)S(1)} %constant_dynamic-slice_fusion), channel_id=1, source_target_pairs={{0,1},{1,0},{2,3},{3,2},{4,5},{5,4},{6,7},{7,6},{8,9},{9,8},{10,11... | collective-permute-start | bytes 3538952 | tf_op jit(solution)/shard_map/ppermute | solution.py:1157
  26.7 69.8 %collective-permute-start.5 = (bf16[384,768]{1,0:T(8,128)(2,1)}, bf16[384,768]{1,0:T(8,128)(2,1)}, u32[]{:S(2)}, u32[]{:S(2)}) collective-permute-start(bf16[384,768]{1,0:T(8,128)(2,1)} %proj_own.3), channel_id=1, source_target_pairs={{0,1},{1,0},{2,3},{3,2},{4,5},{5,4},{6,7},{7,6},{8,9},{9,8},{10,11... | collective-permute-start | bytes 1769480 | tf_op jit(solution)/shard_map/ppermute | solution.py:1157
  96.5 13.8 %collective-permute-start.6 = (bf16[384,1536]{1,0:T(8,128)(2,1)}, bf16[384,1536]{1,0:T(8,128)(2,1)S(1)}, u32[]{:S(2)}, u32[]{:S(2)}) collective-permute-start(bf16[384,1536]{1,0:T(8,128)(2,1)} %collective-permute-done.3.one_b), channel_id=1, source_target_pairs={{0,2},{2,0},{4,6},{6,4},{8,10},{10,8},{12,14},{14,12},{16,18},{18,... | collective-permute-start | bytes 3538952 | tf_op jit(solution)/shard_map/ppermute | solution.py:1042
  96.6 13.8 %collective-permute-start.8 = (bf16[1536,384]{1,0:T(8,128)(2,1)}, bf16[1536,384]{1,0:T(8,128)(2,1)}, u32[]{:S(2)}, u32[]{:S(2)}) collective-permute-start(bf16[1536,384]{1,0:T(8,128)(2,1)} %collective-permute-done.4.two_b), channel_id=1, source_target_pairs={{0,2},{2,0},{4,6},{6,4},{8,10},{10,8},{12,14},{14,12},{16,18},{18,... | collective-permute-start | bytes 3538952 | tf_op jit(solution)/shard_map/ppermute | solution.py:1042
  97.1 13.2 %collective-permute-start.7 = (bf16[1536]{0:T(1024)(128)(2,1)S(1)}, bf16[1536]{0:T(1024)(128)(2,1)S(1)}, u32[]{:S(2)}, u32[]{:S(2)}) collective-permute-start(bf16[1536]{0:T(1024)(128)(2,1)S(1)} %copy-done.29), channel_id=1, source_target_pairs={{0,1},{1,0},{2,3},{3,2},{4,5},{5,4},{6,7},{7,6},{8,9},{9,8},{10,11... | collective-permute-start | bytes 9224 | tf_op jit(solution)/shard_map/ppermute | solution.py:1157
  189.8 18.0 %collective-permute-start.9 = (bf16[2,2,2,2,48,1536]{5,4,3,2,1,0:T(8,128)(2,1)}, bf16[2,2,2,2,48,1536]{5,4,3,2,1,0:T(8,128)(2,1)S(1)}, u32[]{:S(2)}, u32[]{:S(2)}) collective-permute-start(bf16[2,2,2,2,48,1536]{5,4,3,2,1,0:T(8,128)(2,1)} %bitcast.132), channel_id=1, source_target_pairs={{0,2},{2,0},{4,6},{6,4},{8,10},{10,8},{12,14},{14,12},{16,18},{18,... | collective-permute-start | bytes 7077896 | tf_op jit(solution)/shard_map/ppermute | solution.py:1042
  189.8 17.9 %collective-permute-start.10 = (bf16[2,2,2,2,192,384]{5,4,3,2,1,0:T(8,128)(2,1)}, bf16[2,2,2,2,192,384]{5,4,3,2,1,0:T(8,128)(2,1)}, u32[]{:S(2)}, u32[]{:S(2)}) collective-permute-start(bf16[2,2,2,2,192,384]{5,4,3,2,1,0:T(8,128)(2,1)} %bitcast.131), channel_id=1, source_target_pairs={{0,2},{2,0},{4,6},{6,4},{8,10},{10,8},{12,14},{14,12},{16,18},{18,... | collective-permute-start | bytes 7077896 | tf_op jit(solution)/shard_map/ppermute | solution.py:1042
  212.5 28.2 %collective-permute-start.11 = (bf16[2,2,2,48,1536]{4,3,2,1,0:T(8,128)(2,1)}, bf16[2,2,2,48,1536]{4,3,2,1,0:T(8,128)(2,1)S(1)}, u32[]{:S(2)}, u32[]{:S(2)}) collective-permute-start(bf16[2,2,2,48,1536]{4,3,2,1,0:T(8,128)(2,1)} %fusion), channel_id=1, source_target_pairs={{0,1},{1,0},{2,3},{3,2},{4,5},{5,4},{6,7},{7,6},{8,9},{9,8},{10,11... | collective-permute-start | bytes 3538952 | tf_op jit(solution)/shard_map/ppermute | solution.py:1041
  214.2 28.0 %collective-permute-start.12 = (bf16[2,2,2,192,384]{4,3,2,1,0:T(8,128)(2,1)}, bf16[2,2,2,192,384]{4,3,2,1,0:T(8,128)(2,1)}, u32[]{:S(2)}, u32[]{:S(2)}) collective-permute-start(bf16[2,2,2,192,384]{4,3,2,1,0:T(8,128)(2,1)} %fusion.1), channel_id=1, source_target_pairs={{0,4},{2,6},{4,0},{6,2},{8,12},{10,14},{12,8},{14,10},{16,20},{18,... | collective-permute-start | bytes 3538952 | tf_op jit(solution)/shard_map/ppermute | solution.py:1042
  246.8 14.5 %collective-permute-start.13 = (bf16[2,2,48,1536]{3,2,1,0:T(8,128)(2,1)}, bf16[2,2,48,1536]{3,2,1,0:T(8,128)(2,1)}, u32[]{:S(2)}, u32[]{:S(2)}) collective-permute-start(bf16[2,2,48,1536]{3,2,1,0:T(8,128)(2,1)} %fusion.3), channel_id=1, source_target_pairs={{0,4},{2,6},{4,0},{6,2},{8,12},{10,14},{12,8},{14,10},{16,20},{18,... | collective-permute-start | bytes 1769480 | tf_op jit(solution)/shard_map/ppermute | solution.py:1042
  248.2 14.2 %collective-permute-start.14 = (bf16[2,2,192,384]{3,2,1,0:T(8,128)(2,1)}, bf16[2,2,192,384]{3,2,1,0:T(8,128)(2,1)}, u32[]{:S(2)}, u32[]{:S(2)}) collective-permute-start(bf16[2,2,192,384]{3,2,1,0:T(8,128)(2,1)} %fusion.2), channel_id=1, source_target_pairs={{0,8},{2,10},{4,12},{6,14},{8,0},{10,2},{12,4},{14,6},{16,24},{18,... | collective-permute-start | bytes 1769480 | tf_op jit(solution)/shard_map/ppermute | solution.py:1042
  265.7 15.2 %collective-permute-start.15 = (bf16[2,48,1536]{2,1,0:T(8,128)(2,1)}, bf16[2,48,1536]{2,1,0:T(8,128)(2,1)}, u32[]{:S(2)}, u32[]{:S(2)}) collective-permute-start(bf16[2,48,1536]{2,1,0:T(8,128)(2,1)} %fusion.5), channel_id=1, source_target_pairs={{0,8},{2,10},{4,12},{6,14},{8,0},{10,2},{12,4},{14,6},{16,24},{18,... | collective-permute-start | bytes 884744 | tf_op jit(solution)/shard_map/ppermute | solution.py:1042
  267.4 13.6 %collective-permute-start.16 = (bf16[2,192,384]{2,1,0:T(8,128)(2,1)S(1)}, bf16[2,192,384]{2,1,0:T(8,128)(2,1)}, u32[]{:S(2)}, u32[]{:S(2)}) collective-permute-start(bf16[2,192,384]{2,1,0:T(8,128)(2,1)S(1)} %fusion.4), channel_id=1, source_target_pairs={{0,1},{1,0},{2,3},{3,2},{4,5},{5,4},{6,7},{7,6},{8,9},{9,8},{10,11... | collective-permute-start | bytes 884744 | tf_op jit(solution)/shard_map/ppermute | solution.py:1041
  284.1 23.5 %collective-permute-start.17 = (bf16[48,1536]{1,0:T(8,128)(2,1)}, bf16[48,1536]{1,0:T(8,128)(2,1)S(1)}, u32[]{:S(2)}, u32[]{:S(2)}) collective-permute-start(bf16[48,1536]{1,0:T(8,128)(2,1)} %fusion.15), channel_id=1, source_target_pairs={{0,16},{2,18},{4,20},{6,22},{8,24},{10,26},{12,28},{14,30},{16,0},... | collective-permute-start | bytes 442376 | tf_op jit(solution)/shard_map/ppermute | solution.py:1042
  286.7 20.9 %collective-permute-start.18 = (bf16[192,384]{1,0:T(8,128)(2,1)S(1)}, bf16[192,384]{1,0:T(8,128)(2,1)S(1)}, u32[]{:S(2)}, u32[]{:S(2)}) collective-permute-start(bf16[192,384]{1,0:T(8,128)(2,1)S(1)} %fusion.14), channel_id=1, source_target_pairs={{0,16},{2,18},{4,20},{6,22},{8,24},{10,26},{12,28},{14,30},{16,0},... | collective-permute-start | bytes 442376 | tf_op jit(solution)/shard_map/ppermute | solution.py:1042
  287.0 20.5 %collective-permute-start.19 = (bf16[2,768,384]{2,1,0:T(8,128)(2,1)}, bf16[2,768,384]{2,1,0:T(8,128)(2,1)S(1)}, u32[]{:S(2)}, u32[]{:S(2)}) collective-permute-start(bf16[2,768,384]{2,1,0:T(8,128)(2,1)} %get-tuple-element.213), channel_id=1, source_target_pairs={{0,2},{2,0},{4,6},{6,4},{8,10},{10,8},{12,14},{14,12},{16,18},{18,... | collective-permute-start | bytes 3538952 | tf_op jit(solution)/shard_map/ppermute | solution.py:1042
  311.9 36.4 %collective-permute-start.22 = (bf16[2,768,384]{2,1,0:T(8,128)(2,1)S(1)}, bf16[2,768,384]{2,1,0:T(8,128)(2,1)S(1)}, u32[]{:S(2)}, u32[]{:S(2)}) collective-permute-start(bf16[2,768,384]{2,1,0:T(8,128)(2,1)S(1)} %add_convert_fusion), channel_id=1, source_target_pairs={{0,1},{1,0},{2,3},{3,2},{4,5},{5,4},{6,7},{7,6},{8,9},{9,8},{10,11... | collective-permute-start | bytes 3538952 | tf_op jit(solution)/shard_map/ppermute | solution.py:1041
  331.9 15.2 %collective-permute-start.20 = (bf16[48,1536]{1,0:T(8,128)(2,1)}, bf16[48,1536]{1,0:T(8,128)(2,1)S(1)}, u32[]{:S(2)}, u32[]{:S(2)}) collective-permute-start(bf16[48,1536]{1,0:T(8,128)(2,1)} %fusion.13), channel_id=1, source_target_pairs={{0,16},{2,18},{4,20},{6,22},{8,24},{10,26},{12,28},{14,30},{16,0},... | collective-permute-start | bytes 442376 | tf_op jit(solution)/shard_map/ppermute | solution.py:1042
  334.5 13.8 %collective-permute-start.21 = (bf16[192,384]{1,0:T(8,128)(2,1)}, bf16[192,384]{1,0:T(8,128)(2,1)S(1)}, u32[]{:S(2)}, u32[]{:S(2)}) collective-permute-start(bf16[192,384]{1,0:T(8,128)(2,1)} %fusion.11), channel_id=1, source_target_pairs={{0,16},{2,18},{4,20},{6,22},{8,24},{10,26},{12,28},{14,30},{16,0},... | collective-permute-start | bytes 442376 | tf_op jit(solution)/shard_map/ppermute | solution.py:1042
  346.1 23.5 %collective-permute-start.25 = (bf16[640,768]{1,0:T(8,128)(2,1)}, bf16[640,768]{1,0:T(8,128)(2,1)S(1)}, u32[]{:S(2)}, u32[]{:S(2)}) collective-permute-start(bf16[640,768]{1,0:T(8,128)(2,1)} %dynamic-slice_bitcast_fusion), channel_id=1, source_target_pairs={{0,1},{1,0},{2,3},{3,2},{4,5},{5,4},{6,7},{7,6},{8,9},{9,8},{10,11... | collective-permute-start | bytes 2949128 | tf_op jit(solution)/shard_map/ppermute | solution.py:1041
  350.5 19.1 %collective-permute-start.23 = (bf16[2,48,1536]{2,1,0:T(8,128)(2,1)S(1)}, bf16[2,48,1536]{2,1,0:T(8,128)(2,1)S(1)}, u32[]{:S(2)}, u32[]{:S(2)}) collective-permute-start(bf16[2,48,1536]{2,1,0:T(8,128)(2,1)S(1)} %broadcast_select_fusion.5), channel_id=1, source_target_pairs={{0,8},{2,10},{4,12},{6,14},{8,0},{10,2},{12,4},{14,6},{16,24},{18,... | collective-permute-start | bytes 884744 | tf_op jit(solution)/shard_map/ppermute | solution.py:1042
  350.6 19.0 %collective-permute-start.24 = (bf16[2,192,384]{2,1,0:T(8,128)(2,1)S(1)}, bf16[2,192,384]{2,1,0:T(8,128)(2,1)S(1)}, u32[]{:S(2)}, u32[]{:S(2)}) collective-permute-start(bf16[2,192,384]{2,1,0:T(8,128)(2,1)S(1)} %broadcast_select_fusion.4), channel_id=1, source_target_pairs={{0,4},{2,6},{4,0},{6,2},{8,12},{10,14},{12,8},{14,10},{16,20},{18,... | collective-permute-start | bytes 884744 | tf_op jit(solution)/shard_map/ppermute | solution.py:1042
  369.9 16.9 %collective-permute-start.28 = (bf16[2,768,384]{2,1,0:T(8,128)(2,1)}, bf16[2,768,384]{2,1,0:T(8,128)(2,1)}, u32[]{:S(2)}, u32[]{:S(2)}) collective-permute-start(bf16[2,768,384]{2,1,0:T(8,128)(2,1)} %get-tuple-element.241), channel_id=1, source_target_pairs={{0,2},{2,0},{4,6},{6,4},{8,10},{10,8},{12,14},{14,12},{16,18},{18,... | collective-permute-start | bytes 3538952 | tf_op jit(solution)/shard_map/ppermute | solution.py:1042
  370.0 15.7 %collective-permute-start.26 = (bf16[2,2,48,1536]{3,2,1,0:T(8,128)(2,1)S(1)}, bf16[2,2,48,1536]{3,2,1,0:T(8,128)(2,1)S(1)}, u32[]{:S(2)}, u32[]{:S(2)}) collective-permute-start(bf16[2,2,48,1536]{3,2,1,0:T(8,128)(2,1)S(1)} %broadcast_select_fusion.3), channel_id=1, source_target_pairs={{0,4},{2,6},{4,0},{6,2},{8,12},{10,14},{12,8},{14,10},{16,20},{18,... | collective-permute-start | bytes 1769480 | tf_op jit(solution)/shard_map/ppermute | solution.py:1042
  370.6 15.4 %collective-permute-start.27 = (bf16[2,2,192,384]{3,2,1,0:T(8,128)(2,1)S(1)}, bf16[2,2,192,384]{3,2,1,0:T(8,128)(2,1)S(1)}, u32[]{:S(2)}, u32[]{:S(2)}) collective-permute-start(bf16[2,2,192,384]{3,2,1,0:T(8,128)(2,1)S(1)} %broadcast_select_fusion.2), channel_id=1, source_target_pairs={{0,8},{2,10},{4,12},{6,14},{8,0},{10,2},{12,4},{14,6},{16,24},{18,... | collective-permute-start | bytes 1769480 | tf_op jit(solution)/shard_map/ppermute | solution.py:1042
  388.1 6.3 %collective-permute-start.29 = (bf16[2,2,2,48,1536]{4,3,2,1,0:T(8,128)(2,1)S(1)}, bf16[2,2,2,48,1536]{4,3,2,1,0:T(8,128)(2,1)S(1)}, u32[]{:S(2)}, u32[]{:S(2)}) collective-permute-start(bf16[2,2,2,48,1536]{4,3,2,1,0:T(8,128)(2,1)S(1)} %broadcast_select_fusion.1), channel_id=1, source_target_pairs={{0,2},{2,0},{4,6},{6,4},{8,10},{10,8},{12,14},{14,12},{16,18},{18,... | collective-permute-start | bytes 3538952 | tf_op jit(solution)/shard_map/ppermute | solution.py:1042
  392.5 17.7 %collective-permute-start.31 = (bf16[384,384]{1,0:T(8,128)(2,1)}, bf16[384,384]{1,0:T(8,128)(2,1)}, u32[]{:S(2)}, u32[]{:S(2)}) collective-permute-start(bf16[384,384]{1,0:T(8,128)(2,1)} %get-tuple-element.254), channel_id=1, source_target_pairs={{0,4},{2,6},{4,0},{6,2},{8,12},{10,14},{12,8},{14,10},{16,20},{18,... | collective-permute-start | bytes 884744 | tf_op jit(solution)/shard_map/ppermute | solution.py:1042
  394.0 16.3 %collective-permute-start.32 = (bf16[384,384]{1,0:T(8,128)(2,1)}, bf16[384,384]{1,0:T(8,128)(2,1)}, u32[]{:S(2)}, u32[]{:S(2)}) collective-permute-start(bf16[384,384]{1,0:T(8,128)(2,1)} %get-tuple-element.255), channel_id=1, source_target_pairs={{0,8},{2,10},{4,12},{6,14},{8,0},{10,2},{12,4},{14,6},{16,24},{18,... | collective-permute-start | bytes 884744 | tf_op jit(solution)/shard_map/ppermute | solution.py:1042
  (32 other events, 212.4 us)

commit v5 on v4

--- a/solution.py
+++ b/solution.py
@@ -1224,31 +1224,43 @@
     d_b, rel_b0, sums_b0 = back_of(qkv_b, p_b, 1, ctx_grad, (0, 1), d_b)
     d_b = advance(d_b, feed_lines)
     kept_b, sent_b = qkv_grad(spot, xt, d_b, proj_oth)
-    line_b = Line(kept_b, [], [], [("give", CORE), ("pass", PAIRED)], sent_b)
+    line_b = Line(kept_b, [], [], [("give", CORE)], sent_b)
     lines = feed_lines + [line_b]
     ctx_grad, kept_b = lax.optimization_barrier((ctx_grad, kept_b))
     ctx_grad = advance(ctx_grad, lines)
-    d_a, rel_a, sums_a = back_of(qkv_a, p_a, 0, ctx_grad, (1, 3))
+    d_a, rel_a0, sums_a0 = back_of(qkv_a, p_a, 0, ctx_grad, (0, 1))
     d_a = advance(d_a, lines)
+    passes = []
+    for k in range(2):
+        line = Line(None, [], [], [("pass", PAIRED)])
+        line.terms = [(term[k], ()) for term, _ in line_b.terms]
+        passes.append(line)
+    d_a = advance(d_a, passes[:1])
+    d_a, rel_a, sums_a = back_of(qkv_a, p_a, 0, ctx_grad, (1, 3), d_a)
+    d_a = advance(d_a, feed_lines + passes[:1])
+    d_a = advance(d_a, passes[1:])
     up = norm_grad(d_a, d_b, qkv_weight, spot, qkv_mine, qkv_theirs, gather, (1, 3))
     at = [2 - place, (1 - place) * 4 * SIDE, jnp.zeros_like(place)]
-    sent = lax.dynamic_slice(up, at, (1, 10 * SIDE, D)).reshape(10 * SIDE, D)
-    shared_line = Line(sent, [], [], [("pass", PAIRED)])
-    d_a = advance(d_a, [shared_line])
-    d_a, rel_a0, sums_a0 = back_of(qkv_a, p_a, 0, ctx_grad, (0, 1), d_a)
-    d_a = advance(d_a, feed_lines + [line_b])
+    shares = []
+    for first, count in ((0, 6), (6, 4)):
+        start = [at[0], at[1] + first * SIDE, at[2]]
+        part = lax.dynamic_slice(up, start, (1, count * SIDE, D)).reshape(count * SIDE, D)
+        shares.append(Line(part, [], [], [("pass", PAIRED)]))
+    d_a = advance(d_a, feed_lines + passes[1:])
+    d_a = advance(d_a, shares[:1])
     kept_a, sent_a = qkv_grad(spot, xt, d_a, proj_own)
     line_a = Line(kept_a, [], [], [("give", CORE)], sent_a)
     kept_a, d_a = lax.optimization_barrier((kept_a, d_a))
-    d_a = advance(d_a, feed_lines + [line_a, shared_line])
+    d_a = advance(d_a, feed_lines + [line_a] + shares[:1])
+    d_a = advance(d_a, shares[1:])
     up = norm_grad(d_a, d_b, qkv_weight, spot, qkv_mine, qkv_theirs, gather, (0, 1), up)
-    up = advance(up, feed_lines + [line_a])
-    taken = shared_line.terms[0][0]
+    up = advance(up, feed_lines + [line_a] + shares[1:])
+    taken = jnp.concatenate([line.terms[0][0] for line in shares], axis=0)
     q_lines = []
     for k, order in enumerate((bits, turned)):
         line = Line(None, [], [], halves(order[:1]))
-        parts = [term for term, _ in line_a.terms] + [term for term, _ in line_b.terms]
-        line.terms = [(part.reshape(2, 2, D // 2, HALF), ("line", order[0])) for part in parts]
+        line.terms = [(part.reshape(2, 2, D // 2, HALF), ("line", order[0])) for part, _ in line_a.terms]
+        line.terms += [(part.reshape(2, D // 2, HALF), (order[0],)) for part, _ in passes[k].terms]
         line.fixed = {"line": k}
         q_lines.append(line)
     up = advance(up, q_lines)

time: 460 us -> 449 us (0.976)
  waiting for transfers between devices: 22.7 us -> 13.3 us
    ppermute x4 -> x6, waiting for transfers between devices: 10.6 us -> 4.67 us  [exchange(): return lax.ppermute(value, 'mp', [(0, 1), (1, 0)])]
  transfers between devices with their start and end apart: 33 -> 35, of which waited for: 9 -> 5; matrix products, arithmetic and copies ran while one was open for 2% -> 2% of each run, Pallas kernels for 53% -> 54%
where the time goes in v5:
time: 449 us; the launch traced here: 441 us
  Pallas kernels  352 us (78%)
  starting transfers between devices  33.1 us (7%)
  other arithmetic  28 us (6%)
  waiting for transfers between devices  13.3 us (3%)
  local copies, waits for them, and re-layouts  13 us (3%)
    pallas_call x1, Pallas kernels, feed(): pl.pallas_call(feed_kernel, grid_spec=pltpu.PrefetchScalarGridSpec(num_sc...  78.4 us
    pallas_call x2, Pallas kernels, attend(): pl.pallas_call(attend_own if first else attend_other, grid=(3, NWIN), in_...  67.1 us
    pallas_call x4, Pallas kernels, attend_back(): pl.pallas_call(lambda *refs: attend_back_kernel(first, *refs), grid_spec=...  63.3 us
    pallas_call x1, Pallas kernels, last_sums(): pl.pallas_call(lambda *refs: last_kernel(bits, plans, orders, *refs), in_...  33.6 us
    pallas_call x2, Pallas kernels, norm_grad(): pl.pallas_call(norm_grad_kernel, grid=(last - first, 2), in_specs=[block,...  27.4 us
    pallas_call x2, Pallas kernels, qkv_grad(): pl.pallas_call(qkv_grad_kernel, grid=(3,), in_specs=[SCALAR, pl.BlockSpec...  25 us
    convert_element_type x13, other arithmetic, part(): return total.astype(BF)  21.2 us
    ppermute x23, starting transfers between devices, exchange(): lax.ppermute(value, 'dp', [(i, i ^ bit) for i in range(lax.axis_size('dp'...  19 us
  transfers between devices with their start and end apart: 35, of which 5 were waited for; matrix products, arithmetic and copies ran while one was open for 2% of the time, Pallas kernels for 54%

profile of v5, /device:TPU:0, one launch (start us, length us, event | category | flops | bytes accessed | tf_op | source)
XLA Modules:
  0.0 440.9 jit_solution(9922408055090544605)
XLA Ops:
  1.9 3.0 collective-permute-start
  5.0 4.6 %shard_map.334.cot_t = bf16[768,2048]{1,0:T(8,128)(2,1)} custom-call(bf16[2048,768]{1,0:T(8,128)(2,1)} %cot.3), custom_call_target="tpu_custom_call" | custom-call | flops 1000000 | bytes 6000000 | tf_op jit(solution)/shard_map/pallas_call | solution.py:376
  10.2 8.6 %shard_map.333.x = bf16[3,5,256,768]{3,2,1,0:T(8,128)(2,1)} custom-call(s32[2]{0:T(128)} %pad_add_fusion.spot.refs_0_, bf16[4096,768]{1,0:T(8,128)(2,1)} %x.3, bf16[4096,768]{1,0:T(8,128)(2,1)} %x.3, bf16[4096,768]{1,0:T(8,128)(2,1)} %x.3, bf16[4096,768]{1,0:T(8,128)(2,1)} %x.3, bf16[4096,768]{1,0:T(8,128)(2,1)} %x.3, bf16[4096,768]{1,0:T(8,128)(2,1)} %x.3, ...), custom_call_target="tpu_custom_call" | custom-call | flops 660602880 | bytes 10000000 | tf_op jit(solution)/shard_map/pallas_call | solution.py:134
  21.0 3.7 collective-permute-done.mine
  24.6 1.7 collective-permute-start.3
  26.7 1.7 collective-permute-start.5
  28.4 33.9 %shard_map.335 = (bf16[3,5,256,1152]{3,2,1,0:T(8,128)(2,1)}, bf16[3,5,6,224,256]{4,3,2,1,0:T(8,128)(2,1)}, bf16[3,5,256,384]{3,2,1,0:T(8,128)(2,1)}, bf16[768,38...) custom-call(bf16[3,5,256,768]{3,2,1,0:T(8,128)(2,1)} %shard_map.333.x, bf16[2,384]{1,0:T(2,128)(2,1)} %bias.3, ...), custom_call_target="tpu_custom_call" | custom-call | flops 15000000512 | bytes 45000000 | tf_op jit(solution)/shard_map/pallas_call | solution.py:297
  63.3 33.2 %shard_map.336 = (bf16[3,5,256,1152]{3,2,1,0:T(8,128)(2,1)}, bf16[3,5,6,224,256]{4,3,2,1,0:T(8,128)(2,1)}, bf16[3,5,256,384]{3,2,1,0:T(8,128)(2,1)}) custom-call(bf16[3,5,256,768]{3,2,1,0:T(8,128)(2,1)} %shard_map.333.x, bf16[2,384]{1,0:T(2,128)(2,1)} %collective-permute-done.1.bias, s32[2]{0:T(128)} %pad_add_fusion.spot.refs_0_, ...), custom_call_target="tpu_custom_call" | custom-call | flops 15000000512 | bytes 45000000 | tf_op jit(solution)/shard_map/pallas_call | solution.py:297
  97.4 12.9 %shard_map.337 = (bf16[2048,768]{1,0:T(8,128)(2,1)}, bf16[2048,768]{1,0:T(8,128)(2,1)}, bf16[768,2048]{1,0:T(8,128)(2,1)}, bf16[2048,768]{1,0:T(8,128)(2,1)}) custom-call(s32[2]{0:T(128)} %pad_add_fusion.spot.refs_0_, bf16[3,5,256,384]{3,2,1,0:T(8,128)(2,1)} %get-tuple-element.158.own_a.own_b, bf16[3,5,256,384]{3,2,1,0:T(8,128)(2,1)} %get-tuple-element.158.own_a.own_b, ...), custom_call_target="tpu_custom_call" | custom-call | flops 3000000000 | bytes 25000000 | tf_op jit(solution)/shard_map/pallas_call | solution.py:343
  111.4 78.4 %shard_map.338 = (bf16[2048,768]{1,0:T(8,128)(2,1)}, bf16[2048,768]{1,0:T(8,128)(2,1)}, bf16[2,384,1536]{2,1,0:T(8,128)(2,1)}, bf16[2,384,1536]{2,1,0:T(8,128)(2...) custom-call(s32[2]{0:T(128)} %pad_add_fusion.spot.refs_0_, ...), custom_call_target="tpu_custom_call" | custom-call | flops 57999998976 | bytes 60000000 | tf_op jit(solution)/shard_map/pallas_call | solution.py:462
  191.7 16.0 %shard_map.339 = (bf16[2048,768]{1,0:T(8,128)(2,1)}, bf16[2048,768]{1,0:T(8,128)(2,1)}, bf16[2048,768]{1,0:T(8,128)(2,1)}, bf16[768,384]{1,0:T(8,128)(2,1)}, bf16[768,384]{1,0:T(8,128)(2,1)}, /*index=5*/f32[8,768]{1,0:T(8,128)}) custom-call(bf16[2048,768]{1,0:T(8,128)(2,1)} %get-tuple-element.176.middle, bf16[2048,768]{1,0:T(8,128)(2,1)} %get-tuple-element.177.forward, ...), custom_call_target="tpu_custom_call" | custom-call | flops 5000000000 | bytes 40000000 | tf_op jit(solution)/shard_map/pallas_call | solution.py:552
  209.9 2.6 fusion.1
  212.5 1.7 collective-permute-start.11
  215.7 20.3 %shard_map.340 = (bf16[3,5,256,1152]{3,2,1,0:T(8,128)(2,1)}, f32[80,128]{1,0:T(8,128)}, f32[8,1152]{1,0:T(8,128)}) custom-call(s32[2]{0:T(128)} %pad_add_fusion.spot.refs_0_, bf16[3,5,256,1152]{3,2,1,0:T(8,128)(2,1)} %get-tuple-element.194.refs_1_, bf16[3,5,6,224,256]{4,3,2,1,0:T(8,128)(2,1)} %get-tuple-element.195.refs_2_, ...), custom_call_target="tpu_custom_call" | custom-call | flops 13333332992 | bytes 30000000 | tf_op jit(solution)/shard_map/pallas_call | solution.py:692
  236.0 4.7 %collective-permute-done.11 = bf16[2,2,2,48,1536]{4,3,2,1,0:T(8,128)(2,1)S(1)} collective-permute-done((bf16[2,2,2,48,1536]{4,3,2,1,0:T(8,128)(2,1)}, bf16[2,2,2,48,1536]{4,3,2,1,0:T(8,128)(2,1)S(1)}, u32[]{:S(2)}, u32[]{:S(2)}) %collective-permute-start.11) | collective-permute-done | bytes 1179680 | tf_op jit(solution)/shard_map/ppermute | solution.py:1041
  243.5 2.5 fusion.2
  249.0 11.3 %shard_map.341 = (bf16[3,5,256,1152]{3,2,1,0:T(8,128)(2,1)}, f32[80,128]{1,0:T(8,128)}, f32[8,1152]{1,0:T(8,128)}) custom-call(s32[2]{0:T(128)} %pad_add_fusion.spot.refs_0_, bf16[3,5,256,1152]{3,2,1,0:T(8,128)(2,1)} %get-tuple-element.194.refs_1_, bf16[3,5,6,224,256]{4,3,2,1,0:T(8,128)(2,1)} %get-tuple-element.195.refs_2_, ...), custom_call_target="tpu_custom_call", output_to_operand_aliasing={{0}: (8, {})} | custom-call | flops 6666666496 | bytes 15000000 | tf_op jit(solution)/shard_map/pallas_call | solution.py:692
  266.9 12.5 %shard_map.342 = (bf16[2,768,384]{2,1,0:T(8,128)(2,1)}, bf16[2,768,384]{2,1,0:T(8,128)(2,1)}) custom-call(s32[2]{0:T(128)} %pad_add_fusion.spot.refs_0_, bf16[768,3840]{1,0:T(8,128)(2,1)} %get-tuple-element.182.xt, bf16[3840,1152]{1,0:T(8,128)(2,1)} %bitcast.126, bf16[768,384]{1,0:T(8,128)(2,1)} %get-tuple-element.210.proj), custom_call_target="tpu_custom_call" | custom-call | flops 7000000000 | bytes 16000000 | tf_op jit(solution)/shard_map/pallas_call | solution.py:781
  282.1 2.7 collective-permute-start.17
  285.0 11.5 %shard_map.343 = (bf16[3,5,256,1152]{3,2,1,0:T(8,128)(2,1)}, f32[80,128]{1,0:T(8,128)}, f32[8,1152]{1,0:T(8,128)}) custom-call(s32[2]{0:T(128)} %pad_add_fusion.spot.refs_0_, bf16[3,5,256,1152]{3,2,1,0:T(8,128)(2,1)} %get-tuple-element.183.refs_1_, bf16[3,5,6,224,256]{4,3,2,1,0:T(8,128)(2,1)} %get-tuple-element.184.refs_2_, ...), custom_call_target="tpu_custom_call" | custom-call | flops 6666666496 | bytes 15000000 | tf_op jit(solution)/shard_map/pallas_call | solution.py:692
  296.6 2.0 collective-permute-done.18
  303.5 2.2 collective-permute-start.21
  306.7 20.3 %shard_map.344 = (bf16[3,5,256,1152]{3,2,1,0:T(8,128)(2,1)}, f32[80,128]{1,0:T(8,128)}, f32[8,1152]{1,0:T(8,128)}) custom-call(s32[2]{0:T(128)} %pad_add_fusion.spot.refs_0_, bf16[3,5,256,1152]{3,2,1,0:T(8,128)(2,1)} %get-tuple-element.183.refs_1_, bf16[3,5,6,224,256]{4,3,2,1,0:T(8,128)(2,1)} %get-tuple-element.184.refs_2_, ...), custom_call_target="tpu_custom_call", output_to_operand_aliasing={{0}: (8, {})} | custom-call | flops 13333332992 | bytes 30000000 | tf_op jit(solution)/shard_map/pallas_call | solution.py:692
  329.2 16.7 %shard_map.345.refs_0_ = bf16[3,1024,768]{2,1,0:T(8,128)(2,1)} custom-call(bf16[3,5,256,1152]{3,2,1,0:T(8,128)(2,1)} %get-tuple-element.258.own, bf16[3,5,256,1152]{3,2,1,0:T(8,128)(2,1)} %get-tuple-element.209.other, bf16[3,768,384]{2,1,0:T(8,128)(2,1)} %weights_own.3, s32[2]{0:T(128)} %pad_add_fusion.spot.refs_0_, bf16[3,384,384]{2,1,0:T(8,128)(2,1)} %copy-done.19, ...), custom_call_target="tpu_custom_call" | custom-call | flops 9333332992 | bytes 20000000 | tf_op jit(solution)/shard_map/pallas_call | solution.py:746
  349.8 1.7 collective-permute-start.27
  352.5 12.5 %shard_map.346 = (bf16[2,768,384]{2,1,0:T(8,128)(2,1)}, bf16[2,768,384]{2,1,0:T(8,128)(2,1)}) custom-call(s32[2]{0:T(128)} %pad_add_fusion.spot.refs_0_, bf16[768,3840]{1,0:T(8,128)(2,1)} %get-tuple-element.182.xt, bf16[3840,1152]{1,0:T(8,128)(2,1)} %bitcast.127, bf16[768,384]{1,0:T(8,128)(2,1)} %get-tuple-element.247.proj), custom_call_target="tpu_custom_call" | custom-call | flops 7000000000 | bytes 16000000 | tf_op jit(solution)/shard_map/pallas_call | solution.py:781
  368.2 10.6 %shard_map.347.up_a.up_b = bf16[3,1024,768]{2,1,0:T(8,128)(2,1)} custom-call(bf16[3,5,256,1152]{3,2,1,0:T(8,128)(2,1)} %get-tuple-element.258.own, bf16[3,5,256,1152]{3,2,1,0:T(8,128)(2,1)} %get-tuple-element.209.other, bf16[3,768,384]{2,1,0:T(8,128)(2,1)} %weights_own.3, s32[2]{0:T(128)} %pad_add_fusion.spot.refs_0_, ...), custom_call_target="tpu_custom_call", output_to_operand_aliasing={{}: (7, {})} | custom-call | flops 4666666496 | bytes 10000000 | tf_op jit(solution)/shard_map/pallas_call | solution.py:746
  378.9 2.9 fusion.10
  382.6 2.2 pad_maximum_fusion.taken_a.taken_b
  384.8 14.6 %shard_map.348 = (bf16[2048,768]{1,0:T(8,128)(2,1)}, f32[8,768]{1,0:T(8,128)}, f32[2,384,1536]{2,1,0:T(8,128)}, f32[1536,768]{1,0:T(8,128)}) custom-call(s32[2]{0:T(128)} %pad_add_fusion.spot.refs_0_, bf16[4096,768]{1,0:T(8,128)(2,1)} %x.3, bf16[2048,768]{1,0:T(8,128)(2,1)} %get-tuple-element.181.middle_grad, bf16[3,1024,768]{2,1,0:T(8,128)(2,1)} %shard_map.347.up_a.up_b, ...), custom_call_target="tpu_custom_call" | custom-call | flops 100000000 | bytes 35000000 | tf_op jit(solution)/shard_map/pallas_call | solution.py:835
  401.2 33.6 %shard_map.349 = (bf16[4,768,384]{2,1,0:T(8,128)(2,1)S(1)}, f32[24,768]{1,0:T(8,128)S(1)}, f32[56,128]{1,0:T(8,128)S(1)}) custom-call(bf16[384,384]{1,0:T(8,128)(2,1)S(1)} %get-tuple-element.303.refs_0_, bf16[384,384]{1,0:T(8,128)(2,1)S(1)} %get-tuple-element.302.refs_1_, f32[8,768]{1,0:T(8,128)S(1)} %copy-done.10, f32[8,768]{1,0:T(8,128)S(1)} %copy-done.9, ...), custom_call_target="tpu_custom_call" | custom-call | tf_op jit(solution)/shard_map/pallas_call | solution.py:1010
  434.8 2.0 slice_convert_fusion
  (153 shorter events, 50.0 us)
Async XLA Ops:
  1.9 22.7 %collective-permute-start = (bf16[3,384,384]{2,1,0:T(8,128)(2,1)S(1)}, bf16[3,384,384]{2,1,0:T(8,128)(2,1)S(1)}, u32[]{:S(2)}, u32[]{:S(2)}) collective-permute-start(bf16[3,384,384]{2,1,0:T(8,128)(2,1)S(1)} %constant_dynamic-slice_fusion.2), channel_id=1, source_target_pairs={{0,1},{1,0},{2,3},{3,2},{4,5},{5,4},{6,7},{7,6},{8,9},{9,8},{10,11... | collective-permute-start | bytes 2654216 | tf_op jit(solution)/shard_map/ppermute | solution.py:1157
  5.0 57.4 %collective-permute-start.1 = (bf16[2,384]{1,0:T(2,128)(2,1)}, bf16[2,384]{1,0:T(2,128)(2,1)}, u32[]{:S(2)}, u32[]{:S(2)}) collective-permute-start(bf16[2,384]{1,0:T(2,128)(2,1)} %bias.3), channel_id=1, source_target_pairs={{0,1},{1,0},{2,3},{3,2},{4,5},{5,4},{6,7},{7,6},{8,9},{9,8},{10,11... | collective-permute-start | bytes 4616 | tf_op jit(solution)/shard_map/ppermute | solution.py:1157
  24.6 37.7 %collective-permute-start.2 = (bf16[3,384,384]{2,1,0:T(8,128)(2,1)S(1)}, bf16[3,384,384]{2,1,0:T(8,128)(2,1)S(1)}, u32[]{:S(2)}, u32[]{:S(2)}) collective-permute-start(bf16[3,384,384]{2,1,0:T(8,128)(2,1)S(1)} %collective-permute-done.mine), channel_id=1, source_target_pairs={{0,2},{2,0},{4,6},{6,4},{8,10},{10,8},{12,14},{14,12},{16,18},{18,... | collective-permute-start | bytes 2654216 | tf_op jit(solution)/shard_map/ppermute | solution.py:1042
  24.6 71.8 %collective-permute-start.3 = (bf16[384,1536]{1,0:T(8,128)(2,1)S(1)}, bf16[384,1536]{1,0:T(8,128)(2,1)}, u32[]{:S(2)}, u32[]{:S(2)}) collective-permute-start(bf16[384,1536]{1,0:T(8,128)(2,1)S(1)} %constant_dynamic-slice_fusion.1), channel_id=1, source_target_pairs={{0,1},{1,0},{2,3},{3,2},{4,5},{5,4},{6,7},{7,6},{8,9},{9,8},{10,11... | collective-permute-start | bytes 3538952 | tf_op jit(solution)/shard_map/ppermute | solution.py:1157
  26.4 70.1 %collective-permute-start.4 = (bf16[1536,384]{1,0:T(8,128)(2,1)S(1)}, bf16[1536,384]{1,0:T(8,128)(2,1)}, u32[]{:S(2)}, u32[]{:S(2)}) collective-permute-start(bf16[1536,384]{1,0:T(8,128)(2,1)S(1)} %constant_dynamic-slice_fusion), channel_id=1, source_target_pairs={{0,1},{1,0},{2,3},{3,2},{4,5},{5,4},{6,7},{7,6},{8,9},{9,8},{10,11... | collective-permute-start | bytes 3538952 | tf_op jit(solution)/shard_map/ppermute | solution.py:1157
  26.7 69.8 %collective-permute-start.5 = (bf16[384,768]{1,0:T(8,128)(2,1)}, bf16[384,768]{1,0:T(8,128)(2,1)}, u32[]{:S(2)}, u32[]{:S(2)}) collective-permute-start(bf16[384,768]{1,0:T(8,128)(2,1)} %proj_own.3), channel_id=1, source_target_pairs={{0,1},{1,0},{2,3},{3,2},{4,5},{5,4},{6,7},{7,6},{8,9},{9,8},{10,11... | collective-permute-start | bytes 1769480 | tf_op jit(solution)/shard_map/ppermute | solution.py:1157
  96.5 13.8 %collective-permute-start.6 = (bf16[384,1536]{1,0:T(8,128)(2,1)}, bf16[384,1536]{1,0:T(8,128)(2,1)S(1)}, u32[]{:S(2)}, u32[]{:S(2)}) collective-permute-start(bf16[384,1536]{1,0:T(8,128)(2,1)} %collective-permute-done.3.one_b), channel_id=1, source_target_pairs={{0,2},{2,0},{4,6},{6,4},{8,10},{10,8},{12,14},{14,12},{16,18},{18,... | collective-permute-start | bytes 3538952 | tf_op jit(solution)/shard_map/ppermute | solution.py:1042
  96.6 13.8 %collective-permute-start.8 = (bf16[1536,384]{1,0:T(8,128)(2,1)}, bf16[1536,384]{1,0:T(8,128)(2,1)}, u32[]{:S(2)}, u32[]{:S(2)}) collective-permute-start(bf16[1536,384]{1,0:T(8,128)(2,1)} %collective-permute-done.4.two_b), channel_id=1, source_target_pairs={{0,2},{2,0},{4,6},{6,4},{8,10},{10,8},{12,14},{14,12},{16,18},{18,... | collective-permute-start | bytes 3538952 | tf_op jit(solution)/shard_map/ppermute | solution.py:1042
  189.8 18.0 %collective-permute-start.9 = (bf16[2,2,2,2,48,1536]{5,4,3,2,1,0:T(8,128)(2,1)}, bf16[2,2,2,2,48,1536]{5,4,3,2,1,0:T(8,128)(2,1)S(1)}, u32[]{:S(2)}, u32[]{:S(2)}) collective-permute-start(bf16[2,2,2,2,48,1536]{5,4,3,2,1,0:T(8,128)(2,1)} %bitcast.149), channel_id=1, source_target_pairs={{0,2},{2,0},{4,6},{6,4},{8,10},{10,8},{12,14},{14,12},{16,18},{18,... | collective-permute-start | bytes 7077896 | tf_op jit(solution)/shard_map/ppermute | solution.py:1042
  189.9 17.9 %collective-permute-start.10 = (bf16[2,2,2,2,192,384]{5,4,3,2,1,0:T(8,128)(2,1)}, bf16[2,2,2,2,192,384]{5,4,3,2,1,0:T(8,128)(2,1)}, u32[]{:S(2)}, u32[]{:S(2)}) collective-permute-start(bf16[2,2,2,2,192,384]{5,4,3,2,1,0:T(8,128)(2,1)} %bitcast.148), channel_id=1, source_target_pairs={{0,2},{2,0},{4,6},{6,4},{8,10},{10,8},{12,14},{14,12},{16,18},{18,... | collective-permute-start | bytes 7077896 | tf_op jit(solution)/shard_map/ppermute | solution.py:1042
  212.5 28.2 %collective-permute-start.11 = (bf16[2,2,2,48,1536]{4,3,2,1,0:T(8,128)(2,1)}, bf16[2,2,2,48,1536]{4,3,2,1,0:T(8,128)(2,1)S(1)}, u32[]{:S(2)}, u32[]{:S(2)}) collective-permute-start(bf16[2,2,2,48,1536]{4,3,2,1,0:T(8,128)(2,1)} %fusion), channel_id=1, source_target_pairs={{0,1},{1,0},{2,3},{3,2},{4,5},{5,4},{6,7},{7,6},{8,9},{9,8},{10,11... | collective-permute-start | bytes 3538952 | tf_op jit(solution)/shard_map/ppermute | solution.py:1041
  214.2 28.0 %collective-permute-start.12 = (bf16[2,2,2,192,384]{4,3,2,1,0:T(8,128)(2,1)}, bf16[2,2,2,192,384]{4,3,2,1,0:T(8,128)(2,1)}, u32[]{:S(2)}, u32[]{:S(2)}) collective-permute-start(bf16[2,2,2,192,384]{4,3,2,1,0:T(8,128)(2,1)} %fusion.1), channel_id=1, source_target_pairs={{0,4},{2,6},{4,0},{6,2},{8,12},{10,14},{12,8},{14,10},{16,20},{18,... | collective-permute-start | bytes 3538952 | tf_op jit(solution)/shard_map/ppermute | solution.py:1042
  246.0 14.3 %collective-permute-start.13 = (bf16[2,2,48,1536]{3,2,1,0:T(8,128)(2,1)S(1)}, bf16[2,2,48,1536]{3,2,1,0:T(8,128)(2,1)}, u32[]{:S(2)}, u32[]{:S(2)}) collective-permute-start(bf16[2,2,48,1536]{3,2,1,0:T(8,128)(2,1)S(1)} %fusion.3), channel_id=1, source_target_pairs={{0,4},{2,6},{4,0},{6,2},{8,12},{10,14},{12,8},{14,10},{16,20},{18,... | collective-permute-start | bytes 1769480 | tf_op jit(solution)/shard_map/ppermute | solution.py:1042
  247.5 14.2 %collective-permute-start.14 = (bf16[2,2,192,384]{3,2,1,0:T(8,128)(2,1)}, bf16[2,2,192,384]{3,2,1,0:T(8,128)(2,1)}, u32[]{:S(2)}, u32[]{:S(2)}) collective-permute-start(bf16[2,2,192,384]{3,2,1,0:T(8,128)(2,1)} %fusion.2), channel_id=1, source_target_pairs={{0,8},{2,10},{4,12},{6,14},{8,0},{10,2},{12,4},{14,6},{16,24},{18,... | collective-permute-start | bytes 1769480 | tf_op jit(solution)/shard_map/ppermute | solution.py:1042
  264.2 15.2 %collective-permute-start.15 = (bf16[2,48,1536]{2,1,0:T(8,128)(2,1)S(1)}, bf16[2,48,1536]{2,1,0:T(8,128)(2,1)}, u32[]{:S(2)}, u32[]{:S(2)}) collective-permute-start(bf16[2,48,1536]{2,1,0:T(8,128)(2,1)S(1)} %fusion.13), channel_id=1, source_target_pairs={{0,8},{2,10},{4,12},{6,14},{8,0},{10,2},{12,4},{14,6},{16,24},{18,... | collective-permute-start | bytes 884744 | tf_op jit(solution)/shard_map/ppermute | solution.py:1042
  265.9 13.6 %collective-permute-start.16 = (bf16[2,192,384]{2,1,0:T(8,128)(2,1)S(1)}, bf16[2,192,384]{2,1,0:T(8,128)(2,1)}, u32[]{:S(2)}, u32[]{:S(2)}) collective-permute-start(bf16[2,192,384]{2,1,0:T(8,128)(2,1)S(1)} %fusion.12), channel_id=1, source_target_pairs={{0,1},{1,0},{2,3},{3,2},{4,5},{5,4},{6,7},{7,6},{8,9},{9,8},{10,11... | collective-permute-start | bytes 884744 | tf_op jit(solution)/shard_map/ppermute | solution.py:1041
  281.9 16.7 %collective-permute-start.19 = (bf16[2,768,384]{2,1,0:T(8,128)(2,1)}, bf16[2,768,384]{2,1,0:T(8,128)(2,1)}, u32[]{:S(2)}, u32[]{:S(2)}) collective-permute-start(bf16[2,768,384]{2,1,0:T(8,128)(2,1)} %get-tuple-element.223), channel_id=1, source_target_pairs={{0,2},{2,0},{4,6},{6,4},{8,10},{10,8},{12,14},{14,12},{16,18},{18,... | collective-permute-start | bytes 3538952 | tf_op jit(solution)/shard_map/ppermute | solution.py:1042
  282.1 14.5 %collective-permute-start.17 = (bf16[48,1536]{1,0:T(8,128)(2,1)S(1)}, bf16[48,1536]{1,0:T(8,128)(2,1)S(1)}, u32[]{:S(2)}, u32[]{:S(2)}) collective-permute-start(bf16[48,1536]{1,0:T(8,128)(2,1)S(1)} %fusion.19), channel_id=1, source_target_pairs={{0,16},{2,18},{4,20},{6,22},{8,24},{10,26},{12,28},{14,30},{16,0},... | collective-permute-start | bytes 442376 | tf_op jit(solution)/shard_map/ppermute | solution.py:1042
  284.7 13.9 %collective-permute-start.18 = (bf16[192,384]{1,0:T(8,128)(2,1)S(1)}, bf16[192,384]{1,0:T(8,128)(2,1)S(1)}, u32[]{:S(2)}, u32[]{:S(2)}) collective-permute-start(bf16[192,384]{1,0:T(8,128)(2,1)S(1)} %fusion.18), channel_id=1, source_target_pairs={{0,16},{2,18},{4,20},{6,22},{8,24},{10,26},{12,28},{14,30},{16,0},... | collective-permute-start | bytes 442376 | tf_op jit(solution)/shard_map/ppermute | solution.py:1042
  302.7 24.3 %collective-permute-start.20 = (bf16[48,1536]{1,0:T(8,128)(2,1)S(1)}, bf16[48,1536]{1,0:T(8,128)(2,1)S(1)}, u32[]{:S(2)}, u32[]{:S(2)}) collective-permute-start(bf16[48,1536]{1,0:T(8,128)(2,1)S(1)} %fusion.17), channel_id=1, source_target_pairs={{0,16},{2,18},{4,20},{6,22},{8,24},{10,26},{12,28},{14,30},{16,0},... | collective-permute-start | bytes 442376 | tf_op jit(solution)/shard_map/ppermute | solution.py:1042
  303.5 23.5 %collective-permute-start.21 = (bf16[192,384]{1,0:T(8,128)(2,1)S(1)}, bf16[192,384]{1,0:T(8,128)(2,1)S(1)}, u32[]{:S(2)}, u32[]{:S(2)}) collective-permute-start(bf16[192,384]{1,0:T(8,128)(2,1)S(1)} %fusion.15), channel_id=1, source_target_pairs={{0,16},{2,18},{4,20},{6,22},{8,24},{10,26},{12,28},{14,30},{16,0},... | collective-permute-start | bytes 442376 | tf_op jit(solution)/shard_map/ppermute | solution.py:1042
  305.7 21.3 %collective-permute-start.22 = (bf16[768,384]{1,0:T(8,128)(2,1)S(1)}, bf16[768,384]{1,0:T(8,128)(2,1)S(1)}, u32[]{:S(2)}, u32[]{:S(2)}) collective-permute-start(bf16[768,384]{1,0:T(8,128)(2,1)S(1)} %get-tuple-element.233), channel_id=1, source_target_pairs={{0,1},{1,0},{2,3},{3,2},{4,5},{5,4},{6,7},{7,6},{8,9},{9,8},{10,11... | collective-permute-start | bytes 1769480 | tf_op jit(solution)/shard_map/ppermute | solution.py:1041
  327.3 19.8 %collective-permute-start.23 = (bf16[2,48,1536]{2,1,0:T(8,128)(2,1)S(1)}, bf16[2,48,1536]{2,1,0:T(8,128)(2,1)S(1)}, u32[]{:S(2)}, u32[]{:S(2)}) collective-permute-start(bf16[2,48,1536]{2,1,0:T(8,128)(2,1)S(1)} %broadcast_select_fusion.5), channel_id=1, source_target_pairs={{0,8},{2,10},{4,12},{6,14},{8,0},{10,2},{12,4},{14,6},{16,24},{18,... | collective-permute-start | bytes 884744 | tf_op jit(solution)/shard_map/ppermute | solution.py:1042
  327.6 19.4 %collective-permute-start.24 = (bf16[2,192,384]{2,1,0:T(8,128)(2,1)S(1)}, bf16[2,192,384]{2,1,0:T(8,128)(2,1)S(1)}, u32[]{:S(2)}, u32[]{:S(2)}) collective-permute-start(bf16[2,192,384]{2,1,0:T(8,128)(2,1)S(1)} %broadcast_select_fusion.4), channel_id=1, source_target_pairs={{0,4},{2,6},{4,0},{6,2},{8,12},{10,14},{12,8},{14,10},{16,20},{18,... | collective-permute-start | bytes 884744 | tf_op jit(solution)/shard_map/ppermute | solution.py:1042
  328.2 18.9 %collective-permute-start.25 = (bf16[768,384]{1,0:T(8,128)(2,1)S(1)}, bf16[768,384]{1,0:T(8,128)(2,1)S(1)}, u32[]{:S(2)}, u32[]{:S(2)}) collective-permute-start(bf16[768,384]{1,0:T(8,128)(2,1)S(1)} %get-tuple-element.241), channel_id=1, source_target_pairs={{0,1},{1,0},{2,3},{3,2},{4,5},{5,4},{6,7},{7,6},{8,9},{9,8},{10,11... | collective-permute-start | bytes 1769480 | tf_op jit(solution)/shard_map/ppermute | solution.py:1041
  348.2 16.8 %collective-permute-start.26 = (bf16[2,2,48,1536]{3,2,1,0:T(8,128)(2,1)S(1)}, bf16[2,2,48,1536]{3,2,1,0:T(8,128)(2,1)S(1)}, u32[]{:S(2)}, u32[]{:S(2)}) collective-permute-start(bf16[2,2,48,1536]{3,2,1,0:T(8,128)(2,1)S(1)} %broadcast_select_fusion.3), channel_id=1, source_target_pairs={{0,4},{2,6},{4,0},{6,2},{8,12},{10,14},{12,8},{14,10},{16,20},{18,... | collective-permute-start | bytes 1769480 | tf_op jit(solution)/shard_map/ppermute | solution.py:1042
  349.8 15.2 %collective-permute-start.27 = (bf16[2,2,192,384]{3,2,1,0:T(8,128)(2,1)S(1)}, bf16[2,2,192,384]{3,2,1,0:T(8,128)(2,1)S(1)}, u32[]{:S(2)}, u32[]{:S(2)}) collective-permute-start(bf16[2,2,192,384]{3,2,1,0:T(8,128)(2,1)S(1)} %broadcast_select_fusion.2), channel_id=1, source_target_pairs={{0,8},{2,10},{4,12},{6,14},{8,0},{10,2},{12,4},{14,6},{16,24},{18,... | collective-permute-start | bytes 1769480 | tf_op jit(solution)/shard_map/ppermute | solution.py:1042
  351.5 13.5 %collective-permute-start.28 = (bf16[384,768]{1,0:T(8,128)(2,1)S(1)}, bf16[384,768]{1,0:T(8,128)(2,1)}, u32[]{:S(2)}, u32[]{:S(2)}) collective-permute-start(bf16[384,768]{1,0:T(8,128)(2,1)S(1)} %dynamic-slice_bitcast_fusion), channel_id=1, source_target_pairs={{0,1},{1,0},{2,3},{3,2},{4,5},{5,4},{6,7},{7,6},{8,9},{9,8},{10,11... | collective-permute-start | bytes 1769480 | tf_op jit(solution)/shard_map/ppermute | solution.py:1041
  365.4 13.4 %collective-permute-start.29 = (bf16[2,2,2,48,1536]{4,3,2,1,0:T(8,128)(2,1)S(1)}, bf16[2,2,2,48,1536]{4,3,2,1,0:T(8,128)(2,1)S(1)}, u32[]{:S(2)}, u32[]{:S(2)}) collective-permute-start(bf16[2,2,2,48,1536]{4,3,2,1,0:T(8,128)(2,1)S(1)} %broadcast_select_fusion.1), channel_id=1, source_target_pairs={{0,2},{2,0},{4,6},{6,4},{8,10},{10,8},{12,14},{14,12},{16,18},{18,... | collective-permute-start | bytes 3538952 | tf_op jit(solution)/shard_map/ppermute | solution.py:1042
  365.5 13.4 %collective-permute-start.30 = (bf16[2,2,2,192,384]{4,3,2,1,0:T(8,128)(2,1)S(1)}, bf16[2,2,2,192,384]{4,3,2,1,0:T(8,128)(2,1)}, u32[]{:S(2)}, u32[]{:S(2)}) collective-permute-start(bf16[2,2,2,192,384]{4,3,2,1,0:T(8,128)(2,1)S(1)} %broadcast_select_fusion), channel_id=1, source_target_pairs={{0,2},{2,0},{4,6},{6,4},{8,10},{10,8},{12,14},{14,12},{16,18},{18,... | collective-permute-start | bytes 3538952 | tf_op jit(solution)/shard_map/ppermute | solution.py:1042
  381.7 17.8 %collective-permute-start.33 = (bf16[384,384]{1,0:T(8,128)(2,1)}, bf16[384,384]{1,0:T(8,128)(2,1)S(1)}, u32[]{:S(2)}, u32[]{:S(2)}) collective-permute-start(bf16[384,384]{1,0:T(8,128)(2,1)} %get-tuple-element.274), channel_id=1, source_target_pairs={{0,4},{2,6},{4,0},{6,2},{8,12},{10,14},{12,8},{14,10},{16,20},{18,... | collective-permute-start | bytes 884744 | tf_op jit(solution)/shard_map/ppermute | solution.py:1042
  382.3 17.3 %collective-permute-start.34 = (bf16[384,384]{1,0:T(8,128)(2,1)}, bf16[384,384]{1,0:T(8,128)(2,1)}, u32[]{:S(2)}, u32[]{:S(2)}) collective-permute-start(bf16[384,384]{1,0:T(8,128)(2,1)} %get-tuple-element.275), channel_id=1, source_target_pairs={{0,8},{2,10},{4,12},{6,14},{8,0},{10,2},{12,4},{14,6},{16,24},{18,... | collective-permute-start | bytes 884744 | tf_op jit(solution)/shard_map/ppermute | solution.py:1042
  (32 other events, 276.3 us)

commit v6 on v5

--- a/solution.py
+++ b/solution.py
@@ -705,14 +705,14 @@
             ]
             + [pl.BlockSpec(memory_space=pl.ANY)] * len(d_in),
             out_specs=[
-                block,
+                pl.BlockSpec((1, 1, SLOTS, TRIO), lambda s, w, *_: (s + first, w, 0, side)),
                 pl.BlockSpec((GREL, 128), lambda s, w, *_: (0, 0)),
                 pl.BlockSpec((8, TRIO), lambda s, w, *_: (0, 0)),
             ],
             scratch_shapes=[pltpu.VMEM((NWIN, SLOTS, HALF), BF), pltpu.VMEM((HALF, SLOTS), BF)],
         ),
         out_shape=[
-            jax.ShapeDtypeStruct((3, NWIN, SLOTS, TRIO), BF),
+            jax.ShapeDtypeStruct((3, NWIN, SLOTS, 2 * TRIO), BF),
             jax.ShapeDtypeStruct((GREL, 128), F32),
             jax.ShapeDtypeStruct((8, TRIO), F32),
         ],
@@ -722,7 +722,7 @@
     )(spot, qkv, p, ctx_grad, spread, rel_even, rel_odd, fold, *d_in)
 
 
-def norm_grad_kernel(own, other, weights_own, spot, mine, theirs, gather, *refs):
+def norm_grad_kernel(d, weights_own, spot, mine, theirs, gather, *refs):
     out, joined = refs[-2:]
 
     @pl.when((pl.program_id(0) == 0) & (pl.program_id(1) == 0))
@@ -732,30 +732,29 @@
         join_pieces(spot[1], mine, theirs, joined, TRIO)
 
     rows = NWIN * 128
-    left = jnp.concatenate([own[...].reshape(rows, TRIO), other[...].reshape(rows, TRIO)], axis=1)
-    total = dot(left, joined[...], NT).astype(BF).reshape(NWIN, 4, 32, D)
+    total = dot(d[...].reshape(rows, 2 * TRIO), joined[...], NT).astype(BF).reshape(NWIN, 4, 32, D)
     for t in range(4):
         moved = dot(gather[...], total[:, t].reshape(NWIN * 32, D)).astype(BF)
         out[:, t * PAIR : t * PAIR + PAIR, :] = moved.reshape(1, PAIR, D)
 
 
-def norm_grad(own, other, weights_own, core, mine, theirs, gather, bands, *before):
+def norm_grad(d, weights_own, core, mine, theirs, gather, bands, *before):
     first, last = bands
     share = (last - first) / 3
-    block = pl.BlockSpec((1, NWIN, 128, TRIO), lambda s, t: (s + first, 0, t, 0))
+    block = pl.BlockSpec((1, NWIN, 128, 2 * TRIO), lambda s, t: (s + first, 0, t, 0))
     return pl.pallas_call(
         norm_grad_kernel,
         grid=(last - first, 2),
-        in_specs=[block, block, whole((3, D, HALF)), SCALAR]
+        in_specs=[block, whole((3, D, HALF)), SCALAR]
         + [whole((3, HALF, HALF)), whole((3, HALF, HALF)), whole((PAIR, NWIN * 32))]
         + [pl.BlockSpec(memory_space=pl.ANY)] * len(before),
         out_specs=pl.BlockSpec((1, 4 * PAIR, D), lambda s, t: (s + first, t, 0)),
         out_shape=jax.ShapeDtypeStruct((3, 8 * PAIR, D), BF),
-        input_output_aliases={7: 0} if before else {},
+        input_output_aliases={6: 0} if before else {},
         scratch_shapes=[pltpu.VMEM((D, 2 * TRIO), BF)],
         compiler_params=params(),
         cost_estimate=cost(14e9 * share, 30e6 * share),
-    )(own, other, weights_own, core, mine, theirs, gather, *before)
+    )(d, weights_own, core, mine, theirs, gather, *before)
 
 
 def qkv_grad_kernel(spot, xt, d, proj, kept, sent, total):
@@ -774,7 +773,7 @@
             sent[k] = jnp.where(first, values[2 + k], values[k])
 
 
-def qkv_grad(core, xt, d, proj):
+def qkv_grad(core, xt, d, side, proj):
     rows = NWIN * SLOTS
     block = pl.BlockSpec((2, D, HALF), lambda i: (0, 0, 0))
     shape = jax.ShapeDtypeStruct((2, D, HALF), BF)
@@ -784,7 +783,7 @@
         in_specs=[
             SCALAR,
             pl.BlockSpec((D, rows), lambda i: (0, i)),
-            pl.BlockSpec((rows, TRIO), lambda i: (i, 0)),
+            pl.BlockSpec((rows, TRIO), lambda i: (i, side)),
             whole((D, HALF)),
         ],
         out_specs=[block, block],
@@ -792,11 +791,14 @@
         scratch_shapes=[pltpu.VMEM((D, TRIO), F32)],
         compiler_params=params(),
         cost_estimate=cost(7e9, 16e6),
-    )(core, xt, d.reshape(3 * rows, TRIO), proj)
+    )(core, xt, d.reshape(3 * rows, 2 * TRIO), proj)
+
+
+EARLY = 3
 
 
 def input_kernel(
-    spot, x, middle_grad, up_a, up_b, taken_a, taken_b, gain,
+    spot, x, middle_grad, up_a, up_b, early_a, early_b, late_a, late_b, gain,
     one_mine, one_theirs, two_mine, two_theirs, out, sums, one_out, two_out,
 ):
     step = pl.program_id(0)
@@ -812,10 +814,11 @@
     def _():
         sums[...] = jnp.zeros_like(sums)
 
-    for k, (up, taken) in enumerate(((up_a, taken_a), (up_b, taken_b))):
+    for k, (up, early, late) in enumerate(((up_a, early_a, late_a), (up_b, early_b, late_b))):
         rows = slice(k * PAIR, k * PAIR + PAIR)
         scaled, inverse = norm_parts(x[rows, :].astype(F32))
-        shared = taken[...].astype(F32) * taken_pair(spot[0], 2 * step + k)[1].astype(F32)
+        at, some = taken_pair(spot[0], 2 * step + k)
+        shared = jnp.where(at < EARLY, early[...].astype(F32), late[...].astype(F32)) * some.astype(F32)
         upstream = up[0].astype(F32) + shared
         scaled_up = upstream * vec(gain)
         mean = jnp.mean(scaled_up, axis=-1, keepdims=True)
@@ -825,11 +828,12 @@
         add_row(sums, 1, upstream)
 
 
-def input_of(spot, x, middle_grad, up, taken, gain, ones, twos):
+def input_of(spot, x, middle_grad, up, early, late, gain, ones, twos):
     rows = 2 * PAIR
     row_block = pl.BlockSpec((rows, D), lambda i, *_: (i, 0))
     up_at = lambda k: lambda i, spot: band_step(spot[0], 2 * i + k) + (0,)
-    taken_at = lambda k: lambda i, spot: (taken_pair(spot[0], 2 * i + k)[0], 0)
+    early_at = lambda k: lambda i, spot: (jnp.minimum(taken_pair(spot[0], 2 * i + k)[0], EARLY - 1), 0)
+    late_at = lambda k: lambda i, spot: (jnp.maximum(taken_pair(spot[0], 2 * i + k)[0] - EARLY, 0), 0)
     steps = OWN // rows
     one_rows, two_rows = HALF // steps, FF // 2 // steps
     return pl.pallas_call(
@@ -842,8 +846,10 @@
                 row_block,
                 pl.BlockSpec((1, PAIR, D), up_at(0)),
                 pl.BlockSpec((1, PAIR, D), up_at(1)),
-                pl.BlockSpec((PAIR, D), taken_at(0)),
-                pl.BlockSpec((PAIR, D), taken_at(1)),
+                pl.BlockSpec((PAIR, D), early_at(0)),
+                pl.BlockSpec((PAIR, D), early_at(1)),
+                pl.BlockSpec((PAIR, D), late_at(0)),
+                pl.BlockSpec((PAIR, D), late_at(1)),
                 whole((D,)),
             ]
             + [pl.BlockSpec((one_rows, FF // 2), lambda i, *_: (i, 0))] * 2
@@ -863,7 +869,7 @@
         ],
         compiler_params=params(),
         cost_estimate=cost(1e8, 35e6),
-    )(spot, x, middle_grad, up, up, taken, taken, gain, *ones, *twos)
+    )(spot, x, middle_grad, up, up, early, early, late, late, gain, *ones, *twos)
 
 
 MESH = pl.DeviceIdType.MESH
@@ -891,10 +897,10 @@
 
 
 def last_kernel(bits, plans, orders, *refs):
-    (line_a, line_b, one_sums, two_sums, fc1_sums, sums_a, sums_c, sums_b, sums_d) = refs[:9]
-    rel_a, rel_b, rel_c, rel_d, hots, out, small, rel = refs[9:17]
-    small_landed, rel_landed, sends, recvs = refs[17:21]
-    rooms = list(refs[21:])
+    (line_a, line_b, one_sums, two_sums, fc1_sums, sums_a, sums_c, sums_b) = refs[:8]
+    rel_a, rel_b, rel_c, hots, out, small, rel = refs[8:15]
+    small_landed, rel_landed, sends, recvs = refs[15:19]
+    rooms = list(refs[19:])
     dp, mp = lax.axis_index("dp"), lax.axis_index("mp")
     bit_at = lambda bit: mp if bit == 0 else (dp // bit) % 2
 
@@ -978,14 +984,14 @@
     small[2:6, :] = two_sums[0:4, :]
     first = mp == 0
     own = [sums_a[0:1, :] + sums_c[0:1, :], fc1_sums[0:1, 0 : FF // 2]]
-    other = [sums_b[0:1, :] + sums_d[0:1, :], fc1_sums[0:1, FF // 2 :]]
+    other = [sums_b[0:1, :], fc1_sums[0:1, FF // 2 :]]
     for row, flip in ((6, False), (9, True)):
         picked = [jnp.where(first != flip, a, b) for a, b in zip(own, other)]
         small[row : row + 1, 0:HALF] = picked[0][:, 0:HALF]
         small[row : row + 1, HALF:] = picked[0][:, 2 * HALF :]
         small[row + 1 : row + 2, :] = picked[1][:, 0:D]
         small[row + 2 : row + 3, :] = picked[1][:, D:]
-    table = rel_a[...] + rel_b[...] + rel_c[...] + rel_d[...]
+    table = rel_a[...] + rel_b[...] + rel_c[...]
     table = lax.dot_general(hots[...], table, TN, precision=lax.Precision.HIGHEST, preferred_element_type=F32)
     rel[...] = table + pltpu.roll(table, HD, 1)
 
@@ -1219,43 +1225,41 @@
         spot, qkv, p, grad, side, spread, rel_even, rel_odd, fold, bands, *d
     )
     ctx_grad = advance(ctx_grad, feed_lines)
-    d_b, rel_b, sums_b = back_of(qkv_b, p_b, 1, ctx_grad, (1, 3))
-    d_b = advance(d_b, feed_lines)
-    d_b, rel_b0, sums_b0 = back_of(qkv_b, p_b, 1, ctx_grad, (0, 1), d_b)
-    d_b = advance(d_b, feed_lines)
-    kept_b, sent_b = qkv_grad(spot, xt, d_b, proj_oth)
+    d, rel_b, sums_b = back_of(qkv_b, p_b, 1, ctx_grad, (0, 3))
+    d = advance(d, feed_lines)
+    kept_b, sent_b = qkv_grad(spot, xt, d, 1, proj_oth)
     line_b = Line(kept_b, [], [], [("give", CORE)], sent_b)
     lines = feed_lines + [line_b]
-    ctx_grad, kept_b = lax.optimization_barrier((ctx_grad, kept_b))
+    ctx_grad, kept_b, d = lax.optimization_barrier((ctx_grad, kept_b, d))
     ctx_grad = advance(ctx_grad, lines)
-    d_a, rel_a0, sums_a0 = back_of(qkv_a, p_a, 0, ctx_grad, (0, 1))
-    d_a = advance(d_a, lines)
+    d, rel_a0, sums_a0 = back_of(qkv_a, p_a, 0, ctx_grad, (0, 1), d)
+    d = advance(d, lines)
     passes = []
     for k in range(2):
         line = Line(None, [], [], [("pass", PAIRED)])
         line.terms = [(term[k], ()) for term, _ in line_b.terms]
         passes.append(line)
-    d_a = advance(d_a, passes[:1])
-    d_a, rel_a, sums_a = back_of(qkv_a, p_a, 0, ctx_grad, (1, 3), d_a)
-    d_a = advance(d_a, feed_lines + passes[:1])
-    d_a = advance(d_a, passes[1:])
-    up = norm_grad(d_a, d_b, qkv_weight, spot, qkv_mine, qkv_theirs, gather, (1, 3))
+    d = advance(d, passes[:1])
+    d, rel_a, sums_a = back_of(qkv_a, p_a, 0, ctx_grad, (1, 3), d)
+    d = advance(d, feed_lines + passes[:1])
+    d = advance(d, passes[1:])
+    up = norm_grad(d, qkv_weight, spot, qkv_mine, qkv_theirs, gather, (1, 3))
     at = [2 - place, (1 - place) * 4 * SIDE, jnp.zeros_like(place)]
     shares = []
-    for first, count in ((0, 6), (6, 4)):
+    for first, count in ((0, 2 * EARLY), (2 * EARLY, 10 - 2 * EARLY)):
         start = [at[0], at[1] + first * SIDE, at[2]]
         part = lax.dynamic_slice(up, start, (1, count * SIDE, D)).reshape(count * SIDE, D)
         shares.append(Line(part, [], [], [("pass", PAIRED)]))
-    d_a = advance(d_a, feed_lines + passes[1:])
-    d_a = advance(d_a, shares[:1])
-    kept_a, sent_a = qkv_grad(spot, xt, d_a, proj_own)
+    d = advance(d, feed_lines + passes[1:])
+    d = advance(d, shares[:1])
+    kept_a, sent_a = qkv_grad(spot, xt, d, 0, proj_own)
     line_a = Line(kept_a, [], [], [("give", CORE)], sent_a)
-    kept_a, d_a = lax.optimization_barrier((kept_a, d_a))
-    d_a = advance(d_a, feed_lines + [line_a] + shares[:1])
-    d_a = advance(d_a, shares[1:])
-    up = norm_grad(d_a, d_b, qkv_weight, spot, qkv_mine, qkv_theirs, gather, (0, 1), up)
+    kept_a, d = lax.optimization_barrier((kept_a, d))
+    d = advance(d, feed_lines + [line_a] + shares[:1])
+    d = advance(d, shares[1:])
+    up = norm_grad(d, qkv_weight, spot, qkv_mine, qkv_theirs, gather, (0, 1), up)
     up = advance(up, feed_lines + [line_a] + shares[1:])
-    taken = jnp.concatenate([line.terms[0][0] for line in shares], axis=0)
+    early, late = (line.terms[0][0] for line in shares)
     q_lines = []
     for k, order in enumerate((bits, turned)):
         line = Line(None, [], [], halves(order[:1]))
@@ -1267,15 +1271,15 @@
     finish(feed_lines)
     flat = lambda line, rows: (line.value.reshape(rows, -1), line.taken_last.reshape(rows, -1))
     input_grad, one_sums, one_sum, two_sum = input_of(
-        spot, image_tokens, middle_grad, up, taken, norm1_gain, flat(one_line, HALF), flat(two_line, FF // 2)
+        spot, image_tokens, middle_grad, up, early, late, norm1_gain, flat(one_line, HALF), flat(two_line, FF // 2)
     )
     one_sums = advance(one_sums, q_lines)
     four, small, rel = last_sums(
         bits,
         [bits, turned],
         [line.part({}) for line in q_lines],
-        [one_sums, two_sums, fc1_sums, sums_a, sums_a0, sums_b, sums_b0],
-        [rel_a, rel_a0, rel_b, rel_b0],
+        [one_sums, two_sums, fc1_sums, sums_a, sums_a0, sums_b],
+        [rel_a, rel_a0, rel_b],
         hots,
     )
     one_sum = one_sum.reshape(D, FF // 2)

time: 449 us -> 446 us (level)
  waiting for transfers between devices: 13.3 us -> 6.11 us
    ppermute x6, waiting for transfers between devices: 4.67 us -> 0.02 us  [exchange(): return lax.ppermute(value, 'mp', [(0, 1), (1, 0)])]
    pallas_call x4 -> x3, Pallas kernels: 63.3 us -> 61.2 us  [attend_back(): pl.pallas_call(lambda *refs: attend_back_kernel(first, *refs), grid_spec=...]
where the time goes in v6:
time: 446 us; the launch traced here: 438 us
  Pallas kernels  349 us (78%)
  starting transfers between devices  33.3 us (7%)
  other arithmetic  31.2 us (7%)
  local copies, waits for them, and re-layouts  16.4 us (4%)
  waiting for transfers between devices  6.11 us (1%)
    pallas_call x1, Pallas kernels, feed(): pl.pallas_call(feed_kernel, grid_spec=pltpu.PrefetchScalarGridSpec(num_sc...  78.4 us
    pallas_call x2, Pallas kernels, attend(): pl.pallas_call(attend_own if first else attend_other, grid=(3, NWIN), in_...  67.1 us
    pallas_call x3, Pallas kernels, attend_back(): pl.pallas_call(lambda *refs: attend_back_kernel(first, *refs), grid_spec=...  61.2 us
    pallas_call x1, Pallas kernels, last_sums(): pl.pallas_call(lambda *refs: last_kernel(bits, plans, orders, *refs), in_...  32 us
    pallas_call x2, Pallas kernels, norm_grad(): pl.pallas_call(norm_grad_kernel, grid=(last - first, 2), in_specs=[block,...  27.3 us
    convert_element_type x13, other arithmetic, part(): return total.astype(BF)  25.5 us
    pallas_call x2, Pallas kernels, qkv_grad(): pl.pallas_call(qkv_grad_kernel, grid=(3,), in_specs=[SCALAR, pl.BlockSpec...  25 us
    ppermute x23, starting transfers between devices, exchange(): lax.ppermute(value, 'dp', [(i, i ^ bit) for i in range(lax.axis_size('dp'...  19.6 us
  transfers between devices with their start and end apart: 35, of which 5 were waited for; matrix products, arithmetic and copies ran while one was open for 2% of the time, Pallas kernels for 54%

profile of v6, /device:TPU:0, one launch (start us, length us, event | category | flops | bytes accessed | tf_op | source)
XLA Modules:
  0.0 437.5 jit_solution(17834960442034079892)
XLA Ops:
  1.9 3.0 collective-permute-start
  5.0 4.6 %shard_map.334.cot_t = bf16[768,2048]{1,0:T(8,128)(2,1)} custom-call(bf16[2048,768]{1,0:T(8,128)(2,1)} %cot.3), custom_call_target="tpu_custom_call" | custom-call | flops 1000000 | bytes 6000000 | tf_op jit(solution)/shard_map/pallas_call | solution.py:376
  10.2 8.7 %shard_map.333.x = bf16[3,5,256,768]{3,2,1,0:T(8,128)(2,1)} custom-call(s32[2]{0:T(128)} %pad_add_fusion.spot.refs_0_, bf16[4096,768]{1,0:T(8,128)(2,1)} %x.3, bf16[4096,768]{1,0:T(8,128)(2,1)} %x.3, bf16[4096,768]{1,0:T(8,128)(2,1)} %x.3, bf16[4096,768]{1,0:T(8,128)(2,1)} %x.3, bf16[4096,768]{1,0:T(8,128)(2,1)} %x.3, bf16[4096,768]{1,0:T(8,128)(2,1)} %x.3, ...), custom_call_target="tpu_custom_call" | custom-call | flops 660602880 | bytes 10000000 | tf_op jit(solution)/shard_map/pallas_call | solution.py:134
  21.0 3.6 collective-permute-done.mine
  24.6 1.7 collective-permute-start.3
  28.4 33.9 %shard_map.335 = (bf16[3,5,256,1152]{3,2,1,0:T(8,128)(2,1)}, bf16[3,5,6,224,256]{4,3,2,1,0:T(8,128)(2,1)}, bf16[3,5,256,384]{3,2,1,0:T(8,128)(2,1)}, bf16[768,38...) custom-call(bf16[3,5,256,768]{3,2,1,0:T(8,128)(2,1)} %shard_map.333.x, bf16[2,384]{1,0:T(2,128)(2,1)} %bias.3, ...), custom_call_target="tpu_custom_call" | custom-call | flops 15000000512 | bytes 45000000 | tf_op jit(solution)/shard_map/pallas_call | solution.py:297
  63.3 33.2 %shard_map.336 = (bf16[3,5,256,1152]{3,2,1,0:T(8,128)(2,1)}, bf16[3,5,6,224,256]{4,3,2,1,0:T(8,128)(2,1)}, bf16[3,5,256,384]{3,2,1,0:T(8,128)(2,1)}) custom-call(bf16[3,5,256,768]{3,2,1,0:T(8,128)(2,1)} %shard_map.333.x, bf16[2,384]{1,0:T(2,128)(2,1)} %collective-permute-done.1.bias, s32[2]{0:T(128)} %pad_add_fusion.spot.refs_0_, ...), custom_call_target="tpu_custom_call" | custom-call | flops 15000000512 | bytes 45000000 | tf_op jit(solution)/shard_map/pallas_call | solution.py:297
  97.4 12.9 %shard_map.337 = (bf16[2048,768]{1,0:T(8,128)(2,1)}, bf16[2048,768]{1,0:T(8,128)(2,1)}, bf16[768,2048]{1,0:T(8,128)(2,1)}, bf16[2048,768]{1,0:T(8,128)(2,1)}) custom-call(s32[2]{0:T(128)} %pad_add_fusion.spot.refs_0_, bf16[3,5,256,384]{3,2,1,0:T(8,128)(2,1)} %get-tuple-element.153.own_a.own_b, bf16[3,5,256,384]{3,2,1,0:T(8,128)(2,1)} %get-tuple-element.153.own_a.own_b, ...), custom_call_target="tpu_custom_call" | custom-call | flops 3000000000 | bytes 25000000 | tf_op jit(solution)/shard_map/pallas_call | solution.py:343
  111.4 78.4 %shard_map.338 = (bf16[2048,768]{1,0:T(8,128)(2,1)}, bf16[2048,768]{1,0:T(8,128)(2,1)}, bf16[2,384,1536]{2,1,0:T(8,128)(2,1)}, bf16[2,384,1536]{2,1,0:T(8,128)(2...) custom-call(s32[2]{0:T(128)} %pad_add_fusion.spot.refs_0_, ...), custom_call_target="tpu_custom_call" | custom-call | flops 57999998976 | bytes 60000000 | tf_op jit(solution)/shard_map/pallas_call | solution.py:462
  191.7 16.2 %shard_map.339 = (bf16[2048,768]{1,0:T(8,128)(2,1)}, bf16[2048,768]{1,0:T(8,128)(2,1)}, bf16[2048,768]{1,0:T(8,128)(2,1)}, bf16[768,384]{1,0:T(8,128)(2,1)}, bf16[768,384]{1,0:T(8,128)(2,1)}, /*index=5*/f32[8,768]{1,0:T(8,128)}) custom-call(bf16[2048,768]{1,0:T(8,128)(2,1)} %get-tuple-element.171.middle, bf16[2048,768]{1,0:T(8,128)(2,1)} %get-tuple-element.172.forward, ...), custom_call_target="tpu_custom_call" | custom-call | flops 5000000000 | bytes 40000000 | tf_op jit(solution)/shard_map/pallas_call | solution.py:552
  210.0 2.6 fusion.1
  212.6 1.7 collective-permute-start.11
  215.8 29.3 %shard_map.340 = (bf16[3,5,256,2304]{3,2,1,0:T(8,128)(2,1)}, f32[80,128]{1,0:T(8,128)}, f32[8,1152]{1,0:T(8,128)}) custom-call(s32[2]{0:T(128)} %pad_add_fusion.spot.refs_0_, bf16[3,5,256,1152]{3,2,1,0:T(8,128)(2,1)} %get-tuple-element.189.refs_1_, bf16[3,5,6,224,256]{4,3,2,1,0:T(8,128)(2,1)} %get-tuple-element.190.refs_2_, ...), custom_call_target="tpu_custom_call" | custom-call | flops 20000000000 | bytes 45000000 | tf_op jit(solution)/shard_map/pallas_call | solution.py:692
  245.1 2.5 fusion.3
  247.7 2.5 fusion.2
  252.2 12.5 %shard_map.341 = (bf16[2,768,384]{2,1,0:T(8,128)(2,1)}, bf16[2,768,384]{2,1,0:T(8,128)(2,1)}) custom-call(s32[2]{0:T(128)} %pad_add_fusion.spot.refs_0_, bf16[768,3840]{1,0:T(8,128)(2,1)} %get-tuple-element.177.xt, bf16[3840,2304]{1,0:T(8,128)(2,1)} %bitcast.126, bf16[768,384]{1,0:T(8,128)(2,1)} %get-tuple-element.198.proj), custom_call_target="tpu_custom_call" | custom-call | flops 7000000000 | bytes 16000000 | tf_op jit(solution)/shard_map/pallas_call | solution.py:780
  265.5 1.9 fusion.13
  267.4 2.1 fusion.12
  271.6 11.6 %shard_map.342 = (bf16[3,5,256,2304]{3,2,1,0:T(8,128)(2,1)}, f32[80,128]{1,0:T(8,128)}, f32[8,1152]{1,0:T(8,128)}) custom-call(s32[2]{0:T(128)} %pad_add_fusion.spot.refs_0_, bf16[3,5,256,1152]{3,2,1,0:T(8,128)(2,1)} %get-tuple-element.178.refs_1_, bf16[3,5,6,224,256]{4,3,2,1,0:T(8,128)(2,1)} %get-tuple-element.179.refs_2_, ...), custom_call_target="tpu_custom_call", output_to_operand_aliasing={{0}: (8, {})} | custom-call | flops 6666666496 | bytes 15000000 | tf_op jit(solution)/shard_map/pallas_call | solution.py:692
  283.3 2.5 fusion.5
  285.9 2.0 fusion.18
  287.8 1.8 fusion.19
  291.2 2.6 collective-permute-start.18
  294.1 20.3 %shard_map.343 = (bf16[3,5,256,2304]{3,2,1,0:T(8,128)(2,1)}, f32[80,128]{1,0:T(8,128)}, f32[8,1152]{1,0:T(8,128)}) custom-call(s32[2]{0:T(128)} %pad_add_fusion.spot.refs_0_, bf16[3,5,256,1152]{3,2,1,0:T(8,128)(2,1)} %get-tuple-element.178.refs_1_, bf16[3,5,6,224,256]{4,3,2,1,0:T(8,128)(2,1)} %get-tuple-element.179.refs_2_, ...), custom_call_target="tpu_custom_call", output_to_operand_aliasing={{0}: (8, {})} | custom-call | flops 13333332992 | bytes 30000000 | tf_op jit(solution)/shard_map/pallas_call | solution.py:692
  319.1 2.6 collective-permute-start.21
  322.0 16.7 %shard_map.344.refs_0_ = bf16[3,1024,768]{2,1,0:T(8,128)(2,1)} custom-call(bf16[3,5,256,2304]{3,2,1,0:T(8,128)(2,1)} %get-tuple-element.247.d, bf16[3,768,384]{2,1,0:T(8,128)(2,1)} %weights_own.3, s32[2]{0:T(128)} %pad_add_fusion.spot.refs_0_, bf16[3,384,384]{2,1,0:T(8,128)(2,1)} %copy-done.19, bf16[3,384,384]{2,1,0:T(8,128)(2,1)} %copy-done.20, ...), custom_call_target="tpu_custom_call" | custom-call | flops 9333332992 | bytes 20000000 | tf_op jit(solution)/shard_map/pallas_call | solution.py:745
  344.3 12.5 %shard_map.345 = (bf16[2,768,384]{2,1,0:T(8,128)(2,1)}, bf16[2,768,384]{2,1,0:T(8,128)(2,1)}) custom-call(s32[2]{0:T(128)} %pad_add_fusion.spot.refs_0_, bf16[768,3840]{1,0:T(8,128)(2,1)} %get-tuple-element.177.xt, bf16[3840,2304]{1,0:T(8,128)(2,1)} %bitcast.127, bf16[768,384]{1,0:T(8,128)(2,1)} %get-tuple-element.236.proj), custom_call_target="tpu_custom_call" | custom-call | flops 7000000000 | bytes 16000000 | tf_op jit(solution)/shard_map/pallas_call | solution.py:780
  361.0 10.6 %shard_map.346.up_a.up_b = bf16[3,1024,768]{2,1,0:T(8,128)(2,1)} custom-call(bf16[3,5,256,2304]{3,2,1,0:T(8,128)(2,1)} %get-tuple-element.247.d, bf16[3,768,384]{2,1,0:T(8,128)(2,1)} %weights_own.3, s32[2]{0:T(128)} %pad_add_fusion.spot.refs_0_, bf16[3,384,384]{2,1,0:T(8,128)(2,1)} %copy-done.19, ...), custom_call_target="tpu_custom_call", output_to_operand_aliasing={{}: (6, {})} | custom-call | flops 4666666496 | bytes 10000000 | tf_op jit(solution)/shard_map/pallas_call | solution.py:745
  377.6 2.1 fusion.10
  382.4 15.2 %shard_map.347 = (bf16[2048,768]{1,0:T(8,128)(2,1)}, f32[8,768]{1,0:T(8,128)}, f32[2,384,1536]{2,1,0:T(8,128)}, f32[1536,768]{1,0:T(8,128)}) custom-call(s32[2]{0:T(128)} %pad_add_fusion.spot.refs_0_, bf16[4096,768]{1,0:T(8,128)(2,1)} %x.3, bf16[2048,768]{1,0:T(8,128)(2,1)} %get-tuple-element.176.middle_grad, bf16[3,1024,768]{2,1,0:T(8,128)(2,1)} %shard_map.346.up_a.up_b, ...), custom_call_target="tpu_custom_call" | custom-call | flops 100000000 | bytes 35000000 | tf_op jit(solution)/shard_map/pallas_call | solution.py:839
  399.4 32.0 %shard_map.348 = (bf16[4,768,384]{2,1,0:T(8,128)(2,1)S(1)}, f32[24,768]{1,0:T(8,128)S(1)}, f32[56,128]{1,0:T(8,128)S(1)}) custom-call(bf16[384,384]{1,0:T(8,128)(2,1)S(1)} %get-tuple-element.293.refs_0_, bf16[384,384]{1,0:T(8,128)(2,1)S(1)} %get-tuple-element.292.refs_1_, f32[8,768]{1,0:T(8,128)S(1)} %copy-done.8, f32[8,768]{1,0:T(8,128)S(1)} %copy-done.7, ...), custom_call_target="tpu_custom_call" | custom-call | tf_op jit(solution)/shard_map/pallas_call | solution.py:1016
  431.5 2.0 slice_convert_fusion
  (163 shorter events, 49.7 us)
Async XLA Ops:
  1.9 22.7 %collective-permute-start = (bf16[3,384,384]{2,1,0:T(8,128)(2,1)S(1)}, bf16[3,384,384]{2,1,0:T(8,128)(2,1)S(1)}, u32[]{:S(2)}, u32[]{:S(2)}) collective-permute-start(bf16[3,384,384]{2,1,0:T(8,128)(2,1)S(1)} %constant_dynamic-slice_fusion.2), channel_id=1, source_target_pairs={{0,1},{1,0},{2,3},{3,2},{4,5},{5,4},{6,7},{7,6},{8,9},{9,8},{10,11... | collective-permute-start | bytes 2654216 | tf_op jit(solution)/shard_map/ppermute | solution.py:1163
  5.0 57.4 %collective-permute-start.1 = (bf16[2,384]{1,0:T(2,128)(2,1)}, bf16[2,384]{1,0:T(2,128)(2,1)}, u32[]{:S(2)}, u32[]{:S(2)}) collective-permute-start(bf16[2,384]{1,0:T(2,128)(2,1)} %bias.3), channel_id=1, source_target_pairs={{0,1},{1,0},{2,3},{3,2},{4,5},{5,4},{6,7},{7,6},{8,9},{9,8},{10,11... | collective-permute-start | bytes 4616 | tf_op jit(solution)/shard_map/ppermute | solution.py:1163
  24.6 37.7 %collective-permute-start.2 = (bf16[3,384,384]{2,1,0:T(8,128)(2,1)S(1)}, bf16[3,384,384]{2,1,0:T(8,128)(2,1)S(1)}, u32[]{:S(2)}, u32[]{:S(2)}) collective-permute-start(bf16[3,384,384]{2,1,0:T(8,128)(2,1)S(1)} %collective-permute-done.mine), channel_id=1, source_target_pairs={{0,2},{2,0},{4,6},{6,4},{8,10},{10,8},{12,14},{14,12},{16,18},{18,... | collective-permute-start | bytes 2654216 | tf_op jit(solution)/shard_map/ppermute | solution.py:1048
  24.6 71.9 %collective-permute-start.3 = (bf16[384,1536]{1,0:T(8,128)(2,1)S(1)}, bf16[384,1536]{1,0:T(8,128)(2,1)}, u32[]{:S(2)}, u32[]{:S(2)}) collective-permute-start(bf16[384,1536]{1,0:T(8,128)(2,1)S(1)} %constant_dynamic-slice_fusion.1), channel_id=1, source_target_pairs={{0,1},{1,0},{2,3},{3,2},{4,5},{5,4},{6,7},{7,6},{8,9},{9,8},{10,11... | collective-permute-start | bytes 3538952 | tf_op jit(solution)/shard_map/ppermute | solution.py:1163
  26.4 70.1 %collective-permute-start.4 = (bf16[1536,384]{1,0:T(8,128)(2,1)S(1)}, bf16[1536,384]{1,0:T(8,128)(2,1)}, u32[]{:S(2)}, u32[]{:S(2)}) collective-permute-start(bf16[1536,384]{1,0:T(8,128)(2,1)S(1)} %constant_dynamic-slice_fusion), channel_id=1, source_target_pairs={{0,1},{1,0},{2,3},{3,2},{4,5},{5,4},{6,7},{7,6},{8,9},{9,8},{10,11... | collective-permute-start | bytes 3538952 | tf_op jit(solution)/shard_map/ppermute | solution.py:1163
  26.7 69.8 %collective-permute-start.5 = (bf16[384,768]{1,0:T(8,128)(2,1)}, bf16[384,768]{1,0:T(8,128)(2,1)}, u32[]{:S(2)}, u32[]{:S(2)}) collective-permute-start(bf16[384,768]{1,0:T(8,128)(2,1)} %proj_own.3), channel_id=1, source_target_pairs={{0,1},{1,0},{2,3},{3,2},{4,5},{5,4},{6,7},{7,6},{8,9},{9,8},{10,11... | collective-permute-start | bytes 1769480 | tf_op jit(solution)/shard_map/ppermute | solution.py:1163
  96.5 13.8 %collective-permute-start.6 = (bf16[384,1536]{1,0:T(8,128)(2,1)}, bf16[384,1536]{1,0:T(8,128)(2,1)S(1)}, u32[]{:S(2)}, u32[]{:S(2)}) collective-permute-start(bf16[384,1536]{1,0:T(8,128)(2,1)} %collective-permute-done.3.one_b), channel_id=1, source_target_pairs={{0,2},{2,0},{4,6},{6,4},{8,10},{10,8},{12,14},{14,12},{16,18},{18,... | collective-permute-start | bytes 3538952 | tf_op jit(solution)/shard_map/ppermute | solution.py:1048
  96.6 13.8 %collective-permute-start.8 = (bf16[1536,384]{1,0:T(8,128)(2,1)}, bf16[1536,384]{1,0:T(8,128)(2,1)}, u32[]{:S(2)}, u32[]{:S(2)}) collective-permute-start(bf16[1536,384]{1,0:T(8,128)(2,1)} %collective-permute-done.4.two_b), channel_id=1, source_target_pairs={{0,2},{2,0},{4,6},{6,4},{8,10},{10,8},{12,14},{14,12},{16,18},{18,... | collective-permute-start | bytes 3538952 | tf_op jit(solution)/shard_map/ppermute | solution.py:1048
  97.1 13.2 %collective-permute-start.7 = (bf16[1536]{0:T(1024)(128)(2,1)S(1)}, bf16[1536]{0:T(1024)(128)(2,1)S(1)}, u32[]{:S(2)}, u32[]{:S(2)}) collective-permute-start(bf16[1536]{0:T(1024)(128)(2,1)S(1)} %copy-done.33), channel_id=1, source_target_pairs={{0,1},{1,0},{2,3},{3,2},{4,5},{5,4},{6,7},{7,6},{8,9},{9,8},{10,11... | collective-permute-start | bytes 9224 | tf_op jit(solution)/shard_map/ppermute | solution.py:1163
  189.8 18.1 %collective-permute-start.10 = (bf16[2,2,2,2,192,384]{5,4,3,2,1,0:T(8,128)(2,1)}, bf16[2,2,2,2,192,384]{5,4,3,2,1,0:T(8,128)(2,1)}, u32[]{:S(2)}, u32[]{:S(2)}) collective-permute-start(bf16[2,2,2,2,192,384]{5,4,3,2,1,0:T(8,128)(2,1)} %bitcast.148), channel_id=1, source_target_pairs={{0,2},{2,0},{4,6},{6,4},{8,10},{10,8},{12,14},{14,12},{16,18},{18,... | collective-permute-start | bytes 7077896 | tf_op jit(solution)/shard_map/ppermute | solution.py:1048
  189.9 18.0 %collective-permute-start.9 = (bf16[2,2,2,2,48,1536]{5,4,3,2,1,0:T(8,128)(2,1)}, bf16[2,2,2,2,48,1536]{5,4,3,2,1,0:T(8,128)(2,1)S(1)}, u32[]{:S(2)}, u32[]{:S(2)}) collective-permute-start(bf16[2,2,2,2,48,1536]{5,4,3,2,1,0:T(8,128)(2,1)} %bitcast.147), channel_id=1, source_target_pairs={{0,2},{2,0},{4,6},{6,4},{8,10},{10,8},{12,14},{14,12},{16,18},{18,... | collective-permute-start | bytes 7077896 | tf_op jit(solution)/shard_map/ppermute | solution.py:1048
  212.6 32.5 %collective-permute-start.11 = (bf16[2,2,2,48,1536]{4,3,2,1,0:T(8,128)(2,1)}, bf16[2,2,2,48,1536]{4,3,2,1,0:T(8,128)(2,1)S(1)}, u32[]{:S(2)}, u32[]{:S(2)}) collective-permute-start(bf16[2,2,2,48,1536]{4,3,2,1,0:T(8,128)(2,1)} %fusion), channel_id=1, source_target_pairs={{0,1},{1,0},{2,3},{3,2},{4,5},{5,4},{6,7},{7,6},{8,9},{9,8},{10,11... | collective-permute-start | bytes 3538952 | tf_op jit(solution)/shard_map/ppermute | solution.py:1047
  214.4 30.8 %collective-permute-start.12 = (bf16[2,2,2,192,384]{4,3,2,1,0:T(8,128)(2,1)}, bf16[2,2,2,192,384]{4,3,2,1,0:T(8,128)(2,1)}, u32[]{:S(2)}, u32[]{:S(2)}) collective-permute-start(bf16[2,2,2,192,384]{4,3,2,1,0:T(8,128)(2,1)} %fusion.1), channel_id=1, source_target_pairs={{0,4},{2,6},{4,0},{6,2},{8,12},{10,14},{12,8},{14,10},{16,20},{18,... | collective-permute-start | bytes 3538952 | tf_op jit(solution)/shard_map/ppermute | solution.py:1048
  250.1 15.0 %collective-permute-start.13 = (bf16[2,2,48,1536]{3,2,1,0:T(8,128)(2,1)}, bf16[2,2,48,1536]{3,2,1,0:T(8,128)(2,1)}, u32[]{:S(2)}, u32[]{:S(2)}) collective-permute-start(bf16[2,2,48,1536]{3,2,1,0:T(8,128)(2,1)} %fusion.3), channel_id=1, source_target_pairs={{0,4},{2,6},{4,0},{6,2},{8,12},{10,14},{12,8},{14,10},{16,20},{18,... | collective-permute-start | bytes 1769480 | tf_op jit(solution)/shard_map/ppermute | solution.py:1048
  250.7 14.8 %collective-permute-start.14 = (bf16[2,2,192,384]{3,2,1,0:T(8,128)(2,1)}, bf16[2,2,192,384]{3,2,1,0:T(8,128)(2,1)}, u32[]{:S(2)}, u32[]{:S(2)}) collective-permute-start(bf16[2,2,192,384]{3,2,1,0:T(8,128)(2,1)} %fusion.2), channel_id=1, source_target_pairs={{0,8},{2,10},{4,12},{6,14},{8,0},{10,2},{12,4},{14,6},{16,24},{18,... | collective-permute-start | bytes 1769480 | tf_op jit(solution)/shard_map/ppermute | solution.py:1048
  269.5 13.8 %collective-permute-start.17 = (bf16[2,768,384]{2,1,0:T(8,128)(2,1)}, bf16[2,768,384]{2,1,0:T(8,128)(2,1)}, u32[]{:S(2)}, u32[]{:S(2)}) collective-permute-start(bf16[2,768,384]{2,1,0:T(8,128)(2,1)} %get-tuple-element.212), channel_id=1, source_target_pairs={{0,2},{2,0},{4,6},{6,4},{8,10},{10,8},{12,14},{14,12},{16,18},{18,... | collective-permute-start | bytes 3538952 | tf_op jit(solution)/shard_map/ppermute | solution.py:1048
  269.5 13.8 %collective-permute-start.15 = (bf16[2,48,1536]{2,1,0:T(8,128)(2,1)}, bf16[2,48,1536]{2,1,0:T(8,128)(2,1)S(1)}, u32[]{:S(2)}, u32[]{:S(2)}) collective-permute-start(bf16[2,48,1536]{2,1,0:T(8,128)(2,1)} %fusion.13), channel_id=1, source_target_pairs={{0,8},{2,10},{4,12},{6,14},{8,0},{10,2},{12,4},{14,6},{16,24},{18,... | collective-permute-start | bytes 884744 | tf_op jit(solution)/shard_map/ppermute | solution.py:1048
  271.1 12.1 %collective-permute-start.16 = (bf16[2,192,384]{2,1,0:T(8,128)(2,1)}, bf16[2,192,384]{2,1,0:T(8,128)(2,1)}, u32[]{:S(2)}, u32[]{:S(2)}) collective-permute-start(bf16[2,192,384]{2,1,0:T(8,128)(2,1)} %fusion.12), channel_id=1, source_target_pairs={{0,1},{1,0},{2,3},{3,2},{4,5},{5,4},{6,7},{7,6},{8,9},{9,8},{10,11... | collective-permute-start | bytes 884744 | tf_op jit(solution)/shard_map/ppermute | solution.py:1047
  289.6 24.8 %collective-permute-start.20 = (bf16[768,384]{1,0:T(8,128)(2,1)}, bf16[768,384]{1,0:T(8,128)(2,1)S(1)}, u32[]{:S(2)}, u32[]{:S(2)}) collective-permute-start(bf16[768,384]{1,0:T(8,128)(2,1)} %get-tuple-element.222), channel_id=1, source_target_pairs={{0,1},{1,0},{2,3},{3,2},{4,5},{5,4},{6,7},{7,6},{8,9},{9,8},{10,11... | collective-permute-start | bytes 1769480 | tf_op jit(solution)/shard_map/ppermute | solution.py:1047
  291.2 23.2 %collective-permute-start.18 = (bf16[48,1536]{1,0:T(8,128)(2,1)}, bf16[48,1536]{1,0:T(8,128)(2,1)S(1)}, u32[]{:S(2)}, u32[]{:S(2)}) collective-permute-start(bf16[48,1536]{1,0:T(8,128)(2,1)} %fusion.19), channel_id=1, source_target_pairs={{0,16},{2,18},{4,20},{6,22},{8,24},{10,26},{12,28},{14,30},{16,0},... | collective-permute-start | bytes 442376 | tf_op jit(solution)/shard_map/ppermute | solution.py:1048
  293.7 20.7 %collective-permute-start.19 = (bf16[192,384]{1,0:T(8,128)(2,1)}, bf16[192,384]{1,0:T(8,128)(2,1)}, u32[]{:S(2)}, u32[]{:S(2)}) collective-permute-start(bf16[192,384]{1,0:T(8,128)(2,1)} %fusion.18), channel_id=1, source_target_pairs={{0,16},{2,18},{4,20},{6,22},{8,24},{10,26},{12,28},{14,30},{16,0},... | collective-permute-start | bytes 442376 | tf_op jit(solution)/shard_map/ppermute | solution.py:1048
  318.5 21.3 %collective-permute-start.23 = (bf16[768,384]{1,0:T(8,128)(2,1)S(1)}, bf16[768,384]{1,0:T(8,128)(2,1)S(1)}, u32[]{:S(2)}, u32[]{:S(2)}) collective-permute-start(bf16[768,384]{1,0:T(8,128)(2,1)S(1)} %copy-done.21), channel_id=1, source_target_pairs={{0,1},{1,0},{2,3},{3,2},{4,5},{5,4},{6,7},{7,6},{8,9},{9,8},{10,11... | collective-permute-start | bytes 1769480 | tf_op jit(solution)/shard_map/ppermute | solution.py:1047
  319.1 20.7 %collective-permute-start.21 = (bf16[48,1536]{1,0:T(8,128)(2,1)S(1)}, bf16[48,1536]{1,0:T(8,128)(2,1)S(1)}, u32[]{:S(2)}, u32[]{:S(2)}) collective-permute-start(bf16[48,1536]{1,0:T(8,128)(2,1)S(1)} %fusion.17), channel_id=1, source_target_pairs={{0,16},{2,18},{4,20},{6,22},{8,24},{10,26},{12,28},{14,30},{16,0},... | collective-permute-start | bytes 442376 | tf_op jit(solution)/shard_map/ppermute | solution.py:1048
  321.7 18.2 %collective-permute-start.22 = (bf16[192,384]{1,0:T(8,128)(2,1)S(1)}, bf16[192,384]{1,0:T(8,128)(2,1)S(1)}, u32[]{:S(2)}, u32[]{:S(2)}) collective-permute-start(bf16[192,384]{1,0:T(8,128)(2,1)S(1)} %fusion.15), channel_id=1, source_target_pairs={{0,16},{2,18},{4,20},{6,22},{8,24},{10,26},{12,28},{14,30},{16,0},... | collective-permute-start | bytes 442376 | tf_op jit(solution)/shard_map/ppermute | solution.py:1048
  340.8 16.0 %collective-permute-start.26 = (bf16[384,768]{1,0:T(8,128)(2,1)S(1)}, bf16[384,768]{1,0:T(8,128)(2,1)S(1)}, u32[]{:S(2)}, u32[]{:S(2)}) collective-permute-start(bf16[384,768]{1,0:T(8,128)(2,1)S(1)} %dynamic-slice_bitcast_fusion), channel_id=1, source_target_pairs={{0,1},{1,0},{2,3},{3,2},{4,5},{5,4},{6,7},{7,6},{8,9},{9,8},{10,11... | collective-permute-start | bytes 1769480 | tf_op jit(solution)/shard_map/ppermute | solution.py:1047
  342.4 14.5 %collective-permute-start.24 = (bf16[2,48,1536]{2,1,0:T(8,128)(2,1)S(1)}, bf16[2,48,1536]{2,1,0:T(8,128)(2,1)S(1)}, u32[]{:S(2)}, u32[]{:S(2)}) collective-permute-start(bf16[2,48,1536]{2,1,0:T(8,128)(2,1)S(1)} %broadcast_select_fusion.5), channel_id=1, source_target_pairs={{0,8},{2,10},{4,12},{6,14},{8,0},{10,2},{12,4},{14,6},{16,24},{18,... | collective-permute-start | bytes 884744 | tf_op jit(solution)/shard_map/ppermute | solution.py:1048
  342.8 14.0 %collective-permute-start.25 = (bf16[2,192,384]{2,1,0:T(8,128)(2,1)S(1)}, bf16[2,192,384]{2,1,0:T(8,128)(2,1)S(1)}, u32[]{:S(2)}, u32[]{:S(2)}) collective-permute-start(bf16[2,192,384]{2,1,0:T(8,128)(2,1)S(1)} %broadcast_select_fusion.4), channel_id=1, source_target_pairs={{0,4},{2,6},{4,0},{6,2},{8,12},{10,14},{12,8},{14,10},{16,20},{18,... | collective-permute-start | bytes 884744 | tf_op jit(solution)/shard_map/ppermute | solution.py:1048
  357.2 16.6 %collective-permute-start.29 = (bf16[2,768,384]{2,1,0:T(8,128)(2,1)}, bf16[2,768,384]{2,1,0:T(8,128)(2,1)}, u32[]{:S(2)}, u32[]{:S(2)}) collective-permute-start(bf16[2,768,384]{2,1,0:T(8,128)(2,1)} %get-tuple-element.250), channel_id=1, source_target_pairs={{0,2},{2,0},{4,6},{6,4},{8,10},{10,8},{12,14},{14,12},{16,18},{18,... | collective-permute-start | bytes 3538952 | tf_op jit(solution)/shard_map/ppermute | solution.py:1048
  357.2 15.7 %collective-permute-start.27 = (bf16[2,2,48,1536]{3,2,1,0:T(8,128)(2,1)S(1)}, bf16[2,2,48,1536]{3,2,1,0:T(8,128)(2,1)S(1)}, u32[]{:S(2)}, u32[]{:S(2)}) collective-permute-start(bf16[2,2,48,1536]{3,2,1,0:T(8,128)(2,1)S(1)} %broadcast_select_fusion.3), channel_id=1, source_target_pairs={{0,4},{2,6},{4,0},{6,2},{8,12},{10,14},{12,8},{14,10},{16,20},{18,... | collective-permute-start | bytes 1769480 | tf_op jit(solution)/shard_map/ppermute | solution.py:1048
  357.9 15.5 %collective-permute-start.28 = (bf16[2,2,192,384]{3,2,1,0:T(8,128)(2,1)S(1)}, bf16[2,2,192,384]{3,2,1,0:T(8,128)(2,1)}, u32[]{:S(2)}, u32[]{:S(2)}) collective-permute-start(bf16[2,2,192,384]{3,2,1,0:T(8,128)(2,1)S(1)} %broadcast_select_fusion.2), channel_id=1, source_target_pairs={{0,8},{2,10},{4,12},{6,14},{8,0},{10,2},{12,4},{14,6},{16,24},{18,... | collective-permute-start | bytes 1769480 | tf_op jit(solution)/shard_map/ppermute | solution.py:1048
  379.7 18.0 %collective-permute-start.33 = (bf16[384,384]{1,0:T(8,128)(2,1)}, bf16[384,384]{1,0:T(8,128)(2,1)}, u32[]{:S(2)}, u32[]{:S(2)}) collective-permute-start(bf16[384,384]{1,0:T(8,128)(2,1)} %get-tuple-element.266), channel_id=1, source_target_pairs={{0,4},{2,6},{4,0},{6,2},{8,12},{10,14},{12,8},{14,10},{16,20},{18,... | collective-permute-start | bytes 884744 | tf_op jit(solution)/shard_map/ppermute | solution.py:1048
  380.8 16.9 %collective-permute-start.34 = (bf16[384,384]{1,0:T(8,128)(2,1)}, bf16[384,384]{1,0:T(8,128)(2,1)}, u32[]{:S(2)}, u32[]{:S(2)}) collective-permute-start(bf16[384,384]{1,0:T(8,128)(2,1)} %get-tuple-element.267), channel_id=1, source_target_pairs={{0,8},{2,10},{4,12},{6,14},{8,0},{10,2},{12,4},{14,6},{16,24},{18,... | collective-permute-start | bytes 884744 | tf_op jit(solution)/shard_map/ppermute | solution.py:1048
  (38 other events, 243.8 us)

commit v7 on v6

--- a/solution.py
+++ b/solution.py
@@ -417,18 +417,29 @@
         two[:, pl.ds(theirs, HALF)] = two_c[...]
 
     total = jnp.zeros((1, CHUNK), F32)
+    def starts(t):
+        rows = slice(t * 256, t * 256 + 256)
+        return dot(normed[rows, :], one[...]), dot(cot[rows, :], two[...], NT)
+
+    now = starts(0)
     for t in range(OWN // 256):
         rows = slice(t * 256, t * 256 + 256)
-        pre = dot(normed[rows, :], one[...]) + bias[...]
+        ahead = starts(t + 1) if t + 1 < OWN // 256 else None
+        pre = now[0] + bias[...]
         phi = 0.5 * (1.0 + lax.erf(pre * 0.7071067811865476))
         slope = phi + pre * (jnp.exp(-0.5 * pre * pre) * 0.3989422804014327)
         low = (pre * phi).astype(BF)
-        grad = (dot(cot[rows, :], two[...], NT) * slope).astype(BF)
+        grad = (now[1] * slope).astype(BF)
         hidden[rows, :] = low
         grads[rows, :] = grad
         total += jnp.sum(grad.astype(F32), axis=0, keepdims=True)
-        forward[rows, :] += dot(low, two[...])
-        back[rows, :] += dot(grad, one[...], NT)
+        if t:
+            before = slice(t * 256 - 256, t * 256)
+            forward[before, :] += dot(last[0], two[...])
+            back[before, :] += dot(last[1], one[...], NT)
+        last, now = (low, grad), ahead
+    forward[OWN - 256 :, :] += dot(last[0], two[...])
+    back[OWN - 256 :, :] += dot(last[1], one[...], NT)
     sums[...] = total
 
     first = spot[1] == 0

time: 446 us -> 444 us (level)
  transfers between devices with their start and end apart: 35 -> 35, of which waited for: 5 -> 5; matrix products, arithmetic and copies ran while one was open for 2% -> 2% of each run, Pallas kernels for 54% -> 55%
where the time goes in v7:
time: 444 us; the launch traced here: 435 us
  Pallas kernels  346 us (78%)
  starting transfers between devices  33.3 us (7%)
  other arithmetic  31.2 us (7%)
  local copies, waits for them, and re-layouts  16.4 us (4%)
  waiting for transfers between devices  6.12 us (1%)
    pallas_call x1, Pallas kernels, feed(): pl.pallas_call(feed_kernel, grid_spec=pltpu.PrefetchScalarGridSpec(num_sc...  76.1 us
    pallas_call x2, Pallas kernels, attend(): pl.pallas_call(attend_own if first else attend_other, grid=(3, NWIN), in_...  67.1 us
    pallas_call x3, Pallas kernels, attend_back(): pl.pallas_call(lambda *refs: attend_back_kernel(first, *refs), grid_spec=...  61.2 us
    pallas_call x1, Pallas kernels, last_sums(): pl.pallas_call(lambda *refs: last_kernel(bits, plans, orders, *refs), in_...  32 us
    pallas_call x2, Pallas kernels, norm_grad(): pl.pallas_call(norm_grad_kernel, grid=(last - first, 2), in_specs=[block,...  27.3 us
    convert_element_type x13, other arithmetic, part(): return total.astype(BF)  25.5 us
    pallas_call x2, Pallas kernels, qkv_grad(): pl.pallas_call(qkv_grad_kernel, grid=(3,), in_specs=[SCALAR, pl.BlockSpec...  25 us
    ppermute x23, starting transfers between devices, exchange(): lax.ppermute(value, 'dp', [(i, i ^ bit) for i in range(lax.axis_size('dp'...  19.6 us
  transfers between devices with their start and end apart: 35, of which 5 were waited for; matrix products, arithmetic and copies ran while one was open for 2% of the time, Pallas kernels for 55%

profile of v7, /device:TPU:0, one launch (start us, length us, event | category | flops | bytes accessed | tf_op | source)
XLA Modules:
  0.0 435.2 jit_solution(6824151125585927588)
XLA Ops:
  1.9 3.0 collective-permute-start
  5.0 4.6 %shard_map.334.cot_t = bf16[768,2048]{1,0:T(8,128)(2,1)} custom-call(bf16[2048,768]{1,0:T(8,128)(2,1)} %cot.3), custom_call_target="tpu_custom_call" | custom-call | flops 1000000 | bytes 6000000 | tf_op jit(solution)/shard_map/pallas_call | solution.py:376
  10.2 8.7 %shard_map.333.x = bf16[3,5,256,768]{3,2,1,0:T(8,128)(2,1)} custom-call(s32[2]{0:T(128)} %pad_add_fusion.spot.refs_0_, bf16[4096,768]{1,0:T(8,128)(2,1)} %x.3, bf16[4096,768]{1,0:T(8,128)(2,1)} %x.3, bf16[4096,768]{1,0:T(8,128)(2,1)} %x.3, bf16[4096,768]{1,0:T(8,128)(2,1)} %x.3, bf16[4096,768]{1,0:T(8,128)(2,1)} %x.3, bf16[4096,768]{1,0:T(8,128)(2,1)} %x.3, ...), custom_call_target="tpu_custom_call" | custom-call | flops 660602880 | bytes 10000000 | tf_op jit(solution)/shard_map/pallas_call | solution.py:134
  21.0 3.6 collective-permute-done.mine
  24.6 1.7 collective-permute-start.3
  28.4 33.9 %shard_map.335 = (bf16[3,5,256,1152]{3,2,1,0:T(8,128)(2,1)}, bf16[3,5,6,224,256]{4,3,2,1,0:T(8,128)(2,1)}, bf16[3,5,256,384]{3,2,1,0:T(8,128)(2,1)}, bf16[768,38...) custom-call(bf16[3,5,256,768]{3,2,1,0:T(8,128)(2,1)} %shard_map.333.x, bf16[2,384]{1,0:T(2,128)(2,1)} %bias.3, ...), custom_call_target="tpu_custom_call" | custom-call | flops 15000000512 | bytes 45000000 | tf_op jit(solution)/shard_map/pallas_call | solution.py:297
  63.3 33.2 %shard_map.336 = (bf16[3,5,256,1152]{3,2,1,0:T(8,128)(2,1)}, bf16[3,5,6,224,256]{4,3,2,1,0:T(8,128)(2,1)}, bf16[3,5,256,384]{3,2,1,0:T(8,128)(2,1)}) custom-call(bf16[3,5,256,768]{3,2,1,0:T(8,128)(2,1)} %shard_map.333.x, bf16[2,384]{1,0:T(2,128)(2,1)} %collective-permute-done.1.bias, s32[2]{0:T(128)} %pad_add_fusion.spot.refs_0_, ...), custom_call_target="tpu_custom_call" | custom-call | flops 15000000512 | bytes 45000000 | tf_op jit(solution)/shard_map/pallas_call | solution.py:297
  97.4 12.9 %shard_map.337 = (bf16[2048,768]{1,0:T(8,128)(2,1)}, bf16[2048,768]{1,0:T(8,128)(2,1)}, bf16[768,2048]{1,0:T(8,128)(2,1)}, bf16[2048,768]{1,0:T(8,128)(2,1)}) custom-call(s32[2]{0:T(128)} %pad_add_fusion.spot.refs_0_, bf16[3,5,256,384]{3,2,1,0:T(8,128)(2,1)} %get-tuple-element.153.own_a.own_b, bf16[3,5,256,384]{3,2,1,0:T(8,128)(2,1)} %get-tuple-element.153.own_a.own_b, ...), custom_call_target="tpu_custom_call" | custom-call | flops 3000000000 | bytes 25000000 | tf_op jit(solution)/shard_map/pallas_call | solution.py:343
  111.4 76.1 %shard_map.338 = (bf16[2048,768]{1,0:T(8,128)(2,1)}, bf16[2048,768]{1,0:T(8,128)(2,1)}, bf16[2,384,1536]{2,1,0:T(8,128)(2,1)}, bf16[2,384,1536]{2,1,0:T(8,128)(2...) custom-call(s32[2]{0:T(128)} %pad_add_fusion.spot.refs_0_, ...), custom_call_target="tpu_custom_call" | custom-call | flops 57999998976 | bytes 60000000 | tf_op jit(solution)/shard_map/pallas_call | solution.py:473
  189.4 16.2 %shard_map.339 = (bf16[2048,768]{1,0:T(8,128)(2,1)}, bf16[2048,768]{1,0:T(8,128)(2,1)}, bf16[2048,768]{1,0:T(8,128)(2,1)}, bf16[768,384]{1,0:T(8,128)(2,1)}, bf16[768,384]{1,0:T(8,128)(2,1)}, /*index=5*/f32[8,768]{1,0:T(8,128)}) custom-call(bf16[2048,768]{1,0:T(8,128)(2,1)} %get-tuple-element.171.middle, bf16[2048,768]{1,0:T(8,128)(2,1)} %get-tuple-element.172.forward, ...), custom_call_target="tpu_custom_call" | custom-call | flops 5000000000 | bytes 40000000 | tf_op jit(solution)/shard_map/pallas_call | solution.py:563
  207.7 2.6 fusion.1
  210.3 1.8 collective-permute-start.11
  213.5 29.3 %shard_map.340 = (bf16[3,5,256,2304]{3,2,1,0:T(8,128)(2,1)}, f32[80,128]{1,0:T(8,128)}, f32[8,1152]{1,0:T(8,128)}) custom-call(s32[2]{0:T(128)} %pad_add_fusion.spot.refs_0_, bf16[3,5,256,1152]{3,2,1,0:T(8,128)(2,1)} %get-tuple-element.189.refs_1_, bf16[3,5,6,224,256]{4,3,2,1,0:T(8,128)(2,1)} %get-tuple-element.190.refs_2_, ...), custom_call_target="tpu_custom_call" | custom-call | flops 20000000000 | bytes 45000000 | tf_op jit(solution)/shard_map/pallas_call | solution.py:703
  242.8 2.5 fusion.3
  245.4 2.5 fusion.2
  250.0 12.5 %shard_map.341 = (bf16[2,768,384]{2,1,0:T(8,128)(2,1)}, bf16[2,768,384]{2,1,0:T(8,128)(2,1)}) custom-call(s32[2]{0:T(128)} %pad_add_fusion.spot.refs_0_, bf16[768,3840]{1,0:T(8,128)(2,1)} %get-tuple-element.177.xt, bf16[3840,2304]{1,0:T(8,128)(2,1)} %bitcast.126, bf16[768,384]{1,0:T(8,128)(2,1)} %get-tuple-element.198.proj), custom_call_target="tpu_custom_call" | custom-call | flops 7000000000 | bytes 16000000 | tf_op jit(solution)/shard_map/pallas_call | solution.py:791
  263.2 1.9 fusion.13
  265.1 2.1 fusion.12
  269.3 11.6 %shard_map.342 = (bf16[3,5,256,2304]{3,2,1,0:T(8,128)(2,1)}, f32[80,128]{1,0:T(8,128)}, f32[8,1152]{1,0:T(8,128)}) custom-call(s32[2]{0:T(128)} %pad_add_fusion.spot.refs_0_, bf16[3,5,256,1152]{3,2,1,0:T(8,128)(2,1)} %get-tuple-element.178.refs_1_, bf16[3,5,6,224,256]{4,3,2,1,0:T(8,128)(2,1)} %get-tuple-element.179.refs_2_, ...), custom_call_target="tpu_custom_call", output_to_operand_aliasing={{0}: (8, {})} | custom-call | flops 6666666496 | bytes 15000000 | tf_op jit(solution)/shard_map/pallas_call | solution.py:703
  281.0 2.5 fusion.5
  283.6 2.0 fusion.18
  285.5 1.8 fusion.19
  288.9 2.6 collective-permute-start.18
  291.8 20.3 %shard_map.343 = (bf16[3,5,256,2304]{3,2,1,0:T(8,128)(2,1)}, f32[80,128]{1,0:T(8,128)}, f32[8,1152]{1,0:T(8,128)}) custom-call(s32[2]{0:T(128)} %pad_add_fusion.spot.refs_0_, bf16[3,5,256,1152]{3,2,1,0:T(8,128)(2,1)} %get-tuple-element.178.refs_1_, bf16[3,5,6,224,256]{4,3,2,1,0:T(8,128)(2,1)} %get-tuple-element.179.refs_2_, ...), custom_call_target="tpu_custom_call", output_to_operand_aliasing={{0}: (8, {})} | custom-call | flops 13333332992 | bytes 30000000 | tf_op jit(solution)/shard_map/pallas_call | solution.py:703
  316.8 2.6 collective-permute-start.21
  319.7 16.7 %shard_map.344.refs_0_ = bf16[3,1024,768]{2,1,0:T(8,128)(2,1)} custom-call(bf16[3,5,256,2304]{3,2,1,0:T(8,128)(2,1)} %get-tuple-element.247.d, bf16[3,768,384]{2,1,0:T(8,128)(2,1)} %weights_own.3, s32[2]{0:T(128)} %pad_add_fusion.spot.refs_0_, bf16[3,384,384]{2,1,0:T(8,128)(2,1)} %copy-done.19, bf16[3,384,384]{2,1,0:T(8,128)(2,1)} %copy-done.20, ...), custom_call_target="tpu_custom_call" | custom-call | flops 9333332992 | bytes 20000000 | tf_op jit(solution)/shard_map/pallas_call | solution.py:756
  342.0 12.5 %shard_map.345 = (bf16[2,768,384]{2,1,0:T(8,128)(2,1)}, bf16[2,768,384]{2,1,0:T(8,128)(2,1)}) custom-call(s32[2]{0:T(128)} %pad_add_fusion.spot.refs_0_, bf16[768,3840]{1,0:T(8,128)(2,1)} %get-tuple-element.177.xt, bf16[3840,2304]{1,0:T(8,128)(2,1)} %bitcast.127, bf16[768,384]{1,0:T(8,128)(2,1)} %get-tuple-element.236.proj), custom_call_target="tpu_custom_call" | custom-call | flops 7000000000 | bytes 16000000 | tf_op jit(solution)/shard_map/pallas_call | solution.py:791
  358.7 10.6 %shard_map.346.up_a.up_b = bf16[3,1024,768]{2,1,0:T(8,128)(2,1)} custom-call(bf16[3,5,256,2304]{3,2,1,0:T(8,128)(2,1)} %get-tuple-element.247.d, bf16[3,768,384]{2,1,0:T(8,128)(2,1)} %weights_own.3, s32[2]{0:T(128)} %pad_add_fusion.spot.refs_0_, bf16[3,384,384]{2,1,0:T(8,128)(2,1)} %copy-done.19, ...), custom_call_target="tpu_custom_call", output_to_operand_aliasing={{}: (6, {})} | custom-call | flops 4666666496 | bytes 10000000 | tf_op jit(solution)/shard_map/pallas_call | solution.py:756
  375.3 2.1 fusion.10
  380.1 15.2 %shard_map.347 = (bf16[2048,768]{1,0:T(8,128)(2,1)}, f32[8,768]{1,0:T(8,128)}, f32[2,384,1536]{2,1,0:T(8,128)}, f32[1536,768]{1,0:T(8,128)}) custom-call(s32[2]{0:T(128)} %pad_add_fusion.spot.refs_0_, bf16[4096,768]{1,0:T(8,128)(2,1)} %x.3, bf16[2048,768]{1,0:T(8,128)(2,1)} %get-tuple-element.176.middle_grad, bf16[3,1024,768]{2,1,0:T(8,128)(2,1)} %shard_map.346.up_a.up_b, ...), custom_call_target="tpu_custom_call" | custom-call | flops 100000000 | bytes 35000000 | tf_op jit(solution)/shard_map/pallas_call | solution.py:850
  397.1 32.0 %shard_map.348 = (bf16[4,768,384]{2,1,0:T(8,128)(2,1)S(1)}, f32[24,768]{1,0:T(8,128)S(1)}, f32[56,128]{1,0:T(8,128)S(1)}) custom-call(bf16[384,384]{1,0:T(8,128)(2,1)S(1)} %get-tuple-element.293.refs_0_, bf16[384,384]{1,0:T(8,128)(2,1)S(1)} %get-tuple-element.292.refs_1_, f32[8,768]{1,0:T(8,128)S(1)} %copy-done.8, f32[8,768]{1,0:T(8,128)S(1)} %copy-done.7, ...), custom_call_target="tpu_custom_call" | custom-call | tf_op jit(solution)/shard_map/pallas_call | solution.py:1027
  429.2 2.0 slice_convert_fusion
  (163 shorter events, 49.7 us)
Async XLA Ops:
  1.9 22.7 %collective-permute-start = (bf16[3,384,384]{2,1,0:T(8,128)(2,1)S(1)}, bf16[3,384,384]{2,1,0:T(8,128)(2,1)S(1)}, u32[]{:S(2)}, u32[]{:S(2)}) collective-permute-start(bf16[3,384,384]{2,1,0:T(8,128)(2,1)S(1)} %constant_dynamic-slice_fusion.2), channel_id=1, source_target_pairs={{0,1},{1,0},{2,3},{3,2},{4,5},{5,4},{6,7},{7,6},{8,9},{9,8},{10,11... | collective-permute-start | bytes 2654216 | tf_op jit(solution)/shard_map/ppermute | solution.py:1174
  5.0 57.4 %collective-permute-start.1 = (bf16[2,384]{1,0:T(2,128)(2,1)}, bf16[2,384]{1,0:T(2,128)(2,1)}, u32[]{:S(2)}, u32[]{:S(2)}) collective-permute-start(bf16[2,384]{1,0:T(2,128)(2,1)} %bias.3), channel_id=1, source_target_pairs={{0,1},{1,0},{2,3},{3,2},{4,5},{5,4},{6,7},{7,6},{8,9},{9,8},{10,11... | collective-permute-start | bytes 4616 | tf_op jit(solution)/shard_map/ppermute | solution.py:1174
  24.6 37.7 %collective-permute-start.2 = (bf16[3,384,384]{2,1,0:T(8,128)(2,1)S(1)}, bf16[3,384,384]{2,1,0:T(8,128)(2,1)S(1)}, u32[]{:S(2)}, u32[]{:S(2)}) collective-permute-start(bf16[3,384,384]{2,1,0:T(8,128)(2,1)S(1)} %collective-permute-done.mine), channel_id=1, source_target_pairs={{0,2},{2,0},{4,6},{6,4},{8,10},{10,8},{12,14},{14,12},{16,18},{18,... | collective-permute-start | bytes 2654216 | tf_op jit(solution)/shard_map/ppermute | solution.py:1059
  24.6 71.9 %collective-permute-start.3 = (bf16[384,1536]{1,0:T(8,128)(2,1)S(1)}, bf16[384,1536]{1,0:T(8,128)(2,1)}, u32[]{:S(2)}, u32[]{:S(2)}) collective-permute-start(bf16[384,1536]{1,0:T(8,128)(2,1)S(1)} %constant_dynamic-slice_fusion.1), channel_id=1, source_target_pairs={{0,1},{1,0},{2,3},{3,2},{4,5},{5,4},{6,7},{7,6},{8,9},{9,8},{10,11... | collective-permute-start | bytes 3538952 | tf_op jit(solution)/shard_map/ppermute | solution.py:1174
  26.4 70.1 %collective-permute-start.4 = (bf16[1536,384]{1,0:T(8,128)(2,1)S(1)}, bf16[1536,384]{1,0:T(8,128)(2,1)}, u32[]{:S(2)}, u32[]{:S(2)}) collective-permute-start(bf16[1536,384]{1,0:T(8,128)(2,1)S(1)} %constant_dynamic-slice_fusion), channel_id=1, source_target_pairs={{0,1},{1,0},{2,3},{3,2},{4,5},{5,4},{6,7},{7,6},{8,9},{9,8},{10,11... | collective-permute-start | bytes 3538952 | tf_op jit(solution)/shard_map/ppermute | solution.py:1174
  26.7 69.8 %collective-permute-start.5 = (bf16[384,768]{1,0:T(8,128)(2,1)}, bf16[384,768]{1,0:T(8,128)(2,1)}, u32[]{:S(2)}, u32[]{:S(2)}) collective-permute-start(bf16[384,768]{1,0:T(8,128)(2,1)} %proj_own.3), channel_id=1, source_target_pairs={{0,1},{1,0},{2,3},{3,2},{4,5},{5,4},{6,7},{7,6},{8,9},{9,8},{10,11... | collective-permute-start | bytes 1769480 | tf_op jit(solution)/shard_map/ppermute | solution.py:1174
  96.5 13.8 %collective-permute-start.6 = (bf16[384,1536]{1,0:T(8,128)(2,1)}, bf16[384,1536]{1,0:T(8,128)(2,1)S(1)}, u32[]{:S(2)}, u32[]{:S(2)}) collective-permute-start(bf16[384,1536]{1,0:T(8,128)(2,1)} %collective-permute-done.3.one_b), channel_id=1, source_target_pairs={{0,2},{2,0},{4,6},{6,4},{8,10},{10,8},{12,14},{14,12},{16,18},{18,... | collective-permute-start | bytes 3538952 | tf_op jit(solution)/shard_map/ppermute | solution.py:1059
  96.6 13.8 %collective-permute-start.8 = (bf16[1536,384]{1,0:T(8,128)(2,1)}, bf16[1536,384]{1,0:T(8,128)(2,1)}, u32[]{:S(2)}, u32[]{:S(2)}) collective-permute-start(bf16[1536,384]{1,0:T(8,128)(2,1)} %collective-permute-done.4.two_b), channel_id=1, source_target_pairs={{0,2},{2,0},{4,6},{6,4},{8,10},{10,8},{12,14},{14,12},{16,18},{18,... | collective-permute-start | bytes 3538952 | tf_op jit(solution)/shard_map/ppermute | solution.py:1059
  97.1 13.2 %collective-permute-start.7 = (bf16[1536]{0:T(1024)(128)(2,1)S(1)}, bf16[1536]{0:T(1024)(128)(2,1)S(1)}, u32[]{:S(2)}, u32[]{:S(2)}) collective-permute-start(bf16[1536]{0:T(1024)(128)(2,1)S(1)} %copy-done.33), channel_id=1, source_target_pairs={{0,1},{1,0},{2,3},{3,2},{4,5},{5,4},{6,7},{7,6},{8,9},{9,8},{10,11... | collective-permute-start | bytes 9224 | tf_op jit(solution)/shard_map/ppermute | solution.py:1174
  187.5 18.1 %collective-permute-start.10 = (bf16[2,2,2,2,192,384]{5,4,3,2,1,0:T(8,128)(2,1)}, bf16[2,2,2,2,192,384]{5,4,3,2,1,0:T(8,128)(2,1)}, u32[]{:S(2)}, u32[]{:S(2)}) collective-permute-start(bf16[2,2,2,2,192,384]{5,4,3,2,1,0:T(8,128)(2,1)} %bitcast.148), channel_id=1, source_target_pairs={{0,2},{2,0},{4,6},{6,4},{8,10},{10,8},{12,14},{14,12},{16,18},{18,... | collective-permute-start | bytes 7077896 | tf_op jit(solution)/shard_map/ppermute | solution.py:1059
  187.6 18.0 %collective-permute-start.9 = (bf16[2,2,2,2,48,1536]{5,4,3,2,1,0:T(8,128)(2,1)}, bf16[2,2,2,2,48,1536]{5,4,3,2,1,0:T(8,128)(2,1)S(1)}, u32[]{:S(2)}, u32[]{:S(2)}) collective-permute-start(bf16[2,2,2,2,48,1536]{5,4,3,2,1,0:T(8,128)(2,1)} %bitcast.147), channel_id=1, source_target_pairs={{0,2},{2,0},{4,6},{6,4},{8,10},{10,8},{12,14},{14,12},{16,18},{18,... | collective-permute-start | bytes 7077896 | tf_op jit(solution)/shard_map/ppermute | solution.py:1059
  210.3 32.5 %collective-permute-start.11 = (bf16[2,2,2,48,1536]{4,3,2,1,0:T(8,128)(2,1)}, bf16[2,2,2,48,1536]{4,3,2,1,0:T(8,128)(2,1)S(1)}, u32[]{:S(2)}, u32[]{:S(2)}) collective-permute-start(bf16[2,2,2,48,1536]{4,3,2,1,0:T(8,128)(2,1)} %fusion), channel_id=1, source_target_pairs={{0,1},{1,0},{2,3},{3,2},{4,5},{5,4},{6,7},{7,6},{8,9},{9,8},{10,11... | collective-permute-start | bytes 3538952 | tf_op jit(solution)/shard_map/ppermute | solution.py:1058
  212.1 30.8 %collective-permute-start.12 = (bf16[2,2,2,192,384]{4,3,2,1,0:T(8,128)(2,1)}, bf16[2,2,2,192,384]{4,3,2,1,0:T(8,128)(2,1)}, u32[]{:S(2)}, u32[]{:S(2)}) collective-permute-start(bf16[2,2,2,192,384]{4,3,2,1,0:T(8,128)(2,1)} %fusion.1), channel_id=1, source_target_pairs={{0,4},{2,6},{4,0},{6,2},{8,12},{10,14},{12,8},{14,10},{16,20},{18,... | collective-permute-start | bytes 3538952 | tf_op jit(solution)/shard_map/ppermute | solution.py:1059
  247.8 15.0 %collective-permute-start.13 = (bf16[2,2,48,1536]{3,2,1,0:T(8,128)(2,1)}, bf16[2,2,48,1536]{3,2,1,0:T(8,128)(2,1)}, u32[]{:S(2)}, u32[]{:S(2)}) collective-permute-start(bf16[2,2,48,1536]{3,2,1,0:T(8,128)(2,1)} %fusion.3), channel_id=1, source_target_pairs={{0,4},{2,6},{4,0},{6,2},{8,12},{10,14},{12,8},{14,10},{16,20},{18,... | collective-permute-start | bytes 1769480 | tf_op jit(solution)/shard_map/ppermute | solution.py:1059
  248.4 14.8 %collective-permute-start.14 = (bf16[2,2,192,384]{3,2,1,0:T(8,128)(2,1)}, bf16[2,2,192,384]{3,2,1,0:T(8,128)(2,1)}, u32[]{:S(2)}, u32[]{:S(2)}) collective-permute-start(bf16[2,2,192,384]{3,2,1,0:T(8,128)(2,1)} %fusion.2), channel_id=1, source_target_pairs={{0,8},{2,10},{4,12},{6,14},{8,0},{10,2},{12,4},{14,6},{16,24},{18,... | collective-permute-start | bytes 1769480 | tf_op jit(solution)/shard_map/ppermute | solution.py:1059
  267.2 13.8 %collective-permute-start.17 = (bf16[2,768,384]{2,1,0:T(8,128)(2,1)}, bf16[2,768,384]{2,1,0:T(8,128)(2,1)}, u32[]{:S(2)}, u32[]{:S(2)}) collective-permute-start(bf16[2,768,384]{2,1,0:T(8,128)(2,1)} %get-tuple-element.212), channel_id=1, source_target_pairs={{0,2},{2,0},{4,6},{6,4},{8,10},{10,8},{12,14},{14,12},{16,18},{18,... | collective-permute-start | bytes 3538952 | tf_op jit(solution)/shard_map/ppermute | solution.py:1059
  267.2 13.8 %collective-permute-start.15 = (bf16[2,48,1536]{2,1,0:T(8,128)(2,1)}, bf16[2,48,1536]{2,1,0:T(8,128)(2,1)S(1)}, u32[]{:S(2)}, u32[]{:S(2)}) collective-permute-start(bf16[2,48,1536]{2,1,0:T(8,128)(2,1)} %fusion.13), channel_id=1, source_target_pairs={{0,8},{2,10},{4,12},{6,14},{8,0},{10,2},{12,4},{14,6},{16,24},{18,... | collective-permute-start | bytes 884744 | tf_op jit(solution)/shard_map/ppermute | solution.py:1059
  268.8 12.1 %collective-permute-start.16 = (bf16[2,192,384]{2,1,0:T(8,128)(2,1)}, bf16[2,192,384]{2,1,0:T(8,128)(2,1)}, u32[]{:S(2)}, u32[]{:S(2)}) collective-permute-start(bf16[2,192,384]{2,1,0:T(8,128)(2,1)} %fusion.12), channel_id=1, source_target_pairs={{0,1},{1,0},{2,3},{3,2},{4,5},{5,4},{6,7},{7,6},{8,9},{9,8},{10,11... | collective-permute-start | bytes 884744 | tf_op jit(solution)/shard_map/ppermute | solution.py:1058
  287.3 24.8 %collective-permute-start.20 = (bf16[768,384]{1,0:T(8,128)(2,1)}, bf16[768,384]{1,0:T(8,128)(2,1)S(1)}, u32[]{:S(2)}, u32[]{:S(2)}) collective-permute-start(bf16[768,384]{1,0:T(8,128)(2,1)} %get-tuple-element.222), channel_id=1, source_target_pairs={{0,1},{1,0},{2,3},{3,2},{4,5},{5,4},{6,7},{7,6},{8,9},{9,8},{10,11... | collective-permute-start | bytes 1769480 | tf_op jit(solution)/shard_map/ppermute | solution.py:1058
  288.9 23.2 %collective-permute-start.18 = (bf16[48,1536]{1,0:T(8,128)(2,1)}, bf16[48,1536]{1,0:T(8,128)(2,1)S(1)}, u32[]{:S(2)}, u32[]{:S(2)}) collective-permute-start(bf16[48,1536]{1,0:T(8,128)(2,1)} %fusion.19), channel_id=1, source_target_pairs={{0,16},{2,18},{4,20},{6,22},{8,24},{10,26},{12,28},{14,30},{16,0},... | collective-permute-start | bytes 442376 | tf_op jit(solution)/shard_map/ppermute | solution.py:1059
  291.4 20.7 %collective-permute-start.19 = (bf16[192,384]{1,0:T(8,128)(2,1)}, bf16[192,384]{1,0:T(8,128)(2,1)}, u32[]{:S(2)}, u32[]{:S(2)}) collective-permute-start(bf16[192,384]{1,0:T(8,128)(2,1)} %fusion.18), channel_id=1, source_target_pairs={{0,16},{2,18},{4,20},{6,22},{8,24},{10,26},{12,28},{14,30},{16,0},... | collective-permute-start | bytes 442376 | tf_op jit(solution)/shard_map/ppermute | solution.py:1059
  316.2 21.3 %collective-permute-start.23 = (bf16[768,384]{1,0:T(8,128)(2,1)S(1)}, bf16[768,384]{1,0:T(8,128)(2,1)S(1)}, u32[]{:S(2)}, u32[]{:S(2)}) collective-permute-start(bf16[768,384]{1,0:T(8,128)(2,1)S(1)} %copy-done.21), channel_id=1, source_target_pairs={{0,1},{1,0},{2,3},{3,2},{4,5},{5,4},{6,7},{7,6},{8,9},{9,8},{10,11... | collective-permute-start | bytes 1769480 | tf_op jit(solution)/shard_map/ppermute | solution.py:1058
  316.8 20.7 %collective-permute-start.21 = (bf16[48,1536]{1,0:T(8,128)(2,1)S(1)}, bf16[48,1536]{1,0:T(8,128)(2,1)S(1)}, u32[]{:S(2)}, u32[]{:S(2)}) collective-permute-start(bf16[48,1536]{1,0:T(8,128)(2,1)S(1)} %fusion.17), channel_id=1, source_target_pairs={{0,16},{2,18},{4,20},{6,22},{8,24},{10,26},{12,28},{14,30},{16,0},... | collective-permute-start | bytes 442376 | tf_op jit(solution)/shard_map/ppermute | solution.py:1059
  319.4 18.2 %collective-permute-start.22 = (bf16[192,384]{1,0:T(8,128)(2,1)S(1)}, bf16[192,384]{1,0:T(8,128)(2,1)S(1)}, u32[]{:S(2)}, u32[]{:S(2)}) collective-permute-start(bf16[192,384]{1,0:T(8,128)(2,1)S(1)} %fusion.15), channel_id=1, source_target_pairs={{0,16},{2,18},{4,20},{6,22},{8,24},{10,26},{12,28},{14,30},{16,0},... | collective-permute-start | bytes 442376 | tf_op jit(solution)/shard_map/ppermute | solution.py:1059
  338.5 16.1 %collective-permute-start.26 = (bf16[384,768]{1,0:T(8,128)(2,1)S(1)}, bf16[384,768]{1,0:T(8,128)(2,1)S(1)}, u32[]{:S(2)}, u32[]{:S(2)}) collective-permute-start(bf16[384,768]{1,0:T(8,128)(2,1)S(1)} %dynamic-slice_bitcast_fusion), channel_id=1, source_target_pairs={{0,1},{1,0},{2,3},{3,2},{4,5},{5,4},{6,7},{7,6},{8,9},{9,8},{10,11... | collective-permute-start | bytes 1769480 | tf_op jit(solution)/shard_map/ppermute | solution.py:1058
  340.1 14.5 %collective-permute-start.24 = (bf16[2,48,1536]{2,1,0:T(8,128)(2,1)S(1)}, bf16[2,48,1536]{2,1,0:T(8,128)(2,1)S(1)}, u32[]{:S(2)}, u32[]{:S(2)}) collective-permute-start(bf16[2,48,1536]{2,1,0:T(8,128)(2,1)S(1)} %broadcast_select_fusion.5), channel_id=1, source_target_pairs={{0,8},{2,10},{4,12},{6,14},{8,0},{10,2},{12,4},{14,6},{16,24},{18,... | collective-permute-start | bytes 884744 | tf_op jit(solution)/shard_map/ppermute | solution.py:1059
  340.5 14.0 %collective-permute-start.25 = (bf16[2,192,384]{2,1,0:T(8,128)(2,1)S(1)}, bf16[2,192,384]{2,1,0:T(8,128)(2,1)S(1)}, u32[]{:S(2)}, u32[]{:S(2)}) collective-permute-start(bf16[2,192,384]{2,1,0:T(8,128)(2,1)S(1)} %broadcast_select_fusion.4), channel_id=1, source_target_pairs={{0,4},{2,6},{4,0},{6,2},{8,12},{10,14},{12,8},{14,10},{16,20},{18,... | collective-permute-start | bytes 884744 | tf_op jit(solution)/shard_map/ppermute | solution.py:1059
  354.9 16.6 %collective-permute-start.29 = (bf16[2,768,384]{2,1,0:T(8,128)(2,1)}, bf16[2,768,384]{2,1,0:T(8,128)(2,1)}, u32[]{:S(2)}, u32[]{:S(2)}) collective-permute-start(bf16[2,768,384]{2,1,0:T(8,128)(2,1)} %get-tuple-element.250), channel_id=1, source_target_pairs={{0,2},{2,0},{4,6},{6,4},{8,10},{10,8},{12,14},{14,12},{16,18},{18,... | collective-permute-start | bytes 3538952 | tf_op jit(solution)/shard_map/ppermute | solution.py:1059
  354.9 15.7 %collective-permute-start.27 = (bf16[2,2,48,1536]{3,2,1,0:T(8,128)(2,1)S(1)}, bf16[2,2,48,1536]{3,2,1,0:T(8,128)(2,1)S(1)}, u32[]{:S(2)}, u32[]{:S(2)}) collective-permute-start(bf16[2,2,48,1536]{3,2,1,0:T(8,128)(2,1)S(1)} %broadcast_select_fusion.3), channel_id=1, source_target_pairs={{0,4},{2,6},{4,0},{6,2},{8,12},{10,14},{12,8},{14,10},{16,20},{18,... | collective-permute-start | bytes 1769480 | tf_op jit(solution)/shard_map/ppermute | solution.py:1059
  355.6 15.5 %collective-permute-start.28 = (bf16[2,2,192,384]{3,2,1,0:T(8,128)(2,1)S(1)}, bf16[2,2,192,384]{3,2,1,0:T(8,128)(2,1)}, u32[]{:S(2)}, u32[]{:S(2)}) collective-permute-start(bf16[2,2,192,384]{3,2,1,0:T(8,128)(2,1)S(1)} %broadcast_select_fusion.2), channel_id=1, source_target_pairs={{0,8},{2,10},{4,12},{6,14},{8,0},{10,2},{12,4},{14,6},{16,24},{18,... | collective-permute-start | bytes 1769480 | tf_op jit(solution)/shard_map/ppermute | solution.py:1059
  377.4 18.0 %collective-permute-start.33 = (bf16[384,384]{1,0:T(8,128)(2,1)}, bf16[384,384]{1,0:T(8,128)(2,1)}, u32[]{:S(2)}, u32[]{:S(2)}) collective-permute-start(bf16[384,384]{1,0:T(8,128)(2,1)} %get-tuple-element.266), channel_id=1, source_target_pairs={{0,4},{2,6},{4,0},{6,2},{8,12},{10,14},{12,8},{14,10},{16,20},{18,... | collective-permute-start | bytes 884744 | tf_op jit(solution)/shard_map/ppermute | solution.py:1059
  378.5 16.9 %collective-permute-start.34 = (bf16[384,384]{1,0:T(8,128)(2,1)}, bf16[384,384]{1,0:T(8,128)(2,1)}, u32[]{:S(2)}, u32[]{:S(2)}) collective-permute-start(bf16[384,384]{1,0:T(8,128)(2,1)} %get-tuple-element.267), channel_id=1, source_target_pairs={{0,8},{2,10},{4,12},{6,14},{8,0},{10,2},{12,4},{14,6},{16,24},{18,... | collective-permute-start | bytes 884744 | tf_op jit(solution)/shard_map/ppermute | solution.py:1059
  (38 other events, 243.8 us)

commit v8 on v7

--- a/solution.py
+++ b/solution.py
@@ -903,7 +903,7 @@
     return plan + doubles[::-1]
 
 
-PARTS = 2
+PARTS = 3
 PART_ROWS = D // 2 // PARTS
 
 

time: 444 us -> 443 us (level)
  no operation moved by 1% of the time
where the time goes in v8:
time: 443 us; the launch traced here: 435 us
  Pallas kernels  346 us (78%)
  starting transfers between devices  33.3 us (8%)
  other arithmetic  31.2 us (7%)
  local copies, waits for them, and re-layouts  16.4 us (4%)
  waiting for transfers between devices  6.12 us (1%)
    pallas_call x1, Pallas kernels, feed(): pl.pallas_call(feed_kernel, grid_spec=pltpu.PrefetchScalarGridSpec(num_sc...  76.1 us
    pallas_call x2, Pallas kernels, attend(): pl.pallas_call(attend_own if first else attend_other, grid=(3, NWIN), in_...  67.1 us
    pallas_call x3, Pallas kernels, attend_back(): pl.pallas_call(lambda *refs: attend_back_kernel(first, *refs), grid_spec=...  61.2 us
    pallas_call x1, Pallas kernels, last_sums(): pl.pallas_call(lambda *refs: last_kernel(bits, plans, orders, *refs), in_...  32 us
    pallas_call x2, Pallas kernels, norm_grad(): pl.pallas_call(norm_grad_kernel, grid=(last - first, 2), in_specs=[block,...  27.3 us
    convert_element_type x13, other arithmetic, part(): return total.astype(BF)  25.5 us
    pallas_call x2, Pallas kernels, qkv_grad(): pl.pallas_call(qkv_grad_kernel, grid=(3,), in_specs=[SCALAR, pl.BlockSpec...  25 us
    ppermute x23, starting transfers between devices, exchange(): lax.ppermute(value, 'dp', [(i, i ^ bit) for i in range(lax.axis_size('dp'...  19.6 us
  transfers between devices with their start and end apart: 35, of which 5 were waited for; matrix products, arithmetic and copies ran while one was open for 2% of the time, Pallas kernels for 55%

profile of v8, /device:TPU:0, one launch (start us, length us, event | category | flops | bytes accessed | tf_op | source)
XLA Modules:
  0.0 435.2 jit_solution(7084983973883696282)
XLA Ops:
  1.9 3.0 collective-permute-start
  5.0 4.6 %shard_map.334.cot_t = bf16[768,2048]{1,0:T(8,128)(2,1)} custom-call(bf16[2048,768]{1,0:T(8,128)(2,1)} %cot.3), custom_call_target="tpu_custom_call" | custom-call | flops 1000000 | bytes 6000000 | tf_op jit(solution)/shard_map/pallas_call | solution.py:376
  10.2 8.7 %shard_map.333.x = bf16[3,5,256,768]{3,2,1,0:T(8,128)(2,1)} custom-call(s32[2]{0:T(128)} %pad_add_fusion.spot.refs_0_, bf16[4096,768]{1,0:T(8,128)(2,1)} %x.3, bf16[4096,768]{1,0:T(8,128)(2,1)} %x.3, bf16[4096,768]{1,0:T(8,128)(2,1)} %x.3, bf16[4096,768]{1,0:T(8,128)(2,1)} %x.3, bf16[4096,768]{1,0:T(8,128)(2,1)} %x.3, bf16[4096,768]{1,0:T(8,128)(2,1)} %x.3, ...), custom_call_target="tpu_custom_call" | custom-call | flops 660602880 | bytes 10000000 | tf_op jit(solution)/shard_map/pallas_call | solution.py:134
  21.0 3.6 collective-permute-done.mine
  24.6 1.7 collective-permute-start.3
  28.4 33.9 %shard_map.335 = (bf16[3,5,256,1152]{3,2,1,0:T(8,128)(2,1)}, bf16[3,5,6,224,256]{4,3,2,1,0:T(8,128)(2,1)}, bf16[3,5,256,384]{3,2,1,0:T(8,128)(2,1)}, bf16[768,38...) custom-call(bf16[3,5,256,768]{3,2,1,0:T(8,128)(2,1)} %shard_map.333.x, bf16[2,384]{1,0:T(2,128)(2,1)} %bias.3, ...), custom_call_target="tpu_custom_call" | custom-call | flops 15000000512 | bytes 45000000 | tf_op jit(solution)/shard_map/pallas_call | solution.py:297
  63.3 33.2 %shard_map.336 = (bf16[3,5,256,1152]{3,2,1,0:T(8,128)(2,1)}, bf16[3,5,6,224,256]{4,3,2,1,0:T(8,128)(2,1)}, bf16[3,5,256,384]{3,2,1,0:T(8,128)(2,1)}) custom-call(bf16[3,5,256,768]{3,2,1,0:T(8,128)(2,1)} %shard_map.333.x, bf16[2,384]{1,0:T(2,128)(2,1)} %collective-permute-done.1.bias, s32[2]{0:T(128)} %pad_add_fusion.spot.refs_0_, ...), custom_call_target="tpu_custom_call" | custom-call | flops 15000000512 | bytes 45000000 | tf_op jit(solution)/shard_map/pallas_call | solution.py:297
  97.4 12.9 %shard_map.337 = (bf16[2048,768]{1,0:T(8,128)(2,1)}, bf16[2048,768]{1,0:T(8,128)(2,1)}, bf16[768,2048]{1,0:T(8,128)(2,1)}, bf16[2048,768]{1,0:T(8,128)(2,1)}) custom-call(s32[2]{0:T(128)} %pad_add_fusion.spot.refs_0_, bf16[3,5,256,384]{3,2,1,0:T(8,128)(2,1)} %get-tuple-element.153.own_a.own_b, bf16[3,5,256,384]{3,2,1,0:T(8,128)(2,1)} %get-tuple-element.153.own_a.own_b, ...), custom_call_target="tpu_custom_call" | custom-call | flops 3000000000 | bytes 25000000 | tf_op jit(solution)/shard_map/pallas_call | solution.py:343
  111.4 76.1 %shard_map.338 = (bf16[2048,768]{1,0:T(8,128)(2,1)}, bf16[2048,768]{1,0:T(8,128)(2,1)}, bf16[2,384,1536]{2,1,0:T(8,128)(2,1)}, bf16[2,384,1536]{2,1,0:T(8,128)(2...) custom-call(s32[2]{0:T(128)} %pad_add_fusion.spot.refs_0_, ...), custom_call_target="tpu_custom_call" | custom-call | flops 57999998976 | bytes 60000000 | tf_op jit(solution)/shard_map/pallas_call | solution.py:473
  189.4 16.2 %shard_map.339 = (bf16[2048,768]{1,0:T(8,128)(2,1)}, bf16[2048,768]{1,0:T(8,128)(2,1)}, bf16[2048,768]{1,0:T(8,128)(2,1)}, bf16[768,384]{1,0:T(8,128)(2,1)}, bf16[768,384]{1,0:T(8,128)(2,1)}, /*index=5*/f32[8,768]{1,0:T(8,128)}) custom-call(bf16[2048,768]{1,0:T(8,128)(2,1)} %get-tuple-element.171.middle, bf16[2048,768]{1,0:T(8,128)(2,1)} %get-tuple-element.172.forward, ...), custom_call_target="tpu_custom_call" | custom-call | flops 5000000000 | bytes 40000000 | tf_op jit(solution)/shard_map/pallas_call | solution.py:563
  207.7 2.6 fusion.1
  210.3 1.8 collective-permute-start.11
  213.5 29.3 %shard_map.340 = (bf16[3,5,256,2304]{3,2,1,0:T(8,128)(2,1)}, f32[80,128]{1,0:T(8,128)}, f32[8,1152]{1,0:T(8,128)}) custom-call(s32[2]{0:T(128)} %pad_add_fusion.spot.refs_0_, bf16[3,5,256,1152]{3,2,1,0:T(8,128)(2,1)} %get-tuple-element.189.refs_1_, bf16[3,5,6,224,256]{4,3,2,1,0:T(8,128)(2,1)} %get-tuple-element.190.refs_2_, ...), custom_call_target="tpu_custom_call" | custom-call | flops 20000000000 | bytes 45000000 | tf_op jit(solution)/shard_map/pallas_call | solution.py:703
  242.8 2.5 fusion.3
  245.4 2.5 fusion.2
  250.0 12.5 %shard_map.341 = (bf16[2,768,384]{2,1,0:T(8,128)(2,1)}, bf16[2,768,384]{2,1,0:T(8,128)(2,1)}) custom-call(s32[2]{0:T(128)} %pad_add_fusion.spot.refs_0_, bf16[768,3840]{1,0:T(8,128)(2,1)} %get-tuple-element.177.xt, bf16[3840,2304]{1,0:T(8,128)(2,1)} %bitcast.126, bf16[768,384]{1,0:T(8,128)(2,1)} %get-tuple-element.198.proj), custom_call_target="tpu_custom_call" | custom-call | flops 7000000000 | bytes 16000000 | tf_op jit(solution)/shard_map/pallas_call | solution.py:791
  263.2 1.9 fusion.13
  265.1 2.1 fusion.12
  269.3 11.6 %shard_map.342 = (bf16[3,5,256,2304]{3,2,1,0:T(8,128)(2,1)}, f32[80,128]{1,0:T(8,128)}, f32[8,1152]{1,0:T(8,128)}) custom-call(s32[2]{0:T(128)} %pad_add_fusion.spot.refs_0_, bf16[3,5,256,1152]{3,2,1,0:T(8,128)(2,1)} %get-tuple-element.178.refs_1_, bf16[3,5,6,224,256]{4,3,2,1,0:T(8,128)(2,1)} %get-tuple-element.179.refs_2_, ...), custom_call_target="tpu_custom_call", output_to_operand_aliasing={{0}: (8, {})} | custom-call | flops 6666666496 | bytes 15000000 | tf_op jit(solution)/shard_map/pallas_call | solution.py:703
  281.0 2.5 fusion.5
  283.6 2.0 fusion.18
  285.5 1.8 fusion.19
  288.9 2.6 collective-permute-start.18
  291.8 20.3 %shard_map.343 = (bf16[3,5,256,2304]{3,2,1,0:T(8,128)(2,1)}, f32[80,128]{1,0:T(8,128)}, f32[8,1152]{1,0:T(8,128)}) custom-call(s32[2]{0:T(128)} %pad_add_fusion.spot.refs_0_, bf16[3,5,256,1152]{3,2,1,0:T(8,128)(2,1)} %get-tuple-element.178.refs_1_, bf16[3,5,6,224,256]{4,3,2,1,0:T(8,128)(2,1)} %get-tuple-element.179.refs_2_, ...), custom_call_target="tpu_custom_call", output_to_operand_aliasing={{0}: (8, {})} | custom-call | flops 13333332992 | bytes 30000000 | tf_op jit(solution)/shard_map/pallas_call | solution.py:703
  316.8 2.6 collective-permute-start.21
  319.7 16.7 %shard_map.344.refs_0_ = bf16[3,1024,768]{2,1,0:T(8,128)(2,1)} custom-call(bf16[3,5,256,2304]{3,2,1,0:T(8,128)(2,1)} %get-tuple-element.247.d, bf16[3,768,384]{2,1,0:T(8,128)(2,1)} %weights_own.3, s32[2]{0:T(128)} %pad_add_fusion.spot.refs_0_, bf16[3,384,384]{2,1,0:T(8,128)(2,1)} %copy-done.19, bf16[3,384,384]{2,1,0:T(8,128)(2,1)} %copy-done.20, ...), custom_call_target="tpu_custom_call" | custom-call | flops 9333332992 | bytes 20000000 | tf_op jit(solution)/shard_map/pallas_call | solution.py:756
  342.0 12.5 %shard_map.345 = (bf16[2,768,384]{2,1,0:T(8,128)(2,1)}, bf16[2,768,384]{2,1,0:T(8,128)(2,1)}) custom-call(s32[2]{0:T(128)} %pad_add_fusion.spot.refs_0_, bf16[768,3840]{1,0:T(8,128)(2,1)} %get-tuple-element.177.xt, bf16[3840,2304]{1,0:T(8,128)(2,1)} %bitcast.127, bf16[768,384]{1,0:T(8,128)(2,1)} %get-tuple-element.236.proj), custom_call_target="tpu_custom_call" | custom-call | flops 7000000000 | bytes 16000000 | tf_op jit(solution)/shard_map/pallas_call | solution.py:791
  358.7 10.6 %shard_map.346.up_a.up_b = bf16[3,1024,768]{2,1,0:T(8,128)(2,1)} custom-call(bf16[3,5,256,2304]{3,2,1,0:T(8,128)(2,1)} %get-tuple-element.247.d, bf16[3,768,384]{2,1,0:T(8,128)(2,1)} %weights_own.3, s32[2]{0:T(128)} %pad_add_fusion.spot.refs_0_, bf16[3,384,384]{2,1,0:T(8,128)(2,1)} %copy-done.19, ...), custom_call_target="tpu_custom_call", output_to_operand_aliasing={{}: (6, {})} | custom-call | flops 4666666496 | bytes 10000000 | tf_op jit(solution)/shard_map/pallas_call | solution.py:756
  375.3 2.1 fusion.10
  380.1 15.2 %shard_map.347 = (bf16[2048,768]{1,0:T(8,128)(2,1)}, f32[8,768]{1,0:T(8,128)}, f32[2,384,1536]{2,1,0:T(8,128)}, f32[1536,768]{1,0:T(8,128)}) custom-call(s32[2]{0:T(128)} %pad_add_fusion.spot.refs_0_, bf16[4096,768]{1,0:T(8,128)(2,1)} %x.3, bf16[2048,768]{1,0:T(8,128)(2,1)} %get-tuple-element.176.middle_grad, bf16[3,1024,768]{2,1,0:T(8,128)(2,1)} %shard_map.346.up_a.up_b, ...), custom_call_target="tpu_custom_call" | custom-call | flops 100000000 | bytes 35000000 | tf_op jit(solution)/shard_map/pallas_call | solution.py:850
  397.1 32.0 %shard_map.348 = (bf16[4,768,384]{2,1,0:T(8,128)(2,1)S(1)}, f32[24,768]{1,0:T(8,128)S(1)}, f32[56,128]{1,0:T(8,128)S(1)}) custom-call(bf16[384,384]{1,0:T(8,128)(2,1)S(1)} %get-tuple-element.293.refs_0_, bf16[384,384]{1,0:T(8,128)(2,1)S(1)} %get-tuple-element.292.refs_1_, f32[8,768]{1,0:T(8,128)S(1)} %copy-done.8, f32[8,768]{1,0:T(8,128)S(1)} %copy-done.7, ...), custom_call_target="tpu_custom_call" | custom-call | tf_op jit(solution)/shard_map/pallas_call | solution.py:1027
  429.1 2.0 slice_convert_fusion
  (163 shorter events, 49.7 us)
Async XLA Ops:
  1.9 22.7 %collective-permute-start = (bf16[3,384,384]{2,1,0:T(8,128)(2,1)S(1)}, bf16[3,384,384]{2,1,0:T(8,128)(2,1)S(1)}, u32[]{:S(2)}, u32[]{:S(2)}) collective-permute-start(bf16[3,384,384]{2,1,0:T(8,128)(2,1)S(1)} %constant_dynamic-slice_fusion.2), channel_id=1, source_target_pairs={{0,1},{1,0},{2,3},{3,2},{4,5},{5,4},{6,7},{7,6},{8,9},{9,8},{10,11... | collective-permute-start | bytes 2654216 | tf_op jit(solution)/shard_map/ppermute | solution.py:1174
  5.0 57.4 %collective-permute-start.1 = (bf16[2,384]{1,0:T(2,128)(2,1)}, bf16[2,384]{1,0:T(2,128)(2,1)}, u32[]{:S(2)}, u32[]{:S(2)}) collective-permute-start(bf16[2,384]{1,0:T(2,128)(2,1)} %bias.3), channel_id=1, source_target_pairs={{0,1},{1,0},{2,3},{3,2},{4,5},{5,4},{6,7},{7,6},{8,9},{9,8},{10,11... | collective-permute-start | bytes 4616 | tf_op jit(solution)/shard_map/ppermute | solution.py:1174
  24.6 37.7 %collective-permute-start.2 = (bf16[3,384,384]{2,1,0:T(8,128)(2,1)S(1)}, bf16[3,384,384]{2,1,0:T(8,128)(2,1)S(1)}, u32[]{:S(2)}, u32[]{:S(2)}) collective-permute-start(bf16[3,384,384]{2,1,0:T(8,128)(2,1)S(1)} %collective-permute-done.mine), channel_id=1, source_target_pairs={{0,2},{2,0},{4,6},{6,4},{8,10},{10,8},{12,14},{14,12},{16,18},{18,... | collective-permute-start | bytes 2654216 | tf_op jit(solution)/shard_map/ppermute | solution.py:1059
  24.6 71.9 %collective-permute-start.3 = (bf16[384,1536]{1,0:T(8,128)(2,1)S(1)}, bf16[384,1536]{1,0:T(8,128)(2,1)}, u32[]{:S(2)}, u32[]{:S(2)}) collective-permute-start(bf16[384,1536]{1,0:T(8,128)(2,1)S(1)} %constant_dynamic-slice_fusion.1), channel_id=1, source_target_pairs={{0,1},{1,0},{2,3},{3,2},{4,5},{5,4},{6,7},{7,6},{8,9},{9,8},{10,11... | collective-permute-start | bytes 3538952 | tf_op jit(solution)/shard_map/ppermute | solution.py:1174
  26.4 70.1 %collective-permute-start.4 = (bf16[1536,384]{1,0:T(8,128)(2,1)S(1)}, bf16[1536,384]{1,0:T(8,128)(2,1)}, u32[]{:S(2)}, u32[]{:S(2)}) collective-permute-start(bf16[1536,384]{1,0:T(8,128)(2,1)S(1)} %constant_dynamic-slice_fusion), channel_id=1, source_target_pairs={{0,1},{1,0},{2,3},{3,2},{4,5},{5,4},{6,7},{7,6},{8,9},{9,8},{10,11... | collective-permute-start | bytes 3538952 | tf_op jit(solution)/shard_map/ppermute | solution.py:1174
  26.7 69.8 %collective-permute-start.5 = (bf16[384,768]{1,0:T(8,128)(2,1)}, bf16[384,768]{1,0:T(8,128)(2,1)}, u32[]{:S(2)}, u32[]{:S(2)}) collective-permute-start(bf16[384,768]{1,0:T(8,128)(2,1)} %proj_own.3), channel_id=1, source_target_pairs={{0,1},{1,0},{2,3},{3,2},{4,5},{5,4},{6,7},{7,6},{8,9},{9,8},{10,11... | collective-permute-start | bytes 1769480 | tf_op jit(solution)/shard_map/ppermute | solution.py:1174
  96.5 13.8 %collective-permute-start.6 = (bf16[384,1536]{1,0:T(8,128)(2,1)}, bf16[384,1536]{1,0:T(8,128)(2,1)S(1)}, u32[]{:S(2)}, u32[]{:S(2)}) collective-permute-start(bf16[384,1536]{1,0:T(8,128)(2,1)} %collective-permute-done.3.one_b), channel_id=1, source_target_pairs={{0,2},{2,0},{4,6},{6,4},{8,10},{10,8},{12,14},{14,12},{16,18},{18,... | collective-permute-start | bytes 3538952 | tf_op jit(solution)/shard_map/ppermute | solution.py:1059
  96.6 13.8 %collective-permute-start.8 = (bf16[1536,384]{1,0:T(8,128)(2,1)}, bf16[1536,384]{1,0:T(8,128)(2,1)}, u32[]{:S(2)}, u32[]{:S(2)}) collective-permute-start(bf16[1536,384]{1,0:T(8,128)(2,1)} %collective-permute-done.4.two_b), channel_id=1, source_target_pairs={{0,2},{2,0},{4,6},{6,4},{8,10},{10,8},{12,14},{14,12},{16,18},{18,... | collective-permute-start | bytes 3538952 | tf_op jit(solution)/shard_map/ppermute | solution.py:1059
  97.1 13.2 %collective-permute-start.7 = (bf16[1536]{0:T(1024)(128)(2,1)S(1)}, bf16[1536]{0:T(1024)(128)(2,1)S(1)}, u32[]{:S(2)}, u32[]{:S(2)}) collective-permute-start(bf16[1536]{0:T(1024)(128)(2,1)S(1)} %copy-done.33), channel_id=1, source_target_pairs={{0,1},{1,0},{2,3},{3,2},{4,5},{5,4},{6,7},{7,6},{8,9},{9,8},{10,11... | collective-permute-start | bytes 9224 | tf_op jit(solution)/shard_map/ppermute | solution.py:1174
  187.5 18.1 %collective-permute-start.10 = (bf16[2,2,2,2,192,384]{5,4,3,2,1,0:T(8,128)(2,1)}, bf16[2,2,2,2,192,384]{5,4,3,2,1,0:T(8,128)(2,1)}, u32[]{:S(2)}, u32[]{:S(2)}) collective-permute-start(bf16[2,2,2,2,192,384]{5,4,3,2,1,0:T(8,128)(2,1)} %bitcast.148), channel_id=1, source_target_pairs={{0,2},{2,0},{4,6},{6,4},{8,10},{10,8},{12,14},{14,12},{16,18},{18,... | collective-permute-start | bytes 7077896 | tf_op jit(solution)/shard_map/ppermute | solution.py:1059
  187.6 18.0 %collective-permute-start.9 = (bf16[2,2,2,2,48,1536]{5,4,3,2,1,0:T(8,128)(2,1)}, bf16[2,2,2,2,48,1536]{5,4,3,2,1,0:T(8,128)(2,1)S(1)}, u32[]{:S(2)}, u32[]{:S(2)}) collective-permute-start(bf16[2,2,2,2,48,1536]{5,4,3,2,1,0:T(8,128)(2,1)} %bitcast.147), channel_id=1, source_target_pairs={{0,2},{2,0},{4,6},{6,4},{8,10},{10,8},{12,14},{14,12},{16,18},{18,... | collective-permute-start | bytes 7077896 | tf_op jit(solution)/shard_map/ppermute | solution.py:1059
  210.3 32.5 %collective-permute-start.11 = (bf16[2,2,2,48,1536]{4,3,2,1,0:T(8,128)(2,1)}, bf16[2,2,2,48,1536]{4,3,2,1,0:T(8,128)(2,1)S(1)}, u32[]{:S(2)}, u32[]{:S(2)}) collective-permute-start(bf16[2,2,2,48,1536]{4,3,2,1,0:T(8,128)(2,1)} %fusion), channel_id=1, source_target_pairs={{0,1},{1,0},{2,3},{3,2},{4,5},{5,4},{6,7},{7,6},{8,9},{9,8},{10,11... | collective-permute-start | bytes 3538952 | tf_op jit(solution)/shard_map/ppermute | solution.py:1058
  212.1 30.8 %collective-permute-start.12 = (bf16[2,2,2,192,384]{4,3,2,1,0:T(8,128)(2,1)}, bf16[2,2,2,192,384]{4,3,2,1,0:T(8,128)(2,1)}, u32[]{:S(2)}, u32[]{:S(2)}) collective-permute-start(bf16[2,2,2,192,384]{4,3,2,1,0:T(8,128)(2,1)} %fusion.1), channel_id=1, source_target_pairs={{0,4},{2,6},{4,0},{6,2},{8,12},{10,14},{12,8},{14,10},{16,20},{18,... | collective-permute-start | bytes 3538952 | tf_op jit(solution)/shard_map/ppermute | solution.py:1059
  247.8 15.0 %collective-permute-start.13 = (bf16[2,2,48,1536]{3,2,1,0:T(8,128)(2,1)}, bf16[2,2,48,1536]{3,2,1,0:T(8,128)(2,1)}, u32[]{:S(2)}, u32[]{:S(2)}) collective-permute-start(bf16[2,2,48,1536]{3,2,1,0:T(8,128)(2,1)} %fusion.3), channel_id=1, source_target_pairs={{0,4},{2,6},{4,0},{6,2},{8,12},{10,14},{12,8},{14,10},{16,20},{18,... | collective-permute-start | bytes 1769480 | tf_op jit(solution)/shard_map/ppermute | solution.py:1059
  248.4 14.8 %collective-permute-start.14 = (bf16[2,2,192,384]{3,2,1,0:T(8,128)(2,1)}, bf16[2,2,192,384]{3,2,1,0:T(8,128)(2,1)}, u32[]{:S(2)}, u32[]{:S(2)}) collective-permute-start(bf16[2,2,192,384]{3,2,1,0:T(8,128)(2,1)} %fusion.2), channel_id=1, source_target_pairs={{0,8},{2,10},{4,12},{6,14},{8,0},{10,2},{12,4},{14,6},{16,24},{18,... | collective-permute-start | bytes 1769480 | tf_op jit(solution)/shard_map/ppermute | solution.py:1059
  267.2 13.8 %collective-permute-start.17 = (bf16[2,768,384]{2,1,0:T(8,128)(2,1)}, bf16[2,768,384]{2,1,0:T(8,128)(2,1)}, u32[]{:S(2)}, u32[]{:S(2)}) collective-permute-start(bf16[2,768,384]{2,1,0:T(8,128)(2,1)} %get-tuple-element.212), channel_id=1, source_target_pairs={{0,2},{2,0},{4,6},{6,4},{8,10},{10,8},{12,14},{14,12},{16,18},{18,... | collective-permute-start | bytes 3538952 | tf_op jit(solution)/shard_map/ppermute | solution.py:1059
  267.2 13.8 %collective-permute-start.15 = (bf16[2,48,1536]{2,1,0:T(8,128)(2,1)}, bf16[2,48,1536]{2,1,0:T(8,128)(2,1)S(1)}, u32[]{:S(2)}, u32[]{:S(2)}) collective-permute-start(bf16[2,48,1536]{2,1,0:T(8,128)(2,1)} %fusion.13), channel_id=1, source_target_pairs={{0,8},{2,10},{4,12},{6,14},{8,0},{10,2},{12,4},{14,6},{16,24},{18,... | collective-permute-start | bytes 884744 | tf_op jit(solution)/shard_map/ppermute | solution.py:1059
  268.8 12.1 %collective-permute-start.16 = (bf16[2,192,384]{2,1,0:T(8,128)(2,1)}, bf16[2,192,384]{2,1,0:T(8,128)(2,1)}, u32[]{:S(2)}, u32[]{:S(2)}) collective-permute-start(bf16[2,192,384]{2,1,0:T(8,128)(2,1)} %fusion.12), channel_id=1, source_target_pairs={{0,1},{1,0},{2,3},{3,2},{4,5},{5,4},{6,7},{7,6},{8,9},{9,8},{10,11... | collective-permute-start | bytes 884744 | tf_op jit(solution)/shard_map/ppermute | solution.py:1058
  287.3 24.8 %collective-permute-start.20 = (bf16[768,384]{1,0:T(8,128)(2,1)}, bf16[768,384]{1,0:T(8,128)(2,1)S(1)}, u32[]{:S(2)}, u32[]{:S(2)}) collective-permute-start(bf16[768,384]{1,0:T(8,128)(2,1)} %get-tuple-element.222), channel_id=1, source_target_pairs={{0,1},{1,0},{2,3},{3,2},{4,5},{5,4},{6,7},{7,6},{8,9},{9,8},{10,11... | collective-permute-start | bytes 1769480 | tf_op jit(solution)/shard_map/ppermute | solution.py:1058
  288.9 23.2 %collective-permute-start.18 = (bf16[48,1536]{1,0:T(8,128)(2,1)}, bf16[48,1536]{1,0:T(8,128)(2,1)S(1)}, u32[]{:S(2)}, u32[]{:S(2)}) collective-permute-start(bf16[48,1536]{1,0:T(8,128)(2,1)} %fusion.19), channel_id=1, source_target_pairs={{0,16},{2,18},{4,20},{6,22},{8,24},{10,26},{12,28},{14,30},{16,0},... | collective-permute-start | bytes 442376 | tf_op jit(solution)/shard_map/ppermute | solution.py:1059
  291.4 20.7 %collective-permute-start.19 = (bf16[192,384]{1,0:T(8,128)(2,1)}, bf16[192,384]{1,0:T(8,128)(2,1)}, u32[]{:S(2)}, u32[]{:S(2)}) collective-permute-start(bf16[192,384]{1,0:T(8,128)(2,1)} %fusion.18), channel_id=1, source_target_pairs={{0,16},{2,18},{4,20},{6,22},{8,24},{10,26},{12,28},{14,30},{16,0},... | collective-permute-start | bytes 442376 | tf_op jit(solution)/shard_map/ppermute | solution.py:1059
  316.2 21.3 %collective-permute-start.23 = (bf16[768,384]{1,0:T(8,128)(2,1)S(1)}, bf16[768,384]{1,0:T(8,128)(2,1)S(1)}, u32[]{:S(2)}, u32[]{:S(2)}) collective-permute-start(bf16[768,384]{1,0:T(8,128)(2,1)S(1)} %copy-done.21), channel_id=1, source_target_pairs={{0,1},{1,0},{2,3},{3,2},{4,5},{5,4},{6,7},{7,6},{8,9},{9,8},{10,11... | collective-permute-start | bytes 1769480 | tf_op jit(solution)/shard_map/ppermute | solution.py:1058
  316.8 20.7 %collective-permute-start.21 = (bf16[48,1536]{1,0:T(8,128)(2,1)S(1)}, bf16[48,1536]{1,0:T(8,128)(2,1)S(1)}, u32[]{:S(2)}, u32[]{:S(2)}) collective-permute-start(bf16[48,1536]{1,0:T(8,128)(2,1)S(1)} %fusion.17), channel_id=1, source_target_pairs={{0,16},{2,18},{4,20},{6,22},{8,24},{10,26},{12,28},{14,30},{16,0},... | collective-permute-start | bytes 442376 | tf_op jit(solution)/shard_map/ppermute | solution.py:1059
  319.4 18.2 %collective-permute-start.22 = (bf16[192,384]{1,0:T(8,128)(2,1)S(1)}, bf16[192,384]{1,0:T(8,128)(2,1)S(1)}, u32[]{:S(2)}, u32[]{:S(2)}) collective-permute-start(bf16[192,384]{1,0:T(8,128)(2,1)S(1)} %fusion.15), channel_id=1, source_target_pairs={{0,16},{2,18},{4,20},{6,22},{8,24},{10,26},{12,28},{14,30},{16,0},... | collective-permute-start | bytes 442376 | tf_op jit(solution)/shard_map/ppermute | solution.py:1059
  338.5 16.1 %collective-permute-start.26 = (bf16[384,768]{1,0:T(8,128)(2,1)S(1)}, bf16[384,768]{1,0:T(8,128)(2,1)S(1)}, u32[]{:S(2)}, u32[]{:S(2)}) collective-permute-start(bf16[384,768]{1,0:T(8,128)(2,1)S(1)} %dynamic-slice_bitcast_fusion), channel_id=1, source_target_pairs={{0,1},{1,0},{2,3},{3,2},{4,5},{5,4},{6,7},{7,6},{8,9},{9,8},{10,11... | collective-permute-start | bytes 1769480 | tf_op jit(solution)/shard_map/ppermute | solution.py:1058
  340.1 14.5 %collective-permute-start.24 = (bf16[2,48,1536]{2,1,0:T(8,128)(2,1)S(1)}, bf16[2,48,1536]{2,1,0:T(8,128)(2,1)S(1)}, u32[]{:S(2)}, u32[]{:S(2)}) collective-permute-start(bf16[2,48,1536]{2,1,0:T(8,128)(2,1)S(1)} %broadcast_select_fusion.5), channel_id=1, source_target_pairs={{0,8},{2,10},{4,12},{6,14},{8,0},{10,2},{12,4},{14,6},{16,24},{18,... | collective-permute-start | bytes 884744 | tf_op jit(solution)/shard_map/ppermute | solution.py:1059
  340.5 14.0 %collective-permute-start.25 = (bf16[2,192,384]{2,1,0:T(8,128)(2,1)S(1)}, bf16[2,192,384]{2,1,0:T(8,128)(2,1)S(1)}, u32[]{:S(2)}, u32[]{:S(2)}) collective-permute-start(bf16[2,192,384]{2,1,0:T(8,128)(2,1)S(1)} %broadcast_select_fusion.4), channel_id=1, source_target_pairs={{0,4},{2,6},{4,0},{6,2},{8,12},{10,14},{12,8},{14,10},{16,20},{18,... | collective-permute-start | bytes 884744 | tf_op jit(solution)/shard_map/ppermute | solution.py:1059
  354.9 16.6 %collective-permute-start.29 = (bf16[2,768,384]{2,1,0:T(8,128)(2,1)}, bf16[2,768,384]{2,1,0:T(8,128)(2,1)}, u32[]{:S(2)}, u32[]{:S(2)}) collective-permute-start(bf16[2,768,384]{2,1,0:T(8,128)(2,1)} %get-tuple-element.250), channel_id=1, source_target_pairs={{0,2},{2,0},{4,6},{6,4},{8,10},{10,8},{12,14},{14,12},{16,18},{18,... | collective-permute-start | bytes 3538952 | tf_op jit(solution)/shard_map/ppermute | solution.py:1059
  354.9 15.7 %collective-permute-start.27 = (bf16[2,2,48,1536]{3,2,1,0:T(8,128)(2,1)S(1)}, bf16[2,2,48,1536]{3,2,1,0:T(8,128)(2,1)S(1)}, u32[]{:S(2)}, u32[]{:S(2)}) collective-permute-start(bf16[2,2,48,1536]{3,2,1,0:T(8,128)(2,1)S(1)} %broadcast_select_fusion.3), channel_id=1, source_target_pairs={{0,4},{2,6},{4,0},{6,2},{8,12},{10,14},{12,8},{14,10},{16,20},{18,... | collective-permute-start | bytes 1769480 | tf_op jit(solution)/shard_map/ppermute | solution.py:1059
  355.6 15.5 %collective-permute-start.28 = (bf16[2,2,192,384]{3,2,1,0:T(8,128)(2,1)S(1)}, bf16[2,2,192,384]{3,2,1,0:T(8,128)(2,1)}, u32[]{:S(2)}, u32[]{:S(2)}) collective-permute-start(bf16[2,2,192,384]{3,2,1,0:T(8,128)(2,1)S(1)} %broadcast_select_fusion.2), channel_id=1, source_target_pairs={{0,8},{2,10},{4,12},{6,14},{8,0},{10,2},{12,4},{14,6},{16,24},{18,... | collective-permute-start | bytes 1769480 | tf_op jit(solution)/shard_map/ppermute | solution.py:1059
  377.4 18.0 %collective-permute-start.33 = (bf16[384,384]{1,0:T(8,128)(2,1)}, bf16[384,384]{1,0:T(8,128)(2,1)}, u32[]{:S(2)}, u32[]{:S(2)}) collective-permute-start(bf16[384,384]{1,0:T(8,128)(2,1)} %get-tuple-element.266), channel_id=1, source_target_pairs={{0,4},{2,6},{4,0},{6,2},{8,12},{10,14},{12,8},{14,10},{16,20},{18,... | collective-permute-start | bytes 884744 | tf_op jit(solution)/shard_map/ppermute | solution.py:1059
  378.5 16.9 %collective-permute-start.34 = (bf16[384,384]{1,0:T(8,128)(2,1)}, bf16[384,384]{1,0:T(8,128)(2,1)}, u32[]{:S(2)}, u32[]{:S(2)}) collective-permute-start(bf16[384,384]{1,0:T(8,128)(2,1)} %get-tuple-element.267), channel_id=1, source_target_pairs={{0,8},{2,10},{4,12},{6,14},{8,0},{10,2},{12,4},{14,6},{16,24},{18,... | collective-permute-start | bytes 884744 | tf_op jit(solution)/shard_map/ppermute | solution.py:1059
  (38 other events, 243.8 us)
